TPU v7x, 32 devices: a whole 2x2x4 slice. The times are simulated.
32 devices in a mesh: dp: 2 (over x), row: 4 (over y, core), col: 4 (over z).
Axes of the slice: x: 2, y: 2, z: 4, core: 2. Of those that a mesh axis runs over, the one named last changes fastest.
Arguments:
- tokens: bfloat16 [4096, 4, 2048], P('col', 'dp', 'row'), may hold values from -6 to 6
- cotangent: bfloat16 [4096, 4, 2048], P('col', 'dp', 'row'), may hold values from -6 to 6
- block_labels: int32 [4, 4096], P('dp'), may hold values from 0 to 31, never falling along the last dimension, each value on 1 to 256 neighbouring positions
- adapter_selection: int32 [4], P('dp'), may hold values from 0 to 7
- adapter_scale: float32 [1], replicated, may hold values from 0.4 to 1.2
- attention_norm_gain: bfloat16 [2048], P('row'), may hold values from 0.099609375 to 1.8984375
- feedforward_norm_gain: bfloat16 [2048], P('row'), may hold values from 0.099609375 to 1.8984375
- query_weight: bfloat16 [2048, 2048], P('row', 'col'), may hold values from -0.125 to 0.125
- key_weight: bfloat16 [2048, 512], P('row', 'col'), may hold values from -0.125 to 0.125
- value_weight: bfloat16 [2048, 512], P('row', 'col'), may hold values from -0.125 to 0.125
- output_weight: bfloat16 [2048, 2048], P('col', 'row'), may hold values from -0.5 to 0.5
- gate_weight: bfloat16 [2048, 8192], P('row', 'col'), may hold values from -0.125 to 0.125
- up_weight: bfloat16 [2048, 8192], P('row', 'col'), may hold values from -0.125 to 0.125
- down_weight: bfloat16 [8192, 2048], P('col', 'row'), may hold values from -0.0625 to 0.0625
- query_first_factor: bfloat16 [2048, 128], P('row'), may hold values from -0.125 to 0.125
- query_second_factor: bfloat16 [128, 2048], P(None, 'col'), may hold values from -1.5 to 1.5
- key_first_factor: bfloat16 [2048, 128], P('row'), may hold values from -0.125 to 0.125
- key_second_factor: bfloat16 [128, 512], P(None, 'col'), may hold values from -1.5 to 1.5
- value_first_factor: bfloat16 [2048, 128], P('row'), may hold values from -0.125 to 0.125
- value_second_factor: bfloat16 [128, 512], P(None, 'col'), may hold values from -1.5 to 1.5
- output_first_factor: bfloat16 [2048, 128], P('col'), may hold values from -0.5 to 0.5
- output_second_factor: bfloat16 [128, 2048], P(None, 'row'), may hold values from -1.5 to 1.5
- gate_first_factor: bfloat16 [2048, 128], P('row'), may hold values from -0.125 to 0.125
- gate_second_factor: bfloat16 [128, 8192], P(None, 'col'), may hold values from -1.5 to 1.5
- up_first_factor: bfloat16 [2048, 128], P('row'), may hold values from -0.125 to 0.125
- up_second_factor: bfloat16 [128, 8192], P(None, 'col'), may hold values from -1.5 to 1.5
- down_first_factor: bfloat16 [8192, 128], P('col'), may hold values from -0.0625 to 0.0625
- down_second_factor: bfloat16 [128, 2048], P(None, 'row'), may hold values from -1.5 to 1.5
Outputs:
- mixed: bfloat16 [4096, 4, 2048], P('col', 'dp', 'row')
- grad_tokens: bfloat16 [4096, 4, 2048], P('col', 'dp', 'row')
- query_first_gradient: float32 [2048, 128], P('row')
- query_second_gradient: float32 [128, 2048], P(None, 'col')
- key_first_gradient: float32 [2048, 128], P('row')
- key_second_gradient: float32 [128, 512], P(None, 'col')
- value_first_gradient: float32 [2048, 128], P('row')
- value_second_gradient: float32 [128, 512], P(None, 'col')
- output_first_gradient: float32 [2048, 128], P('col')
- output_second_gradient: float32 [128, 2048], P(None, 'row')
- gate_first_gradient: float32 [2048, 128], P('row')
- gate_second_gradient: float32 [128, 8192], P(None, 'col')
- up_first_gradient: float32 [2048, 128], P('row')
- up_second_gradient: float32 [128, 8192], P(None, 'col')
- down_first_gradient: float32 [8192, 128], P('col')
- down_second_gradient: float32 [128, 2048], P(None, 'row')
Inputs may be any that keep to these rules, and one draw needn't show every extreme that they name: `block_labels`: in each sequence block numbers never fall; each block holds 1 to 256 positions, one exactly 256.
All inputs are finite; a program needn't handle non-finite values.
Results may differ from a plain program's by a relative error of at most 0.035.
Values may be sent and summed in bfloat16 or wider, within the bound.
No kernel may reach another device: no remote copies, remote signals or barrier semaphores. Data moves between devices by JAX's collectives and lax.ppermute only.
A program may use at most 704 MiB of HBM per device.

v0:
```python
from functools import reduce
import math

import jax
import jax.numpy as jnp
from jax import lax
from jax.sharding import PartitionSpec as P

D = 2048
HEAD_DIM = 64
RANK = 16


EPS = 1e-05
ROPE_BASE = 500000.0


def split_parts(values):
    high = values.astype(jnp.bfloat16)
    rest = (values - high.astype(jnp.float32)).astype(jnp.bfloat16)
    return (high, rest)


def over_rows(left_rows, right_rows):
    return lax.dot_general(
        left_rows, right_rows, (((0,), (0,)), ((), ())), preferred_element_type=jnp.float32
    )


def transpose_matmul(left_rows, right_rows):
    if left_rows.dtype == jnp.float32:
        high, rest = split_parts(left_rows)
        return over_rows(high, right_rows) + over_rows(rest, right_rows)
    high, rest = split_parts(right_rows)
    return over_rows(left_rows, high) + over_rows(left_rows, rest)


def against_rows(left_rows, right_rows):
    return lax.dot_general(
        left_rows, right_rows, (((1,), (1,)), ((), ())), preferred_element_type=jnp.float32
    )


def split_dot(values, matrix):
    high, rest = split_parts(values)
    return jnp.dot(high, matrix, preferred_element_type=jnp.float32) + jnp.dot(
        rest, matrix, preferred_element_type=jnp.float32
    )


def split_against(values, matrix):
    high, rest = split_parts(values)
    return against_rows(high, matrix) + against_rows(rest, matrix)


def gather_columns(values):
    gathered = lax.all_gather(values, "col", axis=0, tiled=True)
    return gathered.reshape(-1, gathered.shape[-1])


def gather_rows(values):
    gathered = lax.all_gather(values, "row", axis=0, tiled=True)
    return gathered.reshape(-1, gathered.shape[-1])


def build_term(input_rows, weight_matrix, reversed_order, adapter_factor_pairs, adapter_factor):

    def row_terms(first_row, row_count):
        if reversed_order:
            main_portion = against_rows(input_rows, weight_matrix)
        else:
            main_portion = jnp.dot(input_rows, weight_matrix, preferred_element_type=jnp.float32)
        extras = []
        for small, other in adapter_factor_pairs:
            if reversed_order:
                extras.append(split_against(small, other))
            else:
                extras.append(split_dot(small, other))
        if reversed_order:
            adapter_portion = reduce(jnp.add, extras)
        else:
            adapter_portion = jnp.concatenate(extras, axis=1)
        return main_portion + adapter_factor * adapter_portion

    return row_terms


def sum_over_rows(row_terms, row_grand_total):
    return lax.psum_scatter(
        row_terms(jnp.int32(0), row_grand_total // lax.axis_size("row") * lax.axis_size("row")),
        "row",
        scatter_dimension=0,
        tiled=True,
    )


def sum_over_cols(row_terms, row_grand_total):
    return lax.psum_scatter(
        row_terms(jnp.int32(0), row_grand_total // lax.axis_size("col") * lax.axis_size("col")),
        "col",
        scatter_dimension=0,
        tiled=True,
    )


def row_total(values):
    return lax.psum(values, "row")


def norm_forward(residual, norm_gain):
    squares = row_total(jnp.sum(residual * residual, axis=-1))
    inverse = lax.rsqrt(squares / D + EPS)[..., None]
    return (residual * inverse * norm_gain.astype(jnp.float32), inverse)


def norm_backward(residual, norm_gain, inverse, upstream):
    scaled = upstream * norm_gain.astype(jnp.float32)
    weighted = row_total(jnp.sum(scaled * residual, axis=-1))[..., None]
    return inverse * scaled - residual * inverse**3 * weighted / D


def rope_tables(row_offset, row_count, head_dim):
    half_dim = head_dim // 2
    positions = row_offset + jnp.arange(row_count)
    frequency = ROPE_BASE ** (-(jnp.arange(half_dim).astype(jnp.float32) * 2.0) / head_dim)
    angles = positions.astype(jnp.float32)[:, None] * frequency[None, :]
    cosine = jnp.concatenate([jnp.cos(angles), jnp.cos(angles)], axis=-1)
    sine_table = jnp.concatenate([jnp.sin(angles), jnp.sin(angles)], axis=-1)
    return (cosine[:, None, None, :], sine_table[:, None, None, :])


def rope_apply(values, cosine, sine_table):
    half_dim = values.shape[-1] // 2
    turned = jnp.concatenate([-values[..., half_dim:], values[..., :half_dim]], axis=-1)
    return values * cosine + turned * sine_table


def rope_back(upstream, cosine, sine_table):
    half_dim = upstream.shape[-1] // 2
    sine_part = upstream * sine_table
    turned = jnp.concatenate([sine_part[..., half_dim:], -sine_part[..., :half_dim]], axis=-1)
    return upstream * cosine + turned


def split_key_values(key_values, groups, head_dim):
    seq_len = key_values.shape[0]
    kv_width = groups * head_dim
    key_part = key_values[:, :kv_width].reshape(seq_len, groups, head_dim)
    value_part = key_values[:, kv_width:].reshape(seq_len, groups, head_dim)
    return (key_part, value_part)


def block_scores(block_queries, key_part, query_ids, key_ids, factor):
    scores = (
        jnp.einsum("qgre,kge->grqk", block_queries, key_part, preferred_element_type=jnp.float32)
        * factor
    )
    allowed = key_ids[None, :] <= query_ids[:, None]
    return jnp.where(allowed[None, None], scores, -1e30)


def attend_sequence(seq_queries, seq_key_values, seq_ids, row_offset, groups, factor):
    part_rows, heads_dev, head_dim = seq_queries.shape
    repeat = heads_dev // groups
    query_rows = math.gcd(part_rows, 512)
    block_count = part_rows // query_rows
    key_part, value_part = split_key_values(seq_key_values, groups, head_dim)
    grouped = seq_queries.reshape(block_count, query_rows, groups, repeat, head_dim)
    offsets = row_offset + query_rows * jnp.arange(block_count)

    def one_block(block_item):
        block_queries, offset = block_item
        query_ids = lax.dynamic_slice_in_dim(seq_ids, offset, query_rows, 0)
        scores = block_scores(block_queries, key_part, query_ids, seq_ids, factor)
        row_peak = jnp.max(scores, axis=-1, keepdims=True)
        exponents = jnp.exp(scores - row_peak)
        row_sums = jnp.sum(exponents, axis=-1, keepdims=True)
        weight_set = (exponents / row_sums).astype(jnp.bfloat16)
        mixed = jnp.einsum(
            "grqk,kge->qgre", weight_set, value_part, preferred_element_type=jnp.float32
        )
        return (
            mixed.reshape(query_rows, heads_dev * head_dim),
            (row_peak + jnp.log(row_sums))[..., 0],
        )

    mixed, log_sums = lax.map(one_block, (grouped, offsets))
    return (mixed.reshape(part_rows, heads_dev * head_dim), log_sums)


def attend_sequence_back(
    seq_queries, seq_key_values, seq_ids, seq_grad, seq_log_sums, row_offset, groups, factor
):
    part_rows, heads_dev, head_dim = seq_queries.shape
    seq_len = seq_key_values.shape[0]
    repeat = heads_dev // groups
    query_rows = math.gcd(part_rows, 512)
    block_count = part_rows // query_rows
    key_part, value_part = split_key_values(seq_key_values, groups, head_dim)
    grouped = seq_queries.reshape(block_count, query_rows, groups, repeat, head_dim)
    grad_grouped = seq_grad.reshape(block_count, query_rows, groups, repeat, head_dim)
    offsets = row_offset + query_rows * jnp.arange(block_count)

    def one_block(running, block_item):
        key_grad, value_grad = running
        block_queries, block_grad, block_log, offset = block_item
        query_ids = lax.dynamic_slice_in_dim(seq_ids, offset, query_rows, 0)
        scores = block_scores(block_queries, key_part, query_ids, seq_ids, factor)
        probs_full = jnp.exp(scores - block_log[..., None])
        probs_low = probs_full.astype(jnp.bfloat16)
        from_values = jnp.einsum(
            "qgre,kge->grqk", block_grad, value_part, preferred_element_type=jnp.float32
        )
        row_delta = jnp.sum(probs_full * from_values, axis=-1, keepdims=True)
        score_grad = (probs_full * (from_values - row_delta)).astype(jnp.bfloat16)
        query_grad = (
            jnp.einsum("grqk,kge->qgre", score_grad, key_part, preferred_element_type=jnp.float32)
            * factor
        )
        key_grad = (
            key_grad
            + jnp.einsum(
                "grqk,qgre->kge", score_grad, block_queries, preferred_element_type=jnp.float32
            )
            * factor
        )
        value_grad = value_grad + jnp.einsum(
            "grqk,qgre->kge", probs_low, block_grad, preferred_element_type=jnp.float32
        )
        return ((key_grad, value_grad), query_grad.reshape(query_rows, heads_dev * head_dim))

    zero_keys = jnp.zeros((seq_len, groups, head_dim), jnp.float32)
    (key_grad, value_grad), query_grad = lax.scan(
        one_block, (zero_keys, zero_keys), (grouped, grad_grouped, seq_log_sums, offsets)
    )
    joined = jnp.concatenate(
        [key_grad.reshape(seq_len, -1), value_grad.reshape(seq_len, -1)], axis=-1
    )
    return (query_grad.reshape(part_rows, heads_dev * head_dim), joined)


def local(
    tokens,
    cotangent,
    block_labels,
    adapter_selection,
    adapter_scale,
    attention_norm_gain,
    feedforward_norm_gain,
    query_weight,
    key_weight,
    value_weight,
    output_weight,
    gate_weight,
    up_weight,
    down_weight,
    query_first_factor,
    query_second_factor,
    key_first_factor,
    key_second_factor,
    value_first_factor,
    value_second_factor,
    output_first_factor,
    output_second_factor,
    gate_first_factor,
    gate_second_factor,
    up_first_factor,
    up_second_factor,
    down_first_factor,
    down_second_factor,
):
    adapter_factor = adapter_scale[0]
    part_cols = tokens.shape[0]
    seq_dev = tokens.shape[1]
    seq_len = part_cols * lax.axis_size("col")
    part_rows = seq_len // lax.axis_size("row")
    row_grand_total = seq_len * seq_dev
    rank_cols = query_first_factor.shape[1]
    head_dim = HEAD_DIM
    width_q = query_weight.shape[1]
    width_kv = key_weight.shape[1]
    width_ff = gate_weight.shape[1]
    heads_dev = width_q // head_dim
    groups = width_kv // head_dim
    factor = head_dim ** (-0.5)
    row_offset = lax.axis_index("row") * part_rows
    column_owner = jnp.arange(rank_cols) // RANK
    selection_mask = (column_owner[None, :] == adapter_selection[:, None]).astype(jnp.float32)

    def masked(reduced_rows):
        return (reduced_rows.reshape(-1, seq_dev, rank_cols) * selection_mask[None]).reshape(
            reduced_rows.shape
        )

    joined_qkv = jnp.concatenate([query_weight, key_weight, value_weight], axis=1)
    joined_gate_up = jnp.concatenate([gate_weight, up_weight], axis=1)
    residual = tokens.astype(jnp.float32)
    normed, inverse_attn = norm_forward(residual, attention_norm_gain)
    normed_activations = gather_columns(normed.astype(jnp.bfloat16))
    reduced_query = masked(
        jnp.dot(normed_activations, query_first_factor, preferred_element_type=jnp.float32)
    )
    reduced_key = masked(
        jnp.dot(normed_activations, key_first_factor, preferred_element_type=jnp.float32)
    )
    reduced_value = masked(
        jnp.dot(normed_activations, value_first_factor, preferred_element_type=jnp.float32)
    )
    projected = sum_over_rows(
        build_term(
            normed_activations,
            joined_qkv,
            False,
            [
                (reduced_query, query_second_factor),
                (reduced_key, key_second_factor),
                (reduced_value, value_second_factor),
            ],
            adapter_factor,
        ),
        row_grand_total,
    )
    query_raw = projected[:, :width_q].reshape(part_rows, seq_dev, heads_dev, head_dim)
    key_raw = projected[:, width_q : width_q + width_kv].reshape(
        part_rows, seq_dev, groups, head_dim
    )
    value_raw = projected[:, width_q + width_kv :].reshape(part_rows, seq_dev, width_kv)
    cosine, sine_table = rope_tables(row_offset, part_rows, head_dim)
    queries = rope_apply(query_raw, cosine, sine_table).astype(jnp.bfloat16)
    key_rows = rope_apply(key_raw, cosine, sine_table).reshape(part_rows, seq_dev, width_kv)
    key_values = jnp.concatenate([key_rows, value_raw], axis=-1).astype(jnp.bfloat16)
    key_values_all = lax.all_gather(key_values, "row", axis=0, tiled=True)
    seq_queries = jnp.moveaxis(queries, 1, 0)
    seq_key_values = jnp.moveaxis(key_values_all, 1, 0)

    def forward_one(seq_item):
        return attend_sequence(seq_item[0], seq_item[1], seq_item[2], row_offset, groups, factor)

    heads_mixed, log_sums = lax.map(forward_one, (seq_queries, seq_key_values, block_labels))
    heads_out = jnp.moveaxis(heads_mixed, 0, 1).astype(jnp.bfloat16)
    head_outputs = gather_rows(heads_out)
    reduced_output = masked(
        jnp.dot(head_outputs, output_first_factor, preferred_element_type=jnp.float32)
    )
    attended_part = sum_over_cols(
        build_term(
            head_outputs,
            output_weight,
            False,
            [(reduced_output, output_second_factor)],
            adapter_factor,
        ),
        row_grand_total,
    )
    attended = residual + attended_part.reshape(residual.shape)

    def mlp_front(attended_now):
        normed_mlp, inverse_mlp = norm_forward(attended_now, feedforward_norm_gain)
        normed_feedforward = gather_columns(normed_mlp.astype(jnp.bfloat16))
        reduced_gate = masked(
            jnp.dot(normed_feedforward, gate_first_factor, preferred_element_type=jnp.float32)
        )
        reduced_up = masked(
            jnp.dot(normed_feedforward, up_first_factor, preferred_element_type=jnp.float32)
        )
        gate_up = sum_over_rows(
            build_term(
                normed_feedforward,
                joined_gate_up,
                False,
                [(reduced_gate, gate_second_factor), (reduced_up, up_second_factor)],
                adapter_factor,
            ),
            row_grand_total,
        )
        hidden = (jax.nn.silu(gate_up[:, :width_ff]) * gate_up[:, width_ff:]).astype(jnp.bfloat16)
        hidden_activations = gather_rows(hidden.reshape(part_rows, seq_dev, width_ff))
        reduced_down = masked(
            jnp.dot(hidden_activations, down_first_factor, preferred_element_type=jnp.float32)
        )
        return (
            inverse_mlp,
            normed_feedforward,
            reduced_gate,
            reduced_up,
            gate_up,
            hidden_activations,
            reduced_down,
        )

    (
        inverse_mlp,
        normed_feedforward,
        reduced_gate,
        reduced_up,
        gate_up,
        hidden_activations,
        reduced_down,
    ) = mlp_front(attended)
    mlp_part = sum_over_cols(
        build_term(
            hidden_activations,
            down_weight,
            False,
            [(reduced_down, down_second_factor)],
            adapter_factor,
        ),
        row_grand_total,
    )
    mixed = (attended + mlp_part.reshape(residual.shape)).astype(jnp.bfloat16)
    (
        inverse_mlp,
        normed_feedforward,
        reduced_gate,
        reduced_up,
        gate_up,
        hidden_activations,
        reduced_down,
    ) = mlp_front(attended)
    upstream_gradient = gather_columns(cotangent)
    lowered_down = masked(against_rows(upstream_gradient, down_second_factor))
    hidden_grad = sum_over_rows(
        build_term(
            upstream_gradient,
            down_weight,
            True,
            [(lowered_down, down_first_factor)],
            adapter_factor,
        ),
        row_grand_total,
    )
    down_first_gradient = adapter_factor * transpose_matmul(hidden_activations, lowered_down)
    down_second_gradient = adapter_factor * transpose_matmul(reduced_down, upstream_gradient)
    gate_raw = gate_up[:, :width_ff]
    up_raw = gate_up[:, width_ff:]
    sigmoid = jax.nn.sigmoid(gate_raw)
    gate_grad = hidden_grad * up_raw * sigmoid * (1.0 + gate_raw * (1.0 - sigmoid))
    up_grad = hidden_grad * gate_raw * sigmoid
    gate_up_grad = jnp.concatenate([gate_grad, up_grad], axis=1).astype(jnp.bfloat16)
    gate_up_activations = gather_rows(gate_up_grad.reshape(part_rows, seq_dev, 2 * width_ff))
    gate_activations = gate_up_activations[:, :width_ff]
    up_activations = gate_up_activations[:, width_ff:]
    lowered_gate = masked(against_rows(gate_activations, gate_second_factor))
    lowered_up = masked(against_rows(up_activations, up_second_factor))
    normed_mlp_grad = sum_over_cols(
        build_term(
            gate_up_activations,
            joined_gate_up,
            True,
            [(lowered_gate, gate_first_factor), (lowered_up, up_first_factor)],
            adapter_factor,
        ),
        row_grand_total,
    )
    gate_first_gradient = adapter_factor * transpose_matmul(normed_feedforward, lowered_gate)
    up_first_gradient = adapter_factor * transpose_matmul(normed_feedforward, lowered_up)
    gate_second_gradient = adapter_factor * transpose_matmul(reduced_gate, gate_activations)
    up_second_gradient = adapter_factor * transpose_matmul(reduced_up, up_activations)
    attended_grad = cotangent.astype(jnp.float32) + norm_backward(
        attended, feedforward_norm_gain, inverse_mlp, normed_mlp_grad.reshape(residual.shape)
    )
    attended_outputs = gather_columns(attended_grad.astype(jnp.bfloat16))
    lowered_output = masked(against_rows(attended_outputs, output_second_factor))
    heads_grad = sum_over_rows(
        build_term(
            attended_outputs,
            output_weight,
            True,
            [(lowered_output, output_first_factor)],
            adapter_factor,
        ),
        row_grand_total,
    )
    output_first_gradient = adapter_factor * transpose_matmul(head_outputs, lowered_output)
    output_second_gradient = adapter_factor * transpose_matmul(reduced_output, attended_outputs)
    heads_grad_low = heads_grad.reshape(part_rows, seq_dev, heads_dev, head_dim).astype(
        jnp.bfloat16
    )

    def backward_one(seq_item):
        return attend_sequence_back(
            seq_item[0],
            seq_item[1],
            seq_item[2],
            seq_item[3],
            seq_item[4],
            row_offset,
            groups,
            factor,
        )

    query_grad, key_value_grad = lax.map(
        backward_one,
        (seq_queries, seq_key_values, block_labels, jnp.moveaxis(heads_grad_low, 1, 0), log_sums),
    )
    key_value_grad = lax.psum_scatter(
        jnp.moveaxis(key_value_grad, 0, 1), "row", scatter_dimension=0, tiled=True
    )
    query_grad = jnp.moveaxis(query_grad, 0, 1).reshape(part_rows, seq_dev, heads_dev, head_dim)
    query_pre = rope_back(query_grad, cosine, sine_table).reshape(part_rows, seq_dev, width_q)
    key_pre = rope_back(
        key_value_grad[..., :width_kv].reshape(part_rows, seq_dev, groups, head_dim),
        cosine,
        sine_table,
    ).reshape(part_rows, seq_dev, width_kv)
    value_pre = key_value_grad[..., width_kv:]
    projected_grad = jnp.concatenate([query_pre, key_pre, value_pre], axis=-1).astype(jnp.bfloat16)
    projected_all = gather_rows(projected_grad)
    query_activations = projected_all[:, :width_q]
    key_activations = projected_all[:, width_q : width_q + width_kv]
    value_activations = projected_all[:, width_q + width_kv :]
    lowered_query = masked(against_rows(query_activations, query_second_factor))
    lowered_key = masked(against_rows(key_activations, key_second_factor))
    lowered_value = masked(against_rows(value_activations, value_second_factor))
    normed_grad = sum_over_cols(
        build_term(
            projected_all,
            joined_qkv,
            True,
            [
                (lowered_query, query_first_factor),
                (lowered_key, key_first_factor),
                (lowered_value, value_first_factor),
            ],
            adapter_factor,
        ),
        row_grand_total,
    )
    query_first_gradient = adapter_factor * transpose_matmul(normed_activations, lowered_query)
    key_first_gradient = adapter_factor * transpose_matmul(normed_activations, lowered_key)
    value_first_gradient = adapter_factor * transpose_matmul(normed_activations, lowered_value)
    query_second_gradient = adapter_factor * transpose_matmul(reduced_query, query_activations)
    key_second_gradient = adapter_factor * transpose_matmul(reduced_key, key_activations)
    value_second_gradient = adapter_factor * transpose_matmul(reduced_value, value_activations)
    token_grad = attended_grad + norm_backward(
        residual, attention_norm_gain, inverse_attn, normed_grad.reshape(residual.shape)
    )
    by_cols = lax.psum(
        (
            query_first_gradient,
            key_first_gradient,
            value_first_gradient,
            gate_first_gradient,
            up_first_gradient,
            output_second_gradient,
            down_second_gradient,
        ),
        ("dp", "col"),
    )
    by_rows = lax.psum(
        (
            query_second_gradient,
            key_second_gradient,
            value_second_gradient,
            gate_second_gradient,
            up_second_gradient,
            output_first_gradient,
            down_first_gradient,
        ),
        ("dp", "row"),
    )
    return (
        mixed,
        token_grad.astype(jnp.bfloat16),
        by_cols[0],
        by_rows[0],
        by_cols[1],
        by_rows[1],
        by_cols[2],
        by_rows[2],
        by_rows[5],
        by_cols[5],
        by_cols[3],
        by_rows[3],
        by_cols[4],
        by_rows[4],
        by_rows[6],
        by_cols[6],
    )


def solution(mesh):
    in_specs = (
        P("col", "dp", "row"),
        P("col", "dp", "row"),
        P("dp", None),
        P("dp"),
        P(),
        P("row"),
        P("row"),
        P("row", "col"),
        P("row", "col"),
        P("row", "col"),
        P("col", "row"),
        P("row", "col"),
        P("row", "col"),
        P("col", "row"),
        P("row", None),
        P(None, "col"),
        P("row", None),
        P(None, "col"),
        P("row", None),
        P(None, "col"),
        P("col", None),
        P(None, "row"),
        P("row", None),
        P(None, "col"),
        P("row", None),
        P(None, "col"),
        P("col", None),
        P(None, "row"),
    )
    out_specs = (
        P("col", "dp", "row"),
        P("col", "dp", "row"),
        P("row", None),
        P(None, "col"),
        P("row", None),
        P(None, "col"),
        P("row", None),
        P(None, "col"),
        P("col", None),
        P(None, "row"),
        P("row", None),
        P(None, "col"),
        P("row", None),
        P(None, "col"),
        P("col", None),
        P(None, "row"),
    )
    return jax.shard_map(local, mesh=mesh, in_specs=in_specs, out_specs=out_specs, check_vma=False)
```

profile of v0, /device:TPU:0, one launch (start us, length us, event | category | flops | bytes accessed | tf_op | source)
XLA Modules:
  0.0 7715.4 jit_solution(2539873477563594826)
XLA Ops:
  26.3 147.3 %all-gather.10.cloned.1.call-done = bf16[4096,2,512]{2,0,1:T(8,128)(2,1)} async-done(((bf16[1024,2,512]{2,0,1:T(8,128)(2,1)}), bf16[4096,2,512]{2,0,1:T(8,128)(2,1)}) %all-gather.10.cloned.1.call-update) | async-done | bytes 8388624 | tf_op jit(solution)/shard_map/all_gather | solution.py:57
  263.4 37.3 copy.276
  337.4 174.8 %reduce-scatter.11.cloned.1.call-done = f32[2048,768]{1,0:T(8,128)} async-done(((f32[8192,768]{1,0:T(8,128)}), f32[2048,768]{1,0:T(8,128)}) %reduce-scatter.11.cloned.1.call-update) | async-done | bytes 6291472 | tf_op jit(solution)/shard_map/reduce_scatter | solution.py:89
  577.8 351.0 %while.52 = (s32[]{:T(128)}, bf16[2,1024,512]{2,1,0:T(8,128)(2,1)}, f32[2,2,2,4,512]{4,3,2,1,0:T(4,128)}, bf16[2,1024,8,64]{1,3,2,0:T(8,128)(2,1)}, s32[]{:T(128...) while((s32[]{:T(128)}, bf16[2,1024,512]{2,1,0:T(8,128)(2,1)}, ...), condition=%wide.region_8.9_spmd, body=%wide.region_3.8_spmd.sunk | while | flops 4498386944 | bytes 240902128 | solution.py:339
  586.2 164.2 %while.55 = (s32[]{:T(128)}, bf16[2,512,512]{2,1,0:T(8,128)(2,1)}, f32[2,2,4,512]{3,2,1,0:T(4,128)S(1)}, s32[4096]{0:T(1024)S(1)}, s32[2]{0:T(128)S(1)}, /*index...) while((s32[]{:T(128)}, bf16[2,512,512]{2,1,0:T(8,128)(2,1)}, ...), condition=%wide.region_7.7_spmd, body=%wide.region_4.6_spmd.sunk | while | flops 4498386944 | bytes 215112880 | solution.py:187
  761.5 164.2 %while.55 = (s32[]{:T(128)}, bf16[2,512,512]{2,1,0:T(8,128)(2,1)}, f32[2,2,4,512]{3,2,1,0:T(4,128)S(1)}, s32[4096]{0:T(1024)S(1)}, s32[2]{0:T(128)S(1)}, /*index...) while((s32[]{:T(128)}, bf16[2,512,512]{2,1,0:T(8,128)(2,1)}, ...), condition=%wide.region_7.7_spmd, body=%wide.region_4.6_spmd.sunk | while | flops 4498386944 | bytes 215112880 | solution.py:187
  932.2 55.1 all-gather.14.cloned.1.call-done
  1079.6 58.9 all-gather.20.cloned.1.call-done
  1162.8 37.3 copy.308
  1213.4 206.0 %reduce-scatter.13.cloned.1.call-done = f32[2048,512]{1,0:T(8,128)} async-done(((f32[8192,512]{1,0:T(8,128)}), f32[2048,512]{1,0:T(8,128)}) %reduce-scatter.13.cloned.1.call-update) | async-done | bytes 4194320 | tf_op jit(solution)/shard_map/reduce_scatter | solution.py:98
  1441.8 30.9 fusion.224
  1498.2 70.3 multiply_add_fusion.2
  1632.4 37.8 copy.295
  1735.2 48.1 convolution_add_fusion.1
  1783.2 47.5 convolution_add_fusion
  1830.8 99.0 %fusion.48 = f32[8192,4096]{1,0:T(8,128)} fusion(f32[8192,2048]{1,0:T(8,128)} %convolution_add_fusion, f32[8192,2048]{1,0:T(8,128)} %convolution_add_fusion.1, bf16[8192,512]{1,0:T(8,128)(2,1)} %reshape.389, bf16[512,4096]{1,0:T(8,128)(2,1)} %constant_dynamic-update-slice_fusion.6, f32[]{:T(128)} %bitcast.424), kind=kOutput, calls=%fused_computation.73 | convolution fusion | flops 34460401664 | bytes 281018368 | tf_op jit(solution)/shard_map/dot_general | solution.py:72
  1931.7 113.2 %reduce-scatter.25.cloned.1.call-done = f32[2048,2048]{1,0:T(8,128)} async-done(((f32[8192,2048]{1,0:T(8,128)}), f32[2048,2048]{1,0:T(8,128)}) %reduce-scatter.25.cloned.1.call-update) | async-done | bytes 16777232
  2044.9 2180.4 %all-reduce.8.cloned.1.call-done = f32[8192,4096]{1,0:T(8,128)} async-done(((f32[8192,4096]{1,0:T(8,128)}), f32[8192,4096]{1,0:T(8,128)}) %all-reduce.8.cloned.1.call-update) | async-done | bytes 134217744
  4302.8 393.1 %all-gather.22.cloned.1.call-done = bf16[4096,2,4096]{2,1,0:T(2,128)(2,1)} async-done(((bf16[1024,2,4096]{2,1,0:T(2,128)(2,1)}), bf16[4096,2,4096]{2,1,0:T(2,128)(2,1)}) %all-gather.22.cloned.1.call-update) | async-done | bytes 67108880 | tf_op jit(solution)/shard_map/all_gather | solution.py:62
  4696.0 95.9 %reshape.398 = bf16[8192,4096]{1,0:T(8,128)(2,1)} reshape(bf16[4096,2,4096]{2,1,0:T(2,128)(2,1)} %all-gather.22.cloned.1.call-done) | data formatting | bytes 134217728 | tf_op jit(solution)/shard_map/reshape | solution.py:63
  4867.7 56.3 multiply_add_fusion.5
  4924.0 280.4 %reduce-scatter.17.cloned.1.call-done = f32[2048,512]{1,0:T(8,128)} async-done(((f32[8192,512]{1,0:T(8,128)}), f32[2048,512]{1,0:T(8,128)}) %reduce-scatter.17.cloned.1.call-update) | async-done | bytes 4194320 | tf_op jit(solution)/shard_map/reduce_scatter | solution.py:98
  5230.7 150.0 %all-gather.24.cloned.1.call-done = bf16[4096,2,512]{2,0,1:T(8,128)(2,1)} async-done(((bf16[1024,2,512]{2,0,1:T(8,128)(2,1)}), bf16[4096,2,512]{2,0,1:T(8,128)(2,1)}) %all-gather.24.cloned.1.call-update) | async-done | bytes 8388624 | tf_op jit(solution)/shard_map/all_gather | solution.py:57
  5473.9 124.4 %reduce-scatter.19.cloned.1.call-done = f32[2048,512]{1,0:T(8,128)} async-done(((f32[8192,512]{1,0:T(8,128)}), f32[2048,512]{1,0:T(8,128)}) %reduce-scatter.19.cloned.1.call-update) | async-done | bytes 4194320 | tf_op jit(solution)/shard_map/reduce_scatter | solution.py:89
  5613.7 859.4 %while.54 = (s32[]{:T(128)}, f32[2,1024,512]{1,2,0:T(8,128)}, f32[2,4096,256]{1,2,0:T(8,128)}, bf16[2,1024,8,64]{1,3,2,0:T(8,128)(2,1)}, bf16[2,1024,8,64]{1,3,2...) while((s32[]{:T(128)}, f32[2,1024,512]{1,2,0:T(8,128)}, ...), condition=%wide.region_23.24_spmd, body=%wide.region_19.23_spmd.sunk | while | flops 10995101696 | bytes 568567808 | solution.py:492
  5631.3 401.5 %while.56 = (s32[]{:T(128)}, f32[4096,2,64]{0,2,1:T(8,128)}, f32[4096,2,64]{0,2,1:T(8,128)}, f32[2,512,512]{2,1,0:T(8,128)}, bf16[2,512,2,4,64]{1,4,3,2,0:T(8,12...) while((s32[]{:T(128)}, f32[4096,2,64]{0,2,1:T(8,128)}, ...), condition=%wide.region_22.22_spmd.clone, body=%wide.region_20.21_spmd.clone.sunk | while | flops 10994053120 | bytes 530719424 | solution.py:233
  5662.9 47.7 fusion.337
  5710.7 53.3 fusion.338
  5803.5 28.0 fusion.340
  5863.1 47.7 fusion.337
  5910.8 53.3 fusion.338
  6004.2 28.7 fusion.340
  6060.7 401.5 %while.56 = (s32[]{:T(128)}, f32[4096,2,64]{0,2,1:T(8,128)}, f32[4096,2,64]{0,2,1:T(8,128)}, f32[2,512,512]{2,1,0:T(8,128)}, bf16[2,512,2,4,64]{1,4,3,2,0:T(8,12...) while((s32[]{:T(128)}, f32[4096,2,64]{0,2,1:T(8,128)}, ...), condition=%wide.region_22.22_spmd.clone, body=%wide.region_20.21_spmd.clone.sunk | while | flops 10994053120 | bytes 530719424 | solution.py:233
  6092.3 47.7 fusion.337
  6140.0 53.3 fusion.338
  6232.8 28.0 fusion.340
  6292.5 47.7 fusion.337
  6340.2 53.3 fusion.338
  6433.5 28.7 fusion.340
  6551.5 196.5 %all-gather.18.cloned.1.call-done = bf16[4096,2,2048]{2,0,1:T(8,128)(2,1)} async-done(((bf16[1024,2,2048]{2,0,1:T(8,128)(2,1)}), bf16[4096,2,2048]{2,0,1:T(8,128)(2,1)}) %all-gather.18.cloned.1.call-update) | async-done | bytes 33554448 | tf_op jit(solution)/shard_map/all_gather | solution.py:62
  6748.0 60.3 copy.303
  6808.3 48.6 reshape.393
  6903.7 34.0 multiply_add_fusion.6
  6937.8 31.5 copy.321
  7061.3 41.4 multiply_add_fusion.3
  7299.0 202.6 %reduce-scatter.23.cloned.1.call-done = f32[2048,512]{1,0:T(8,128)} async-done(((f32[8192,512]{1,0:T(8,128)}), f32[2048,512]{1,0:T(8,128)}) %reduce-scatter.23.cloned.1.call-update) | async-done | bytes 4194320 | tf_op jit(solution)/shard_map/reduce_scatter | solution.py:98
  7536.2 70.8 all-reduce.10.cloned.1.call-done
  7607.0 82.1 %all-reduce.12.cloned.1.call-done = (f32[128,512]{1,0:T(8,128)}, f32[128,128]{1,0:T(8,128)}, f32[128,128]{1,0:T(8,128)}, f32[512,128]{1,0:T(8,128)}, f32[128,204...) async-done(((f32[128,512]{1,0:T(8,128)}, f32[128,128]{1,0:T(8,128)}, f32[128,128]{1,0:T(8,128)}, f32[512,128]{1,0:T(8,128)}, f32[128,2048]{1,0:T(8,128)}, ...) | async-done | bytes 3801104 | tf_op jit(solution)/shard_map/psum | solution.py:550
  (621 shorter events, 1951.8 us)
Async XLA Ops:
  7.2 1434.6 %copy-start = (bf16[2048,512]{1,0:T(8,128)(2,1)S(1)}, bf16[2048,512]{1,0:T(8,128)(2,1)}, u32[]{:S(2)}) copy-start(bf16[2048,512]{1,0:T(8,128)(2,1)} %param.49) | copy-start | bytes 6291460
  7.2 166.4 %all-gather.10.cloned.1.call-start = ((), (), s32[]{:S(2)}) async-start(), calls=%async_computation.8 | async-start | bytes 10485760 | tf_op jit(solution)/shard_map/all_gather | solution.py:57
  9.5 164.1 %copy-start.75 = (bf16[512,128]{1,0:T(8,128)(2,1)S(1)}, bf16[512,128]{1,0:T(8,128)(2,1)}, u32[]{:S(2)}) copy-start(bf16[512,128]{1,0:T(8,128)(2,1)} %param.50) | copy-start | bytes 393220
  23.6 488.6 %reduce-scatter.11.cloned.1.call-start = ((), (), s32[]{:S(2)}) async-start(), calls=%async_computation.9 | async-start | bytes 31457280 | tf_op jit(solution)/shard_map/reduce_scatter | solution.py:89
  26.2 287.7 %copy-start.85 = (bf16[512,768]{1,0:T(8,128)(2,1)}, bf16[512,768]{1,0:T(8,128)(2,1)S(1)}, u32[]{:S(2)}) copy-start(bf16[512,768]{1,0:T(8,128)(2,1)S(1)} %constant_dynamic-update-slice_fusion.3) | copy-start | bytes 2359300
  26.3 214.3 %copy-start.55 = (f32[2,128]{1,0:T(2,128)}, f32[2,128]{1,0:T(2,128)S(1)}, u32[]{:S(2)}) copy-start(f32[2,128]{1,0:T(2,128)S(1)} %compare_convert_fusion) | copy-start | bytes 3076
  195.2 22.5 slice-start.4
  333.4 244.5 %all-gather.12.cloned.1.call-start = ((), (), s32[]{:S(2)}) async-start(), calls=%async_computation.10 | async-start | bytes 5242880 | tf_op jit(solution)/shard_map/all_gather | solution.py:332
  337.4 197.6 %copy-start.42 = (f32[1024,64]{0,1:T(8,128)}, f32[1024,64]{0,1:T(8,128)S(1)}, u32[]{:S(2)}) copy-start(f32[1024,64]{0,1:T(8,128)S(1)} %copy.289) | copy-start | bytes 786436
  538.4 448.9 %all-gather.14.cloned.1.call-start = ((), (), s32[]{:S(2)}) async-start(), calls=%async_computation.11 | async-start | bytes 10485760 | tf_op jit(solution)/shard_map/all_gather | solution.py:62
  586.2 166.4 %copy-start.83 = (f32[2,2,2,4,512]{4,3,2,1,0:T(4,128)S(1)}, f32[2,2,2,4,512]{4,3,2,1,0:T(4,128)}, u32[]{:S(2)}) copy-start(f32[2,2,2,4,512]{4,3,2,1,0:T(4,128)} %get-tuple-element.952) | copy-start | bytes 196612 | tf_op jit(solution)/shard_map/while
  761.5 166.4 %copy-start.83 = (f32[2,2,2,4,512]{4,3,2,1,0:T(4,128)S(1)}, f32[2,2,2,4,512]{4,3,2,1,0:T(4,128)}, u32[]{:S(2)}) copy-start(f32[2,2,2,4,512]{4,3,2,1,0:T(4,128)} %get-tuple-element.952) | copy-start | bytes 196612 | tf_op jit(solution)/shard_map/while
  928.8 209.6 %all-gather.20.cloned.1.call-start = ((), (), s32[]{:S(2)}) async-start(), calls=%async_computation.16 | async-start | bytes 10485760 | tf_op jit(solution)/shard_map/all_gather | solution.py:57
  932.1 487.2 %reduce-scatter.13.cloned.1.call-start = ((), (), s32[]{:S(2)}) async-start(), calls=%async_computation.12 | async-start | bytes 20971520 | tf_op jit(solution)/shard_map/reduce_scatter | solution.py:98
  1024.8 25.7 slice-start.14
  1078.9 59.6 copy-start.69
  1078.9 512.8 %all-gather.16.cloned.1.call-start = ((), (), s32[]{:S(2)}) async-start(), calls=%async_computation.13 | async-start | bytes 10485760 | tf_op jit(solution)/shard_map/all_gather | solution.py:57
  1079.6 356.5 %copy-start.102 = (f32[512]{0:T(512)}, f32[512]{0:T(512)S(1)}, u32[]{:S(2)}) copy-start(f32[512]{0:T(512)S(1)} %convert_element_type.319) | copy-start | bytes 6148
  1441.7 31.0 copy-start.51
  1441.7 603.2 %reduce-scatter.25.cloned.1.call-start = ((), (), s32[]{:S(2)}) async-start(), calls=%async_computation.25 | async-start | bytes 83886080
  1568.6 23.2 copy-start.57
  1568.6 23.2 copy-start.61
  1568.6 2656.8 %all-reduce.8.cloned.1.call-start = ((), (), s32[]{:S(2)}) async-start(), calls=%async_computation.24 | async-start | bytes 268435456
  1591.8 22.1 copy-start.63
  1683.9 26.5 copy-start.27
  1683.9 26.5 copy-start.47
  1929.8 2766.1 %all-gather.22.cloned.1.call-start = ((), (), s32[]{:S(2)}) async-start(), calls=%async_computation.17 | async-start | bytes 83886080 | tf_op jit(solution)/shard_map/all_gather | solution.py:62
  4302.8 489.1 %copy-start.58 = (f32[2,128]{1,0:T(2,128)S(1)}, f32[2,128]{1,0:T(2,128)}, u32[]{:S(2)}) copy-start(f32[2,128]{1,0:T(2,128)} %copy-done.55) | copy-start | bytes 3076
  4302.8 901.6 %reduce-scatter.17.cloned.1.call-start = ((), (), s32[]{:S(2)}) async-start(), calls=%async_computation.18 | async-start | bytes 20971520 | tf_op jit(solution)/shard_map/reduce_scatter | solution.py:98
  4923.9 286.3 %copy-start.103 = (f32[512]{0:T(512)S(1)}, f32[512]{0:T(512)}, u32[]{:S(2)}) copy-start(f32[512]{0:T(512)} %copy-done.102) | copy-start | bytes 6148
  4924.0 456.7 %all-gather.24.cloned.1.call-start = ((), (), s32[]{:S(2)}) async-start(), calls=%async_computation.19 | async-start | bytes 10485760 | tf_op jit(solution)/shard_map/all_gather | solution.py:57
  5230.6 367.7 %reduce-scatter.19.cloned.1.call-start = ((), (), s32[]{:S(2)}) async-start(), calls=%async_computation.20 | async-start | bytes 20971520 | tf_op jit(solution)/shard_map/reduce_scatter | solution.py:89
  5473.9 1071.1 %reduce-scatter.21.cloned.1.call-start = ((), (), s32[]{:S(2)}) async-start(), calls=%async_computation.21 | async-start | bytes 10485760 | tf_op jit(solution)/shard_map/reduce_scatter | solution.py:496
  6473.1 274.9 %all-gather.18.cloned.1.call-start = ((), (), s32[]{:S(2)}) async-start(), calls=%async_computation.14 | async-start | bytes 41943040 | tf_op jit(solution)/shard_map/all_gather | solution.py:62
  6499.0 438.8 %all-gather.26.cloned.1.call-start = ((), (), s32[]{:S(2)}) async-start(), calls=%async_computation.22 | async-start | bytes 15728640 | tf_op jit(solution)/shard_map/all_gather | solution.py:62
  6551.4 741.8 %reduce-scatter.15.cloned.1.call-start = ((), (), s32[]{:S(2)}) async-start(), calls=%async_computation.15 | async-start | bytes 20971520 | tf_op jit(solution)/shard_map/reduce_scatter | solution.py:98
  6808.3 48.6 copy-start.52
  6808.3 48.6 copy-start.60
  6937.8 563.8 %reduce-scatter.23.cloned.1.call-start = ((), (), s32[]{:S(2)}) async-start(), calls=%async_computation.23 | async-start | bytes 20971520 | tf_op jit(solution)/shard_map/reduce_scatter | solution.py:98
  6969.3 26.3 copy-start.88
  7000.0 43.3 copy-start.7
  7003.8 18.0 slice-start.8
  7003.8 18.0 slice-start.9
  7102.8 504.2 %all-reduce.10.cloned.1.call-start = ((), (), s32[]{:S(2)}) async-start(), calls=%async_computation.26 | async-start | bytes 3670016 | tf_op jit(solution)/shard_map/psum | solution.py:538
  7131.6 18.0 copy-start.22
  7276.3 412.8 %all-reduce.12.cloned.1.call-start = ((), (), s32[]{:S(2)}) async-start(), calls=%async_computation.27 | async-start | bytes 7602176 | tf_op jit(solution)/shard_map/psum | solution.py:550
  7299.0 208.4 %copy-start.106 = (f32[512]{0:T(512)S(1)}, f32[512]{0:T(512)}, u32[]{:S(2)}) copy-start(f32[512]{0:T(512)} %copy-done.105) | copy-start | bytes 6148
  7607.0 98.0 %copy-start.92 = (f32[512,128]{1,0:T(8,128)S(1)}, f32[512,128]{1,0:T(8,128)}, u32[]{:S(2)}) copy-start(f32[512,128]{1,0:T(8,128)} %get-tuple-element.1028) | copy-start | bytes 786436
  (102 other events, 850.5 us)
Sparse Core Ops, SparseCore 0:
  23.7 149.9 all-gather.9
  333.5 178.5 reduce-scatter.10
  538.6 34.4 all-gather.11
  929.0 58.3 all-gather.13
  988.8 149.6 all-gather.19
  1140.8 278.4 reduce-scatter.12
  1441.8 149.9 all-gather.15
  1594.3 450.5 reduce-scatter.24
  2047.6 2177.7 all-reduce.7
  4302.9 393.0 all-gather.21
  4924.1 280.2 reduce-scatter.16
  5230.8 149.9 all-gather.23
  5474.0 124.2 reduce-scatter.18
  6473.2 71.6 reduce-scatter.20
  6546.4 201.5 all-gather.17
  6749.4 82.0 all-gather.25
  6937.9 280.2 reduce-scatter.14
  7220.5 281.0 reduce-scatter.22
  7507.3 99.6 all-reduce.9
  7612.1 76.8 all-reduce.11
where the time goes:
time: 7730 us; the launch traced here: 7720 us
  waiting for transfers between devices  4460 us (58%)
  matrix products  1780 us (23%)
  local copies, waits for them, and re-layouts  916 us (12%)
  other arithmetic  503 us (7%)
    unnamed x22, waiting for transfers between devices  2290 us
    reduce_scatter x4, waiting for transfers between devices, sum_over_cols(): lax.psum_scatter(row_terms(jnp.int32(0), row_grand_total // lax.axis_size...  689 us
    all_gather x4, waiting for transfers between devices, gather_rows(): gathered = lax.all_gather(values, 'row', axis=0, tiled=True)  645 us
    dot_general x25, matrix products, against_rows(): lax.dot_general(left_rows, right_rows, (((1,), (1,)), ((), ())), preferre...  414 us
    all_gather x4, waiting for transfers between devices, gather_columns(): gathered = lax.all_gather(values, 'col', axis=0, tiled=True)  374 us
    reduce_scatter x2, waiting for transfers between devices, sum_over_rows(): lax.psum_scatter(row_terms(jnp.int32(0), row_grand_total // lax.axis_size...  299 us
    convert_element_type x4, other arithmetic, one_block(): score_grad = (probs_full * (from_values - row_delta)).astype(jnp.bfloat16)  213 us
    dot_general x8, matrix products, block_scores(): jnp.einsum('qgre,kge->grqk', block_queries, key_part, preferred_element_t...  205 us
  transfers between devices with their start and end apart: 20, of which 17 were waited for; matrix products, arithmetic and copies ran while one was open for 17% of the time, Pallas kernels for 0%

commit v1 on v0

v1 whole, which is shorter than its diff:
```python
import functools, math
import jax, jax.numpy as jnp
from jax import lax
from jax.sharding import PartitionSpec as P
from jax.experimental import pallas as pl
from jax.experimental.pallas import tpu as pltpu

HEAD_DIM = 64
RANK = 16
BLOCKS = 32
EPS = 1e-05
ROPE_BASE = 500000.0
TILE = 512
REACH = 256
LOG2E = math.log2(math.e)
NEG = -1e30


def nt(a, b):
    return lax.dot_general(a, b, (((1,), (1,)), ((), ())), preferred_element_type=jnp.float32)


def nn(a, b):
    return lax.dot_general(a, b, (((1,), (0,)), ((), ())), preferred_element_type=jnp.float32)


def half_of(x, e):
    lane = lax.broadcasted_iota(jnp.int32, x.shape, 1)
    return jnp.where((lane < 64) if e == 0 else (lane >= 64), x, jnp.zeros_like(x))


def fwd_kernel(heads, factor, end_ref, q_ref, k2_ref, vt_ref, o_ref, lse_ref, acc_ref, m_ref, l_ref):
    i = pl.program_id(0)
    tq = q_ref.shape[0]
    q0 = i * tq
    c = factor * LOG2E
    ends = end_ref[...]
    m_ref[...] = jnp.full_like(m_ref, NEG)
    l_ref[...] = jnp.zeros_like(l_ref)
    acc_ref[...] = jnp.zeros_like(acc_ref)

    def tile(k0, size, masked):
        kk = k2_ref[pl.ds(k0, size), :]
        vv = vt_ref[:, pl.ds(k0, size)]
        if masked:
            allowed = (lax.broadcasted_iota(jnp.int32, (size, tq), 0) + k0) < ends
        for h in range(heads):
            qh = half_of(q_ref[:, (h // 2) * 128:(h // 2 + 1) * 128], h % 2)
            s = nt(kk, qh) * c
            if masked:
                s = jnp.where(allowed, s, NEG)
            m_old = m_ref[h:h + 1, :]
            m_new = jnp.maximum(m_old, jnp.max(s, axis=0, keepdims=True))
            p = jnp.exp2(s - m_new)
            alpha = jnp.exp2(m_old - m_new)
            l_ref[h:h + 1, :] = l_ref[h:h + 1, :] * alpha + jnp.sum(p, axis=0, keepdims=True)
            m_ref[h:h + 1, :] = m_new
            a = pl.ds(h * 64, 64)
            acc_ref[a, :] = acc_ref[a, :] * alpha + nn(vv, p.astype(jnp.bfloat16))

    def body(j, _):
        tile(pl.multiple_of(j * tq, tq), tq, False)
        return 0

    lax.fori_loop(0, i, body, 0)
    tile(pl.multiple_of(q0, tq), tq, True)

    @pl.when(i < pl.num_programs(0) - 1)
    def _():
        tile(pl.multiple_of(q0 + tq, REACH), REACH, True)

    lse_ref[...] = m_ref[...] + jnp.log2(l_ref[...])
    inv = 1.0 / l_ref[...]
    for p in range(o_ref.shape[1] // 128):
        parts = []
        for h in (2 * p, 2 * p + 1):
            if h < heads:
                parts.append(acc_ref[h * 64:(h + 1) * 64, :] * inv[h:h + 1, :])
            else:
                parts.append(jnp.zeros((64, tq), jnp.float32))
        o_ref[:, p * 128:(p + 1) * 128] = jnp.concatenate(parts, axis=0).T.astype(o_ref.dtype)


def attend(q, k2, vt, ends, heads, factor):
    length, width = q.shape
    tq = min(TILE, length)
    rows = 8
    return pl.pallas_call(
        functools.partial(fwd_kernel, heads, factor),
        grid=(length // tq,),
        in_specs=[
            pl.BlockSpec((1, tq), lambda i: (0, i)),
            pl.BlockSpec((tq, width), lambda i: (i, 0)),
            pl.BlockSpec((length, 128), lambda i: (0, 0)),
            pl.BlockSpec((64, length), lambda i: (0, 0)),
        ],
        out_specs=[
            pl.BlockSpec((tq, width), lambda i: (i, 0)),
            pl.BlockSpec((rows, tq), lambda i: (0, i)),
        ],
        out_shape=[
            jax.ShapeDtypeStruct((length, width), jnp.bfloat16),
            jax.ShapeDtypeStruct((rows, length), jnp.float32),
        ],
        scratch_shapes=[
            pltpu.VMEM((heads * 64, tq), jnp.float32),
            pltpu.VMEM((rows, tq), jnp.float32),
            pltpu.VMEM((rows, tq), jnp.float32),
        ],
        compiler_params=pltpu.CompilerParams(vmem_limit_bytes=48 * 2**20),
        cost_estimate=pl.CostEstimate(
            flops=2 * heads * length * length * 64, bytes_accessed=4 * length * width + length * 384, transcendentals=heads * length * length // 2
        ),
        name="attend_forward",
    )(ends, q, k2, vt)


def bwd_kernel(heads, factor, end_ref, q_ref, do_ref, o_ref, lse_ref, k2_ref, v2_ref, kt_ref, dq_ref, dkv_ref, dqt_ref, delta_ref, dk_ref, dv_ref):
    j = pl.program_id(0)
    n = pl.num_programs(0)
    tk = k2_ref.shape[0]
    length, width = q_ref.shape
    c = factor * LOG2E

    @pl.when(j == 0)
    def _():
        dqt_ref[...] = jnp.zeros_like(dqt_ref)
        delta_ref[...] = jnp.zeros_like(delta_ref)
        for t in range(length // tk):
            rows = slice(t * tk, (t + 1) * tk)
            for p in range(width // 128):
                prod = do_ref[rows, p * 128:(p + 1) * 128].astype(jnp.float32) * o_ref[rows, p * 128:(p + 1) * 128].astype(jnp.float32)
                turned = prod.T
                for h in (2 * p, 2 * p + 1):
                    if h < heads:
                        delta_ref[h:h + 1, rows] = jnp.sum(turned[(h % 2) * 64:(h % 2 + 1) * 64, :], axis=0, keepdims=True)

    dk_ref[...] = jnp.zeros_like(dk_ref)
    dv_ref[...] = jnp.zeros_like(dv_ref)

    def tile(q0, size, masked):
        rows = pl.ds(q0, tk)
        kk = k2_ref[:size, :]
        vv = v2_ref[:size, :]
        kt = kt_ref[:, :size]
        if masked:
            allowed = (lax.broadcasted_iota(jnp.int32, (size, tk), 0) + j * tk) < end_ref[:, rows]
        for h in range(heads):
            lanes = slice((h // 2) * 128, (h // 2 + 1) * 128)
            qh = half_of(q_ref[rows, lanes], h % 2)
            gh = half_of(do_ref[rows, lanes], h % 2)
            s = nt(kk, qh) * c - lse_ref[h:h + 1, rows]
            if masked:
                s = jnp.where(allowed, s, NEG)
            p = jnp.exp2(s)
            dp = nt(vv, gh)
            ds = (p * (dp - delta_ref[h:h + 1, rows])).astype(jnp.bfloat16)
            dv_ref[:size, :] += nn(p.astype(jnp.bfloat16), gh)
            dk_ref[:size, :] += nn(ds, qh)
            dqt_ref[h * 64:(h + 1) * 64, rows] += nn(kt, ds)

    @pl.when(j > 0)
    def _():
        tile(pl.multiple_of((j - 1) * tk, tk), REACH, True)

    tile(pl.multiple_of(j * tk, tk), tk, True)

    def body(i, _):
        tile(pl.multiple_of(i * tk, tk), tk, False)
        return 0

    lax.fori_loop(j + 1, n, body, 0)

    lane = lax.broadcasted_iota(jnp.int32, (tk, 128), 1)
    dk = dk_ref[...]
    dv = dv_ref[...]
    dk = (dk + pltpu.roll(dk, 64, 1)) * factor
    dv = dv + pltpu.roll(dv, 64, 1)
    dkv_ref[...] = jnp.where(lane < 64, dk, dv).astype(dkv_ref.dtype)

    @pl.when(j == n - 1)
    def _():
        for t in range(length // tk):
            rows = slice(t * tk, (t + 1) * tk)
            for p in range(width // 128):
                lo = 2 * p * 64
                if 2 * p + 1 < heads:
                    blk = dqt_ref[lo:lo + 128, rows]
                else:
                    blk = jnp.concatenate([dqt_ref[lo:lo + 64, rows], jnp.zeros((64, tk), jnp.float32)], axis=0)
                dq_ref[rows, p * 128:(p + 1) * 128] = (blk.T * factor).astype(dq_ref.dtype)


def attend_back(q, do, o, lse, k2, v2, kt, ends, heads, factor, out_dtype=jnp.bfloat16):
    length, width = q.shape
    tk = min(TILE, length)
    whole = lambda shape: pl.BlockSpec(shape, lambda j: (0, 0))
    return pl.pallas_call(
        functools.partial(bwd_kernel, heads, factor),
        grid=(length // tk,),
        in_specs=[
            whole((1, length)),
            whole((length, width)),
            whole((length, width)),
            whole((length, width)),
            whole((8, length)),
            pl.BlockSpec((tk, 128), lambda j: (j, 0)),
            pl.BlockSpec((tk, 128), lambda j: (j, 0)),
            pl.BlockSpec((64, tk), lambda j: (0, j)),
        ],
        out_specs=[
            whole((length, width)),
            pl.BlockSpec((tk, 128), lambda j: (j, 0)),
        ],
        out_shape=[
            jax.ShapeDtypeStruct((length, width), out_dtype),
            jax.ShapeDtypeStruct((length, 128), out_dtype),
        ],
        scratch_shapes=[
            pltpu.VMEM((heads * 64, length), jnp.float32),
            pltpu.VMEM((8, length), jnp.float32),
            pltpu.VMEM((tk, 128), jnp.float32),
            pltpu.VMEM((tk, 128), jnp.float32),
        ],
        compiler_params=pltpu.CompilerParams(vmem_limit_bytes=48 * 2**20),
        cost_estimate=pl.CostEstimate(
            flops=5 * heads * length * length * 64, bytes_accessed=8 * length * width + length * 512, transcendentals=heads * length * length // 2
        ),
        name="attend_backward",
    )(ends, q, do, o, lse, k2, v2, kt)


def dot(left, right):
    return lax.dot_general(left, right, (((1,), (0,)), ((), ())), preferred_element_type=jnp.float32)


def dot_turned(left, right):
    return lax.dot_general(left, right, (((1,), (1,)), ((), ())), preferred_element_type=jnp.float32)


def over_tokens(left, right):
    return lax.dot_general(left, right, (((0,), (0,)), ((), ())), preferred_element_type=jnp.float32)


def low(values):
    return values.astype(jnp.bfloat16)


def inverse_rms(values):
    return lax.rsqrt(jnp.mean(values * values, axis=-1, keepdims=True) + EPS)


def norm_back(values, gain, inverse, upstream):
    scaled = upstream * gain
    weighted = jnp.mean(scaled * values, axis=-1, keepdims=True)
    return inverse * scaled - values * (inverse * inverse * inverse) * weighted


def to_tokens(values):
    rows = lax.axis_size("row")
    part, seqs, features = values.shape
    cut = values.reshape(rows, part // rows, seqs, features).transpose(0, 2, 1, 3)
    moved = lax.all_to_all(cut, "row", 0, 0, tiled=True)
    return moved.transpose(1, 2, 0, 3).reshape(seqs * (part // rows), rows * features)


def to_features(values, seqs):
    rows = lax.axis_size("row")
    width = values.shape[1] // rows
    cut = values.reshape(seqs, -1, rows, width).transpose(2, 0, 1, 3)
    moved = lax.all_to_all(cut, "row", 0, 0, tiled=True)
    return moved.transpose(0, 2, 1, 3).reshape(-1, seqs, width)


def rope_tables(positions, lanes):
    half = HEAD_DIM // 2
    frequency = ROPE_BASE ** (-(jnp.arange(half).astype(jnp.float32) * 2.0) / HEAD_DIM)
    angles = positions.astype(jnp.float32)[:, None] * frequency[None, :]
    copies = (1, lanes // half)
    return lax.optimization_barrier((jnp.tile(jnp.cos(angles), copies), jnp.tile(jnp.sin(angles), copies)))


def spread(table, width):
    return jnp.concatenate([table] * pl.cdiv(width, table.shape[1]), axis=1)[:, :width]


def turn(values, sign):
    half = HEAD_DIM // 2
    ahead = jnp.concatenate([values[:, half:], values[:, :half]], axis=1)
    behind = jnp.concatenate([values[:, -half:], values[:, :-half]], axis=1)
    lane = lax.broadcasted_iota(jnp.int32, values.shape, 1)
    return jnp.where(lane % HEAD_DIM < half, sign * ahead, -sign * behind)


def rope(values, cosine, sine):
    width = values.shape[1]
    return values * spread(cosine, width) + turn(values, -1.0) * spread(sine, width)


def rope_back(values, cosine, sine):
    width = values.shape[1]
    return values * spread(cosine, width) + turn(values * spread(sine, width), 1.0)


def diagonal(blocks):
    total = sum(b.shape[1] for b in blocks)
    out, at = [], 0
    for b in blocks:
        out.append(jnp.pad(b, ((0, 0), (at, total - at - b.shape[1]))))
        at += b.shape[1]
    return jnp.concatenate(out, axis=0)


def local(
    tokens,
    cotangent,
    block_labels,
    adapter_selection,
    adapter_scale,
    attention_norm_gain,
    feedforward_norm_gain,
    query_weight,
    key_weight,
    value_weight,
    output_weight,
    gate_weight,
    up_weight,
    down_weight,
    query_first_factor,
    query_second_factor,
    key_first_factor,
    key_second_factor,
    value_first_factor,
    value_second_factor,
    output_first_factor,
    output_second_factor,
    gate_first_factor,
    gate_second_factor,
    up_first_factor,
    up_second_factor,
    down_first_factor,
    down_second_factor,
):
    copies, rows, cols = lax.axis_size("dp"), lax.axis_size("row"), lax.axis_size("col")
    me = lax.axis_index("dp")
    units = rows * cols
    both, turned_both = ("row", "col"), ("col", "row")
    seqs = tokens.shape[1]
    part = tokens.shape[0] // rows
    length = part * units
    features = tokens.shape[2] * rows
    scale = adapter_scale[0]
    width_q, width_kv = query_weight.shape[1], key_weight.shape[1]
    width_qkv = width_q + 2 * width_kv
    width_ff = gate_weight.shape[1] // copies
    kv_heads = width_kv * cols // HEAD_DIM
    heads = width_q * cols // HEAD_DIM * seqs // units
    kv_copies = max(1, units // (seqs * kv_heads))
    adapter_cols = query_first_factor.shape[1]
    rank = seqs * RANK
    factor = HEAD_DIM ** (-0.5)

    picked = lax.all_gather(adapter_selection, "dp", axis=0, tiled=True)
    owner = jnp.arange(adapter_cols)
    slot = jnp.arange(copies * rank)
    choose = (owner[:, None] // RANK == picked[slot // RANK][None, :]) & (owner[:, None] % RANK == slot[None, :] % RANK)
    choose_low = choose.astype(jnp.bfloat16)
    choose_wide = choose.astype(jnp.float32)
    choose_own = lax.dynamic_slice_in_dim(choose_low, me * rank, rank, 1)

    def first_of(matrix, chosen):
        return low(dot(matrix, chosen))

    def second_of(matrix, chosen):
        return low(over_tokens(chosen, matrix))

    half = me * width_ff
    gate_half = lax.dynamic_slice_in_dim(gate_weight, half, width_ff, 1)
    up_half = lax.dynamic_slice_in_dim(up_weight, half, width_ff, 1)
    down_half = lax.dynamic_slice_in_dim(down_weight, half, width_ff, 0)
    gate_second_half = lax.dynamic_slice_in_dim(gate_second_factor, half, width_ff, 1)
    up_second_half = lax.dynamic_slice_in_dim(up_second_factor, half, width_ff, 1)
    down_first_half = lax.dynamic_slice_in_dim(down_first_factor, half, width_ff, 0)

    first_parts = [first_of(m, choose_own) for m in (query_first_factor, key_first_factor, value_first_factor)]
    first_parts += [first_of(m, choose_low) for m in (gate_first_factor, up_first_factor)]
    first_parts += [attention_norm_gain[:, None], feedforward_norm_gain[:, None]]
    first_rows = lax.all_gather(jnp.concatenate(first_parts, axis=1), "row", axis=0, tiled=True)
    qkv_weight = lax.all_gather(
        jnp.concatenate([query_weight, key_weight, value_weight], axis=1), turned_both, axis=0, tiled=True
    ).reshape(cols, features, width_qkv)
    qkv_second = lax.all_gather(
        diagonal([second_of(m, choose_own) for m in (query_second_factor, key_second_factor, value_second_factor)]),
        "col",
    )
    out_weight = lax.all_gather(output_weight, both, axis=0, tiled=True).reshape(rows, -1, output_weight.shape[1])
    second_rows = lax.all_gather(
        jnp.concatenate([second_of(output_second_factor, choose_own), second_of(down_second_factor, choose_low)], axis=0),
        "row",
    )
    out_first = lax.all_gather(first_of(output_first_factor, choose_own), "col", axis=0, tiled=True)
    front_weight = lax.all_gather(
        jnp.concatenate([gate_half, up_half], axis=1), turned_both, axis=0, tiled=True
    ).reshape(cols, features, 2 * width_ff)
    gate_second = second_of(gate_second_half, choose_low)
    up_second = second_of(up_second_half, choose_low)
    front_second = lax.all_gather(
        jnp.concatenate(
            [diagonal([gate_second[g * rank : (g + 1) * rank], up_second[g * rank : (g + 1) * rank]]) for g in range(copies)],
            axis=0,
        ),
        "col",
    )
    back_weight = lax.all_gather(down_half, both, axis=0, tiled=True).reshape(rows, -1, down_half.shape[1])
    down_first = lax.all_gather(first_of(down_first_half, choose_low), "col", axis=0, tiled=True)

    qkv_first = first_rows[:, : 3 * rank]
    gate_first = first_rows[:, 3 * rank : (3 + copies) * rank]
    up_first = first_rows[:, (3 + copies) * rank : (3 + 2 * copies) * rank]
    gains = first_rows[:, (3 + 2 * copies) * rank :].astype(jnp.float32).T
    out_second = second_rows[:, :rank]
    down_second = second_rows[:, rank:]

    row_seq = jnp.arange(seqs * part) // part
    mask = (row_seq[:, None] == jnp.arange(rank)[None, :] // RANK).astype(jnp.float32) * scale

    def masked(values):
        return low(values * jnp.tile(mask, (1, values.shape[1] // rank)))

    residual = to_tokens(tokens).astype(jnp.float32)
    upstream = to_tokens(cotangent)
    inverse_attn = inverse_rms(residual)
    normed = low(residual * inverse_attn * gains[0:1])
    low_qkv = masked(dot(normed, qkv_first))
    positions = (lax.axis_index("col") * rows + lax.axis_index("row")) * part + jnp.arange(part)
    cosine, sine = rope_tables(jnp.tile(positions, seqs), 2 * HEAD_DIM)
    query_parts, key_parts, value_parts = [], [], []
    for c in range(cols):
        raw = dot(normed, qkv_weight[c]) + dot(low_qkv, qkv_second[c])
        turned = low(rope(raw[:, : width_q + width_kv], cosine, sine))
        query_parts.append(turned[:, :width_q])
        key_parts.append(turned[:, width_q:])
        value_parts.append(low(raw[:, width_q + width_kv :]))

    def to_units(values, groups):
        return values.reshape(seqs, part, groups, -1).transpose(0, 2, 1, 3)

    def from_units(values):
        return values.transpose(0, 2, 1, 3).reshape(seqs * part, -1)

    def exchange(values):
        return lax.all_to_all(values.reshape(units, part, -1), turned_both, 0, 0, tiled=True)

    unit_width = heads * HEAD_DIM
    sent_queries = to_units(jnp.concatenate(query_parts, axis=1), units // seqs)
    sent_kv = jnp.concatenate(
        [to_units(jnp.concatenate(key_parts, axis=1), kv_heads), to_units(jnp.concatenate(value_parts, axis=1), kv_heads)],
        axis=-1,
    )
    sent_kv = jnp.repeat(sent_kv, kv_copies, axis=1)
    unit_in = exchange(jnp.concatenate([sent_queries, sent_kv], axis=-1)).reshape(length, -1)
    pad_width = -unit_width % 128
    unit_queries = jnp.pad(unit_in[:, :unit_width], ((0, 0), (0, pad_width)))
    unit_keys = unit_in[:, unit_width : unit_width + HEAD_DIM]
    unit_values = unit_in[:, unit_width + HEAD_DIM :]
    keys_twice = jnp.concatenate([unit_keys, unit_keys], axis=1)
    values_twice = jnp.concatenate([unit_values, unit_values], axis=1)
    unit_seq = (lax.axis_index("col") * rows + lax.axis_index("row")) * seqs // units
    labels = lax.dynamic_index_in_dim(block_labels, unit_seq, 0, keepdims=True)
    numbers = jnp.arange(BLOCKS)[:, None]
    ends_of = jnp.sum((labels <= numbers).astype(jnp.int32), axis=1, keepdims=True)
    ends = jnp.sum(jnp.where(labels == numbers, ends_of, 0), axis=0, keepdims=True)
    unit_out, log_sums = attend(unit_queries, keys_twice, unit_values.T, ends, heads, factor)
    heads_out = from_units(exchange(unit_out[:, :unit_width]).reshape(seqs, units // seqs, part, -1))
    low_out = masked(dot(heads_out, out_first))
    attended = residual + jnp.concatenate(
        [dot(heads_out, out_weight[r]) + dot(low_out, out_second[r]) for r in range(rows)], axis=1
    )
    inverse_mlp = inverse_rms(attended)
    normed_mlp = low(attended * inverse_mlp * gains[1:2])

    def swap(values, step):
        return lax.ppermute(values, "dp", [(i, (i + step) % copies) for i in range(copies)])

    mixed_part, grad_part = None, None
    row_sums, col_sums = [], []
    for step in range(copies):
        group = (me - step) % copies
        h = normed_mlp if step == 0 else swap(normed_mlp, step)
        e = upstream if step == 0 else swap(upstream, step)

        def of_group(values, axis):
            return lax.dynamic_slice_in_dim(values, group * rank, rank, axis)

        front_first = jnp.concatenate([of_group(gate_first, 1), of_group(up_first, 1)], axis=1)
        front_second_now = lax.dynamic_slice_in_dim(front_second, group * 2 * rank, 2 * rank, 1)
        down_first_now = of_group(down_first, 1)
        down_second_now = of_group(down_second, 1)
        low_front = masked(dot(h, front_first))
        lowered_down = masked(
            sum(dot_turned(e[:, r * features // rows : (r + 1) * features // rows], down_second_now[r]) for r in range(rows))
        )
        hidden_grad = jnp.einsum(
            "mrn,rfn->mf", e.reshape(e.shape[0], rows, -1), back_weight, preferred_element_type=jnp.float32
        ) + dot_turned(lowered_down, down_first_now)
        hidden_parts, front_parts = [], []
        for c in range(cols):
            raw = dot(h, front_weight[c]) + dot(low_front, front_second_now[c])
            gate, up = raw[:, :width_ff], raw[:, width_ff:]
            upstream_now = hidden_grad[:, c * width_ff : (c + 1) * width_ff]
            sigmoid = jax.nn.sigmoid(gate)
            hidden_parts.append(low(gate * sigmoid * up))
            front_parts.append(
                jnp.concatenate(
                    [low(upstream_now * up * sigmoid * (1.0 + gate * (1.0 - sigmoid))), low(upstream_now * gate * sigmoid)],
                    axis=1,
                )
            )
        hidden = jnp.concatenate(hidden_parts, axis=1)
        lowered_front = masked(sum(dot_turned(front_parts[c], front_second_now[c]) for c in range(cols)))
        grad = sum(dot_turned(front_parts[c], front_weight[c]) for c in range(cols)) + dot_turned(lowered_front, front_first)
        low_down = masked(dot(hidden, down_first_now))
        mixed = jnp.concatenate(
            [dot(hidden, back_weight[r]) + dot(low_down, down_second_now[r]) for r in range(rows)], axis=1
        )
        row_sums.append(jnp.concatenate([over_tokens(lowered_front, h), over_tokens(low_down, e)], axis=0))
        gate_up_sums = [over_tokens(low_front, front_parts[c]) for c in range(cols)]
        col_sums.append(
            jnp.concatenate(
                [
                    jnp.concatenate([g[:rank, :width_ff] for g in gate_up_sums], axis=1),
                    jnp.concatenate([g[rank:, width_ff:] for g in gate_up_sums], axis=1),
                    over_tokens(lowered_down, hidden),
                ],
                axis=0,
            )
        )
        if step == 0:
            mixed_part, grad_part = mixed, grad
        else:
            grad_part = grad_part + swap(low(grad), -step).astype(jnp.float32)
            mixed_part = mixed_part + swap(low(mixed), -step).astype(jnp.float32)

    def by_group(values):
        stacked = jnp.stack(values)
        return jnp.concatenate(
            [lax.dynamic_index_in_dim(stacked, (me - g) % copies, 0, keepdims=False) for g in range(copies)], axis=0
        )

    def own_group(values):
        return jnp.concatenate([jnp.where(me == g, values, 0.0) for g in range(copies)], axis=0)

    def sum_rows(values):
        cut = values.reshape(values.shape[0], rows, -1).transpose(1, 0, 2)
        return lax.psum(lax.psum_scatter(cut, "row", scatter_dimension=0), ("col", "dp"))

    def sum_cols(values, axes):
        cut = values.reshape(values.shape[0], cols, -1).transpose(1, 0, 2)
        return lax.psum(lax.psum_scatter(cut, "col", scatter_dimension=0), axes)

    def slots(values, count, at):
        return values.reshape(copies, count, rank, -1)[:, at].reshape(copies * rank, -1)

    def wide_second(values):
        return lax.dot_general(
            choose_wide, values, (((1,), (0,)), ((), ())), precision=lax.Precision.HIGHEST, preferred_element_type=jnp.float32
        )

    def wide_first(values):
        return lax.dot_general(
            values, choose_wide, (((0,), (1,)), ((), ())), precision=lax.Precision.HIGHEST, preferred_element_type=jnp.float32
        )

    mlp_rows = sum_rows(by_group(row_sums))
    gate_first_gradient, up_first_gradient = (wide_first(slots(mlp_rows, 3, i)) for i in range(2))
    down_second_gradient = wide_second(slots(mlp_rows, 3, 2))
    mlp_cols = lax.all_gather(sum_cols(by_group(col_sums), "row"), "dp", axis=1, tiled=True)
    gate_second_gradient, up_second_gradient = (wide_second(slots(mlp_cols, 3, i)) for i in range(2))
    down_first_gradient = wide_first(slots(mlp_cols, 3, 2))

    mixed_tokens = low(attended + mixed_part)
    attended_grad = upstream.astype(jnp.float32) + norm_back(attended, gains[1:2], inverse_mlp, grad_part)

    out_grad = low(attended_grad)
    row_width = features // rows
    lowered_out = masked(
        sum(dot_turned(out_grad[:, r * row_width : (r + 1) * row_width], out_second[r]) for r in range(rows))
    )
    heads_grad = low(
        sum(dot_turned(out_grad[:, r * row_width : (r + 1) * row_width], out_weight[r]) for r in range(rows))
        + dot_turned(lowered_out, out_first)
    )
    unit_grad = exchange(to_units(heads_grad, units // seqs)).reshape(length, -1)
    unit_grad = jnp.pad(unit_grad, ((0, 0), (0, pad_width)))
    query_grad, kv_grad = attend_back(
        unit_queries, unit_grad, unit_out, log_sums, keys_twice, values_twice, unit_keys.T, ends, heads, factor
    )
    moved = exchange(jnp.concatenate([query_grad[:, :unit_width], kv_grad], axis=1))
    moved = moved.reshape(seqs, units // seqs, part, -1)
    query_moved = from_units(moved[..., :unit_width]).astype(jnp.float32)
    kv_moved = moved[..., unit_width:].astype(jnp.float32).reshape(seqs, kv_heads, kv_copies, part, -1).sum(axis=2)
    key_moved = from_units(kv_moved[..., :HEAD_DIM])
    value_moved = from_units(kv_moved[..., HEAD_DIM:])
    query_back = low(rope_back(query_moved, cosine, sine))
    key_back = low(rope_back(key_moved, cosine, sine))
    value_back = low(value_moved)
    qkv_grad = [
        jnp.concatenate(
            [
                query_back[:, c * width_q : (c + 1) * width_q],
                key_back[:, c * width_kv : (c + 1) * width_kv],
                value_back[:, c * width_kv : (c + 1) * width_kv],
            ],
            axis=1,
        )
        for c in range(cols)
    ]
    lowered_qkv = masked(sum(dot_turned(qkv_grad[c], qkv_second[c]) for c in range(cols)))
    normed_grad = sum(dot_turned(qkv_grad[c], qkv_weight[c]) for c in range(cols)) + dot_turned(lowered_qkv, qkv_first)
    token_grad = low(attended_grad + norm_back(residual, gains[0:1], inverse_attn, normed_grad))

    attn_rows = sum_rows(own_group(jnp.concatenate([over_tokens(lowered_qkv, normed), over_tokens(low_out, out_grad)], axis=0)))
    query_first_gradient, key_first_gradient, value_first_gradient = (
        wide_first(slots(attn_rows, 4, i)) for i in range(3)
    )
    output_second_gradient = wide_second(slots(attn_rows, 4, 3))
    qkv_sums = [over_tokens(low_qkv, qkv_grad[c]) for c in range(cols)]
    out_sums = over_tokens(lowered_out, heads_out).reshape(rank, cols, -1)
    attn_cols = sum_cols(
        own_group(
            jnp.concatenate(
                [
                    jnp.concatenate(
                        [
                            qkv_sums[c][:rank, :width_q],
                            out_sums[:, c],
                            qkv_sums[c][rank : 2 * rank, width_q : width_q + width_kv],
                            qkv_sums[c][2 * rank :, width_q + width_kv :],
                        ],
                        axis=1,
                    )
                    for c in range(cols)
                ],
                axis=1,
            )
        ),
        ("row", "dp"),
    )
    query_second_gradient = wide_second(attn_cols[:, :width_q])
    output_first_gradient = wide_first(attn_cols[:, width_q : 2 * width_q])
    key_second_gradient = wide_second(attn_cols[:, 2 * width_q : 2 * width_q + width_kv])
    value_second_gradient = wide_second(attn_cols[:, 2 * width_q + width_kv :])

    return (
        to_features(mixed_tokens, seqs),
        to_features(token_grad, seqs),
        query_first_gradient,
        query_second_gradient,
        key_first_gradient,
        key_second_gradient,
        value_first_gradient,
        value_second_gradient,
        output_first_gradient,
        output_second_gradient,
        gate_first_gradient,
        gate_second_gradient,
        up_first_gradient,
        up_second_gradient,
        down_first_gradient,
        down_second_gradient,
    )


def solution(mesh):
    in_specs = (
        P("col", "dp", "row"),
        P("col", "dp", "row"),
        P("dp", None),
        P("dp"),
        P(),
        P("row"),
        P("row"),
        P("row", "col"),
        P("row", "col"),
        P("row", "col"),
        P("col", "row"),
        P("row", "col"),
        P("row", "col"),
        P("col", "row"),
        P("row", None),
        P(None, "col"),
        P("row", None),
        P(None, "col"),
        P("row", None),
        P(None, "col"),
        P("col", None),
        P(None, "row"),
        P("row", None),
        P(None, "col"),
        P("row", None),
        P(None, "col"),
        P("col", None),
        P(None, "row"),
    )
    out_specs = (
        P("col", "dp", "row"),
        P("col", "dp", "row"),
        P("row", None),
        P(None, "col"),
        P("row", None),
        P(None, "col"),
        P("row", None),
        P(None, "col"),
        P("col", None),
        P(None, "row"),
        P("row", None),
        P(None, "col"),
        P("row", None),
        P(None, "col"),
        P("col", None),
        P(None, "row"),
    )
    return jax.shard_map(local, mesh=mesh, in_specs=in_specs, out_specs=out_specs, check_vma=False)
```

time: 7730 us -> 1500 us (0.19)
  waiting for transfers between devices: 4460 us -> 310 us
  matrix products: 1780 us -> 382 us
  local copies, waits for them, and re-layouts: 916 us -> 192 us
  other arithmetic: 503 us -> 104 us
  Pallas kernels: 0 us -> 209 us
  blocking collectives: 28.4 us -> 196 us
    unnamed x22 -> x13, waiting for transfers between devices: 2290 us -> 0.88 us
    dot_general x106 -> x151, matrix products: 1780 us -> 382 us  [the longest x61 172 us: dot(): lax.dot_general(left, right, (((1,), (0,)), ((), ())), preferred_element_...]
    all_gather x9 -> x6, waiting for transfers between devices: 1020 us -> 6.23 us  [the longest x1 6.16 us: local(): lax.all_gather(jnp.concatenate([query_weight, key_weight, value_weight],...]
    reduce_scatter x7 -> x4, waiting for transfers between devices: 990 us -> 0.01 us  [the longest x2 0.01 us: sum_cols(): return lax.psum(lax.psum_scatter(cut, 'col', scatter_dimension=0), axes)]
    reshape x25 -> x8, local copies, waits for them, and re-layouts: 320 us -> 29.2 us  [the longest x2 17.8 us: to_tokens(): values.reshape(rows, part // rows, seqs, features).transpose(0, 2, 1, 3)]
    all_gather x7 -> x0, local copies, waits for them, and re-layouts: 237 us -> none  [the longest x4 129 us: gather_columns(): gathered = lax.all_gather(values, 'col', axis=0, tiled=True)]
    pallas_call x0 -> x2, Pallas kernels: none -> 209 us  [the longest x1 116 us: attend_back(): pl.pallas_call(functools.partial(bwd_kernel, heads, factor), grid=(length...]
    convert_element_type x12 -> x16, other arithmetic: 246 us -> 51.1 us  [the longest x14 44 us: low(): return values.astype(jnp.bfloat16)]
  transfers between devices with their start and end apart: 20 -> 25, of which waited for: 17 -> 12; matrix products, arithmetic and copies ran while one was open for 17% -> 32% of each run, Pallas kernels for 0% -> 14%
where the time goes in v1:
time: 1500 us; the launch traced here: 1490 us
  matrix products  382 us (25%)
  waiting for transfers between devices  310 us (21%)
  Pallas kernels  209 us (14%)
  blocking collectives  196 us (13%)
  local copies, waits for them, and re-layouts  192 us (13%)
  other arithmetic  104 us (7%)
  starting transfers between devices  77.2 us (5%)
  between operations  19.7 us (1%)
    dot_general x61, matrix products, dot(): lax.dot_general(left, right, (((1,), (0,)), ((), ())), preferred_element_...  172 us
    dot_general x46, matrix products, dot_turned(): lax.dot_general(left, right, (((1,), (1,)), ((), ())), preferred_element_...  136 us
    all_gather x1, blocking collectives, local(): lax.all_gather(first_of(down_first_half, choose_low), 'col', axis=0, tile...  121 us
    pallas_call x1, Pallas kernels, attend_back(): pl.pallas_call(functools.partial(bwd_kernel, heads, factor), grid=(length...  116 us
    pallas_call x1, Pallas kernels, attend(): pl.pallas_call(functools.partial(fwd_kernel, heads, factor), grid=(length...  93 us
    psum x1, waiting for transfers between devices, sum_rows(): lax.psum(lax.psum_scatter(cut, 'row', scatter_dimension=0), ('col', 'dp'))  72.2 us
    all_to_all x4, waiting for transfers between devices, exchange(): lax.all_to_all(values.reshape(units, part, -1), turned_both, 0, 0, tiled=...  70.5 us
    psum x2, waiting for transfers between devices, sum_cols(): return lax.psum(lax.psum_scatter(cut, 'col', scatter_dimension=0), axes)  64 us
  transfers between devices with their start and end apart: 25, of which 12 were waited for; matrix products, arithmetic and copies ran while one was open for 32% of the time, Pallas kernels for 14%

profile of v1, /device:TPU:0, one launch (start us, length us, event | category | flops | bytes accessed | tf_op | source)
XLA Modules:
  0.0 1490.7 jit_solution(18237998918926921036)
XLA Ops:
  27.9 7.3 copy.279
  41.3 10.5 copy.300
  63.0 25.3 %all-gather = bf16[384,768]{1,0:T(8,128)(2,1)} all-gather(bf16[96,768]{1,0:T(8,128)(2,1)S(1)} %fusion.215), channel_id=2, replica_groups=mesh['dp'=2,'row'=4,'col'=4] {'col'}, dimensions={0}, use_global_device_ids=true | all-gather | bytes 737280 | tf_op jit(solution)/shard_map/all_gather | solution.py:392
  88.4 15.1 %all_gather.46 = bf16[2048,226]{0,1:T(8,128)(2,1)S(1)} all-gather(bf16[512,226]{0,1:T(8,128)(2,1)S(1)} %concatenate.217), channel_id=1, replica_groups=mesh['dp'=2,'row'=4,'col'=4] {'row'}, dimensions={0}, use_global_device_ids=true | all-gather | bytes 1157120 | tf_op jit(solution)/shard_map/all_gather | solution.py:388
  121.8 6.2 all-gather.10.cloned.1.call-done
  180.2 14.6 all-gather.1
  195.2 121.5 %all_gather.58 = bf16[4096,64]{0,1:T(8,128)(2,1)S(1)} all-gather(bf16[1024,64]{0,1:T(8,128)(2,1)S(1)} %convolution_convert_fusion), channel_id=1, replica_groups=mesh['dp'=2,'row'=4,'col'=4] {'col'}, dimensions={0}, use_global_device_ids=true | all-gather | bytes 655360 | tf_op jit(solution)/shard_map/all_gather | solution.py:415
  321.4 14.4 all_gather.51
  339.3 6.4 copy.301
  351.7 15.2 %collective-permute-done.2 = bf16[512,2048]{0,1:T(8,128)(2,1)} collective-permute-done((bf16[512,2048]{0,1:T(8,128)(2,1)S(1)}, bf16[512,2048]{0,1:T(8,128)(2,1)}, u32[]{:S(2)}, u32[]{:S(2)}) %collective-permute-start.2) | collective-permute-done | bytes 2097184 | tf_op jit(solution)/shard_map/ppermute | solution.py:483
  381.2 93.0 %attend_forward.1 = (bf16[4096,256]{1,0:T(8,128)(2,1)S(1)}, f32[8,4096]{1,0:T(8,128)S(1)}) custom-call(s32[1,4096]{1,0:T(1,128)S(1)} %bitcast.424, bf16[4096,256]{1,0:T(8,128)(2,1)S(1)} %copy.296.q_ref, bf16[4096,128]{1,0:T(8,128)(2,1)S(1)} %copy.297.k2_ref, bf16[64,4096]{1,0:T(8,128)(2,1)S(1)} %copy-done.6), custom_call_target="tpu_custom_call" | custom-call | flops 8589934592 | bytes 5767168 | tf_op jit(solution)/shard_map/attend_forward/pallas_call | solution.py:88
  491.1 16.3 %bitcast_add_fusion = f32[512,4096]{1,0:T(8,128)} fusion(f32[512,4096]{1,0:T(8,128)} %fusion.205, bf16[4,4096,512]{2,1,0:T(8,128)(2,1)} %bitcast.583, bf16[512,4,512]{0,2,1:T(8,128)(2,1)} %bitcast.66), kind=kOutput, calls=%fused_computation | convolution fusion | flops 8592031744 | bytes 35651584 | tf_op jit(solution)/shard_map/mrn,rfn->mf/dot_general | solution.py:503
  507.4 45.5 %all-to-all-done.2 = bf16[16,256,256]{2,1,0:T(8,128)(2,1)S(1)} async-done(((bf16[16,256,256]{2,1,0:T(8,128)(2,1)}), bf16[16,256,256]{2,1,0:T(8,128)(2,1)S(1)}, u32[]{:S(2)}, u32[]{:S(2)}) %all-to-all-start.2) | async-done | bytes 2097184 | tf_op jit(solution)/shard_map/all_to_all | solution.py:452
  574.1 6.0 concatenate.237
  580.1 6.0 fusion.37
  592.8 15.1 %bitcast_add_fusion.1 = f32[512,4096]{1,0:T(8,128)} fusion(f32[512,4096]{1,0:T(8,128)S(1)} %bitcast.477, bf16[4,4096,512]{2,1,0:T(8,128)(2,1)} %bitcast.584, bf16[512,4,512]{2,0,1:T(8,128)(2,1)S(1)} %bitcast.534), kind=kOutput, calls=%fused_computation.1 | convolution fusion | flops 8592031744 | bytes 35651584 | tf_op jit(solution)/shard_map/mrn,rfn->mf/dot_general | solution.py:503
  610.0 27.6 %collective-permute-done = bf16[512,2048]{0,1:T(8,128)(2,1)S(1)} collective-permute-done((bf16[512,2048]{0,1:T(8,128)(2,1)S(1)}, bf16[512,2048]{0,1:T(8,128)(2,1)S(1)}, u32[]{:S(2)}, u32[]{:S(2)}) %collective-permute-start) | collective-permute-done | bytes 2097184 | tf_op jit(solution)/shard_map/ppermute | solution.py:483
  654.1 7.1 fusion.30
  669.9 7.5 fusion.55
  683.0 7.1 fusion.58
  692.9 9.7 fusion.61
  702.5 9.7 fusion.64
  712.2 6.5 multiply_convert_fusion.7
  723.6 7.3 fusion.6
  731.6 6.9 fusion.14
  739.3 7.3 fusion.22
  765.1 7.2 fusion.16
  772.3 7.0 fusion.24
  779.4 7.0 fusion.8
  786.4 7.6 fusion
  803.2 7.2 fusion.18
  810.4 7.2 fusion.26
  817.6 7.2 fusion.10
  829.5 9.8 fusion.2
  869.2 7.6 all-to-all-start.5
  908.2 25.0 %all-to-all-done.5 = bf16[16,256,256]{2,1,0:T(8,128)(2,1)} async-done(((bf16[16,256,256]{2,1,0:T(8,128)(2,1)}), bf16[16,256,256]{2,1,0:T(8,128)(2,1)}, u32[]{:S(2)}, u32[]{:S(2)}) %all-to-all-start.5) | async-done | bytes 2097184 | tf_op jit(solution)/shard_map/all_to_all | solution.py:452
  935.5 116.4 %attend_backward.1 = (bf16[4096,256]{1,0:T(8,128)(2,1)S(1)}, bf16[4096,128]{1,0:T(8,128)(2,1)S(1)}) custom-call(s32[1,4096]{1,0:T(1,128)S(1)} %bitcast.425, bf16[4096,256]{1,0:T(8,128)(2,1)} %copy-done.2, bf16[4096,256]{1,0:T(8,128)(2,1)} %bitcast.72.do_ref, bf16[4096,256]{1,0:T(8,128)(2,1)} %copy-done.3, f32[8,4096]{1,0:T(8,128)S(1)} %get-tuple-element.25.lse_ref, ...), custom_call_target="tpu_custom_call" | custom-call | flops 21474836480 | bytes 10485760 | tf_op jit(solution)/shard_map/attend_backward/pallas_call | solution.py:198
  1053.9 37.0 %all-to-all-start.6 = ((bf16[16,256,384]{2,1,0:T(8,128)(2,1)}), bf16[16,256,384]{2,1,0:T(8,128)(2,1)}, u32[]{:S(2)}, u32[]{:S(2)}) async-start(bf16[16,256,384]{2,1,0:T(8,128)(2,1)} %bitcast.487), calls=%async_computation.6 | async-start | bytes 6291456 | tf_op jit(solution)/shard_map/all_to_all | solution.py:452
  1115.4 5.9 fusion.53
  1128.0 36.9 %all-reduce.15.cloned.1.call-done = f32[192,1024]{1,0:T(8,128)} async-done(((f32[192,1024]{1,0:T(8,128)}), f32[192,1024]{1,0:T(8,128)}) %all-reduce.15.cloned.1.call-update) | async-done | bytes 786448 | tf_op jit(solution)/shard_map/psum | solution.py:559
  1169.1 7.3 copy.319
  1277.9 6.6 add_convert_fusion
  1295.3 35.0 %all-to-all-done.3 = bf16[4,2,256,512]{2,1,3,0:T(2,128)(2,1)} async-done(((bf16[4,2,256,512]{2,1,3,0:T(2,128)(2,1)}), bf16[4,2,256,512]{2,1,3,0:T(2,128)(2,1)}, u32[]{:S(2)}, u32[]{:S(2)}) %all-to-all-start.3) | async-done | bytes 2097184 | tf_op jit(solution)/shard_map/all_to_all | solution.py:271
  1340.8 10.4 copy.299
  1351.2 9.6 all-to-all-done.7
  1360.8 7.3 copy.327
  1368.1 27.1 %all-reduce.13.cloned.1.call-done = f32[64,1280]{1,0:T(8,128)} async-done(((f32[64,1280]{1,0:T(8,128)}), f32[64,1280]{1,0:T(8,128)}) %all-reduce.13.cloned.1.call-update) | async-done | bytes 327696 | tf_op jit(solution)/shard_map/psum | solution.py:559
  1402.5 72.2 %all-reduce.17.cloned.1.call-done = (f32[2,4,32,512]{3,2,1,0:T(8,128)}, f32[2,3,32,512]{3,2,1,0:T(8,128)}) async-done(((f32[2,4,32,512]{3,2,1,0:T(8,128)}, f32[2,3,32,512]{3,2,1,0:T(8,128)}), (f32[2,4,32,512]{3,2,1,0:T(8,128)}, f32[2,3,32,512]{3,2,1,0:T(8,128)})) %all-reduce.17.cloned.1.call-update) | async-done | bytes 917520 | tf_op jit(solution)/shard_map/psum | solution.py:555
  (963 shorter events, 491.8 us)
Async XLA Ops:
  7.2 120.8 %all-gather.10.cloned.1.call-start = ((), (), s32[]{:S(2)}) async-start(), calls=%async_computation.12 | async-start | bytes 13369344 | tf_op jit(solution)/shard_map/all_gather | solution.py:389
  9.5 481.5 %all-gather.16.cloned.1.call-start = ((), (), s32[]{:S(2)}) async-start(), calls=%async_computation.15 | async-start | bytes 17825792 | tf_op jit(solution)/shard_map/all_gather | solution.py:414
  10.7 549.0 %all-gather.12.cloned.1.call-start = ((), (), s32[]{:S(2)}) async-start(), calls=%async_computation.13 | async-start | bytes 8912896 | tf_op jit(solution)/shard_map/all_gather | solution.py:396
  11.4 628.0 %all-gather.20.cloned.1.call-start = ((), (), s32[]{:S(2)}) async-start(), calls=%async_computation.23 | async-start | bytes 2621440 | tf_op jit(solution)/shard_map/all_gather | solution.py:407
  18.2 176.7 %copy-start.182 = (s32[64]{0:T(128)}, s32[64]{0:T(128)S(1)}, u32[]{:S(2)}) copy-start(s32[64]{0:T(128)S(1)} %and_select_fusion.1) | copy-start | bytes 772
  21.4 173.5 %copy-start.178 = (s32[64]{0:T(128)}, s32[64]{0:T(128)S(1)}, u32[]{:S(2)}) copy-start(s32[64]{0:T(128)S(1)} %fusion.297) | copy-start | bytes 772
  21.4 173.5 %copy-start.184 = (s32[128]{0:T(128)}, s32[128]{0:T(128)S(1)}, u32[]{:S(2)}) copy-start(s32[128]{0:T(128)S(1)} %get-tuple-element.166) | copy-start | bytes 1540
  21.4 173.5 %copy-start.186 = (s32[128]{0:T(128)}, s32[128]{0:T(128)S(1)}, u32[]{:S(2)}) copy-start(s32[128]{0:T(128)S(1)} %get-tuple-element.167) | copy-start | bytes 1540
  23.0 631.2 %all-gather.14.cloned.1.call-start = ((), (), s32[]{:S(2)}) async-start(), calls=%async_computation.14 | async-start | bytes 35651584 | tf_op jit(solution)/shard_map/all_gather | solution.py:402
  35.2 69.1 %all-to-all-start = ((bf16[4,2,256,512]{2,1,3,0:T(2,128)(2,1)}), bf16[4,2,256,512]{2,1,3,0:T(2,128)(2,1)}, u32[]{:S(2)}, u32[]{:S(2)}) async-start(bf16[4,2,256,512]{2,1,3,0:T(2,128)(2,1)} %bitcast.1), calls=%async_computation | async-start | bytes 4194304 | tf_op jit(solution)/shard_map/all_to_all | solution.py:263
  40.9 138.3 %copy-start.10 = (f32[512,4,32]{0,2,1:T(8,128)}, f32[512,4,32]{0,2,1:T(8,128)S(1)}, u32[]{:S(2)}) copy-start(f32[512,4,32]{0,2,1:T(8,128)S(1)} %tile.21) | copy-start | bytes 786436
  40.9 138.3 %copy-start.12 = (f32[512,4,32]{0,2,1:T(8,128)}, f32[512,4,32]{0,2,1:T(8,128)S(1)}, u32[]{:S(2)}) copy-start(f32[512,4,32]{0,2,1:T(8,128)S(1)} %tile.23) | copy-start | bytes 786436
  53.3 35.0 %copy-start.235 = (s32[512]{0:T(512)}, s32[512]{0:T(512)S(1)}, u32[]{:S(2)}) copy-start(s32[512]{0:T(512)S(1)} %add_select_fusion) | copy-start | bytes 6148
  58.5 29.9 %copy-start.45 = (f32[512,2048]{0,1:T(8,128)}, f32[512,2048]{0,1:T(8,128)S(1)}, u32[]{:S(2)}) copy-start(f32[512,2048]{0,1:T(8,128)S(1)} %constant_dynamic-update-slice_fusion.11) | copy-start | bytes 12582916
  88.4 31.2 %copy-start.150 = (f32[512,32]{0,1:T(8,128)}, f32[512,32]{0,1:T(8,128)S(1)}, u32[]{:S(2)}) copy-start(f32[512,32]{0,1:T(8,128)S(1)} %compare_select_fusion) | copy-start | bytes 196612
  104.3 62.5 %all-to-all-start.4 = ((bf16[4,2,256,512]{2,1,3,0:T(2,128)(2,1)}), bf16[4,2,256,512]{2,1,3,0:T(2,128)(2,1)}, u32[]{:S(2)}, u32[]{:S(2)}) async-start(bf16[4,2,256,512]{2,1,3,0:T(2,128)(2,1)} %bitcast.492), calls=%async_computation.4 | async-start | bytes 4194304 | tf_op jit(solution)/shard_map/all_to_all | solution.py:263
  166.8 203.8 %all-to-all-start.1 = ((bf16[16,256,384]{1,2,0:T(8,128)(2,1)}), bf16[16,256,384]{1,2,0:T(8,128)(2,1)}, u32[]{:S(2)}, u32[]{:S(2)}) async-start(bf16[16,256,384]{1,2,0:T(8,128)(2,1)} %bitcast.486), calls=%async_computation.1 | async-start | bytes 6291456 | tf_op jit(solution)/shard_map/all_to_all | solution.py:452
  176.8 139.8 %copy-start.203 = (bf16[512,128]{1,0:T(8,128)(2,1)S(1)}, bf16[512,128]{1,0:T(8,128)(2,1)}, u32[]{:S(2)}) copy-start(bf16[512,128]{1,0:T(8,128)(2,1)} %param.48) | copy-start | bytes 393220
  176.8 140.1 %copy-start.43 = (bf16[2048,226]{0,1:T(8,128)(2,1)S(1)}, bf16[2048,226]{0,1:T(8,128)(2,1)}, u32[]{:S(2)}) copy-start(bf16[2048,226]{0,1:T(8,128)(2,1)} %copy-done.42) | copy-start | bytes 2777092
  194.9 140.9 %copy-start.71 = (bf16[384,512]{1,0:T(8,128)(2,1)}, bf16[384,512]{1,0:T(8,128)(2,1)S(1)}, u32[]{:S(2)}) copy-start(bf16[384,512]{1,0:T(8,128)(2,1)S(1)} %all-gather.1) | copy-start | bytes 1179652
  316.7 30.3 %copy-start.62 = (bf16[4096,64]{0,1:T(8,128)(2,1)}, bf16[4096,64]{0,1:T(8,128)(2,1)S(1)}, u32[]{:S(2)}) copy-start(bf16[4096,64]{0,1:T(8,128)(2,1)S(1)} %all_gather.58) | copy-start | bytes 1572868
  319.8 26.9 %copy-start.16 = (bf16[256,8,2,256]{3,1,2,0:T(8,128)(2,1)}, bf16[256,8,2,256]{3,1,2,0:T(8,128)(2,1)S(1)}, u32[]{:S(2)}) copy-start(bf16[256,8,2,256]{3,1,2,0:T(8,128)(2,1)S(1)} %copy.363) | copy-start | bytes 6291460
  319.9 47.0 %collective-permute-start.2 = (bf16[512,2048]{0,1:T(8,128)(2,1)S(1)}, bf16[512,2048]{0,1:T(8,128)(2,1)}, u32[]{:S(2)}, u32[]{:S(2)}) collective-permute-start(bf16[512,2048]{0,1:T(8,128)(2,1)S(1)} %bitcast.466), channel_id=1, source_target_pairs={{0,16},{16,0},{1,17},{17,1},{2,18},{18,2},{3,19},{19,3},{4,20},{20... | collective-permute-start | bytes 6291464 | tf_op jit(solution)/shard_map/ppermute | solution.py:483
  335.8 144.8 %copy-start.58 = (bf16[4,64,512]{2,1,0:T(8,128)(2,1)}, bf16[4,64,512]{2,1,0:T(8,128)(2,1)S(1)}, u32[]{:S(2)}) copy-start(bf16[4,64,512]{2,1,0:T(8,128)(2,1)S(1)} %slice.947) | copy-start | bytes 786436
  379.8 94.5 %copy-start.2 = (bf16[4096,256]{1,0:T(8,128)(2,1)}, bf16[4096,256]{1,0:T(8,128)(2,1)S(1)}, u32[]{:S(2)}) copy-start(bf16[4096,256]{1,0:T(8,128)(2,1)S(1)} %copy.296.q_ref) | copy-start | bytes 6291460
  475.6 77.3 %all-to-all-start.2 = ((bf16[16,256,256]{2,1,0:T(8,128)(2,1)}), bf16[16,256,256]{2,1,0:T(8,128)(2,1)S(1)}, u32[]{:S(2)}, u32[]{:S(2)}) async-start(bf16[16,256,256]{2,1,0:T(8,128)(2,1)} %bitcast.423), calls=%async_computation.2 | async-start | bytes 4194304 | tf_op jit(solution)/shard_map/all_to_all | solution.py:452
  590.5 148.8 %copy-start.25 = (bf16[512,2048]{0,1:T(8,128)(2,1)}, bf16[512,2048]{0,1:T(8,128)(2,1)S(1)}, u32[]{:S(2)}) copy-start(bf16[512,2048]{0,1:T(8,128)(2,1)S(1)} %get-tuple-element.30) | copy-start | bytes 6291460
  590.5 47.1 %collective-permute-start = (bf16[512,2048]{0,1:T(8,128)(2,1)S(1)}, bf16[512,2048]{0,1:T(8,128)(2,1)S(1)}, u32[]{:S(2)}, u32[]{:S(2)}) collective-permute-start(bf16[512,2048]{0,1:T(8,128)(2,1)S(1)} %get-tuple-element.30), channel_id=1, source_target_pairs={{0,16},{16,0},{1,17},{17,1},{2,18},{18,2},{3,19},{19,3},{4,20},{20... | collective-permute-start | bytes 6291464 | tf_op jit(solution)/shard_map/ppermute | solution.py:483
  608.0 31.0 %copy-start.77 = (bf16[2048,32]{0,1:T(8,128)(2,1)S(1)}, bf16[2048,32]{0,1:T(8,128)(2,1)}, u32[]{:S(2)}) copy-start(bf16[2048,32]{0,1:T(8,128)(2,1)} %get-tuple-element.146) | copy-start | bytes 393220
  608.0 31.0 %copy-start.79 = (bf16[2048,32]{0,1:T(8,128)(2,1)S(1)}, bf16[2048,32]{0,1:T(8,128)(2,1)}, u32[]{:S(2)}) copy-start(bf16[2048,32]{0,1:T(8,128)(2,1)} %get-tuple-element.148) | copy-start | bytes 393220
  608.6 29.1 %copy-start.83 = (f32[512,2,32]{0,2,1:T(8,128)}, f32[512,2,32]{0,2,1:T(8,128)S(1)}, u32[]{:S(2)}) copy-start(f32[512,2,32]{0,2,1:T(8,128)S(1)} %tile.25) | copy-start | bytes 393220
  765.1 28.9 %copy-start.174 = (bf16[512,64]{0,1:T(8,128)(2,1)}, bf16[512,64]{0,1:T(8,128)(2,1)S(1)}, u32[]{:S(2)}) copy-start(bf16[512,64]{0,1:T(8,128)(2,1)S(1)} %fusion.127) | copy-start | bytes 196612
  796.5 46.6 %collective-permute-start.3 = (bf16[512,2048]{0,1:T(8,128)(2,1)}, bf16[512,2048]{0,1:T(8,128)(2,1)S(1)}, u32[]{:S(2)}, u32[]{:S(2)}) collective-permute-start(bf16[512,2048]{0,1:T(8,128)(2,1)} %add_convert_fusion.2), channel_id=1, source_target_pairs={{0,16},{16,0},{1,17},{17,1},{2,18},{18,2},{3,19},{19,3},{4,20},{20... | collective-permute-start | bytes 6291464 | tf_op jit(solution)/shard_map/ppermute | solution.py:483
  869.2 64.0 %all-to-all-start.5 = ((bf16[16,256,256]{2,1,0:T(8,128)(2,1)}), bf16[16,256,256]{2,1,0:T(8,128)(2,1)}, u32[]{:S(2)}, u32[]{:S(2)}) async-start(bf16[16,256,256]{2,1,0:T(8,128)(2,1)} %bitcast.493), calls=%async_computation.5 | async-start | bytes 4194304 | tf_op jit(solution)/shard_map/all_to_all | solution.py:452
  876.8 244.4 %reduce-scatter.11.cloned.1.call-start = ((), (), s32[]{:S(2)}) async-start(), calls=%async_computation.20 | async-start | bytes 3932160 | tf_op jit(solution)/shard_map/reduce_scatter | solution.py:559
  1053.9 37.5 %copy-start.96 = (bf16[512,1024]{1,0:T(8,128)(2,1)S(1)}, bf16[512,1024]{1,0:T(8,128)(2,1)}, u32[]{:S(2)}) copy-start(bf16[512,1024]{1,0:T(8,128)(2,1)} %get-tuple-element.67) | copy-start | bytes 3145732
  1053.9 37.5 %copy-start.98 = (bf16[512,1024]{1,0:T(8,128)(2,1)S(1)}, bf16[512,1024]{1,0:T(8,128)(2,1)}, u32[]{:S(2)}) copy-start(bf16[512,1024]{1,0:T(8,128)(2,1)} %multiply_convert_fusion.20) | copy-start | bytes 3145732
  1053.9 111.2 %all-to-all-start.6 = ((bf16[16,256,384]{2,1,0:T(8,128)(2,1)}), bf16[16,256,384]{2,1,0:T(8,128)(2,1)}, u32[]{:S(2)}, u32[]{:S(2)}) async-start(bf16[16,256,384]{2,1,0:T(8,128)(2,1)} %bitcast.487), calls=%async_computation.6 | async-start | bytes 6291456 | tf_op jit(solution)/shard_map/all_to_all | solution.py:452
  1090.9 74.1 %all-reduce.15.cloned.1.call-start = ((), (), s32[]{:S(2)}) async-start(), calls=%async_computation.21 | async-start | bytes 1572864 | tf_op jit(solution)/shard_map/psum | solution.py:559
  1121.3 212.7 %all-gather.18.cloned.1.call-start = ((), (), s32[]{:S(2)}) async-start(), calls=%async_computation.22 | async-start | bytes 2359296 | tf_op jit(solution)/shard_map/all_gather | solution.py:577
  1165.0 174.1 %reduce-scatter.7.cloned.1.call-start = ((), (), s32[]{:S(2)}) async-start(), calls=%async_computation.17 | async-start | bytes 1638400 | tf_op jit(solution)/shard_map/reduce_scatter | solution.py:559
  1210.3 157.8 %reduce-scatter.9.cloned.1.call-start = ((), (), s32[]{:S(2)}) async-start(), calls=%async_computation.19 | async-start | bytes 1966080 | tf_op jit(solution)/shard_map/reduce_scatter | solution.py:555
  1229.4 138.8 %reduce-scatter.5.cloned.1.call-start = ((), (), s32[]{:S(2)}) async-start(), calls=%async_computation.16 | async-start | bytes 2621440 | tf_op jit(solution)/shard_map/reduce_scatter | solution.py:555
  1231.3 46.5 %collective-permute-start.1 = (bf16[512,2048]{0,1:T(8,128)(2,1)}, bf16[512,2048]{0,1:T(8,128)(2,1)}, u32[]{:S(2)}, u32[]{:S(2)}) collective-permute-start(bf16[512,2048]{0,1:T(8,128)(2,1)} %pad_maximum_fusion.7), channel_id=1, source_target_pairs={{0,16},{16,0},{1,17},{17,1},{2,18},{18,2},{3,19},{19,3},{4,20},{20... | collective-permute-start | bytes 6291464 | tf_op jit(solution)/shard_map/ppermute | solution.py:483
  1288.7 41.6 %all-to-all-start.3 = ((bf16[4,2,256,512]{2,1,3,0:T(2,128)(2,1)}), bf16[4,2,256,512]{2,1,3,0:T(2,128)(2,1)}, u32[]{:S(2)}, u32[]{:S(2)}) async-start(bf16[4,2,256,512]{2,1,3,0:T(2,128)(2,1)} %bitcast.498), calls=%async_computation.3 | async-start | bytes 4194304 | tf_op jit(solution)/shard_map/all_to_all | solution.py:271
  1330.2 30.6 %all-to-all-start.7 = ((bf16[4,2,256,512]{2,1,3,0:T(2,128)(2,1)}), bf16[4,2,256,512]{2,1,3,0:T(2,128)(2,1)S(1)}, u32[]{:S(2)}, u32[]{:S(2)}) async-start(bf16[4,2,256,512]{2,1,3,0:T(2,128)(2,1)} %bitcast.494), calls=%async_computation.7 | async-start | bytes 4194304 | tf_op jit(solution)/shard_map/all_to_all | solution.py:271
  1333.9 61.4 %all-reduce.13.cloned.1.call-start = ((), (), s32[]{:S(2)}) async-start(), calls=%async_computation.18 | async-start | bytes 655360 | tf_op jit(solution)/shard_map/psum | solution.py:559
  1339.1 135.5 %all-reduce.17.cloned.1.call-start = ((), (), s32[]{:S(2)}) async-start(), calls=%async_computation.24 | async-start | bytes 1835008 | tf_op jit(solution)/shard_map/psum | solution.py:555
  (251 other events, 1218.4 us)
Sparse Core Ops, SparseCore 0:
  10.9 117.0 all-gather.9
  130.7 190.9 all-gather.15
  324.0 73.3 all-gather.11
  398.8 44.1 all-gather.19
  444.5 200.4 all-gather.13
  894.2 78.9 reduce-scatter.10
  1121.4 43.5 all-reduce.14
  1166.5 31.1 all-gather.17
  1210.4 35.0 reduce-scatter.6
  1247.9 26.8 reduce-scatter.8
  1277.5 42.6 reduce-scatter.4
  1339.3 55.9 all-reduce.12
  1398.8 75.8 all-reduce.16

commit v2 on v1

v2 whole, which is shorter than its diff:
```python
import functools, math
import jax, jax.numpy as jnp
from jax import lax
from jax.sharding import PartitionSpec as P
from jax.experimental import pallas as pl
from jax.experimental.pallas import tpu as pltpu

HEAD_DIM = 64
RANK = 16
BLOCKS = 32
EPS = 1e-05
ROPE_BASE = 500000.0
TILE = 512
REACH = 256
LOG2E = math.log2(math.e)
NEG = -1e30


def nt(a, b):
    return lax.dot_general(a, b, (((1,), (1,)), ((), ())), preferred_element_type=jnp.float32)


def nn(a, b):
    return lax.dot_general(a, b, (((1,), (0,)), ((), ())), preferred_element_type=jnp.float32)


def half_of(x, e):
    lane = lax.broadcasted_iota(jnp.int32, x.shape, 1)
    return jnp.where((lane < 64) if e == 0 else (lane >= 64), x, jnp.zeros_like(x))


def fwd_kernel(heads, factor, end_ref, q_ref, k2_ref, vt_ref, o_ref, lse_ref, acc_ref, m_ref, l_ref):
    i = pl.program_id(0)
    tq = q_ref.shape[0]
    q0 = i * tq
    c = factor * LOG2E
    ends = end_ref[...]
    m_ref[...] = jnp.full_like(m_ref, NEG)
    l_ref[...] = jnp.zeros_like(l_ref)
    acc_ref[...] = jnp.zeros_like(acc_ref)

    def tile(k0, size, masked):
        kk = k2_ref[pl.ds(k0, size), :]
        vv = vt_ref[:, pl.ds(k0, size)]
        if masked:
            allowed = (lax.broadcasted_iota(jnp.int32, (size, tq), 0) + k0) < ends
        for h in range(heads):
            qh = half_of(q_ref[:, (h // 2) * 128:(h // 2 + 1) * 128], h % 2)
            s = nt(kk, qh) * c
            if masked:
                s = jnp.where(allowed, s, NEG)
            m_old = m_ref[h:h + 1, :]
            m_new = jnp.maximum(m_old, jnp.max(s, axis=0, keepdims=True))
            p = jnp.exp2(s - m_new)
            alpha = jnp.exp2(m_old - m_new)
            l_ref[h:h + 1, :] = l_ref[h:h + 1, :] * alpha + jnp.sum(p, axis=0, keepdims=True)
            m_ref[h:h + 1, :] = m_new
            a = pl.ds(h * 64, 64)
            acc_ref[a, :] = acc_ref[a, :] * alpha + nn(vv, p.astype(jnp.bfloat16))

    def body(j, _):
        tile(pl.multiple_of(j * tq, tq), tq, False)
        return 0

    lax.fori_loop(0, i, body, 0)
    tile(pl.multiple_of(q0, tq), tq, True)

    @pl.when(i < pl.num_programs(0) - 1)
    def _():
        tile(pl.multiple_of(q0 + tq, REACH), REACH, True)

    lse_ref[...] = m_ref[...] + jnp.log2(l_ref[...])
    inv = 1.0 / l_ref[...]
    for p in range(o_ref.shape[1] // 128):
        parts = []
        for h in (2 * p, 2 * p + 1):
            if h < heads:
                parts.append(acc_ref[h * 64:(h + 1) * 64, :] * inv[h:h + 1, :])
            else:
                parts.append(jnp.zeros((64, tq), jnp.float32))
        o_ref[:, p * 128:(p + 1) * 128] = jnp.concatenate(parts, axis=0).T.astype(o_ref.dtype)


def attend(q, k2, vt, ends, heads, factor):
    length, width = q.shape
    tq = min(TILE, length)
    rows = 8
    return pl.pallas_call(
        functools.partial(fwd_kernel, heads, factor),
        grid=(length // tq,),
        in_specs=[
            pl.BlockSpec((1, tq), lambda i: (0, i)),
            pl.BlockSpec((tq, width), lambda i: (i, 0)),
            pl.BlockSpec((length, 128), lambda i: (0, 0)),
            pl.BlockSpec((64, length), lambda i: (0, 0)),
        ],
        out_specs=[
            pl.BlockSpec((tq, width), lambda i: (i, 0)),
            pl.BlockSpec((rows, tq), lambda i: (0, i)),
        ],
        out_shape=[
            jax.ShapeDtypeStruct((length, width), jnp.bfloat16),
            jax.ShapeDtypeStruct((rows, length), jnp.float32),
        ],
        scratch_shapes=[
            pltpu.VMEM((heads * 64, tq), jnp.float32),
            pltpu.VMEM((rows, tq), jnp.float32),
            pltpu.VMEM((rows, tq), jnp.float32),
        ],
        compiler_params=pltpu.CompilerParams(vmem_limit_bytes=48 * 2**20),
        cost_estimate=pl.CostEstimate(
            flops=2 * heads * length * length * 64, bytes_accessed=4 * length * width + length * 384, transcendentals=heads * length * length // 2
        ),
        name="attend_forward",
    )(ends, q, k2, vt)


def turn_back(values, cosine, sine):
    high, rest = values[:32, :], values[32:, :]
    return jnp.concatenate([high * cosine + rest * sine, rest * cosine - high * sine], axis=0)


def bwd_kernel(heads, factor, end_ref, cos_ref, sin_ref, q_ref, do_ref, o_ref, lse_ref, k2_ref, v2_ref, kt_ref, dq_ref, dkv_ref, dqt_ref, delta_ref, dk_ref, dv_ref):
    j = pl.program_id(0)
    n = pl.num_programs(0)
    tk = k2_ref.shape[0]
    length, width = q_ref.shape
    c = factor * LOG2E

    @pl.when(j == 0)
    def _():
        dqt_ref[...] = jnp.zeros_like(dqt_ref)
        delta_ref[...] = jnp.zeros_like(delta_ref)
        for t in range(length // tk):
            rows = slice(t * tk, (t + 1) * tk)
            for p in range(width // 128):
                prod = do_ref[rows, p * 128:(p + 1) * 128].astype(jnp.float32) * o_ref[rows, p * 128:(p + 1) * 128].astype(jnp.float32)
                turned = prod.T
                for h in (2 * p, 2 * p + 1):
                    if h < heads:
                        delta_ref[h:h + 1, rows] = jnp.sum(turned[(h % 2) * 64:(h % 2 + 1) * 64, :], axis=0, keepdims=True)

    dk_ref[...] = jnp.zeros_like(dk_ref)
    dv_ref[...] = jnp.zeros_like(dv_ref)

    def tile(q0, size, masked):
        rows = pl.ds(q0, tk)
        kk = k2_ref[:size, :]
        vv = v2_ref[:size, :]
        kt = kt_ref[:, :size]
        if masked:
            allowed = (lax.broadcasted_iota(jnp.int32, (size, tk), 0) + j * tk) < end_ref[:, rows]
        for h in range(heads):
            lanes = slice((h // 2) * 128, (h // 2 + 1) * 128)
            qh = half_of(q_ref[rows, lanes], h % 2)
            gh = half_of(do_ref[rows, lanes], h % 2)
            s = nt(kk, qh) * c - lse_ref[h:h + 1, rows]
            if masked:
                s = jnp.where(allowed, s, NEG)
            p = jnp.exp2(s)
            dp = nt(vv, gh)
            ds = (p * (dp - delta_ref[h:h + 1, rows])).astype(jnp.bfloat16)
            dv_ref[:size, :] += nn(p.astype(jnp.bfloat16), gh)
            dk_ref[:size, :] += nn(ds, qh)
            dqt_ref[h * 64:(h + 1) * 64, rows] += nn(kt, ds)

    @pl.when(j > 0)
    def _():
        tile(pl.multiple_of((j - 1) * tk, tk), REACH, True)

    tile(pl.multiple_of(j * tk, tk), tk, True)

    def body(i, _):
        tile(pl.multiple_of(i * tk, tk), tk, False)
        return 0

    lax.fori_loop(j + 1, n, body, 0)

    own = pl.ds(pl.multiple_of(j * tk, tk), tk)
    dk = dk_ref[...].T
    dv = dv_ref[...].T
    dk = turn_back(dk[:64] + dk[64:], cos_ref[:, own], sin_ref[:, own]) * factor
    dkv_ref[...] = jnp.concatenate([dk, dv[:64] + dv[64:]], axis=0).T.astype(dkv_ref.dtype)

    @pl.when(j == n - 1)
    def _():
        for t in range(length // tk):
            rows = slice(t * tk, (t + 1) * tk)
            for p in range(width // 128):
                parts = []
                for h in (2 * p, 2 * p + 1):
                    if h < heads:
                        parts.append(turn_back(dqt_ref[h * 64:(h + 1) * 64, rows], cos_ref[:, rows], sin_ref[:, rows]) * factor)
                    else:
                        parts.append(jnp.zeros((64, tk), jnp.float32))
                dq_ref[rows, p * 128:(p + 1) * 128] = jnp.concatenate(parts, axis=0).T.astype(dq_ref.dtype)


def attend_back(q, do, o, lse, k2, v2, kt, ends, cosine, sine, heads, factor):
    length, width = q.shape
    tk = min(TILE, length)
    whole = lambda shape: pl.BlockSpec(shape, lambda j: (0, 0))
    return pl.pallas_call(
        functools.partial(bwd_kernel, heads, factor),
        grid=(length // tk,),
        in_specs=[
            whole((1, length)),
            whole((32, length)),
            whole((32, length)),
            whole((length, width)),
            whole((length, width)),
            whole((length, width)),
            whole((8, length)),
            pl.BlockSpec((tk, 128), lambda j: (j, 0)),
            pl.BlockSpec((tk, 128), lambda j: (j, 0)),
            pl.BlockSpec((64, tk), lambda j: (0, j)),
        ],
        out_specs=[
            whole((length, width)),
            pl.BlockSpec((tk, 128), lambda j: (j, 0)),
        ],
        out_shape=[
            jax.ShapeDtypeStruct((length, width), jnp.bfloat16),
            jax.ShapeDtypeStruct((length, 128), jnp.float32),
        ],
        scratch_shapes=[
            pltpu.VMEM((heads * 64, length), jnp.float32),
            pltpu.VMEM((8, length), jnp.float32),
            pltpu.VMEM((tk, 128), jnp.float32),
            pltpu.VMEM((tk, 128), jnp.float32),
        ],
        compiler_params=pltpu.CompilerParams(vmem_limit_bytes=48 * 2**20),
        cost_estimate=pl.CostEstimate(
            flops=5 * heads * length * length * 64, bytes_accessed=8 * length * width + length * 512, transcendentals=heads * length * length // 2
        ),
        name="attend_backward",
    )(ends, cosine, sine, q, do, o, lse, k2, v2, kt)


def buffered_once(shape, index_map):
    return pl.BlockSpec(shape, index_map, pipeline_mode=pl.Buffered(1))


def normalized(values, gain):
    inverse = lax.rsqrt(jnp.mean(values * values, axis=-1, keepdims=True) + EPS)
    return inverse, (values * inverse * gain).astype(jnp.bfloat16)


def norm_back(values, inverse, gain, upstream):
    scaled = upstream * gain
    weighted = jnp.mean(scaled * values, axis=-1, keepdims=True)
    return inverse * scaled - values * (inverse * inverse * inverse * weighted)


def qkv_kernel(pairs, kv_heads, token_ref, gain_ref, mask_ref, first_ref, second_ref, cos_ref, sin_ref, *refs):
    weight_refs, refs = refs[:3], refs[3:]
    message_refs, low_ref, normed_ref = refs[:pairs], refs[pairs], refs[pairs + 1]
    rows, lanes, chunk = weight_refs[0].shape[1:]
    count = token_ref.shape[0]
    seqs, _, units, part, _ = message_refs[0].shape
    pair_width = message_refs[0].shape[4] - 2 * HEAD_DIM

    @pl.when(pl.program_id(0) == 0)
    def _():
        _, normed = normalized(token_ref[...].astype(jnp.float32), gain_ref[...])
        normed_ref[...] = normed
        low_ref[...] = (nt(normed, first_ref[...]) * mask_ref[...]).astype(jnp.bfloat16)

    raw = jnp.concatenate(
        [nn(normed_ref[...], w[0].reshape(rows * lanes, chunk)) for w in weight_refs], axis=1
    ) + nn(low_ref[...], second_ref[0])
    width = raw.shape[1]
    lane = lax.broadcasted_iota(jnp.int32, raw.shape, 1)
    turned = jnp.where(lane % HEAD_DIM < HEAD_DIM // 2, -pltpu.roll(raw, width - HEAD_DIM // 2, 1), pltpu.roll(raw, HEAD_DIM // 2, 1))
    out = (raw * cos_ref[...] + turned * sin_ref[...]).astype(jnp.bfloat16)
    head_width = width // kv_heads
    for s in range(seqs):
        at = slice(s * part, (s + 1) * part)
        for u in range(units):
            base = u * kv_heads // units * head_width
            inside = u % (units // kv_heads) * pairs * pair_width
            kv = out[at, base + head_width - 2 * HEAD_DIM : base + head_width]
            for p in range(pairs):
                begin = base + inside + p * pair_width
                queries = out[at, begin : begin + pair_width]
                message_refs[p][s, 0, u] = jnp.concatenate([queries, kv], axis=1) if p == 0 else queries


def project_qkv(tokens, gain, mask, first, second, cosine, sine, weight, seqs, units, pairs, pair_width, kv_heads):
    count, features = tokens.shape
    cols, rows, lanes, _ = weight.shape
    width = second.shape[2]
    chunk = width // 3
    part = count // seqs
    ahead = lanes // chunk
    whole = lambda shape: pl.BlockSpec(shape, lambda c: (0,) * len(shape))
    message = lambda wide: (seqs, cols, units // (seqs * cols), part, wide)
    widths = [pair_width + 2 * HEAD_DIM] + [pair_width] * (pairs - 1)
    block = lambda wide: pl.BlockSpec((seqs, 1) + message(wide)[2:], lambda c: (0, c, 0, 0, 0))
    weights = lambda at: pl.BlockSpec((1, rows, lanes, chunk), lambda c: (c, 0, 0, ahead + at))
    return pl.pallas_call(
        functools.partial(qkv_kernel, pairs, kv_heads),
        grid=(cols,),
        in_specs=[
            whole((count, features)),
            whole((1, features)),
            whole(mask.shape),
            whole(first.shape),
            pl.BlockSpec((1,) + second.shape[1:], lambda c: (c, 0, 0)),
            whole((count, width)),
            whole((count, width)),
            weights(0),
            weights(1),
            weights(2),
        ],
        out_specs=[block(w) for w in widths] + [whole(mask.shape)],
        out_shape=[jax.ShapeDtypeStruct(message(w), jnp.bfloat16) for w in widths]
        + [jax.ShapeDtypeStruct(mask.shape, jnp.bfloat16)],
        scratch_shapes=[pltpu.VMEM((count, features), jnp.bfloat16)],
        compiler_params=pltpu.CompilerParams(vmem_limit_bytes=48 * 2**20),
        cost_estimate=pl.CostEstimate(
            flops=2 * count * features * cols * width,
            bytes_accessed=2 * features * cols * width + 4 * count * features,
            transcendentals=count,
        ),
        name="project_qkv",
    )(tokens, gain, mask, first, second, cosine, sine, weight, weight, weight)


def qkv_back_kernel(
    pairs, token_ref, attended_ref, gain_ref, mask_ref, first_ref, second_ref, low_ref, kv_ref, *refs
):
    query_refs, refs = refs[:pairs], refs[pairs:]
    weight_refs, refs = refs[:3], refs[3:]
    out_ref, rows_ref, cols_ref, grad_ref, lowered_ref, low_turned_ref = refs
    c = pl.program_id(0)
    rows, lanes, chunk = weight_refs[0].shape[1:]
    seqs, _, kv_heads, part, _ = kv_ref.shape
    units = query_refs[0].shape[2]
    rank = mask_ref.shape[1] // 3

    @pl.when(c == 0)
    def _():
        grad_ref[...] = jnp.zeros_like(grad_ref)
        lowered_ref[...] = jnp.zeros_like(lowered_ref)
        low_turned_ref[...] = low_ref[...].astype(jnp.float32).T.astype(jnp.bfloat16)

    parts = []
    for j in range(kv_heads):
        for u in range(j * units // kv_heads, (j + 1) * units // kv_heads):
            parts += [jnp.concatenate([q[s, 0, u] for s in range(seqs)], axis=0) for q in query_refs]
        parts.append(jnp.concatenate([kv_ref[s, 0, j] for s in range(seqs)], axis=0))
    e = jnp.concatenate(parts, axis=1)
    for r in range(rows):
        total = nt(e[:, :chunk], weight_refs[0][0, r])
        for i in (1, 2):
            total += nt(e[:, i * chunk : (i + 1) * chunk], weight_refs[i][0, r])
        grad_ref[:, r * lanes : (r + 1) * lanes] += total
    lowered_ref[...] += nt(e, second_ref[0])
    sums = nn(low_turned_ref[...], e)
    lane = lax.broadcasted_iota(jnp.int32, (rank, sums.shape[1]), 1) % (sums.shape[1] // kv_heads)
    query_lanes = sums.shape[1] // kv_heads - 2 * HEAD_DIM
    cols_ref[0] = jnp.where(
        lane < query_lanes,
        sums[:rank],
        jnp.where(lane < query_lanes + HEAD_DIM, sums[rank : 2 * rank], sums[2 * rank :]),
    ).astype(cols_ref.dtype)

    @pl.when(c == pl.num_programs(0) - 1)
    def _():
        lowered = lowered_ref[...] * mask_ref[...]
        grad = grad_ref[...] + nn(lowered.astype(jnp.bfloat16), first_ref[...])
        values = token_ref[...].astype(jnp.float32)
        inverse, normed = normalized(values, gain_ref[...])
        turned = nn(lowered.T.astype(jnp.bfloat16), normed)
        out = (attended_ref[...] + norm_back(values, inverse, gain_ref[...], grad)).astype(jnp.bfloat16)
        for r in range(rows):
            at = slice(r * lanes, (r + 1) * lanes)
            out_ref[r] = out[:, at]
            rows_ref[r] = turned[:, at].astype(rows_ref.dtype)


def project_qkv_back(tokens, attended_grad, gain, mask, first, second, low_qkv, kv, queries, weight):
    count, features = tokens.shape
    cols, rows, lanes, _ = weight.shape
    width = second.shape[2]
    chunk = width // 3
    ahead = lanes // chunk
    rank = mask.shape[1] // 3
    pairs = len(queries)
    whole = lambda shape: buffered_once(shape, lambda c: (0,) * len(shape))
    by_unit = lambda v: pl.BlockSpec((v.shape[0], 1) + v.shape[2:], lambda c: (0, c, 0, 0, 0))
    weights = lambda at: pl.BlockSpec((1, rows, lanes, chunk), lambda c: (c, 0, 0, ahead + at))
    return pl.pallas_call(
        functools.partial(qkv_back_kernel, pairs),
        grid=(cols,),
        in_specs=[
            whole((count, features)),
            whole((count, features)),
            whole((1, features)),
            whole(mask.shape),
            whole(first.shape),
            pl.BlockSpec((1,) + second.shape[1:], lambda c: (c, 0, 0)),
            whole(low_qkv.shape),
            by_unit(kv),
        ]
        + [by_unit(q) for q in queries]
        + [weights(0), weights(1), weights(2)],
        out_specs=[
            pl.BlockSpec((rows, count, lanes), lambda c: (0, 0, 0)),
            pl.BlockSpec((rows, 3 * rank, lanes), lambda c: (0, 0, 0)),
            pl.BlockSpec((1, rank, width), lambda c: (c, 0, 0)),
        ],
        out_shape=[
            jax.ShapeDtypeStruct((rows, count, lanes), jnp.bfloat16),
            jax.ShapeDtypeStruct((rows, 3 * rank, lanes), jnp.bfloat16),
            jax.ShapeDtypeStruct((cols, rank, width), jnp.bfloat16),
        ],
        scratch_shapes=[
            pltpu.VMEM((count, features), jnp.float32),
            pltpu.VMEM((count, 3 * rank), jnp.float32),
            pltpu.VMEM((3 * rank, count), jnp.bfloat16),
        ],
        compiler_params=pltpu.CompilerParams(vmem_limit_bytes=60 * 2**20),
        cost_estimate=pl.CostEstimate(
            flops=2 * count * features * cols * width,
            bytes_accessed=2 * features * cols * width + 10 * count * features,
            transcendentals=count,
        ),
        name="project_qkv_back",
    )(tokens, attended_grad, gain, mask, first, second, low_qkv, kv, *queries, weight, weight, weight)


def mlp_kernel(goes_on, group_ref, h_ref, e_ref, mask_ref, first_ref, second_ref, gate_ref, up_ref, down_ref, mids_ref, *refs):
    if goes_on:
        rows_in_ref, _, grad_in_ref, mixed_in_ref = refs[:4]
        refs = refs[4:]
    else:
        refs = refs[2:]
    rows_ref, cols_ref, grad_out_ref, mixed_out_ref = refs[:4]
    low_ref, low_turned_ref, lowered_ref, lowered_turned_ref, sum_front_ref, sum_down_ref = refs[4:10]
    grad_ref, mixed_ref = refs[10:] if len(refs) > 10 else (grad_out_ref, mixed_out_ref)
    c = pl.program_id(0)
    rows, lanes = gate_ref.shape[1], gate_ref.shape[3]
    rank = second_ref.shape[0]

    @pl.when(c == 0)
    def _():
        low_now = nt(h_ref[...], first_ref[...]) * mask_ref[...]
        low_ref[...] = low_now.astype(jnp.bfloat16)
        low_turned_ref[...] = low_now.T.astype(jnp.bfloat16)
        lowered_now = nt(e_ref[...], second_ref[...]) * mask_ref[:, :rank]
        lowered_ref[...] = lowered_now.astype(jnp.bfloat16)
        lowered_turned_ref[...] = lowered_now.T.astype(jnp.bfloat16)
        sum_front_ref[...] = jnp.zeros_like(sum_front_ref)
        sum_down_ref[...] = jnp.zeros_like(sum_down_ref)
        if goes_on:
            grad_ref[...] = grad_in_ref[...]
            mixed_ref[...] = mixed_in_ref[...]
        else:
            grad_ref[...] = jnp.zeros_like(grad_ref)
            mixed_ref[...] = jnp.zeros_like(mixed_ref)

    h = h_ref[...]
    gate_second, up_second, down_first = mids_ref[0, 0, 0], mids_ref[0, 0, 1], mids_ref[0, 0, 2, :rank]
    gate = nn(h, gate_ref[0].reshape(rows * lanes, lanes)) + nn(low_ref[...], gate_second)
    up = nn(h, up_ref[0].reshape(rows * lanes, lanes)) + nn(low_ref[...], up_second)
    upstream = nn(lowered_ref[...], down_first)
    for r in range(rows):
        upstream += nt(e_ref[:, r * lanes : (r + 1) * lanes], down_ref[0, r])
    sigmoid = 1.0 / (1.0 + jnp.exp(-gate))
    swish = gate * sigmoid
    hidden = (swish * up).astype(jnp.bfloat16)
    gate_grad = (upstream * up * (sigmoid + swish * (1.0 - sigmoid))).astype(jnp.bfloat16)
    up_grad = (upstream * swish).astype(jnp.bfloat16)
    for r in range(rows):
        at = slice(r * lanes, (r + 1) * lanes)
        grad_ref[:, at] += nt(gate_grad, gate_ref[0, r]) + nt(up_grad, up_ref[0, r])
        mixed_ref[:, at] += nn(hidden, down_ref[0, r])
    sum_front_ref[...] += nt(gate_grad, gate_second) + nt(up_grad, up_second)
    sum_down_ref[...] += nt(hidden, down_first)
    cols_ref[0, :rank] = nn(low_turned_ref[:rank], gate_grad)
    cols_ref[0, rank : 2 * rank] = nn(low_turned_ref[rank:], up_grad)
    cols_ref[0, 2 * rank :] = nn(lowered_turned_ref[...], hidden)

    @pl.when(c == pl.num_programs(0) - 1)
    def _():
        front_now = sum_front_ref[...] * mask_ref[...]
        grad_out_ref[...] = (grad_ref[...] + nn(front_now.astype(jnp.bfloat16), first_ref[...])).astype(grad_out_ref.dtype)
        down_now = sum_down_ref[...] * mask_ref[:, :rank]
        mixed_out_ref[...] = (mixed_ref[...] + nn(down_now.astype(jnp.bfloat16), second_ref[...])).astype(mixed_out_ref.dtype)
        front_sum = nn(front_now.T.astype(jnp.bfloat16), h_ref[...])
        down_sum = nn(down_now.T.astype(jnp.bfloat16), e_ref[...])
        for r in range(rows):
            at = slice(r * lanes, (r + 1) * lanes)
            now = jnp.concatenate([front_sum[:, at], down_sum[:, at]], axis=0)
            rows_ref[r] = now + rows_in_ref[r] if goes_on else now


def feed_forward(group, block, h, e, mask, first, second, weight, mids, row_sums, col_sums, earlier, dtype):
    count, features = h.shape
    cols, rows, _, lanes = weight.shape
    rank = mids.shape[3] // 2
    groups = mids.shape[1]
    blocks = col_sums.shape[1] // (groups * 3 * rank)
    goes_on = earlier is not None
    whole = lambda shape: buffered_once(shape, lambda c, g: (0,) * len(shape))
    weights = lambda at: pl.BlockSpec((1, rows, lanes, lanes), lambda c, g: (c, 0, at, 0))
    row_spec = pl.BlockSpec((rows, 3 * rank, lanes), lambda c, g: (0, g[0], 0))
    anywhere = pl.BlockSpec(memory_space=pl.ANY)
    scratch = [
        pltpu.VMEM((count, 2 * rank), jnp.bfloat16),
        pltpu.VMEM((2 * rank, count), jnp.bfloat16),
        pltpu.VMEM((count, rank), jnp.bfloat16),
        pltpu.VMEM((rank, count), jnp.bfloat16),
        pltpu.VMEM((count, 2 * rank), jnp.float32),
        pltpu.VMEM((count, rank), jnp.float32),
    ]
    if dtype != jnp.float32:
        scratch += [pltpu.VMEM((count, features), jnp.float32)] * 2
    return pl.pallas_call(
        functools.partial(mlp_kernel, goes_on),
        grid_spec=pltpu.PrefetchScalarGridSpec(
            num_scalar_prefetch=1,
            grid=(cols,),
            in_specs=[
                whole((count, features)),
                whole((count, features)),
                whole((count, 2 * rank)),
                pl.BlockSpec((2 * rank, features), lambda c, g: (g[0], 0)),
                pl.BlockSpec((rank, features), lambda c, g: (g[0], 0)),
                weights(0),
                weights(1),
                weights(2),
                pl.BlockSpec((1, 1, 3, 2 * rank, lanes), lambda c, g: (c, g[0], 0, 0, 0)),
                row_spec if goes_on else anywhere,
                anywhere,
            ]
            + ([whole((count, features))] * 2 if goes_on else []),
            out_specs=[
                row_spec,
                pl.BlockSpec((1, 3 * rank, lanes), lambda c, g: (c, g[0] * blocks + block, 0)),
                pl.BlockSpec((count, features), lambda c, g: (0, 0)),
                pl.BlockSpec((count, features), lambda c, g: (0, 0)),
            ],
            scratch_shapes=scratch,
        ),
        out_shape=[
            jax.ShapeDtypeStruct(row_sums.shape, jnp.float32),
            jax.ShapeDtypeStruct(col_sums.shape, jnp.float32),
            jax.ShapeDtypeStruct((count, features), dtype),
            jax.ShapeDtypeStruct((count, features), dtype),
        ],
        input_output_aliases={10: 0, 11: 1},
        compiler_params=pltpu.CompilerParams(vmem_limit_bytes=60 * 2**20),
        cost_estimate=pl.CostEstimate(
            flops=12 * count * features * cols * lanes,
            bytes_accessed=6 * features * cols * lanes + 12 * count * features,
            transcendentals=count * cols * lanes,
        ),
        name="feed_forward",
    )(group, h, e, mask, first, second, weight, weight, weight, mids, row_sums, col_sums, *(earlier or ()))


def out_kernel(heads_ref, residual_ref, gain_ref, mask_ref, first_ref, second_ref, weight_ref, attended_ref, normed_ref, low_ref):
    r = pl.program_id(0)
    cols, lanes = weight_ref.shape[0], weight_ref.shape[3]

    @pl.when(r == 0)
    def _():
        low_ref[...] = (nt(heads_ref[...], first_ref[...]) * mask_ref[...]).astype(jnp.bfloat16)

    at = pl.ds(pl.multiple_of(r * lanes, lanes), lanes)
    attended_ref[:, at] = (
        residual_ref[...].astype(jnp.float32)
        + nn(heads_ref[...], weight_ref[:, 0].reshape(cols * lanes, lanes))
        + nn(low_ref[...], second_ref[0])
    )

    @pl.when(r == pl.num_programs(0) - 1)
    def _():
        normed_ref[...] = normalized(attended_ref[...], gain_ref[...])[1]


def project_out(heads, residual, gain, mask, first, second, weight):
    count, features = residual.shape
    cols, rows, lanes, _ = weight.shape
    rank = mask.shape[1]
    whole = lambda shape: pl.BlockSpec(shape, lambda r: (0,) * len(shape))
    return pl.pallas_call(
        out_kernel,
        grid=(rows,),
        in_specs=[
            whole(heads.shape),
            pl.BlockSpec((count, lanes), lambda r: (0, r)),
            whole((1, features)),
            whole((count, rank)),
            whole(first.shape),
            pl.BlockSpec((1, rank, lanes), lambda r: (r, 0, 0)),
            pl.BlockSpec((cols, 1, lanes, lanes), lambda r: (0, r, 0, 0)),
        ],
        out_specs=[whole((count, features)), whole((count, features)), whole((count, rank))],
        out_shape=[
            jax.ShapeDtypeStruct((count, features), jnp.float32),
            jax.ShapeDtypeStruct((count, features), jnp.bfloat16),
            jax.ShapeDtypeStruct((count, rank), jnp.bfloat16),
        ],
        compiler_params=pltpu.CompilerParams(vmem_limit_bytes=48 * 2**20),
        cost_estimate=pl.CostEstimate(
            flops=2 * count * features * heads.shape[1],
            bytes_accessed=2 * features * heads.shape[1] + 10 * count * features,
            transcendentals=count,
        ),
        name="project_out",
    )(heads, residual, gain, mask, first, second, weight)


def out_back_kernel(
    pairs, pair_width, own_ref, other_ref, upstream_ref, attended_ref, gain_ref, mask_ref, first_ref, second_ref, heads_ref, low_ref, weight_ref,
    attended_grad_ref, rows_ref, cols_ref, *refs,
):
    message_refs = refs[:pairs]
    e_ref, lowered_ref, lowered_turned_ref = refs[pairs:]
    c = pl.program_id(0)
    rows, lanes = weight_ref.shape[1], weight_ref.shape[3]
    seqs, _, units, part, _ = message_refs[0].shape

    @pl.when(c == 0)
    def _():
        values = attended_ref[...]
        inverse = lax.rsqrt(jnp.mean(values * values, axis=-1, keepdims=True) + EPS)
        upstream = own_ref[...] + other_ref[...].astype(jnp.float32)
        total = upstream_ref[...].astype(jnp.float32) + norm_back(values, inverse, gain_ref[...], upstream)
        attended_grad_ref[...] = total
        e = total.astype(jnp.bfloat16)
        e_ref[...] = e
        lowered = nt(e, second_ref[...]) * mask_ref[...]
        lowered_ref[...] = lowered.astype(jnp.bfloat16)
        lowered_turned_ref[...] = lowered.T.astype(jnp.bfloat16)
        turned = nn(low_ref[...].astype(jnp.float32).T.astype(jnp.bfloat16), e)
        for r in range(rows):
            rows_ref[r] = turned[:, r * lanes : (r + 1) * lanes].astype(rows_ref.dtype)

    grad = nn(lowered_ref[...], first_ref[...])
    for r in range(rows):
        grad += nt(e_ref[:, r * lanes : (r + 1) * lanes], weight_ref[0, r])
    grad = grad.astype(jnp.bfloat16)
    for s in range(seqs):
        for u in range(units):
            for p in range(pairs):
                begin = (u * pairs + p) * pair_width
                message_refs[p][s, 0, u] = grad[s * part : (s + 1) * part, begin : begin + pair_width]
    cols_ref[0] = nn(lowered_turned_ref[...], heads_ref[...]).astype(cols_ref.dtype)


def project_out_back(own, other, upstream, attended, gain, mask, first, second, heads, low_out, weight, seqs, units, pairs, pair_width):
    count, features = attended.shape
    cols, rows, lanes, _ = weight.shape
    rank = mask.shape[1]
    whole = lambda shape: buffered_once(shape, lambda c: (0,) * len(shape))
    message = (seqs, cols, units // (seqs * cols), count // seqs, pair_width)
    return pl.pallas_call(
        functools.partial(out_back_kernel, pairs, pair_width),
        grid=(cols,),
        in_specs=[whole((count, features))] * 4
        + [
            whole((1, features)),
            whole((count, rank)),
            pl.BlockSpec((rank, lanes), lambda c: (0, c)),
            whole((rank, features)),
            pl.BlockSpec((count, lanes), lambda c: (0, c)),
            whole((count, rank)),
            pl.BlockSpec((1, rows, lanes, lanes), lambda c: (c, 0, 0, 0)),
        ],
        out_specs=[
            pl.BlockSpec((count, features), lambda c: (0, 0)),
            pl.BlockSpec((rows, rank, lanes), lambda c: (0, 0, 0)),
            pl.BlockSpec((1, rank, lanes), lambda c: (c, 0, 0)),
        ]
        + [pl.BlockSpec((seqs, 1) + message[2:], lambda c: (0, c, 0, 0, 0))] * pairs,
        out_shape=[
            jax.ShapeDtypeStruct((count, features), jnp.float32),
            jax.ShapeDtypeStruct((rows, rank, lanes), jnp.bfloat16),
            jax.ShapeDtypeStruct((cols, rank, lanes), jnp.bfloat16),
        ]
        + [jax.ShapeDtypeStruct(message, jnp.bfloat16)] * pairs,
        scratch_shapes=[
            pltpu.VMEM((count, features), jnp.bfloat16),
            pltpu.VMEM((count, rank), jnp.bfloat16),
            pltpu.VMEM((rank, count), jnp.bfloat16),
        ],
        compiler_params=pltpu.CompilerParams(vmem_limit_bytes=60 * 2**20),
        cost_estimate=pl.CostEstimate(
            flops=2 * count * features * cols * lanes,
            bytes_accessed=2 * features * cols * lanes + 18 * count * features,
            transcendentals=count,
        ),
        name="project_out_back",
    )(own, other, upstream, attended, gain, mask, first, second, heads, low_out, weight)


def dot(left, right):
    return lax.dot_general(left, right, (((1,), (0,)), ((), ())), preferred_element_type=jnp.float32)


def over_tokens(left, right):
    return lax.dot_general(left, right, (((0,), (0,)), ((), ())), preferred_element_type=jnp.float32)


def low(values):
    return values.astype(jnp.bfloat16)


def after(values, earlier):
    return lax.optimization_barrier((values, earlier))[0]


def to_tokens(values):
    rows = lax.axis_size("row")
    part, seqs, features = values.shape
    cut = values.reshape(rows, part // rows, seqs, features).transpose(0, 2, 1, 3)
    moved = lax.all_to_all(cut, "row", 0, 0, tiled=True)
    return moved.transpose(1, 2, 0, 3).reshape(seqs * (part // rows), rows * features)


def to_features(blocks, seqs):
    rows, _, width = blocks.shape
    me = lax.axis_index("row")
    parts = []
    for step in range(rows):
        block = lax.dynamic_index_in_dim(blocks, (me + step) % rows, 0, keepdims=False)
        if step:
            block = lax.ppermute(block, "row", [(i, (i + step) % rows) for i in range(rows)])
        parts.append(block)
    stacked = jnp.stack(parts)
    moved = jnp.stack(
        [lax.dynamic_index_in_dim(stacked, (me - source) % rows, 0, keepdims=False) for source in range(rows)]
    ).reshape(rows, seqs, -1, width)
    return moved.transpose(0, 2, 1, 3).reshape(-1, seqs, width)


def rope_tables(positions):
    half = HEAD_DIM // 2
    frequency = ROPE_BASE ** (-(jnp.arange(half).astype(jnp.float32) * 2.0) / HEAD_DIM)
    angles = positions.astype(jnp.float32)[:, None] * frequency[None, :]
    return lax.optimization_barrier((jnp.cos(angles), jnp.sin(angles)))


def diagonal(blocks):
    total = sum(b.shape[1] for b in blocks)
    out, at = [], 0
    for b in blocks:
        out.append(jnp.pad(b, ((0, 0), (at, total - at - b.shape[1]))))
        at += b.shape[1]
    return jnp.concatenate(out, axis=0)


def local(
    tokens,
    cotangent,
    block_labels,
    adapter_selection,
    adapter_scale,
    attention_norm_gain,
    feedforward_norm_gain,
    query_weight,
    key_weight,
    value_weight,
    output_weight,
    gate_weight,
    up_weight,
    down_weight,
    query_first_factor,
    query_second_factor,
    key_first_factor,
    key_second_factor,
    value_first_factor,
    value_second_factor,
    output_first_factor,
    output_second_factor,
    gate_first_factor,
    gate_second_factor,
    up_first_factor,
    up_second_factor,
    down_first_factor,
    down_second_factor,
):
    copies, rows, cols = lax.axis_size("dp"), lax.axis_size("row"), lax.axis_size("col")
    me = lax.axis_index("dp")
    units = rows * cols
    both, turned_both = ("row", "col"), ("col", "row")
    seqs = tokens.shape[1]
    part = tokens.shape[0] // rows
    length = part * units
    lanes = tokens.shape[2]
    scale = adapter_scale[0]
    width_q, width_kv = query_weight.shape[1], key_weight.shape[1]
    width_ff = gate_weight.shape[1] // copies
    blocks_ff = width_ff // lanes
    kv_heads = width_kv // HEAD_DIM
    heads = width_q * cols // HEAD_DIM * seqs // units
    pairs = -(-heads // 2)
    pair_heads = heads // pairs
    pair_width = pair_heads * HEAD_DIM
    pair_pad = -pair_width % 128
    kv_copies = max(1, units // (seqs * kv_heads * cols))
    adapter_cols = query_first_factor.shape[1]
    rank = seqs * RANK
    factor = HEAD_DIM ** (-0.5)
    head_q = width_q // kv_heads

    picked = lax.all_gather(adapter_selection, "dp", axis=0, tiled=True)
    owner = jnp.arange(adapter_cols)
    slot = jnp.arange(copies * rank)
    choose = (owner[:, None] // RANK == picked[slot // RANK][None, :]) & (owner[:, None] % RANK == slot[None, :] % RANK)
    choose_low = choose.astype(jnp.bfloat16)
    choose_wide = choose.astype(jnp.float32)
    choose_own = lax.dynamic_slice_in_dim(choose_low, me * rank, rank, 1)

    def first_of(matrix, chosen):
        return low(lax.dot_general(chosen, matrix, (((0,), (1,)), ((), ())), preferred_element_type=jnp.float32))

    def second_of(matrix, chosen):
        return low(over_tokens(chosen, matrix))

    def pack(by_row, by_col):
        shares = []
        for group, count, at in zip((by_row, by_col), (cols, rows), ("col", "row")):
            if not group:
                shares.append(jnp.zeros((0, lanes), jnp.bfloat16))
                continue
            joined = jnp.concatenate([v.reshape(-1, lanes) for v in group], axis=0)
            joined = jnp.pad(joined, ((0, -joined.shape[0] % count), (0, 0)))
            piece = joined.shape[0] // count
            shares.append(lax.dynamic_slice_in_dim(joined, lax.axis_index(at) * piece, piece, 0))
        return jnp.concatenate(shares, axis=0), shares[0].shape[0]

    def unpack(moved, share, by_row, by_col):
        of_rows = moved[:, :, :share].transpose(1, 0, 2, 3).reshape(rows, -1, lanes)
        of_cols = moved[:, :, share:].reshape(cols, -1, lanes)
        outs = []
        for group, source in zip((by_row, by_col), (of_rows, of_cols)):
            at, out = 0, []
            for v in group:
                size = v.size // lanes
                out.append(source[:, at : at + size].reshape((source.shape[0],) + v.shape))
                at += size
            outs.append(out)
        return outs

    def joined_rows(values):
        return values.transpose(1, 0, 2).reshape(values.shape[1], -1)

    def by_head(query, key, value):
        parts = []
        for j in range(kv_heads):
            at = slice(j * HEAD_DIM, (j + 1) * HEAD_DIM)
            parts += [query[:, j * head_q : (j + 1) * head_q], key[:, at], value[:, at]]
        return jnp.concatenate(parts, axis=1)

    half = me * width_ff
    gate_half = lax.dynamic_slice_in_dim(gate_weight, half, width_ff, 1)
    up_half = lax.dynamic_slice_in_dim(up_weight, half, width_ff, 1)
    down_half = lax.dynamic_slice_in_dim(down_weight, half, width_ff, 0)
    gate_second_half = lax.dynamic_slice_in_dim(gate_second_factor, half, width_ff, 1)
    up_second_half = lax.dynamic_slice_in_dim(up_second_factor, half, width_ff, 1)
    down_first_half = lax.dynamic_slice_in_dim(down_first_factor, half, width_ff, 0)

    attn_weight = lax.all_gather(
        jnp.concatenate([output_weight, by_head(query_weight, key_weight, value_weight)], axis=1),
        turned_both,
        axis=0,
        tiled=True,
    ).reshape(cols, rows, lanes, -1)
    attn_small = (
        [
            jnp.concatenate([first_of(m, choose_own) for m in (query_first_factor, key_first_factor, value_first_factor)]),
            jnp.stack([attention_norm_gain, feedforward_norm_gain]),
            second_of(output_second_factor, choose_own),
        ],
        [
            second_of(query_second_factor, choose_own),
            second_of(key_second_factor, choose_own),
            second_of(value_second_factor, choose_own),
            first_of(output_first_factor, choose_own),
        ],
    )
    packed, share = pack(*attn_small)
    (qkv_first, gains, out_second), (query_second, key_second, value_second, out_first) = unpack(
        lax.all_gather(packed, turned_both).reshape(cols, rows, -1, lanes), share, *attn_small
    )
    qkv_first = joined_rows(qkv_first)
    gains = joined_rows(gains).astype(jnp.float32)
    out_first = joined_rows(out_first)
    nothing = lambda m: jnp.zeros_like(m)
    qkv_second = jnp.stack(
        [
            jnp.concatenate(
                [
                    by_head(query_second[c], nothing(key_second[c]), nothing(value_second[c])),
                    by_head(nothing(query_second[c]), key_second[c], nothing(value_second[c])),
                    by_head(nothing(query_second[c]), nothing(key_second[c]), value_second[c]),
                ],
                axis=0,
            )
            for c in range(cols)
        ]
    )

    first_parts = [first_of(m, choose_low) for m in (gate_first_factor, up_first_factor)]
    hidden_parts = [
        second_of(gate_second_half, choose_low),
        second_of(up_second_half, choose_low),
        first_of(down_first_half, choose_low),
    ]
    of_group = lambda values, g: values[g * rank : (g + 1) * rank]
    mlp_small = [
        jnp.concatenate([of_group(m, g) for g in range(copies) for m in first_parts]),
        second_of(down_second_factor, choose_low),
    ]

    def middle(n):
        at = slice(n * lanes, (n + 1) * lanes)
        return jnp.stack(
            [
                jnp.stack(
                    [
                        jnp.pad(of_group(m, g)[:, at], ((rank, 0), (0, 0)) if i == 1 else ((0, rank), (0, 0)))
                        for i, m in enumerate(hidden_parts)
                    ]
                )
                for g in range(copies)
            ]
        )

    packs = [pack(mlp_small if n == 0 else [], [middle(n)]) for n in range(blocks_ff)]
    mlp_shards = [
        jnp.concatenate(
            [
                gate_half[:, n * lanes : (n + 1) * lanes],
                up_half[:, n * lanes : (n + 1) * lanes],
                down_half[n * lanes : (n + 1) * lanes],
                packs[n][0],
            ],
            axis=0,
        )
        for n in range(blocks_ff)
    ]

    row_seq = jnp.arange(seqs * part) // part
    mask = (row_seq[:, None] == jnp.arange(rank)[None, :] // RANK).astype(jnp.float32) * scale
    mask_twice, mask_thrice = jnp.tile(mask, (1, 2)), jnp.tile(mask, (1, 3))

    residual = to_tokens(tokens)
    upstream = to_tokens(after(cotangent, residual))
    residual, upstream = lax.optimization_barrier((residual, upstream))
    positions = (lax.axis_index("col") * rows + lax.axis_index("row")) * part + jnp.arange(part)
    cosine, sine = rope_tables(jnp.tile(positions, seqs))
    flat, none = jnp.ones((seqs * part, HEAD_DIM), jnp.float32), jnp.zeros((seqs * part, HEAD_DIM), jnp.float32)
    turning = head_q // HEAD_DIM + 1
    cosine, sine = (
        jnp.tile(jnp.concatenate([jnp.tile(table, (1, 2 * turning)), rest], axis=1), (1, kv_heads))
        for table, rest in ((cosine, flat), (sine, none))
    )
    *messages, low_qkv = project_qkv(
        residual, gains[0:1], mask_thrice, qkv_first, qkv_second, cosine, sine, attn_weight, seqs, units, pairs, pair_width, kv_heads
    )

    def exchange(values):
        return lax.all_to_all(values.reshape(units, part, -1), turned_both, 0, 0, tiled=True)

    def from_pairs(parts):
        split = jnp.stack([v.reshape(seqs, units // seqs, part, pair_width) for v in parts])
        return split.transpose(1, 3, 2, 0, 4).reshape(seqs * part, -1)

    def padded(values):
        return jnp.pad(values, ((0, 0), (0, pair_pad)))

    mlp_weights, earlier = [], residual
    for n in range(blocks_ff):
        shard = after(mlp_shards[n], earlier)
        mlp_weights.append(lax.all_gather(shard, turned_both).reshape(cols, rows, -1, lanes))
        earlier = messages[0]
    first_in = exchange(messages[0]).reshape(length, -1)
    unit_queries = [first_in[:, :pair_width]] + [exchange(v).reshape(length, -1) for v in messages[1:]]
    unit_queries = [padded(v) for v in unit_queries]
    unit_keys = first_in[:, pair_width : pair_width + HEAD_DIM]
    unit_values = first_in[:, pair_width + HEAD_DIM :]
    keys_twice = jnp.concatenate([unit_keys, unit_keys], axis=1)
    values_twice = jnp.concatenate([unit_values, unit_values], axis=1)
    keys_turned, values_turned = unit_keys.T, unit_values.T
    unit_seq = (lax.axis_index("col") * rows + lax.axis_index("row")) * seqs // units
    labels = lax.dynamic_index_in_dim(block_labels, unit_seq, 0, keepdims=True)
    numbers = jnp.arange(BLOCKS)[:, None]
    ends_of = jnp.sum((labels <= numbers).astype(jnp.int32), axis=1, keepdims=True)
    ends = jnp.sum(jnp.where(labels == numbers, ends_of, 0), axis=0, keepdims=True)
    unit_outs, log_sums = [], []
    for p in range(pairs):
        out, log_sum = attend(unit_queries[p], keys_twice, values_turned, ends, pair_heads, factor)
        unit_outs.append(out)
        log_sums.append(log_sum)
    heads_out = from_pairs([exchange(v[:, :pair_width]) for v in unit_outs])
    attended, normed_mlp, low_out = project_out(
        heads_out, residual, gains[1:2], mask, out_first, out_second, attn_weight
    )

    unpacked = [
        unpack(mlp_weights[n][:, :, 3 * lanes :], packs[n][1], mlp_small if n == 0 else [], [middle(n)])
        for n in range(blocks_ff)
    ]
    front_first, down_second = (joined_rows(v) for v in unpacked[0][0])

    def swap(values, step):
        return lax.ppermute(values, "dp", [(i, (i + step) % copies) for i in range(copies)])

    tokens_of = [(normed_mlp, upstream)]
    for step in range(1, copies):
        tokens_of.append((swap(normed_mlp, step), swap(upstream, step)))
    row_sums = jnp.zeros((rows, copies * 3 * rank, lanes), jnp.float32)
    col_sums = jnp.zeros((cols, copies * blocks_ff * 3 * rank, lanes), jnp.float32)
    sums = [None] * copies
    for n in range(blocks_ff):
        order = list(range(copies))
        for step in order if n < blocks_ff - 1 else order[1:] + order[:1]:
            row_sums, col_sums, *sums[step] = feed_forward(
                ((me - step) % copies).reshape(1),
                n,
                *tokens_of[step],
                mask_twice,
                front_first,
                down_second,
                mlp_weights[n],
                unpacked[n][1][0],
                row_sums,
                col_sums,
                sums[step],
                jnp.float32 if n < blocks_ff - 1 or step == 0 else jnp.bfloat16,
            )
    grad_part, mixed_part = sums[0]
    mixed_backs = []
    for step in range(1, copies):
        grad_back, mixed_back = (swap(v, -step) for v in sums[step])
        grad_other = grad_back if step == 1 else grad_other + grad_back
        mixed_backs.append(mixed_back)

    attended_grad, out_rows, out_cols, *grad_messages = project_out_back(
        grad_part,
        grad_other,
        upstream,
        attended,
        gains[1:2],
        mask,
        out_first,
        joined_rows(out_second),
        heads_out,
        low_out,
        attn_weight,
        seqs,
        units,
        pairs,
        pair_width,
    )
    row_sums, col_sums, _ = lax.optimization_barrier((row_sums, col_sums, grad_messages))
    row_shares = lax.psum_scatter(row_sums.reshape(units, -1, lanes), both, scatter_dimension=0)
    col_shares = lax.psum_scatter(col_sums.reshape(units, -1, lanes), turned_both, scatter_dimension=0)
    unit_grads = [padded(exchange(v).reshape(length, -1)) for v in grad_messages]
    full_cosine, full_sine = (table.T for table in rope_tables(jnp.arange(length)))
    query_moved, kv_grad = [], None
    for p in range(pairs):
        if p == pairs - 1 and p > 0:
            mixed_backs, _ = lax.optimization_barrier((mixed_backs, kv_now))
            mixed_part = sum((v.astype(jnp.float32) for v in mixed_backs), mixed_part)
            mixed_out = low(attended + mixed_part).reshape(seqs * part, rows, lanes).transpose(1, 0, 2)
            ends, mixed_out = lax.optimization_barrier((ends, mixed_out))
        query_now, kv_now = attend_back(
            unit_queries[p],
            unit_grads[p],
            unit_outs[p],
            log_sums[p],
            keys_twice,
            values_twice,
            keys_turned,
            ends,
            full_cosine,
            full_sine,
            pair_heads,
            factor,
        )
        kv_grad = kv_now if kv_grad is None else kv_grad + kv_now
        if p == pairs - 1:
            query_now = jnp.concatenate([query_now[:, :pair_width], low(kv_grad)], axis=1)
            if pairs == 1:
                mixed_part = sum((v.astype(jnp.float32) for v in mixed_backs), mixed_part)
                mixed_out = low(attended + mixed_part).reshape(seqs * part, rows, lanes).transpose(1, 0, 2)
            mixed_out = to_features(mixed_out, seqs)
            query_now, mixed_out, row_shares, col_shares, query_moved = lax.optimization_barrier(
                (query_now, mixed_out, row_shares, col_shares, query_moved)
            )
        query_moved.append(exchange(query_now[:, : query_now.shape[1] if p == pairs - 1 else pair_width]))
    row_height = row_shares.shape[0]
    row_total = lax.all_gather(jnp.pad(row_shares, ((0, -row_height % 64), (0, 0))), ("dp", "col"))[..., :row_height, :]
    col_total = lax.all_gather(col_shares, ("dp", "row"))
    kv_moved = query_moved[-1][..., pair_width:].reshape(seqs, cols, kv_heads, kv_copies, part, -1)
    kv_moved = low(kv_moved.astype(jnp.float32).sum(axis=3)) if kv_copies > 1 else kv_moved[:, :, :, 0]
    query_moved[-1] = query_moved[-1][..., :pair_width]
    query_moved = [v.reshape(seqs, cols, -1, part, pair_width) for v in query_moved]
    token_grad, qkv_rows, qkv_cols = project_qkv_back(
        residual, attended_grad, gains[0:1], mask_thrice, qkv_first, qkv_second, low_qkv, kv_moved, query_moved, attn_weight
    )

    row_total, col_total, _ = lax.optimization_barrier((row_total, col_total, token_grad))

    def everywhere(values, axes, count):
        copied = jnp.broadcast_to(values[None], (count,) + values.shape)
        return lax.all_to_all(copied, axes, 0, 0, tiled=True).reshape(copies, -1, lanes)

    def wide_second(values):
        return lax.dot_general(
            choose_wide, values, (((1,), (0,)), ((), ())), precision=lax.Precision.HIGHEST, preferred_element_type=jnp.float32
        )

    def wide_first(values):
        return lax.dot_general(
            values, choose_wide, (((0,), (1,)), ((), ())), precision=lax.Precision.HIGHEST, preferred_element_type=jnp.float32
        )

    row_total = row_total.reshape(copies, copies, 3, rank, lanes).sum(axis=0)
    gate_first_gradient, up_first_gradient = (wide_first(row_total[:, i].reshape(-1, lanes)) for i in range(2))
    down_second_gradient = wide_second(row_total[:, 2].reshape(-1, lanes))
    col_total = col_total.reshape(copies, copies, blocks_ff, 3, rank, lanes)
    pieces = [
        [col_total[x, :, n, i].reshape(-1, lanes) for x in range(copies) for n in range(blocks_ff)] for i in range(3)
    ]
    gate_second_gradient, up_second_gradient = (
        jnp.concatenate([wide_second(v) for v in pieces[i]], axis=1) for i in range(2)
    )
    down_first_gradient = jnp.concatenate([wide_first(v) for v in pieces[2]], axis=0)

    row_cut = jnp.concatenate([qkv_rows, out_rows], axis=1).reshape(rows, cols, -1, lanes)
    col_cut = jnp.concatenate([qkv_cols.reshape(cols, -1, lanes), out_cols], axis=1)
    col_cut = col_cut.reshape(cols, rows, -1, lanes).transpose(1, 0, 2, 3)
    cut = row_cut.shape[2]
    attn_shares = jnp.concatenate([row_cut, col_cut], axis=2).reshape(units, -1, lanes)
    attn_sums = jnp.sum(lax.all_to_all(attn_shares, both, 0, 0, tiled=True).astype(jnp.float32), axis=0)
    attn_rows = everywhere(attn_sums[:cut], ("dp", "col"), copies * cols).reshape(copies, 4, rank, lanes)
    attn_cols = everywhere(attn_sums[cut:], ("dp", "row"), copies * rows)
    query_first_gradient, key_first_gradient, value_first_gradient = (
        wide_first(attn_rows[:, i].reshape(-1, lanes)) for i in range(3)
    )
    output_second_gradient = wide_second(attn_rows[:, 3].reshape(-1, lanes))
    output_first_gradient = wide_first(attn_cols[:, -rank:].reshape(-1, lanes))
    qkv_second_gradient = wide_second(attn_cols[:, :-rank].reshape(copies * rank, -1)).reshape(
        adapter_cols, kv_heads, -1
    )
    query_second_gradient = qkv_second_gradient[..., :head_q].reshape(adapter_cols, -1)
    key_second_gradient = qkv_second_gradient[..., head_q : head_q + HEAD_DIM].reshape(adapter_cols, -1)
    value_second_gradient = qkv_second_gradient[..., head_q + HEAD_DIM :].reshape(adapter_cols, -1)

    return (
        mixed_out,
        to_features(token_grad, seqs),
        query_first_gradient,
        query_second_gradient,
        key_first_gradient,
        key_second_gradient,
        value_first_gradient,
        value_second_gradient,
        output_first_gradient,
        output_second_gradient,
        gate_first_gradient,
        gate_second_gradient,
        up_first_gradient,
        up_second_gradient,
        down_first_gradient,
        down_second_gradient,
    )


def solution(mesh):
    in_specs = (
        P("col", "dp", "row"),
        P("col", "dp", "row"),
        P("dp", None),
        P("dp"),
        P(),
        P("row"),
        P("row"),
        P("row", "col"),
        P("row", "col"),
        P("row", "col"),
        P("col", "row"),
        P("row", "col"),
        P("row", "col"),
        P("col", "row"),
        P("row", None),
        P(None, "col"),
        P("row", None),
        P(None, "col"),
        P("row", None),
        P(None, "col"),
        P("col", None),
        P(None, "row"),
        P("row", None),
        P(None, "col"),
        P("row", None),
        P(None, "col"),
        P("col", None),
        P(None, "row"),
    )
    out_specs = (
        P("col", "dp", "row"),
        P("col", "dp", "row"),
        P("row", None),
        P(None, "col"),
        P("row", None),
        P(None, "col"),
        P("row", None),
        P(None, "col"),
        P("col", None),
        P(None, "row"),
        P("row", None),
        P(None, "col"),
        P("row", None),
        P(None, "col"),
        P("col", None),
        P(None, "row"),
    )
    return jax.shard_map(local, mesh=mesh, in_specs=in_specs, out_specs=out_specs, check_vma=False)
```

time: 1500 us -> 1080 us (0.72)
  matrix products: 382 us -> 23.6 us
  Pallas kernels: 209 us -> 464 us
  blocking collectives: 196 us -> 31.4 us
  other arithmetic: 104 us -> 26.3 us
  local copies, waits for them, and re-layouts: 192 us -> 133 us
    dot_general x109 -> x7, matrix products: 340 us -> 1.24 us  [first_of(): lax.dot_general(chosen, matrix, (((0,), (1,)), ((), ())), preferred_eleme...]
    pallas_call x0 -> x8, Pallas kernels: none -> 237 us  [the longest x4 176 us: feed_forward(): pl.pallas_call(functools.partial(mlp_kernel, goes_on), grid_spec=pltpu.Pr...]
    all_gather x5 -> x1, blocking collectives: 191 us -> 26.8 us  [local(): lax.all_gather(packed, turned_both).reshape(cols, rows, -1, lanes)]
    psum x3 -> x0, waiting for transfers between devices: 136 us -> none  [the longest x1 72.2 us: sum_rows(): lax.psum(lax.psum_scatter(cut, 'row', scatter_dimension=0), ('col', 'dp'))]
    all_to_all x2, waiting for transfers between devices: 0.01 us -> 79.4 us  [to_tokens(): moved = lax.all_to_all(cut, 'row', 0, 0, tiled=True)]
    all_gather x6 -> x5, waiting for transfers between devices: 6.23 us -> 62.7 us  [the longest x1 59.6 us: local(): lax.all_gather(jnp.pad(row_shares, ((0, -row_height % 64), (0, 0))), ('dp...]
    all_to_all x4 -> x8, waiting for transfers between devices: 70.5 us -> 127 us  [exchange(): lax.all_to_all(values.reshape(units, part, -1), turned_both, 0, 0, tiled=...]
    ppermute x4, waiting for transfers between devices: 51.9 us -> 0.12 us  [swap(): lax.ppermute(values, 'dp', [(i, (i + step) % copies) for i in range(copie...]
  transfers between devices with their start and end apart: 25 -> 30, of which waited for: 12 -> 12; matrix products, arithmetic and copies ran while one was open for 32% -> 13% of each run, Pallas kernels for 14% -> 38%
where the time goes in v2:
time: 1080 us; the launch traced here: 1070 us
  Pallas kernels  464 us (43%)
  waiting for transfers between devices  300 us (28%)
  local copies, waits for them, and re-layouts  133 us (12%)
  starting transfers between devices  75.2 us (7%)
  blocking collectives  31.4 us (3%)
  other arithmetic  26.3 us (2%)
  matrix products  23.6 us (2%)
  between operations  18.1 us (2%)
    pallas_call x4, Pallas kernels, feed_forward(): pl.pallas_call(functools.partial(mlp_kernel, goes_on), grid_spec=pltpu.Pr...  176 us
    all_to_all x8, waiting for transfers between devices, exchange(): lax.all_to_all(values.reshape(units, part, -1), turned_both, 0, 0, tiled=...  127 us
    pallas_call x2, Pallas kernels, attend_back(): pl.pallas_call(functools.partial(bwd_kernel, heads, factor), grid=(length...  127 us
    pallas_call x2, Pallas kernels, attend(): pl.pallas_call(functools.partial(fwd_kernel, heads, factor), grid=(length...  99.8 us
    all_to_all x2, waiting for transfers between devices, to_tokens(): moved = lax.all_to_all(cut, 'row', 0, 0, tiled=True)  79.4 us
    all_gather x1, waiting for transfers between devices, local(): lax.all_gather(jnp.pad(row_shares, ((0, -row_height % 64), (0, 0))), ('dp...  59.6 us
    all_to_all x8, starting transfers between devices, exchange(): lax.all_to_all(values.reshape(units, part, -1), turned_both, 0, 0, tiled=...  41.9 us
    unnamed x240, local copies, waits for them, and re-layouts  28.7 us
  transfers between devices with their start and end apart: 30, of which 12 were waited for; matrix products, arithmetic and copies ran while one was open for 13% of the time, Pallas kernels for 38%

profile of v2, /device:TPU:0, one launch (start us, length us, event | category | flops | bytes accessed | tf_op | source)
XLA Modules:
  0.0 1072.2 jit_solution(5310023218994173219)
XLA Ops:
  10.2 3.3 concatenate.128
  17.0 4.2 all-to-all-start
  21.3 4.6 all-reduce.16
  36.1 33.3 %all-to-all-done = bf16[4,2,256,512]{3,2,1,0:T(8,128)(2,1)S(1)} async-done(((bf16[4,2,256,512]{3,2,1,0:T(8,128)(2,1)}), bf16[4,2,256,512]{3,2,1,0:T(8,128)(2,1)S(1)}, u32[]{:S(2)}, u32[]{:S(2)}) %all-to-all-start) | async-done | bytes 2097184 | tf_op jit(solution)/shard_map/all_to_all | solution.py:722
  74.9 3.8 all-to-all-start.1
  81.1 46.1 %all-to-all-done.1 = bf16[4,2,256,512]{3,2,1,0:T(8,128)(2,1)S(1)} async-done(((bf16[4,2,256,512]{3,2,1,0:T(8,128)(2,1)}), bf16[4,2,256,512]{3,2,1,0:T(8,128)(2,1)S(1)}, u32[]{:S(2)}, u32[]{:S(2)}) %all-to-all-start.1) | async-done | bytes 2097184 | tf_op jit(solution)/shard_map/all_to_all | solution.py:722
  132.7 26.8 %all-gather.5 = bf16[16,53,512]{2,1,0:T(8,128)(2,1)S(1)} all-gather(bf16[1,53,512]{2,1,0:T(8,128)(2,1)S(1)} %maximum_bitcast_fusion.5), channel_id=2, replica_groups=mesh['dp'=2,'row'=4,'col'=4] {'col','row'}, dimensions={0}, use_global_device_ids=true | all-gather | bytes 922624 | tf_op jit(solution)/shard_map/all_gather | solution.py:890
  201.1 15.7 %project_qkv.1 = (bf16[2,4,2,256,256]{4,3,2,1,0:T(8,128)(2,1)}, bf16[2,4,2,256,128]{4,3,2,1,0:T(8,128)(2,1)}, bf16[512,96]{1,0:T(8,128)(2,1)S(1)}) custom-call(bf16[512,2048]{1,0:T(8,128)(2,1)} %bitcast.308, f32[1,2048]{1,0:T(1,128)S(1)} %bitcast.286, f32[512,96]{1,0:T(8,128)S(1)} %copy-done.6, bf16[96,2048]{1,0:T(8,128)(2,1)S(1)} %bitcast.272, ...), custom_call_target="tpu_custom_call" | custom-call | flops 6442450944 | bytes 16777216 | tf_op jit(solution)/shard_map/project_qkv/pallas_call | solution.py:301
  217.4 4.1 copy.277
  221.5 3.9 all-to-all-start.2
  225.4 73.5 %all-to-all-done.2 = bf16[16,256,256]{1,2,0:T(8,128)(2,1)S(1)} async-done(((bf16[16,256,256]{1,2,0:T(8,128)(2,1)}), bf16[16,256,256]{1,2,0:T(8,128)(2,1)S(1)}, u32[]{:S(2)}, u32[]{:S(2)}) %all-to-all-start.2) | async-done | bytes 2097184 | tf_op jit(solution)/shard_map/all_to_all | solution.py:970
  298.9 3.9 all-to-all-start.4
  311.5 49.5 %attend_forward.2 = (bf16[4096,128]{1,0:T(8,128)(2,1)S(1)}, f32[8,4096]{1,0:T(8,128)S(1)}) custom-call(s32[1,4096]{1,0:T(1,128)S(1)} %bitcast.288, bf16[4096,128]{1,0:T(8,128)(2,1)S(1)} %copy.279.q_ref, bf16[4096,128]{1,0:T(8,128)(2,1)S(1)} %copy.280.k2_ref, bf16[64,4096]{1,0:T(8,128)(2,1)S(1)} %copy-done.21), custom_call_target="tpu_custom_call" | custom-call | flops 4294967296 | bytes 3670016 | tf_op jit(solution)/shard_map/attend_forward/pallas_call | solution.py:88
  362.7 6.2 all-to-all-start.3
  368.9 50.3 %attend_forward.3 = (bf16[4096,128]{1,0:T(8,128)(2,1)}, f32[8,4096]{1,0:T(8,128)S(1)}) custom-call(s32[1,4096]{1,0:T(1,128)S(1)} %bitcast.289, bf16[4096,128]{1,0:T(8,128)(2,1)S(1)} %bitcast.276, bf16[4096,128]{1,0:T(8,128)(2,1)S(1)} %copy.280.k2_ref, bf16[64,4096]{1,0:T(8,128)(2,1)S(1)} %copy-done.22), custom_call_target="tpu_custom_call" | custom-call | flops 4294967296 | bytes 3670016 | tf_op jit(solution)/shard_map/attend_forward/pallas_call | solution.py:88
  419.2 6.4 all-to-all-start.5
  430.0 35.4 %all-to-all-done.5 = bf16[16,256,128]{2,1,0:T(8,128)(2,1)S(1)} async-done(((bf16[16,256,128]{2,1,0:T(8,128)(2,1)}), bf16[16,256,128]{2,1,0:T(8,128)(2,1)S(1)}, u32[]{:S(2)}, u32[]{:S(2)}) %all-to-all-start.5) | async-done | bytes 1048608 | tf_op jit(solution)/shard_map/all_to_all | solution.py:970
  466.8 3.5 copy.282
  470.3 3.3 reshape.477.heads_ref
  473.7 12.7 %project_out.1 = (f32[512,2048]{1,0:T(8,128)}, bf16[512,2048]{1,0:T(8,128)(2,1)}, bf16[512,32]{1,0:T(8,128)(2,1)S(1)}) custom-call(bf16[512,2048]{1,0:T(8,128)(2,1)S(1)} %reshape.477.heads_ref, bf16[512,2048]{1,0:T(8,128)(2,1)} %bitcast.309, f32[1,2048]{1,0:T(1,128)S(1)} %bitcast.284, f32[512,32]{1,0:T(8,128)S(1)} %compare_select_fusion.mask_ref, ...), custom_call_target="tpu_custom_call" | custom-call | flops 4294967296 | bytes 18874368 | tf_op jit(solution)/shard_map/project_out/pallas_call | solution.py:590
  487.9 2.7 slice.568
  497.0 43.2 %feed_forward.4 = (f32[4,192,512]{2,1,0:T(8,128)}, f32[4,384,512]{2,1,0:T(8,128)}, f32[512,2048]{1,0:T(8,128)}, f32[512,2048]{1,0:T(8,128)}) custom-call(s32[1]{0:T(128)} %bitcast.45.group_ref, bf16[512,2048]{1,0:T(8,128)(2,1)} %get-tuple-element.84.h_ref, ...), custom_call_target="tpu_custom_call", output_to_operand_aliasing={{0}: (10, {}), {1}: (11, {})} | custom-call | flops 25769803776 | bytes 37748736 | tf_op jit(solution)/shard_map/feed_forward/pallas_call | solution.py:521
  541.6 42.9 %feed_forward.5 = (f32[4,192,512]{2,1,0:T(8,128)}, f32[4,384,512]{2,1,0:T(8,128)}, f32[512,2048]{1,0:T(8,128)}, f32[512,2048]{1,0:T(8,128)}) custom-call(s32[1]{0:T(128)} %bitcast.72.group_ref, bf16[512,2048]{1,0:T(8,128)(2,1)} %copy-done.33, bf16[512,2048]{1,0:T(8,128)(2,1)} %collective-permute-done.1.e_ref, ...), custom_call_target="tpu_custom_call", output_to_operand_aliasing={{0}: (10, {}), {1}: (11, {})} | custom-call | flops 25769803776 | bytes 37748736 | tf_op jit(solution)/shard_map/feed_forward/pallas_call | solution.py:521
  584.6 2.7 slice.567
  587.3 44.2 %feed_forward.6 = (f32[4,192,512]{2,1,0:T(8,128)}, f32[4,384,512]{2,1,0:T(8,128)}, bf16[512,2048]{1,0:T(8,128)(2,1)}, bf16[512,2048]{1,0:T(8,128)(2,1)}) custom-call(s32[1]{0:T(128)} %bitcast.72.group_ref, bf16[512,2048]{1,0:T(8,128)(2,1)} %copy-done.33, ...), custom_call_target="tpu_custom_call", output_to_operand_aliasing={{0}: (10, {}), {1}: (11, {})} | custom-call | flops 25769803776 | bytes 37748736 | tf_op jit(solution)/shard_map/feed_forward/pallas_call | solution.py:521
  632.6 45.7 %feed_forward.7 = (f32[4,192,512]{2,1,0:T(8,128)}, f32[4,384,512]{2,1,0:T(8,128)}, f32[512,2048]{1,0:T(8,128)}, f32[512,2048]{1,0:T(8,128)}) custom-call(s32[1]{0:T(128)} %bitcast.45.group_ref, bf16[512,2048]{1,0:T(8,128)(2,1)} %get-tuple-element.84.h_ref, ...), custom_call_target="tpu_custom_call", output_to_operand_aliasing={{0}: (10, {}), {1}: (11, {})} | custom-call | flops 25769803776 | bytes 37748736 | tf_op jit(solution)/shard_map/feed_forward/pallas_call | solution.py:521
  679.8 15.4 %project_out_back.1 = (f32[512,2048]{1,0:T(8,128)}, bf16[4,32,512]{2,1,0:T(8,128)(2,1)}, bf16[4,32,512]{2,1,0:T(8,128)(2,1)}, bf16[2,4,2,256,128]{4,3,2,1,0:T(8,128)(2,1)}, bf16[2,4,2,256,128]{4,3,2,1,0:T(8,128)(2,1)}) custom-call(f32[512,2048]{1,0:T(8,128)} %get-tuple-element.102.own_ref, bf16[512,2048]{1,0:T(8,128)(2,1)} %copy-done.34, ...), custom_call_target="tpu_custom_call" | custom-call | flops 4294967296 | bytes 27262976 | tf_op jit(solution)/shard_map/project_out_back/pallas_call | solution.py:662
  695.2 3.7 all-to-all-start.6
  700.9 3.0 multiply_sine_fusion
  703.8 18.0 %all-to-all-done.6 = bf16[16,256,128]{2,1,0:T(8,128)(2,1)S(1)} async-done(((bf16[16,256,128]{2,1,0:T(8,128)(2,1)}), bf16[16,256,128]{2,1,0:T(8,128)(2,1)S(1)}, u32[]{:S(2)}, u32[]{:S(2)}) %all-to-all-start.6) | async-done | bytes 1048608 | tf_op jit(solution)/shard_map/all_to_all | solution.py:970
  721.8 6.9 all-to-all-start.7
  734.9 63.1 %attend_backward.2 = (bf16[4096,128]{1,0:T(8,128)(2,1)}, f32[4096,128]{1,0:T(8,128)}) custom-call(s32[1,4096]{1,0:T(1,128)S(1)} %bitcast.290, f32[32,4096]{1,0:T(8,128)S(1)} %bitcast.282, f32[32,4096]{1,0:T(8,128)S(1)} %bitcast.280, bf16[4096,128]{1,0:T(8,128)(2,1)S(1)} %copy-done.12, bf16[4096,128]{1,0:T(8,128)(2,1)S(1)} %bitcast.279, ...), custom_call_target="tpu_custom_call" | custom-call | flops 10737418240 | bytes 6291456 | tf_op jit(solution)/shard_map/attend_backward/pallas_call | solution.py:203
  798.0 4.0 add_convert_fusion
  806.9 4.9 all-to-all-start.8
  811.8 63.5 %attend_backward.3 = (bf16[4096,128]{1,0:T(8,128)(2,1)S(1)}, f32[4096,128]{1,0:T(8,128)}) custom-call(s32[1,4096]{1,0:T(1,128)S(1)} %bitcast.291, f32[32,4096]{1,0:T(8,128)S(1)} %bitcast.283, f32[32,4096]{1,0:T(8,128)S(1)} %bitcast.281, bf16[4096,128]{1,0:T(8,128)(2,1)S(1)} %bitcast.277, bf16[4096,128]{1,0:T(8,128)(2,1)} %bitcast.82.do_ref, ...), custom_call_target="tpu_custom_call" | custom-call | flops 10737418240 | bytes 6291456 | tf_op jit(solution)/shard_map/attend_backward/pallas_call | solution.py:203
  880.8 3.5 copy.299
  884.3 6.2 all-to-all-start.9
  892.8 59.6 %all-gather.18.cloned.1.call-done = f32[512,512]{1,0:T(8,128)} async-done(((f32[64,512]{1,0:T(8,128)}), f32[512,512]{1,0:T(8,128)}) %all-gather.18.cloned.1.call-update) | async-done | bytes 1048592 | tf_op jit(solution)/shard_map/all_gather | solution.py:1101
  955.5 17.6 %project_qkv_back.1 = (bf16[4,512,512]{2,1,0:T(8,128)(2,1)}, bf16[4,96,512]{2,1,0:T(8,128)(2,1)}, bf16[4,32,768]{2,1,0:T(8,128)(2,1)}) custom-call(bf16[512,2048]{1,0:T(8,128)(2,1)} %bitcast.310, f32[512,2048]{1,0:T(8,128)} %get-tuple-element.121.attended_ref, f32[1,2048]{1,0:T(1,128)} %bitcast.287, f32[512,96]{1,0:T(8,128)} %copy.276.mask_ref, ...), custom_call_target="tpu_custom_call" | custom-call | flops 6442450944 | bytes 23068672 | tf_op jit(solution)/shard_map/project_qkv_back/pallas_call | solution.py:394
  973.0 2.7 constant_dynamic-slice_fusion.4
  975.8 3.1 all-gather.20.cloned.1.call-done
  993.7 5.7 all-to-all-start.10
  1008.7 14.8 %all-to-all-done.10 = bf16[16,52,512]{2,1,0:T(8,128)(2,1)S(1)} async-done(((bf16[16,52,512]{2,1,0:T(8,128)(2,1)}), bf16[16,52,512]{2,1,0:T(8,128)(2,1)S(1)}, u32[]{:S(2)}, u32[]{:S(2)}) %all-to-all-start.10) | async-done | bytes 852000 | tf_op jit(solution)/shard_map/all_to_all | solution.py:1144
  1024.5 3.5 all-to-all-start.12
  1029.1 6.0 collective-permute-done.9
  1040.0 4.9 all-to-all-start.11
  1045.4 3.5 copy.301
  1053.3 7.0 all-to-all-done.11
  (486 shorter events, 161.8 us)
Async XLA Ops:
  7.2 22.0 %copy-start = (bf16[128,2048]{1,0:T(8,128)(2,1)S(1)}, bf16[128,2048]{1,0:T(8,128)(2,1)}, u32[]{:S(2)}) copy-start(bf16[128,2048]{1,0:T(8,128)(2,1)} %param.53) | copy-start | bytes 1572868
  7.2 190.7 %all-gather.12.cloned.1.call-start = ((), (), s32[]{:S(2)}) async-start(), calls=%async_computation.15 | async-start | bytes 22282240 | tf_op jit(solution)/shard_map/all_gather | solution.py:869
  17.0 52.4 %all-to-all-start = ((bf16[4,2,256,512]{3,2,1,0:T(8,128)(2,1)}), bf16[4,2,256,512]{3,2,1,0:T(8,128)(2,1)S(1)}, u32[]{:S(2)}, u32[]{:S(2)}) async-start(bf16[4,2,256,512]{3,2,1,0:T(8,128)(2,1)} %copy.262), calls=%async_computation | async-start | bytes 4194304 | tf_op jit(solution)/shard_map/all_to_all | solution.py:722
  25.9 105.0 %copy-start.61 = (s32[64]{0:T(128)}, s32[64]{0:T(128)S(1)}, u32[]{:S(2)}) copy-start(s32[64]{0:T(128)S(1)} %and_select_fusion.1) | copy-start | bytes 772
  29.1 101.8 %copy-start.59 = (s32[64]{0:T(128)}, s32[64]{0:T(128)S(1)}, u32[]{:S(2)}) copy-start(s32[64]{0:T(128)S(1)} %fusion.33) | copy-start | bytes 772
  29.1 101.8 %copy-start.63 = (s32[128]{0:T(128)}, s32[128]{0:T(128)S(1)}, u32[]{:S(2)}) copy-start(s32[128]{0:T(128)S(1)} %get-tuple-element.332) | copy-start | bytes 1540
  29.1 101.8 %copy-start.65 = (s32[128]{0:T(128)}, s32[128]{0:T(128)S(1)}, u32[]{:S(2)}) copy-start(s32[128]{0:T(128)S(1)} %get-tuple-element.333) | copy-start | bytes 1540
  74.9 52.2 %all-to-all-start.1 = ((bf16[4,2,256,512]{3,2,1,0:T(8,128)(2,1)}), bf16[4,2,256,512]{3,2,1,0:T(8,128)(2,1)S(1)}, u32[]{:S(2)}, u32[]{:S(2)}) async-start(bf16[4,2,256,512]{3,2,1,0:T(8,128)(2,1)} %copy.265), calls=%async_computation.1 | async-start | bytes 4194304 | tf_op jit(solution)/shard_map/all_to_all | solution.py:722
  78.7 409.2 %all-gather.14.cloned.1.call-start = ((), (), s32[]{:S(2)}) async-start(), calls=%async_computation.18 | async-start | bytes 29245440 | tf_op jit(solution)/shard_map/all_gather | solution.py:982
  130.8 453.7 %all-gather.16.cloned.1.call-start = ((), (), s32[]{:S(2)}) async-start(), calls=%async_computation.19 | async-start | bytes 28409856 | tf_op jit(solution)/shard_map/all_gather | solution.py:982
  167.3 30.6 %copy-start.26 = (f32[1,1,4,512]{3,1,2,0:T(1,128)}, f32[1,1,4,512]{3,1,2,0:T(1,128)S(1)}, u32[]{:S(2)}) copy-start(f32[1,1,4,512]{3,1,2,0:T(1,128)S(1)} %copy.332) | copy-start | bytes 24580
  170.7 302.9 %copy-start.4 = (f32[512,32]{1,0:T(8,128)}, f32[512,32]{1,0:T(8,128)S(1)}, u32[]{:S(2)}) copy-start(f32[512,32]{1,0:T(8,128)S(1)} %compare_select_fusion.mask_ref) | copy-start | bytes 196612
  221.5 77.4 %all-to-all-start.2 = ((bf16[16,256,256]{1,2,0:T(8,128)(2,1)}), bf16[16,256,256]{1,2,0:T(8,128)(2,1)S(1)}, u32[]{:S(2)}, u32[]{:S(2)}) async-start(bf16[16,256,256]{1,2,0:T(8,128)(2,1)} %copy.277), calls=%async_computation.2 | async-start | bytes 4194304 | tf_op jit(solution)/shard_map/all_to_all | solution.py:970
  298.9 63.8 %all-to-all-start.4 = ((bf16[16,256,128]{2,1,0:T(8,128)(2,1)}), bf16[16,256,128]{2,1,0:T(8,128)(2,1)S(1)}, u32[]{:S(2)}, u32[]{:S(2)}) async-start(bf16[16,256,128]{2,1,0:T(8,128)(2,1)} %bitcast.39), calls=%async_computation.4 | async-start | bytes 2097152 | tf_op jit(solution)/shard_map/all_to_all | solution.py:970
  308.0 60.9 %copy-start.10 = (bf16[4096,128]{1,0:T(8,128)(2,1)}, bf16[4096,128]{1,0:T(8,128)(2,1)S(1)}, u32[]{:S(2)}) copy-start(bf16[4096,128]{1,0:T(8,128)(2,1)S(1)} %copy.280.k2_ref) | copy-start | bytes 3145732
  310.1 51.0 %copy-start.11 = (bf16[4096,128]{1,0:T(8,128)(2,1)}, bf16[4096,128]{1,0:T(8,128)(2,1)S(1)}, u32[]{:S(2)}) copy-start(bf16[4096,128]{1,0:T(8,128)(2,1)S(1)} %copy.279.q_ref) | copy-start | bytes 3145732
  362.7 56.5 %copy-start.8 = (bf16[16,256,128]{2,1,0:T(8,128)(2,1)}, bf16[16,256,128]{2,1,0:T(8,128)(2,1)S(1)}, u32[]{:S(2)}) copy-start(bf16[16,256,128]{2,1,0:T(8,128)(2,1)S(1)} %all-to-all-done.4) | copy-start | bytes 3145732
  362.7 56.5 %all-to-all-start.3 = ((bf16[16,256,128]{2,1,0:T(8,128)(2,1)}), bf16[16,256,128]{2,1,0:T(8,128)(2,1)}, u32[]{:S(2)}, u32[]{:S(2)}) async-start(bf16[16,256,128]{2,1,0:T(8,128)(2,1)} %bitcast.278), calls=%async_computation.3 | async-start | bytes 2097152 | tf_op jit(solution)/shard_map/all_to_all | solution.py:970
  419.2 46.2 %all-to-all-start.5 = ((bf16[16,256,128]{2,1,0:T(8,128)(2,1)}), bf16[16,256,128]{2,1,0:T(8,128)(2,1)S(1)}, u32[]{:S(2)}, u32[]{:S(2)}) async-start(bf16[16,256,128]{2,1,0:T(8,128)(2,1)} %bitcast.41), calls=%async_computation.5 | async-start | bytes 2097152 | tf_op jit(solution)/shard_map/all_to_all | solution.py:970
  427.6 46.1 %copy-start.25 = (f32[1,1,4,512]{3,1,2,0:T(1,128)}, f32[1,1,4,512]{3,1,2,0:T(1,128)S(1)}, u32[]{:S(2)}) copy-start(f32[1,1,4,512]{3,1,2,0:T(1,128)S(1)} %copy.337) | copy-start | bytes 24580
  427.6 46.0 %copy-start.7 = (bf16[4,8,4,512]{3,1,2,0:T(8,128)(2,1)}, bf16[4,8,4,512]{3,1,2,0:T(8,128)(2,1)S(1)}, u32[]{:S(2)}) copy-start(bf16[4,8,4,512]{3,1,2,0:T(8,128)(2,1)S(1)} %copy.338) | copy-start | bytes 393220
  429.2 111.1 %collective-permute-start.1 = (bf16[512,2048]{1,0:T(8,128)(2,1)}, bf16[512,2048]{1,0:T(8,128)(2,1)}, u32[]{:S(2)}, u32[]{:S(2)}) collective-permute-start(bf16[512,2048]{1,0:T(8,128)(2,1)} %bitcast.166.e_ref.upstream_ref), channel_id=1, source_target_pairs={{0,16},{16,0},{1,17},{17,1},{2,18},{18,2},{3,19},{19,3},{4,20},{20... | collective-permute-start | bytes 6291464 | tf_op jit(solution)/shard_map/ppermute | solution.py:1014
  473.6 12.7 %copy-start.2 = (bf16[512,2048]{1,0:T(8,128)(2,1)}, bf16[512,2048]{1,0:T(8,128)(2,1)S(1)}, u32[]{:S(2)}) copy-start(bf16[512,2048]{1,0:T(8,128)(2,1)S(1)} %reshape.477.heads_ref) | copy-start | bytes 6291460
  487.0 53.3 %collective-permute-start = (bf16[512,2048]{1,0:T(8,128)(2,1)}, bf16[512,2048]{1,0:T(8,128)(2,1)S(1)}, u32[]{:S(2)}, u32[]{:S(2)}) collective-permute-start(bf16[512,2048]{1,0:T(8,128)(2,1)} %get-tuple-element.84.h_ref), channel_id=1, source_target_pairs={{0,16},{16,0},{1,17},{17,1},{2,18},{18,2},{3,19},{19,3},{4,20},{20... | collective-permute-start | bytes 6291464 | tf_op jit(solution)/shard_map/ppermute | solution.py:1014
  631.5 47.0 %collective-permute-start.3 = (bf16[512,2048]{1,0:T(8,128)(2,1)}, bf16[512,2048]{1,0:T(8,128)(2,1)S(1)}, u32[]{:S(2)}, u32[]{:S(2)}) collective-permute-start(bf16[512,2048]{1,0:T(8,128)(2,1)} %get-tuple-element.103), channel_id=1, source_target_pairs={{0,16},{16,0},{1,17},{17,1},{2,18},{18,2},{3,19},{19,3},{4,20},{20... | collective-permute-start | bytes 6291464 | tf_op jit(solution)/shard_map/ppermute | solution.py:1014
  695.2 26.6 %all-to-all-start.6 = ((bf16[16,256,128]{2,1,0:T(8,128)(2,1)}), bf16[16,256,128]{2,1,0:T(8,128)(2,1)S(1)}, u32[]{:S(2)}, u32[]{:S(2)}) async-start(bf16[16,256,128]{2,1,0:T(8,128)(2,1)} %bitcast.364), calls=%async_computation.6 | async-start | bytes 2097152 | tf_op jit(solution)/shard_map/all_to_all | solution.py:970
  698.9 185.3 %reduce-scatter.3.cloned.1.call-start = ((), (), s32[]{:S(2)}) async-start(), calls=%async_computation.16 | async-start | bytes 1671168 | tf_op jit(solution)/shard_map/reduce_scatter | solution.py:1064
  698.9 29.8 %copy-start.38 = (bf16[4096,64]{0,1:T(8,128)(2,1)S(1)}, bf16[4096,64]{0,1:T(8,128)(2,1)}, u32[]{:S(2)}) copy-start(bf16[4096,64]{0,1:T(8,128)(2,1)} %get-tuple-element.242) | copy-start | bytes 1572868
  699.6 98.4 %collective-permute-start.2 = (bf16[512,2048]{1,0:T(8,128)(2,1)}, bf16[512,2048]{1,0:T(8,128)(2,1)}, u32[]{:S(2)}, u32[]{:S(2)}) collective-permute-start(bf16[512,2048]{1,0:T(8,128)(2,1)} %get-tuple-element.99), channel_id=1, source_target_pairs={{0,16},{16,0},{1,17},{17,1},{2,18},{18,2},{3,19},{19,3},{4,20},{20... | collective-permute-start | bytes 6291464 | tf_op jit(solution)/shard_map/ppermute | solution.py:1014
  721.8 85.1 %all-to-all-start.7 = ((bf16[16,256,128]{2,1,0:T(8,128)(2,1)}), bf16[16,256,128]{2,1,0:T(8,128)(2,1)}, u32[]{:S(2)}, u32[]{:S(2)}) async-start(bf16[16,256,128]{2,1,0:T(8,128)(2,1)} %bitcast.81), calls=%async_computation.7 | async-start | bytes 2097152 | tf_op jit(solution)/shard_map/all_to_all | solution.py:970
  728.7 155.6 %reduce-scatter.5.cloned.1.call-start = ((), (), s32[]{:S(2)}) async-start(), calls=%async_computation.17 | async-start | bytes 3342336 | tf_op jit(solution)/shard_map/reduce_scatter | solution.py:1065
  734.9 63.1 %copy-start.29 = (f32[512,2048]{1,0:T(8,128)S(1)}, f32[512,2048]{1,0:T(8,128)}, u32[]{:S(2)}) copy-start(f32[512,2048]{1,0:T(8,128)} %get-tuple-element.83.attended_ref) | copy-start | bytes 12582916
  803.5 75.2 %collective-permute-start.4 = (bf16[512,512]{1,0:T(8,128)(2,1)}, bf16[512,512]{1,0:T(8,128)(2,1)}, u32[]{:S(2)}, u32[]{:S(2)}) collective-permute-start(bf16[512,512]{1,0:T(8,128)(2,1)} %get-tuple-element.239), channel_id=1, source_target_pairs={{0,4},{4,8},{8,12},{12,0},{1,5},{5,9},{9,13},{13,1},{2,6},{6,10},{... | collective-permute-start | bytes 1572872 | tf_op jit(solution)/shard_map/ppermute | solution.py:733
  803.9 74.8 %collective-permute-start.5 = (bf16[512,512]{1,0:T(8,128)(2,1)}, bf16[512,512]{1,0:T(8,128)(2,1)}, u32[]{:S(2)}, u32[]{:S(2)}) collective-permute-start(bf16[512,512]{1,0:T(8,128)(2,1)} %get-tuple-element.238), channel_id=1, source_target_pairs={{0,8},{4,12},{8,0},{12,4},{1,9},{5,13},{9,1},{13,5},{2,10},{6,14},... | collective-permute-start | bytes 1572872 | tf_op jit(solution)/shard_map/ppermute | solution.py:733
  805.5 73.2 %collective-permute-start.6 = (bf16[512,512]{1,0:T(8,128)(2,1)}, bf16[512,512]{1,0:T(8,128)(2,1)}, u32[]{:S(2)}, u32[]{:S(2)}) collective-permute-start(bf16[512,512]{1,0:T(8,128)(2,1)} %get-tuple-element.237), channel_id=1, source_target_pairs={{0,12},{4,0},{8,4},{12,8},{1,13},{5,1},{9,5},{13,9},{2,14},{6,2},{... | collective-permute-start | bytes 1572872 | tf_op jit(solution)/shard_map/ppermute | solution.py:733
  806.9 77.4 %all-to-all-start.8 = ((bf16[16,256,128]{2,1,0:T(8,128)(2,1)}), bf16[16,256,128]{2,1,0:T(8,128)(2,1)}, u32[]{:S(2)}, u32[]{:S(2)}) async-start(bf16[16,256,128]{2,1,0:T(8,128)(2,1)} %bitcast.96), calls=%async_computation.10 | async-start | bytes 2097152 | tf_op jit(solution)/shard_map/all_to_all | solution.py:970
  811.8 63.5 %copy-start.37 = (f32[4096,128]{1,0:T(8,128)S(1)}, f32[4096,128]{1,0:T(8,128)}, u32[]{:S(2)}) copy-start(f32[4096,128]{1,0:T(8,128)} %get-tuple-element.107) | copy-start | bytes 6291460
  884.3 69.3 %all-to-all-start.9 = ((bf16[16,256,256]{2,1,0:T(8,128)(2,1)}), bf16[16,256,256]{2,1,0:T(8,128)(2,1)S(1)}, u32[]{:S(2)}, u32[]{:S(2)}) async-start(bf16[16,256,256]{2,1,0:T(8,128)(2,1)} %bitcast.97), calls=%async_computation.11 | async-start | bytes 4194304 | tf_op jit(solution)/shard_map/all_to_all | solution.py:970
  890.5 61.8 %all-gather.18.cloned.1.call-start = ((), (), s32[]{:S(2)}) async-start(), calls=%async_computation.20 | async-start | bytes 1179648 | tf_op jit(solution)/shard_map/all_gather | solution.py:1101
  891.3 87.6 %all-gather.20.cloned.1.call-start = ((), (), s32[]{:S(2)}) async-start(), calls=%async_computation.21 | async-start | bytes 1769472 | tf_op jit(solution)/shard_map/all_gather | solution.py:1102
  993.7 10.7 %copy-start.46 = (f32[512,128]{1,0:T(8,128)S(1)}, f32[512,128]{1,0:T(8,128)}, u32[]{:S(2)}) copy-start(f32[512,128]{1,0:T(8,128)} %fusion.38) | copy-start | bytes 786436
  993.7 29.9 %all-to-all-start.10 = ((bf16[16,52,512]{2,1,0:T(8,128)(2,1)}), bf16[16,52,512]{2,1,0:T(8,128)(2,1)S(1)}, u32[]{:S(2)}, u32[]{:S(2)}) async-start(bf16[16,52,512]{2,1,0:T(8,128)(2,1)} %pad_maximum_fusion.11), calls=%async_computation.12 | async-start | bytes 1835008 | tf_op jit(solution)/shard_map/all_to_all | solution.py:1144
  999.5 29.6 %collective-permute-start.7 = (bf16[512,512]{1,0:T(8,128)(2,1)}, bf16[512,512]{1,0:T(8,128)(2,1)}, u32[]{:S(2)}, u32[]{:S(2)}) collective-permute-start(bf16[512,512]{1,0:T(8,128)(2,1)} %get-tuple-element.229), channel_id=1, source_target_pairs={{0,4},{4,8},{8,12},{12,0},{1,5},{5,9},{9,13},{13,1},{2,6},{6,10},{... | collective-permute-start | bytes 1572872 | tf_op jit(solution)/shard_map/ppermute | solution.py:733
  999.9 29.2 %collective-permute-start.8 = (bf16[512,512]{1,0:T(8,128)(2,1)}, bf16[512,512]{1,0:T(8,128)(2,1)}, u32[]{:S(2)}, u32[]{:S(2)}) collective-permute-start(bf16[512,512]{1,0:T(8,128)(2,1)} %get-tuple-element.228), channel_id=1, source_target_pairs={{0,8},{4,12},{8,0},{12,4},{1,9},{5,13},{9,1},{13,5},{2,10},{6,14},... | collective-permute-start | bytes 1572872 | tf_op jit(solution)/shard_map/ppermute | solution.py:733
  1001.6 33.5 %collective-permute-start.9 = (bf16[512,512]{1,0:T(8,128)(2,1)}, bf16[512,512]{1,0:T(8,128)(2,1)}, u32[]{:S(2)}, u32[]{:S(2)}) collective-permute-start(bf16[512,512]{1,0:T(8,128)(2,1)} %get-tuple-element.227), channel_id=1, source_target_pairs={{0,12},{4,0},{8,4},{12,8},{1,13},{5,1},{9,5},{13,9},{2,14},{6,2},{... | collective-permute-start | bytes 1572872 | tf_op jit(solution)/shard_map/ppermute | solution.py:733
  1024.5 14.5 %all-to-all-start.12 = ((f32[8,20,512]{2,1,0:T(8,128)}), f32[8,20,512]{2,1,0:T(8,128)S(1)}, u32[]{:S(2)}, u32[]{:S(2)}) async-start(f32[8,20,512]{2,1,0:T(8,128)} %broadcast_in_dim.28), calls=%async_computation.14 | async-start | bytes 786432 | tf_op jit(solution)/shard_map/all_to_all | solution.py:1115
  1040.0 20.3 %all-to-all-start.11 = ((f32[8,32,512]{2,1,0:T(8,128)}), f32[8,32,512]{2,1,0:T(8,128)S(1)}, u32[]{:S(2)}, u32[]{:S(2)}) async-start(f32[8,32,512]{2,1,0:T(8,128)} %broadcast_in_dim.27), calls=%async_computation.13 | async-start | bytes 1048576 | tf_op jit(solution)/shard_map/all_to_all | solution.py:1115
  1049.6 15.2 %copy-start.1 = (bf16[128,2048]{1,0:T(8,128)(2,1)S(1)}, bf16[128,2048]{1,0:T(8,128)(2,1)}, u32[]{:S(2)}) copy-start(bf16[128,2048]{1,0:T(8,128)(2,1)} %param.53) | copy-start | bytes 1572868
  (85 other events, 321.2 us)
Sparse Core Ops, SparseCore 0:
  13.7 164.3 all-gather.11
  179.7 204.0 all-gather.13
  385.4 178.2 all-gather.15
  703.1 69.7 reduce-scatter.2
  777.0 83.6 reduce-scatter.4
  894.0 58.3 all-gather.17
  954.4 24.4 all-gather.19

commit v3 on v2

--- a/solution.py
+++ b/solution.py
@@ -10,6 +10,7 @@
 BLOCKS = 32
 EPS = 1e-05
 ROPE_BASE = 500000.0
+GATHER_ROWS = 128
 TILE = 512
 REACH = 256
 LOG2E = math.log2(math.e)
@@ -29,11 +30,26 @@
     return jnp.where((lane < 64) if e == 0 else (lane >= 64), x, jnp.zeros_like(x))
 
 
-def fwd_kernel(heads, factor, end_ref, q_ref, k2_ref, vt_ref, o_ref, lse_ref, acc_ref, m_ref, l_ref):
+def doubled(kv):
+    wide = kv.astype(jnp.float32)
+    turned = pltpu.roll(wide, 64, 1)
+    lane = lax.broadcasted_iota(jnp.int32, wide.shape, 1)
+    return jnp.where(lane < 64, wide, turned).astype(jnp.bfloat16), jnp.where(lane < 64, turned, wide).astype(jnp.bfloat16)
+
+
+def fwd_kernel(heads, factor, end_ref, q_ref, kv_ref, o_ref, lse_ref, acc_ref, m_ref, l_ref, k2_ref, vt_ref):
     i = pl.program_id(0)
     tq = q_ref.shape[0]
     q0 = i * tq
     c = factor * LOG2E
+
+    @pl.when(i == 0)
+    def _():
+        for t in range(kv_ref.shape[0] // tq):
+            rows = slice(t * tq, (t + 1) * tq)
+            k2_ref[rows, :] = doubled(kv_ref[rows, :])[0]
+            vt_ref[:, rows] = kv_ref[rows, :].astype(jnp.float32).T[64:, :].astype(jnp.bfloat16)
+
     ends = end_ref[...]
     m_ref[...] = jnp.full_like(m_ref, NEG)
     l_ref[...] = jnp.zeros_like(l_ref)
@@ -59,15 +75,19 @@
             acc_ref[a, :] = acc_ref[a, :] * alpha + nn(vv, p.astype(jnp.bfloat16))
 
     def body(j, _):
-        tile(pl.multiple_of(j * tq, tq), tq, False)
+        tile(pl.multiple_of(j * 2 * tq, tq), 2 * tq, False)
         return 0
 
-    lax.fori_loop(0, i, body, 0)
-    tile(pl.multiple_of(q0, tq), tq, True)
-
-    @pl.when(i < pl.num_programs(0) - 1)
-    def _():
-        tile(pl.multiple_of(q0 + tq, REACH), REACH, True)
+    lax.fori_loop(0, i // 2, body, 0)
+    last = pl.num_programs(0) - 1
+
+    for odd in (False, True):
+        for reach in (REACH, 0):
+
+            @pl.when((i % 2 == int(odd)) & ((i < last) if reach else (i == last)))
+            def _():
+                before = tq if odd else 0
+                tile(pl.multiple_of(q0 - before, tq), before + tq + reach, True)
 
     lse_ref[...] = m_ref[...] + jnp.log2(l_ref[...])
     inv = 1.0 / l_ref[...]
@@ -81,8 +101,9 @@
         o_ref[:, p * 128:(p + 1) * 128] = jnp.concatenate(parts, axis=0).T.astype(o_ref.dtype)
 
 
-def attend(q, k2, vt, ends, heads, factor):
-    length, width = q.shape
+def attend(q, kv, ends, heads, factor):
+    (q, q_at), (kv, kv_at) = q, kv
+    length, width = q.shape[0], 128
     tq = min(TILE, length)
     rows = 8
     return pl.pallas_call(
@@ -90,9 +111,8 @@
         grid=(length // tq,),
         in_specs=[
             pl.BlockSpec((1, tq), lambda i: (0, i)),
-            pl.BlockSpec((tq, width), lambda i: (i, 0)),
-            pl.BlockSpec((length, 128), lambda i: (0, 0)),
-            pl.BlockSpec((64, length), lambda i: (0, 0)),
+            pl.BlockSpec((tq, width), lambda i: (i, q_at)),
+            pl.BlockSpec((length, 128), lambda i: (0, kv_at)),
         ],
         out_specs=[
             pl.BlockSpec((tq, width), lambda i: (i, 0)),
@@ -106,13 +126,15 @@
             pltpu.VMEM((heads * 64, tq), jnp.float32),
             pltpu.VMEM((rows, tq), jnp.float32),
             pltpu.VMEM((rows, tq), jnp.float32),
+            pltpu.VMEM((length, 128), jnp.bfloat16),
+            pltpu.VMEM((64, length), jnp.bfloat16),
         ],
         compiler_params=pltpu.CompilerParams(vmem_limit_bytes=48 * 2**20),
         cost_estimate=pl.CostEstimate(
             flops=2 * heads * length * length * 64, bytes_accessed=4 * length * width + length * 384, transcendentals=heads * length * length // 2
         ),
         name="attend_forward",
-    )(ends, q, k2, vt)
+    )(ends, q, kv)
 
 
 def turn_back(values, cosine, sine):
@@ -120,12 +142,19 @@
     return jnp.concatenate([high * cosine + rest * sine, rest * cosine - high * sine], axis=0)
 
 
-def bwd_kernel(heads, factor, end_ref, cos_ref, sin_ref, q_ref, do_ref, o_ref, lse_ref, k2_ref, v2_ref, kt_ref, dq_ref, dkv_ref, dqt_ref, delta_ref, dk_ref, dv_ref):
+def bwd_kernel(heads, factor, last, end_ref, cos_ref, sin_ref, q_ref, do_ref, o_ref, lse_ref, kv_ref, *refs):
+    if last:
+        earlier_ref, dq_ref, *refs = refs
+    else:
+        dq_ref, dkv_ref, *refs = refs
+    dqt_ref, delta_ref, dk_ref, dv_ref, k2_ref, v2_ref, kt_ref = refs
     j = pl.program_id(0)
     n = pl.num_programs(0)
-    tk = k2_ref.shape[0]
+    tk = kv_ref.shape[0]
     length, width = q_ref.shape
     c = factor * LOG2E
+    k2_ref[...], v2_ref[...] = doubled(kv_ref[...])
+    kt_ref[...] = kv_ref[...].astype(jnp.float32).T[:64, :].astype(jnp.bfloat16)
 
     @pl.when(j == 0)
     def _():
@@ -143,13 +172,13 @@
     dk_ref[...] = jnp.zeros_like(dk_ref)
     dv_ref[...] = jnp.zeros_like(dv_ref)
 
-    def tile(q0, size, masked):
-        rows = pl.ds(q0, tk)
+    def tile(q0, count, size, masked):
+        rows = pl.ds(q0, count)
         kk = k2_ref[:size, :]
         vv = v2_ref[:size, :]
         kt = kt_ref[:, :size]
         if masked:
-            allowed = (lax.broadcasted_iota(jnp.int32, (size, tk), 0) + j * tk) < end_ref[:, rows]
+            allowed = (lax.broadcasted_iota(jnp.int32, (size, count), 0) + j * tk) < end_ref[:, rows]
         for h in range(heads):
             lanes = slice((h // 2) * 128, (h // 2 + 1) * 128)
             qh = half_of(q_ref[rows, lanes], h % 2)
@@ -166,21 +195,30 @@
 
     @pl.when(j > 0)
     def _():
-        tile(pl.multiple_of((j - 1) * tk, tk), REACH, True)
-
-    tile(pl.multiple_of(j * tk, tk), tk, True)
+        tile(pl.multiple_of((j - 1) * tk, tk), tk, REACH, True)
+
+    rest = n - 1 - j
+    for odd in (False, True):
+
+        @pl.when(rest % 2 == int(odd))
+        def _():
+            tile(pl.multiple_of(j * tk, tk), 2 * tk if odd else tk, tk, True)
 
     def body(i, _):
-        tile(pl.multiple_of(i * tk, tk), tk, False)
+        tile(pl.multiple_of((j + 1 + rest % 2 + 2 * i) * tk, tk), 2 * tk, tk, False)
         return 0
 
-    lax.fori_loop(j + 1, n, body, 0)
+    lax.fori_loop(0, rest // 2, body, 0)
 
     own = pl.ds(pl.multiple_of(j * tk, tk), tk)
     dk = dk_ref[...].T
     dv = dv_ref[...].T
     dk = turn_back(dk[:64] + dk[64:], cos_ref[:, own], sin_ref[:, own]) * factor
-    dkv_ref[...] = jnp.concatenate([dk, dv[:64] + dv[64:]], axis=0).T.astype(dkv_ref.dtype)
+    dkv = jnp.concatenate([dk, dv[:64] + dv[64:]], axis=0).T
+    if last:
+        dq_ref[own, width:] = (dkv if earlier_ref is None else dkv + earlier_ref[...]).astype(dq_ref.dtype)
+    else:
+        dkv_ref[...] = dkv
 
     @pl.when(j == n - 1)
     def _():
@@ -196,45 +234,49 @@
                 dq_ref[rows, p * 128:(p + 1) * 128] = jnp.concatenate(parts, axis=0).T.astype(dq_ref.dtype)
 
 
-def attend_back(q, do, o, lse, k2, v2, kt, ends, cosine, sine, heads, factor):
-    length, width = q.shape
+def attend_back(q, do, o, lse, kv, ends, cosine, sine, heads, factor, earlier=None, last=True):
+    (q, q_at), (kv, kv_at) = q, kv
+    length, width = o.shape
     tk = min(TILE, length)
-    whole = lambda shape: pl.BlockSpec(shape, lambda j: (0, 0))
+    whole = lambda shape, at=0: pl.BlockSpec(shape, lambda j: (0, at))
+    by_block = lambda at=0: pl.BlockSpec((tk, 128), lambda j: (j, at))
+    if last and earlier is None:
+        earlier = jnp.zeros((length, 128), jnp.float32)
     return pl.pallas_call(
-        functools.partial(bwd_kernel, heads, factor),
+        functools.partial(bwd_kernel, heads, factor, last),
         grid=(length // tk,),
         in_specs=[
             whole((1, length)),
             whole((32, length)),
             whole((32, length)),
-            whole((length, width)),
+            whole((length, width), q_at),
             whole((length, width)),
             whole((length, width)),
             whole((8, length)),
-            pl.BlockSpec((tk, 128), lambda j: (j, 0)),
-            pl.BlockSpec((tk, 128), lambda j: (j, 0)),
-            pl.BlockSpec((64, tk), lambda j: (0, j)),
-        ],
-        out_specs=[
-            whole((length, width)),
-            pl.BlockSpec((tk, 128), lambda j: (j, 0)),
-        ],
-        out_shape=[
-            jax.ShapeDtypeStruct((length, width), jnp.bfloat16),
-            jax.ShapeDtypeStruct((length, 128), jnp.float32),
-        ],
+            by_block(kv_at),
+        ]
+        + ([by_block()] if last else []),
+        out_specs=[whole((length, width + 128))] if last else [whole((length, width)), by_block()],
+        out_shape=[jax.ShapeDtypeStruct((length, width + 128), jnp.bfloat16)]
+        if last
+        else [jax.ShapeDtypeStruct((length, width), jnp.bfloat16), jax.ShapeDtypeStruct((length, 128), jnp.float32)],
         scratch_shapes=[
             pltpu.VMEM((heads * 64, length), jnp.float32),
             pltpu.VMEM((8, length), jnp.float32),
             pltpu.VMEM((tk, 128), jnp.float32),
             pltpu.VMEM((tk, 128), jnp.float32),
+            pltpu.VMEM((tk, 128), jnp.bfloat16),
+            pltpu.VMEM((tk, 128), jnp.bfloat16),
+            pltpu.VMEM((64, tk), jnp.bfloat16),
         ],
         compiler_params=pltpu.CompilerParams(vmem_limit_bytes=48 * 2**20),
         cost_estimate=pl.CostEstimate(
-            flops=5 * heads * length * length * 64, bytes_accessed=8 * length * width + length * 512, transcendentals=heads * length * length // 2
+            flops=5 * heads * length * length * 64,
+            bytes_accessed=8 * length * width + length * 512,
+            transcendentals=heads * length * length // 2,
         ),
         name="attend_backward",
-    )(ends, cosine, sine, q, do, o, lse, k2, v2, kt)
+    )(ends, cosine, sine, q, do, o, lse, kv, *([earlier] if last else []))
 
 
 def buffered_once(shape, index_map):
@@ -327,35 +369,31 @@
     )(tokens, gain, mask, first, second, cosine, sine, weight, weight, weight)
 
 
-def qkv_back_kernel(
-    pairs, token_ref, attended_ref, gain_ref, mask_ref, first_ref, second_ref, low_ref, kv_ref, *refs
-):
-    query_refs, refs = refs[:pairs], refs[pairs:]
-    weight_refs, refs = refs[:3], refs[3:]
-    out_ref, rows_ref, cols_ref, grad_ref, lowered_ref, low_turned_ref = refs
-    c = pl.program_id(0)
-    rows, lanes, chunk = weight_refs[0].shape[1:]
-    seqs, _, kv_heads, part, _ = kv_ref.shape
+def joined_messages(query_refs, kv_ref):
+    seqs, _, kv_heads = kv_ref.shape[:3]
     units = query_refs[0].shape[2]
-    rank = mask_ref.shape[1] // 3
-
-    @pl.when(c == 0)
-    def _():
-        grad_ref[...] = jnp.zeros_like(grad_ref)
-        lowered_ref[...] = jnp.zeros_like(lowered_ref)
-        low_turned_ref[...] = low_ref[...].astype(jnp.float32).T.astype(jnp.bfloat16)
-
     parts = []
     for j in range(kv_heads):
         for u in range(j * units // kv_heads, (j + 1) * units // kv_heads):
             parts += [jnp.concatenate([q[s, 0, u] for s in range(seqs)], axis=0) for q in query_refs]
         parts.append(jnp.concatenate([kv_ref[s, 0, j] for s in range(seqs)], axis=0))
-    e = jnp.concatenate(parts, axis=1)
-    for r in range(rows):
-        total = nt(e[:, :chunk], weight_refs[0][0, r])
-        for i in (1, 2):
-            total += nt(e[:, i * chunk : (i + 1) * chunk], weight_refs[i][0, r])
-        grad_ref[:, r * lanes : (r + 1) * lanes] += total
+    return jnp.concatenate(parts, axis=1)
+
+
+def qkv_sums_kernel(token_ref, gain_ref, mask_ref, second_ref, low_ref, kv_ref, *refs):
+    query_refs, refs = refs[:-5], refs[-5:]
+    lowered_out_ref, rows_ref, cols_ref, lowered_ref, low_turned_ref = refs
+    c = pl.program_id(0)
+    rows, _, lanes = rows_ref.shape
+    kv_heads = kv_ref.shape[2]
+    rank = mask_ref.shape[1] // 3
+
+    @pl.when(c == 0)
+    def _():
+        lowered_ref[...] = jnp.zeros_like(lowered_ref)
+        low_turned_ref[...] = low_ref[...].astype(jnp.float32).T.astype(jnp.bfloat16)
+
+    e = joined_messages(query_refs, kv_ref)
     lowered_ref[...] += nt(e, second_ref[0])
     sums = nn(low_turned_ref[...], e)
     lane = lax.broadcasted_iota(jnp.int32, (rank, sums.shape[1]), 1) % (sums.shape[1] // kv_heads)
@@ -369,77 +407,126 @@
     @pl.when(c == pl.num_programs(0) - 1)
     def _():
         lowered = lowered_ref[...] * mask_ref[...]
-        grad = grad_ref[...] + nn(lowered.astype(jnp.bfloat16), first_ref[...])
+        lowered_out_ref[...] = lowered.astype(jnp.bfloat16)
+        _, normed = normalized(token_ref[...].astype(jnp.float32), gain_ref[...])
+        turned = nn(lowered.T.astype(jnp.bfloat16), normed)
+        for r in range(rows):
+            rows_ref[r] = turned[:, r * lanes : (r + 1) * lanes].astype(rows_ref.dtype)
+
+
+def qkv_grad_sums(tokens, gain, mask, second, low_qkv, kv, queries, rows):
+    count, features = tokens.shape
+    cols, _, width = second.shape
+    rank = mask.shape[1] // 3
+    lanes = features // rows
+    whole = lambda shape: buffered_once(shape, lambda c: (0,) * len(shape))
+    by_unit = lambda v: pl.BlockSpec((v.shape[0], 1) + v.shape[2:], lambda c: (0, c, 0, 0, 0))
+    return pl.pallas_call(
+        qkv_sums_kernel,
+        grid=(cols,),
+        in_specs=[
+            whole((count, features)),
+            whole((1, features)),
+            whole(mask.shape),
+            pl.BlockSpec((1,) + second.shape[1:], lambda c: (c, 0, 0)),
+            whole(low_qkv.shape),
+            by_unit(kv),
+        ]
+        + [by_unit(q) for q in queries],
+        out_specs=[
+            pl.BlockSpec(mask.shape, lambda c: (0, 0)),
+            pl.BlockSpec((rows, 3 * rank, lanes), lambda c: (0, 0, 0)),
+            pl.BlockSpec((1, rank, width), lambda c: (c, 0, 0)),
+        ],
+        out_shape=[
+            jax.ShapeDtypeStruct(mask.shape, jnp.bfloat16),
+            jax.ShapeDtypeStruct((rows, 3 * rank, lanes), jnp.bfloat16),
+            jax.ShapeDtypeStruct((cols, rank, width), jnp.bfloat16),
+        ],
+        scratch_shapes=[
+            pltpu.VMEM((count, 3 * rank), jnp.float32),
+            pltpu.VMEM((3 * rank, count), jnp.bfloat16),
+        ],
+        compiler_params=pltpu.CompilerParams(vmem_limit_bytes=48 * 2**20),
+        cost_estimate=pl.CostEstimate(
+            flops=2 * count * features * cols * width,
+            bytes_accessed=2 * count * cols * width + 2 * count * features,
+            transcendentals=count,
+        ),
+        name="qkv_grad_sums",
+    )(tokens, gain, mask, second, low_qkv, kv, *queries)
+
+
+def qkv_back_kernel(token_ref, attended_ref, gain_ref, first_ref, lowered_ref, kv_ref, *refs):
+    query_refs, refs = refs[:-5], refs[-5:]
+    weight_refs, (out_ref, grad_ref) = refs[:3], refs[3:]
+    c = pl.program_id(0)
+    rows, lanes, chunk = weight_refs[0].shape[1:]
+
+    @pl.when(c == 0)
+    def _():
+        grad_ref[...] = nn(lowered_ref[...], first_ref[...])
+
+    e = joined_messages(query_refs, kv_ref)
+    for r in range(rows):
+        total = nt(e[:, :chunk], weight_refs[0][0, r])
+        for i in (1, 2):
+            total += nt(e[:, i * chunk : (i + 1) * chunk], weight_refs[i][0, r])
+        grad_ref[:, r * lanes : (r + 1) * lanes] += total
+
+    @pl.when(c == pl.num_programs(0) - 1)
+    def _():
         values = token_ref[...].astype(jnp.float32)
-        inverse, normed = normalized(values, gain_ref[...])
-        turned = nn(lowered.T.astype(jnp.bfloat16), normed)
-        out = (attended_ref[...] + norm_back(values, inverse, gain_ref[...], grad)).astype(jnp.bfloat16)
+        inverse = lax.rsqrt(jnp.mean(values * values, axis=-1, keepdims=True) + EPS)
+        out = (attended_ref[...] + norm_back(values, inverse, gain_ref[...], grad_ref[...])).astype(jnp.bfloat16)
         for r in range(rows):
-            at = slice(r * lanes, (r + 1) * lanes)
-            out_ref[r] = out[:, at]
-            rows_ref[r] = turned[:, at].astype(rows_ref.dtype)
-
-
-def project_qkv_back(tokens, attended_grad, gain, mask, first, second, low_qkv, kv, queries, weight):
+            out_ref[r] = out[:, r * lanes : (r + 1) * lanes]
+
+
+def project_qkv_back(tokens, attended_grad, gain, first, lowered, kv, queries, weight):
     count, features = tokens.shape
-    cols, rows, lanes, _ = weight.shape
-    width = second.shape[2]
+    cols, rows, lanes, wide = weight.shape
+    width = wide - lanes
     chunk = width // 3
     ahead = lanes // chunk
-    rank = mask.shape[1] // 3
-    pairs = len(queries)
     whole = lambda shape: buffered_once(shape, lambda c: (0,) * len(shape))
     by_unit = lambda v: pl.BlockSpec((v.shape[0], 1) + v.shape[2:], lambda c: (0, c, 0, 0, 0))
     weights = lambda at: pl.BlockSpec((1, rows, lanes, chunk), lambda c: (c, 0, 0, ahead + at))
     return pl.pallas_call(
-        functools.partial(qkv_back_kernel, pairs),
+        qkv_back_kernel,
         grid=(cols,),
         in_specs=[
             whole((count, features)),
             whole((count, features)),
             whole((1, features)),
-            whole(mask.shape),
             whole(first.shape),
-            pl.BlockSpec((1,) + second.shape[1:], lambda c: (c, 0, 0)),
-            whole(low_qkv.shape),
+            whole(lowered.shape),
             by_unit(kv),
         ]
         + [by_unit(q) for q in queries]
         + [weights(0), weights(1), weights(2)],
-        out_specs=[
-            pl.BlockSpec((rows, count, lanes), lambda c: (0, 0, 0)),
-            pl.BlockSpec((rows, 3 * rank, lanes), lambda c: (0, 0, 0)),
-            pl.BlockSpec((1, rank, width), lambda c: (c, 0, 0)),
-        ],
-        out_shape=[
-            jax.ShapeDtypeStruct((rows, count, lanes), jnp.bfloat16),
-            jax.ShapeDtypeStruct((rows, 3 * rank, lanes), jnp.bfloat16),
-            jax.ShapeDtypeStruct((cols, rank, width), jnp.bfloat16),
-        ],
-        scratch_shapes=[
-            pltpu.VMEM((count, features), jnp.float32),
-            pltpu.VMEM((count, 3 * rank), jnp.float32),
-            pltpu.VMEM((3 * rank, count), jnp.bfloat16),
-        ],
+        out_specs=pl.BlockSpec((rows, count, lanes), lambda c: (0, 0, 0)),
+        out_shape=jax.ShapeDtypeStruct((rows, count, lanes), jnp.bfloat16),
+        scratch_shapes=[pltpu.VMEM((count, features), jnp.float32)],
         compiler_params=pltpu.CompilerParams(vmem_limit_bytes=60 * 2**20),
         cost_estimate=pl.CostEstimate(
-            flops=2 * count * features * cols * width,
+            flops=8 * count * features * cols * width,
             bytes_accessed=2 * features * cols * width + 10 * count * features,
             transcendentals=count,
         ),
         name="project_qkv_back",
-    )(tokens, attended_grad, gain, mask, first, second, low_qkv, kv, *queries, weight, weight, weight)
-
-
-def mlp_kernel(goes_on, group_ref, h_ref, e_ref, mask_ref, first_ref, second_ref, gate_ref, up_ref, down_ref, mids_ref, *refs):
+    )(tokens, attended_grad, gain, first, lowered, kv, *queries, weight, weight, weight)
+
+
+def mlp_kernel(fresh, goes_on, block, group_ref, h_ref, e_ref, mask_ref, first_ref, second_ref, gate_ref, up_ref, down_ref, mids_ref, *refs):
     if goes_on:
-        rows_in_ref, _, grad_in_ref, mixed_in_ref = refs[:4]
-        refs = refs[4:]
-    else:
+        sums_in_ref, grad_in_ref = refs[:2]
         refs = refs[2:]
-    rows_ref, cols_ref, grad_out_ref, mixed_out_ref = refs[:4]
+    elif not fresh:
+        refs = refs[1:]
+    sums_ref, grad_out_ref, hidden_ref, low_down_ref = refs[:4]
     low_ref, low_turned_ref, lowered_ref, lowered_turned_ref, sum_front_ref, sum_down_ref = refs[4:10]
-    grad_ref, mixed_ref = refs[10:] if len(refs) > 10 else (grad_out_ref, mixed_out_ref)
+    grad_ref = refs[10] if len(refs) > 10 else grad_out_ref
     c = pl.program_id(0)
     rows, lanes = gate_ref.shape[1], gate_ref.shape[3]
     rank = second_ref.shape[0]
@@ -456,10 +543,10 @@
         sum_down_ref[...] = jnp.zeros_like(sum_down_ref)
         if goes_on:
             grad_ref[...] = grad_in_ref[...]
-            mixed_ref[...] = mixed_in_ref[...]
+            sums_ref[...] = sums_in_ref[...]
         else:
             grad_ref[...] = jnp.zeros_like(grad_ref)
-            mixed_ref[...] = jnp.zeros_like(mixed_ref)
+            sums_ref[...] = jnp.zeros_like(sums_ref)
 
     h = h_ref[...]
     gate_second, up_second, down_first = mids_ref[0, 0, 0], mids_ref[0, 0, 1], mids_ref[0, 0, 2, :rank]
@@ -476,37 +563,48 @@
     for r in range(rows):
         at = slice(r * lanes, (r + 1) * lanes)
         grad_ref[:, at] += nt(gate_grad, gate_ref[0, r]) + nt(up_grad, up_ref[0, r])
-        mixed_ref[:, at] += nn(hidden, down_ref[0, r])
+    hidden_ref[...] = hidden
     sum_front_ref[...] += nt(gate_grad, gate_second) + nt(up_grad, up_second)
     sum_down_ref[...] += nt(hidden, down_first)
-    cols_ref[0, :rank] = nn(low_turned_ref[:rank], gate_grad)
-    cols_ref[0, rank : 2 * rank] = nn(low_turned_ref[rank:], up_grad)
-    cols_ref[0, 2 * rank :] = nn(lowered_turned_ref[...], hidden)
+    col_sum = jnp.concatenate(
+        [nn(low_turned_ref[:rank], gate_grad), nn(low_turned_ref[rank:], up_grad), nn(lowered_turned_ref[...], hidden)],
+        axis=0,
+    )
+    row_share, col_share = 3 * rank // sums_ref.shape[1], 3 * rank // rows
+    begin = share_height(row_share) + block * share_height(col_share)
+    for r in range(rows):
+        sums_ref[r, c, begin : begin + col_share] = col_sum[r * col_share : (r + 1) * col_share]
 
     @pl.when(c == pl.num_programs(0) - 1)
     def _():
         front_now = sum_front_ref[...] * mask_ref[...]
         grad_out_ref[...] = (grad_ref[...] + nn(front_now.astype(jnp.bfloat16), first_ref[...])).astype(grad_out_ref.dtype)
         down_now = sum_down_ref[...] * mask_ref[:, :rank]
-        mixed_out_ref[...] = (mixed_ref[...] + nn(down_now.astype(jnp.bfloat16), second_ref[...])).astype(mixed_out_ref.dtype)
+        low_down_ref[...] = down_now.astype(jnp.bfloat16)
         front_sum = nn(front_now.T.astype(jnp.bfloat16), h_ref[...])
         down_sum = nn(down_now.T.astype(jnp.bfloat16), e_ref[...])
         for r in range(rows):
             at = slice(r * lanes, (r + 1) * lanes)
             now = jnp.concatenate([front_sum[:, at], down_sum[:, at]], axis=0)
-            rows_ref[r] = now + rows_in_ref[r] if goes_on else now
-
-
-def feed_forward(group, block, h, e, mask, first, second, weight, mids, row_sums, col_sums, earlier, dtype):
+            for to in range(sums_ref.shape[1]):
+                sums_ref[r, to, :row_share] += now[to * row_share : (to + 1) * row_share]
+
+
+def share_height(count):
+    return -(-count // 8) * 8
+
+
+def feed_forward(group, block, blocks, h, e, mask, first, second, weight, mids, sums, earlier, dtype):
     count, features = h.shape
     cols, rows, _, lanes = weight.shape
     rank = mids.shape[3] // 2
     groups = mids.shape[1]
-    blocks = col_sums.shape[1] // (groups * 3 * rank)
     goes_on = earlier is not None
+    fresh = sums is None
     whole = lambda shape: buffered_once(shape, lambda c, g: (0,) * len(shape))
     weights = lambda at: pl.BlockSpec((1, rows, lanes, lanes), lambda c, g: (c, 0, at, 0))
-    row_spec = pl.BlockSpec((rows, 3 * rank, lanes), lambda c, g: (0, g[0], 0))
+    height = share_height(3 * rank // cols) + blocks * share_height(3 * rank // rows)
+    sums_shape = (rows, cols, height, lanes)
     anywhere = pl.BlockSpec(memory_space=pl.ANY)
     scratch = [
         pltpu.VMEM((count, 2 * rank), jnp.bfloat16),
@@ -517,9 +615,9 @@
         pltpu.VMEM((count, rank), jnp.float32),
     ]
     if dtype != jnp.float32:
-        scratch += [pltpu.VMEM((count, features), jnp.float32)] * 2
+        scratch += [pltpu.VMEM((count, features), jnp.float32)]
     return pl.pallas_call(
-        functools.partial(mlp_kernel, goes_on),
+        functools.partial(mlp_kernel, fresh, goes_on, block),
         grid_spec=pltpu.PrefetchScalarGridSpec(
             num_scalar_prefetch=1,
             grid=(cols,),
@@ -533,41 +631,85 @@
                 weights(1),
                 weights(2),
                 pl.BlockSpec((1, 1, 3, 2 * rank, lanes), lambda c, g: (c, g[0], 0, 0, 0)),
-                row_spec if goes_on else anywhere,
-                anywhere,
             ]
-            + ([whole((count, features))] * 2 if goes_on else []),
+            + ([] if fresh else [buffered_once(sums_shape, lambda c, g: (0, 0, g[0], 0)) if goes_on else anywhere])
+            + ([whole((count, features))] if goes_on else []),
             out_specs=[
-                row_spec,
-                pl.BlockSpec((1, 3 * rank, lanes), lambda c, g: (c, g[0] * blocks + block, 0)),
+                pl.BlockSpec(sums_shape, lambda c, g: (0, 0, g[0], 0)),
                 pl.BlockSpec((count, features), lambda c, g: (0, 0)),
-                pl.BlockSpec((count, features), lambda c, g: (0, 0)),
+                pl.BlockSpec((count, lanes), lambda c, g: (0, c)),
+                pl.BlockSpec((count, rank), lambda c, g: (0, 0)),
             ],
             scratch_shapes=scratch,
         ),
         out_shape=[
-            jax.ShapeDtypeStruct(row_sums.shape, jnp.float32),
-            jax.ShapeDtypeStruct(col_sums.shape, jnp.float32),
+            jax.ShapeDtypeStruct((rows, cols, groups * height, lanes), jnp.float32),
             jax.ShapeDtypeStruct((count, features), dtype),
-            jax.ShapeDtypeStruct((count, features), dtype),
+            jax.ShapeDtypeStruct((count, cols * lanes), jnp.bfloat16),
+            jax.ShapeDtypeStruct((count, rank), jnp.bfloat16),
         ],
-        input_output_aliases={10: 0, 11: 1},
+        input_output_aliases={} if fresh else {10: 0},
         compiler_params=pltpu.CompilerParams(vmem_limit_bytes=60 * 2**20),
         cost_estimate=pl.CostEstimate(
-            flops=12 * count * features * cols * lanes,
+            flops=10 * count * features * cols * lanes,
             bytes_accessed=6 * features * cols * lanes + 12 * count * features,
             transcendentals=count * cols * lanes,
         ),
         name="feed_forward",
-    )(group, h, e, mask, first, second, weight, weight, weight, mids, row_sums, col_sums, *(earlier or ()))
-
-
-def out_kernel(heads_ref, residual_ref, gain_ref, mask_ref, first_ref, second_ref, weight_ref, attended_ref, normed_ref, low_ref):
+    )(group, h, e, mask, first, second, weight, weight, weight, mids, *([] if fresh else [sums]), *([earlier] if goes_on else []))
+
+
+def down_kernel(second_ref, hidden_ref, low_ref, weight_ref, *refs):
+    kept_refs, out_ref = refs[:-1], refs[-1]
+    cols, lanes = weight_ref.shape[0], weight_ref.shape[3]
+    total = nn(low_ref[...], second_ref[...]) + nn(hidden_ref[...], weight_ref[:, 0].reshape(cols * lanes, lanes))
+    for v in kept_refs:
+        total += (v[0] if len(v.shape) == 3 else v[...]).astype(jnp.float32)
+    out_ref[0] = total.astype(out_ref.dtype)
+
+
+def project_down(second, hidden, low_down, weight, kept, dtype):
+    count = hidden.shape[0]
+    cols, rows, _, lanes = weight.shape
+    rank = low_down.shape[1]
+    whole = lambda v: buffered_once(v.shape, lambda r: (0, 0))
+    by_block = pl.BlockSpec((1, count, lanes), lambda r: (r, 0, 0))
+    return pl.pallas_call(
+        down_kernel,
+        grid=(rows,),
+        in_specs=[
+            pl.BlockSpec((rank, lanes), lambda r: (0, r)),
+            whole(hidden),
+            whole(low_down),
+            pl.BlockSpec((cols, 1, lanes, lanes), lambda r: (0, r, 2, 0)),
+        ]
+        + [by_block if v.ndim == 3 else pl.BlockSpec((count, lanes), lambda r: (0, r)) for v in kept],
+        out_specs=by_block,
+        out_shape=jax.ShapeDtypeStruct((rows, count, lanes), dtype),
+        compiler_params=pltpu.CompilerParams(vmem_limit_bytes=48 * 2**20),
+        cost_estimate=pl.CostEstimate(
+            flops=2 * count * rows * lanes * cols * lanes,
+            bytes_accessed=2 * rows * lanes * cols * lanes + 8 * count * rows * lanes,
+            transcendentals=0,
+        ),
+        name="project_down",
+    )(second, hidden, low_down, weight, *kept)
+
+
+def out_kernel(pairs, *refs):
+    message_refs, refs = refs[:pairs], refs[pairs:]
+    residual_ref, gain_ref, mask_ref, first_ref, second_ref, weight_ref, attended_ref, normed_ref, low_ref, heads_ref = refs
     r = pl.program_id(0)
     cols, lanes = weight_ref.shape[0], weight_ref.shape[3]
 
     @pl.when(r == 0)
     def _():
+        seqs, _, units, part, width = message_refs[0].shape
+        for s in range(seqs):
+            for u in range(cols * units):
+                for p in range(pairs):
+                    begin = (u * pairs + p) * width
+                    heads_ref[s * part : (s + 1) * part, begin : begin + width] = message_refs[p][s, u // units, u % units]
         low_ref[...] = (nt(heads_ref[...], first_ref[...]) * mask_ref[...]).astype(jnp.bfloat16)
 
     at = pl.ds(pl.multiple_of(r * lanes, lanes), lanes)
@@ -582,16 +724,16 @@
         normed_ref[...] = normalized(attended_ref[...], gain_ref[...])[1]
 
 
-def project_out(heads, residual, gain, mask, first, second, weight):
+def project_out(messages, residual, gain, mask, first, second, weight):
     count, features = residual.shape
     cols, rows, lanes, _ = weight.shape
     rank = mask.shape[1]
     whole = lambda shape: pl.BlockSpec(shape, lambda r: (0,) * len(shape))
     return pl.pallas_call(
-        out_kernel,
+        functools.partial(out_kernel, len(messages)),
         grid=(rows,),
-        in_specs=[
-            whole(heads.shape),
+        in_specs=[buffered_once(m.shape, lambda r: (0,) * 5) for m in messages]
+        + [
             pl.BlockSpec((count, lanes), lambda r: (0, r)),
             whole((1, features)),
             whole((count, rank)),
@@ -605,20 +747,22 @@
             jax.ShapeDtypeStruct((count, features), jnp.bfloat16),
             jax.ShapeDtypeStruct((count, rank), jnp.bfloat16),
         ],
+        scratch_shapes=[pltpu.VMEM((count, cols * lanes), jnp.bfloat16)],
         compiler_params=pltpu.CompilerParams(vmem_limit_bytes=48 * 2**20),
         cost_estimate=pl.CostEstimate(
-            flops=2 * count * features * heads.shape[1],
-            bytes_accessed=2 * features * heads.shape[1] + 10 * count * features,
+            flops=2 * count * features * cols * lanes,
+            bytes_accessed=2 * features * cols * lanes + 10 * count * features,
             transcendentals=count,
         ),
         name="project_out",
-    )(heads, residual, gain, mask, first, second, weight)
+    )(*messages, residual, gain, mask, first, second, weight)
 
 
 def out_back_kernel(
-    pairs, pair_width, own_ref, other_ref, upstream_ref, attended_ref, gain_ref, mask_ref, first_ref, second_ref, heads_ref, low_ref, weight_ref,
-    attended_grad_ref, rows_ref, cols_ref, *refs,
+    pairs, pair_width, own_ref, other_ref, upstream_ref, attended_ref, gain_ref, mask_ref, first_ref, second_ref, low_ref, weight_ref, *refs
 ):
+    heads_refs, refs = refs[:pairs], refs[pairs:]
+    attended_grad_ref, rows_ref, cols_ref, *refs = refs
     message_refs = refs[:pairs]
     e_ref, lowered_ref, lowered_turned_ref = refs[pairs:]
     c = pl.program_id(0)
@@ -650,7 +794,8 @@
             for p in range(pairs):
                 begin = (u * pairs + p) * pair_width
                 message_refs[p][s, 0, u] = grad[s * part : (s + 1) * part, begin : begin + pair_width]
-    cols_ref[0] = nn(lowered_turned_ref[...], heads_ref[...]).astype(cols_ref.dtype)
+    heads = [jnp.concatenate([h[s, 0, u] for s in range(seqs)], axis=0) for u in range(units) for h in heads_refs]
+    cols_ref[0] = nn(lowered_turned_ref[...], jnp.concatenate(heads, axis=1)).astype(cols_ref.dtype)
 
 
 def project_out_back(own, other, upstream, attended, gain, mask, first, second, heads, low_out, weight, seqs, units, pairs, pair_width):
@@ -668,10 +813,10 @@
             whole((count, rank)),
             pl.BlockSpec((rank, lanes), lambda c: (0, c)),
             whole((rank, features)),
-            pl.BlockSpec((count, lanes), lambda c: (0, c)),
             whole((count, rank)),
             pl.BlockSpec((1, rows, lanes, lanes), lambda c: (c, 0, 0, 0)),
-        ],
+        ]
+        + [pl.BlockSpec((seqs, 1) + message[2:], lambda c: (0, c, 0, 0, 0))] * pairs,
         out_specs=[
             pl.BlockSpec((count, features), lambda c: (0, 0)),
             pl.BlockSpec((rows, rank, lanes), lambda c: (0, 0, 0)),
@@ -696,7 +841,7 @@
             transcendentals=count,
         ),
         name="project_out_back",
-    )(own, other, upstream, attended, gain, mask, first, second, heads, low_out, weight)
+    )(own, other, upstream, attended, gain, mask, first, second, low_out, weight, *heads)
 
 
 def dot(left, right):
@@ -711,8 +856,7 @@
     return values.astype(jnp.bfloat16)
 
 
-def after(values, earlier):
-    return lax.optimization_barrier((values, earlier))[0]
+ordered = lax.optimization_barrier
 
 
 def to_tokens(values):
@@ -723,15 +867,22 @@
     return moved.transpose(1, 2, 0, 3).reshape(seqs * (part // rows), rows * features)
 
 
-def to_features(blocks, seqs):
-    rows, _, width = blocks.shape
+def send_features(*terms):
+    rows = terms[0].shape[0]
     me = lax.axis_index("row")
     parts = []
     for step in range(rows):
-        block = lax.dynamic_index_in_dim(blocks, (me + step) % rows, 0, keepdims=False)
+        blocks = [lax.dynamic_index_in_dim(v, (me + step) % rows, 0, keepdims=False) for v in terms]
+        block = low(sum(v.astype(jnp.float32) for v in blocks)) if len(blocks) > 1 else blocks[0]
         if step:
             block = lax.ppermute(block, "row", [(i, (i + step) % rows) for i in range(rows)])
         parts.append(block)
+    return parts
+
+
+def join_features(parts, seqs):
+    rows, width = len(parts), parts[0].shape[1]
+    me = lax.axis_index("row")
     stacked = jnp.stack(parts)
     moved = jnp.stack(
         [lax.dynamic_index_in_dim(stacked, (me - source) % rows, 0, keepdims=False) for source in range(rows)]
@@ -951,9 +1102,6 @@
     mask = (row_seq[:, None] == jnp.arange(rank)[None, :] // RANK).astype(jnp.float32) * scale
     mask_twice, mask_thrice = jnp.tile(mask, (1, 2)), jnp.tile(mask, (1, 3))
 
-    residual = to_tokens(tokens)
-    upstream = to_tokens(after(cotangent, residual))
-    residual, upstream = lax.optimization_barrier((residual, upstream))
     positions = (lax.axis_index("col") * rows + lax.axis_index("row")) * part + jnp.arange(part)
     cosine, sine = rope_tables(jnp.tile(positions, seqs))
     flat, none = jnp.ones((seqs * part, HEAD_DIM), jnp.float32), jnp.zeros((seqs * part, HEAD_DIM), jnp.float32)
@@ -962,6 +1110,13 @@
         jnp.tile(jnp.concatenate([jnp.tile(table, (1, 2 * turning)), rest], axis=1), (1, kv_heads))
         for table, rest in ((cosine, flat), (sine, none))
     )
+    tokens, gains = ordered((tokens, gains))
+    residual = to_tokens(tokens)
+    cotangent, residual, mlp_shards, qkv_first, qkv_second, cosine, sine, mask_thrice, gains = ordered(
+        (cotangent, residual, mlp_shards, qkv_first, qkv_second, cosine, sine, mask_thrice, gains)
+    )
+    upstream = to_tokens(cotangent)
+    residual, upstream, mlp_shards[0] = ordered((residual, upstream, mlp_shards[0]))
     *messages, low_qkv = project_qkv(
         residual, gains[0:1], mask_thrice, qkv_first, qkv_second, cosine, sine, attn_weight, seqs, units, pairs, pair_width, kv_heads
     )
@@ -969,26 +1124,22 @@
     def exchange(values):
         return lax.all_to_all(values.reshape(units, part, -1), turned_both, 0, 0, tiled=True)
 
-    def from_pairs(parts):
-        split = jnp.stack([v.reshape(seqs, units // seqs, part, pair_width) for v in parts])
-        return split.transpose(1, 3, 2, 0, 4).reshape(seqs * part, -1)
+    def to_messages(parts):
+        return [v.reshape(seqs, cols, -1, part, pair_width) for v in parts]
 
     def padded(values):
         return jnp.pad(values, ((0, 0), (0, pair_pad)))
 
-    mlp_weights, earlier = [], residual
-    for n in range(blocks_ff):
-        shard = after(mlp_shards[n], earlier)
-        mlp_weights.append(lax.all_gather(shard, turned_both).reshape(cols, rows, -1, lanes))
-        earlier = messages[0]
     first_in = exchange(messages[0]).reshape(length, -1)
-    unit_queries = [first_in[:, :pair_width]] + [exchange(v).reshape(length, -1) for v in messages[1:]]
-    unit_queries = [padded(v) for v in unit_queries]
-    unit_keys = first_in[:, pair_width : pair_width + HEAD_DIM]
-    unit_values = first_in[:, pair_width + HEAD_DIM :]
-    keys_twice = jnp.concatenate([unit_keys, unit_keys], axis=1)
-    values_twice = jnp.concatenate([unit_values, unit_values], axis=1)
-    keys_turned, values_turned = unit_keys.T, unit_values.T
+    first_in, messages[1:], mlp_shards[1:] = ordered((first_in, messages[1:], mlp_shards[1:]))
+    mlp_weights = [lax.all_gather(v, turned_both).reshape(cols, rows, -1, lanes) for v in mlp_shards]
+    if pair_pad:
+        unit_kv = (first_in[:, pair_width:], 0)
+        unit_queries = [(padded(first_in[:, :pair_width]), 0)]
+    else:
+        unit_kv = (first_in, 1)
+        unit_queries = [(first_in, 0)]
+    unit_queries += [(padded(exchange(v).reshape(length, -1)), 0) for v in messages[1:]]
     unit_seq = (lax.axis_index("col") * rows + lax.axis_index("row")) * seqs // units
     labels = lax.dynamic_index_in_dim(block_labels, unit_seq, 0, keepdims=True)
     numbers = jnp.arange(BLOCKS)[:, None]
@@ -996,19 +1147,21 @@
     ends = jnp.sum(jnp.where(labels == numbers, ends_of, 0), axis=0, keepdims=True)
     unit_outs, log_sums = [], []
     for p in range(pairs):
-        out, log_sum = attend(unit_queries[p], keys_twice, values_turned, ends, pair_heads, factor)
+        out, log_sum = attend(unit_queries[p], unit_kv, ends, pair_heads, factor)
         unit_outs.append(out)
         log_sums.append(log_sum)
-    heads_out = from_pairs([exchange(v[:, :pair_width]) for v in unit_outs])
-    attended, normed_mlp, low_out = project_out(
-        heads_out, residual, gains[1:2], mask, out_first, out_second, attn_weight
-    )
-
+    heads_out = to_messages([exchange(v[:, :pair_width]) for v in unit_outs])
     unpacked = [
         unpack(mlp_weights[n][:, :, 3 * lanes :], packs[n][1], mlp_small if n == 0 else [], [middle(n)])
         for n in range(blocks_ff)
     ]
     front_first, down_second = (joined_rows(v) for v in unpacked[0][0])
+    heads_out, front_first, down_second, unpacked[0][1][0] = ordered(
+        (heads_out, front_first, down_second, unpacked[0][1][0])
+    )
+    attended, normed_mlp, low_out = project_out(
+        heads_out, residual, gains[1:2], mask, out_first, out_second, attn_weight
+    )
 
     def swap(values, step):
         return lax.ppermute(values, "dp", [(i, (i + step) % copies) for i in range(copies)])
@@ -1016,32 +1169,39 @@
     tokens_of = [(normed_mlp, upstream)]
     for step in range(1, copies):
         tokens_of.append((swap(normed_mlp, step), swap(upstream, step)))
-    row_sums = jnp.zeros((rows, copies * 3 * rank, lanes), jnp.float32)
-    col_sums = jnp.zeros((cols, copies * blocks_ff * 3 * rank, lanes), jnp.float32)
-    sums = [None] * copies
+    def second_of_group(step):
+        return lax.dynamic_slice_in_dim(down_second, (me - step) % copies * rank, rank, 0)
+
+    adapter_sums, grads, mixed = None, [None] * copies, [()] * copies
     for n in range(blocks_ff):
+        last = n == blocks_ff - 1
         order = list(range(copies))
-        for step in order if n < blocks_ff - 1 else order[1:] + order[:1]:
-            row_sums, col_sums, *sums[step] = feed_forward(
+        hidden, low_down = [None] * copies, [None] * copies
+        for step in order[1:] + order[:1] if last else order:
+            adapter_sums, grads[step], hidden[step], low_down[step] = feed_forward(
                 ((me - step) % copies).reshape(1),
                 n,
+                blocks_ff,
                 *tokens_of[step],
                 mask_twice,
                 front_first,
                 down_second,
                 mlp_weights[n],
                 unpacked[n][1][0],
-                row_sums,
-                col_sums,
-                sums[step],
-                jnp.float32 if n < blocks_ff - 1 or step == 0 else jnp.bfloat16,
+                adapter_sums,
+                grads[step],
+                jnp.float32 if not last or step == 0 else jnp.bfloat16,
             )
-    grad_part, mixed_part = sums[0]
-    mixed_backs = []
+        if not last:
+            mixed = [
+                (project_down(second_of_group(step), hidden[step], low_down[step], mlp_weights[n], mixed[step], jnp.float32),)
+                for step in range(copies)
+            ]
+            mlp_weights[n + 1], mixed = ordered((mlp_weights[n + 1], mixed))
+    grad_part = grads[0]
     for step in range(1, copies):
-        grad_back, mixed_back = (swap(v, -step) for v in sums[step])
+        grad_back = swap(grads[step], -step)
         grad_other = grad_back if step == 1 else grad_other + grad_back
-        mixed_backs.append(mixed_back)
 
     attended_grad, out_rows, out_cols, *grad_messages = project_out_back(
         grad_part,
@@ -1060,55 +1220,76 @@
         pairs,
         pair_width,
     )
-    row_sums, col_sums, _ = lax.optimization_barrier((row_sums, col_sums, grad_messages))
-    row_shares = lax.psum_scatter(row_sums.reshape(units, -1, lanes), both, scatter_dimension=0)
-    col_shares = lax.psum_scatter(col_sums.reshape(units, -1, lanes), turned_both, scatter_dimension=0)
-    unit_grads = [padded(exchange(v).reshape(length, -1)) for v in grad_messages]
+    shares = low(adapter_sums)
+    row_share, col_share = 3 * rank // cols, 3 * rank // rows
+    row_height, col_height = share_height(row_share), share_height(col_share)
+    grad_messages, hidden = ordered((grad_messages, hidden))
+    mixed_own, *mixed_others = [
+        project_down(
+            second_of_group(step),
+            hidden[step],
+            low_down[step],
+            mlp_weights[-1],
+            mixed[step] + (() if step else (attended,)),
+            jnp.bfloat16 if step else jnp.float32,
+        )
+        for step in range(copies)
+    ]
+    unit_grads = [padded(exchange(grad_messages[0]).reshape(length, -1))]
+    ends, mixed_own, mixed_others, shares, unit_grads[0] = ordered((ends, mixed_own, mixed_others, shares, unit_grads[0]))
+    shares = lax.psum_scatter(shares.reshape(units, -1, lanes), both, scatter_dimension=0)
+    mixed_backs = [swap(v, -step) for step, v in enumerate(mixed_others, 1)]
+    unit_grads[0], grad_messages[1:] = ordered((unit_grads[0], grad_messages[1:]))
+    unit_grads += [padded(exchange(v).reshape(length, -1)) for v in grad_messages[1:]]
     full_cosine, full_sine = (table.T for table in rope_tables(jnp.arange(length)))
     query_moved, kv_grad = [], None
     for p in range(pairs):
-        if p == pairs - 1 and p > 0:
-            mixed_backs, _ = lax.optimization_barrier((mixed_backs, kv_now))
-            mixed_part = sum((v.astype(jnp.float32) for v in mixed_backs), mixed_part)
-            mixed_out = low(attended + mixed_part).reshape(seqs * part, rows, lanes).transpose(1, 0, 2)
-            ends, mixed_out = lax.optimization_barrier((ends, mixed_out))
-        query_now, kv_now = attend_back(
+        last = p == pairs - 1
+        if last:
+            if p > 0:
+                shares, mixed_backs, kv_grad = ordered((shares, mixed_backs, kv_grad))
+            mixed_parts = send_features(mixed_own, *mixed_backs)
+            shares = shares.reshape(copies, -1, lanes)
+            parts = (
+                shares[:, :row_share].reshape(-1, lanes),
+                shares[:, row_height:].reshape(copies, blocks_ff, col_height, lanes)[:, :, :col_share].reshape(-1, lanes),
+            )
+            counts = [v.shape[0] for v in parts]
+            parts = [jnp.pad(low(v), ((0, -v.shape[0] % GATHER_ROWS), (0, 0))) for v in parts]
+            row_total = lax.all_gather(parts[0], ("dp", "col"))[..., : counts[0], :]
+            col_total = lax.all_gather(parts[1], ("dp", "row"))[..., : counts[1], :]
+        query_now, *kv_now = attend_back(
             unit_queries[p],
             unit_grads[p],
             unit_outs[p],
             log_sums[p],
-            keys_twice,
-            values_twice,
-            keys_turned,
+            unit_kv,
             ends,
             full_cosine,
             full_sine,
             pair_heads,
             factor,
+            kv_grad,
+            last,
         )
-        kv_grad = kv_now if kv_grad is None else kv_grad + kv_now
-        if p == pairs - 1:
-            query_now = jnp.concatenate([query_now[:, :pair_width], low(kv_grad)], axis=1)
-            if pairs == 1:
-                mixed_part = sum((v.astype(jnp.float32) for v in mixed_backs), mixed_part)
-                mixed_out = low(attended + mixed_part).reshape(seqs * part, rows, lanes).transpose(1, 0, 2)
-            mixed_out = to_features(mixed_out, seqs)
-            query_now, mixed_out, row_shares, col_shares, query_moved = lax.optimization_barrier(
-                (query_now, mixed_out, row_shares, col_shares, query_moved)
+        if last:
+            query_now, mixed_parts, row_total, col_total, query_moved = ordered(
+                (query_now, mixed_parts, row_total, col_total, query_moved)
             )
-        query_moved.append(exchange(query_now[:, : query_now.shape[1] if p == pairs - 1 else pair_width]))
-    row_height = row_shares.shape[0]
-    row_total = lax.all_gather(jnp.pad(row_shares, ((0, -row_height % 64), (0, 0))), ("dp", "col"))[..., :row_height, :]
-    col_total = lax.all_gather(col_shares, ("dp", "row"))
+            if pair_pad:
+                query_now = jnp.concatenate([query_now[:, :pair_width], query_now[:, -2 * HEAD_DIM :]], axis=1)
+        else:
+            kv_grad = kv_now[0]
+            query_now = query_now[:, :pair_width]
+        query_moved.append(exchange(query_now))
+    mixed_out = join_features(mixed_parts, seqs)
     kv_moved = query_moved[-1][..., pair_width:].reshape(seqs, cols, kv_heads, kv_copies, part, -1)
     kv_moved = low(kv_moved.astype(jnp.float32).sum(axis=3)) if kv_copies > 1 else kv_moved[:, :, :, 0]
     query_moved[-1] = query_moved[-1][..., :pair_width]
-    query_moved = [v.reshape(seqs, cols, -1, part, pair_width) for v in query_moved]
-    token_grad, qkv_rows, qkv_cols = project_qkv_back(
-        residual, attended_grad, gains[0:1], mask_thrice, qkv_first, qkv_second, low_qkv, kv_moved, query_moved, attn_weight
-    )
-
-    row_total, col_total, _ = lax.optimization_barrier((row_total, col_total, token_grad))
+    query_moved = to_messages(query_moved)
+    lowered_qkv, qkv_rows, qkv_cols = qkv_grad_sums(
+        residual, gains[0:1], mask_thrice, qkv_second, low_qkv, kv_moved, query_moved, rows
+    )
 
     def everywhere(values, axes, count):
         copied = jnp.broadcast_to(values[None], (count,) + values.shape)
@@ -1124,10 +1305,12 @@
             values, choose_wide, (((0,), (1,)), ((), ())), precision=lax.Precision.HIGHEST, preferred_element_type=jnp.float32
         )
 
-    row_total = row_total.reshape(copies, copies, 3, rank, lanes).sum(axis=0)
+    row_total = row_total.astype(jnp.float32).reshape(copies, cols, copies, row_share, lanes).sum(axis=0)
+    row_total = row_total.transpose(1, 0, 2, 3).reshape(copies, 3, rank, lanes)
     gate_first_gradient, up_first_gradient = (wide_first(row_total[:, i].reshape(-1, lanes)) for i in range(2))
     down_second_gradient = wide_second(row_total[:, 2].reshape(-1, lanes))
-    col_total = col_total.reshape(copies, copies, blocks_ff, 3, rank, lanes)
+    col_total = col_total.astype(jnp.float32).reshape(copies, rows, copies, blocks_ff, col_share, lanes)
+    col_total = col_total.transpose(0, 2, 3, 1, 4, 5).reshape(copies, copies, blocks_ff, 3, rank, lanes)
     pieces = [
         [col_total[x, :, n, i].reshape(-1, lanes) for x in range(copies) for n in range(blocks_ff)] for i in range(3)
     ]
@@ -1141,9 +1324,17 @@
     col_cut = col_cut.reshape(cols, rows, -1, lanes).transpose(1, 0, 2, 3)
     cut = row_cut.shape[2]
     attn_shares = jnp.concatenate([row_cut, col_cut], axis=2).reshape(units, -1, lanes)
+    attn_shares, lowered_qkv = ordered((attn_shares, lowered_qkv))
+    token_grad = project_qkv_back(
+        residual, attended_grad, gains[0:1], qkv_first, lowered_qkv, kv_moved, query_moved, attn_weight
+    )
     attn_sums = jnp.sum(lax.all_to_all(attn_shares, both, 0, 0, tiled=True).astype(jnp.float32), axis=0)
-    attn_rows = everywhere(attn_sums[:cut], ("dp", "col"), copies * cols).reshape(copies, 4, rank, lanes)
-    attn_cols = everywhere(attn_sums[cut:], ("dp", "row"), copies * rows)
+    token_parts = send_features(token_grad)
+    attn_rows, token_parts[0] = ordered((attn_sums[:cut], token_parts[0]))
+    attn_rows = everywhere(attn_rows, ("dp", "col"), copies * cols)
+    attn_cols, attn_rows = ordered((attn_sums[cut:], attn_rows))
+    attn_rows = attn_rows.reshape(copies, 4, rank, lanes)
+    attn_cols = everywhere(attn_cols, ("dp", "row"), copies * rows)
     query_first_gradient, key_first_gradient, value_first_gradient = (
         wide_first(attn_rows[:, i].reshape(-1, lanes)) for i in range(3)
     )
@@ -1158,7 +1349,7 @@
 
     return (
         mixed_out,
-        to_features(token_grad, seqs),
+        join_features(token_parts, seqs),
         query_first_gradient,
         query_second_gradient,
         key_first_gradient,

time: 1080 us -> 1010 us (0.935)
  waiting for transfers between devices: 300 us -> 128 us
  blocking collectives: 31.4 us -> 164 us
  local copies, waits for them, and re-layouts: 133 us -> 111 us
    all_to_all x0 -> x2, blocking collectives: none -> 129 us  [the longest x1 78.5 us: exchange(): lax.all_to_all(values.reshape(units, part, -1), turned_both, 0, 0, tiled=...]
    all_to_all x8 -> x7, waiting for transfers between devices: 127 us -> 24.8 us  [exchange(): lax.all_to_all(values.reshape(units, part, -1), turned_both, 0, 0, tiled=...]
    all_to_all x2 -> x1, waiting for transfers between devices: 79.4 us -> 10.2 us  [to_tokens(): moved = lax.all_to_all(cut, 'row', 0, 0, tiled=True)]
    pallas_call x8 -> x13, Pallas kernels: 333 us -> 350 us  [the longest x4 154 us: feed_forward(): pl.pallas_call(functools.partial(mlp_kernel, fresh, goes_on, block), grid...]
    pallas_call x2, Pallas kernels: 99.8 us -> 82.8 us  [attend(): pl.pallas_call(functools.partial(fwd_kernel, heads, factor), grid=(length...]
    all_to_all x1, waiting for transfers between devices: 14.8 us -> 2.44 us  [local(): lax.all_to_all(attn_shares, both, 0, 0, tiled=True).astype(jnp.float32)]
    unnamed x240 -> x236, local copies, waits for them, and re-layouts: 28.7 us -> 40.4 us
    all_to_all x8 -> x7, starting transfers between devices: 41.9 us -> 38.6 us  [exchange(): lax.all_to_all(values.reshape(units, part, -1), turned_both, 0, 0, tiled=...]
  transfers between devices with their start and end apart: 30 -> 27, of which waited for: 12 -> 11; matrix products, arithmetic and copies ran while one was open for 13% -> 11% of each run, Pallas kernels for 38% -> 40%
where the time goes in v3:
time: 1010 us
  Pallas kernels  464 us (46%)
  blocking collectives  164 us (16%)
  waiting for transfers between devices  128 us (13%)
  local copies, waits for them, and re-layouts  111 us (11%)
  starting transfers between devices  75.7 us (7%)
  other arithmetic  28.9 us (3%)
  between operations  18 us (2%)
  matrix products  17.3 us (2%)
    pallas_call x4, Pallas kernels, feed_forward(): pl.pallas_call(functools.partial(mlp_kernel, fresh, goes_on, block), grid...  154 us
    pallas_call x2, Pallas kernels, attend_back(): pl.pallas_call(functools.partial(bwd_kernel, heads, factor, last), grid=(...  126 us
    pallas_call x2, Pallas kernels, attend(): pl.pallas_call(functools.partial(fwd_kernel, heads, factor), grid=(length...  82.8 us
    all_to_all x1, blocking collectives, exchange(): lax.all_to_all(values.reshape(units, part, -1), turned_both, 0, 0, tiled=...  78.5 us
    all_gather x2, waiting for transfers between devices, local(): lax.all_gather(v, turned_both).reshape(cols, rows, -1, lanes)  63.3 us
    all_to_all x1, blocking collectives, to_tokens(): moved = lax.all_to_all(cut, 'row', 0, 0, tiled=True)  51 us
    unnamed x236, local copies, waits for them, and re-layouts  40.4 us
    all_to_all x7, starting transfers between devices, exchange(): lax.all_to_all(values.reshape(units, part, -1), turned_both, 0, 0, tiled=...  38.6 us
  transfers between devices with their start and end apart: 27, of which 11 were waited for; matrix products, arithmetic and copies ran while one was open for 11% of the time, Pallas kernels for 40%

profile of v3, /device:TPU:0, one launch (start us, length us, event | category | flops | bytes accessed | tf_op | source)
XLA Modules:
  0.0 1007.4 jit_solution(9632338786584476664)
XLA Ops:
  13.7 5.2 all-reduce.17
  24.0 29.6 %all-gather.5 = bf16[16,53,512]{2,1,0:T(8,128)(2,1)S(1)} all-gather(bf16[1,53,512]{2,1,0:T(8,128)(2,1)S(1)} %maximum_bitcast_fusion.4), channel_id=2, replica_groups=mesh['dp'=2,'row'=4,'col'=4] {'col','row'}, dimensions={0}, use_global_device_ids=true | all-gather | bytes 922624 | tf_op jit(solution)/shard_map/all_gather | solution.py:1041
  56.5 4.5 all-to-all-start
  99.4 10.2 %all-to-all-done = bf16[4,2,256,512]{3,2,1,0:T(8,128)(2,1)} async-done(((bf16[4,2,256,512]{3,2,1,0:T(8,128)(2,1)}), bf16[4,2,256,512]{3,2,1,0:T(8,128)(2,1)}, u32[]{:S(2)}, u32[]{:S(2)}) %all-to-all-start) | async-done | bytes 2097184 | tf_op jit(solution)/shard_map/all_to_all | solution.py:866
  109.6 3.2 copy.210
  115.9 51.0 %all_to_all.65 = bf16[4,2,256,512]{3,2,1,0:T(8,128)(2,1)S(1)} all-to-all(bf16[4,2,256,512]{3,2,1,0:T(8,128)(2,1)S(1)} %copy.220), channel_id=1, replica_groups=mesh['dp'=2,'row'=4,'col'=4] {'row'}, dimensions={0} | all-to-all | bytes 4194304 | tf_op jit(solution)/shard_map/all_to_all | solution.py:866
  172.9 4.4 all-gather.12.cloned.1.call-done
  180.3 15.6 %project_qkv.1 = (bf16[2,4,2,256,256]{4,3,2,1,0:T(8,128)(2,1)}, bf16[2,4,2,256,128]{4,3,2,1,0:T(8,128)(2,1)S(1)}, bf16[512,96]{1,0:T(8,128)(2,1)S(1)}) custom-call(bf16[512,2048]{1,0:T(8,128)(2,1)} %bitcast.334, f32[1,2048]{1,0:T(1,128)S(1)} %get-tuple-element.374.gain_ref, f32[512,96]{1,0:T(8,128)S(1)} %copy-done.14, bf16[96,2048]{1,0:T(8,128)(2,1)S(1)} %bitcast.278, ...), custom_call_target="tpu_custom_call" | custom-call | flops 6442450944 | bytes 16777216 | tf_op jit(solution)/shard_map/project_qkv/pallas_call | solution.py:343
  196.9 78.5 %all_to_all.66 = bf16[16,256,256]{2,1,0:T(8,128)(2,1)S(1)} all-to-all(bf16[16,256,256]{2,1,0:T(8,128)(2,1)} %bitcast.379), channel_id=1, replica_groups=mesh['dp'=2,'row'=4,'col'=4] {'col','row'}, dimensions={0} | all-to-all | bytes 4194304 | tf_op jit(solution)/shard_map/all_to_all | solution.py:1125
  275.4 3.7 all-to-all-start.4
  279.4 41.6 %attend_forward.2 = (bf16[4096,128]{1,0:T(8,128)(2,1)S(1)}, f32[8,4096]{1,0:T(8,128)S(1)}) custom-call(s32[1,4096]{1,0:T(1,128)S(1)} %bitcast.299, bf16[4096,256]{1,0:T(8,128)(2,1)S(1)} %bitcast.271, bf16[4096,256]{1,0:T(8,128)(2,1)S(1)} %bitcast.272), custom_call_target="tpu_custom_call" | custom-call | flops 4294967296 | bytes 3670016 | tf_op jit(solution)/shard_map/attend_forward/pallas_call | solution.py:109
  323.6 6.1 all-to-all-start.3
  331.0 41.3 %attend_forward.3 = (bf16[4096,128]{1,0:T(8,128)(2,1)S(1)}, f32[8,4096]{1,0:T(8,128)S(1)}) custom-call(s32[1,4096]{1,0:T(1,128)S(1)} %bitcast.300, bf16[4096,128]{1,0:T(8,128)(2,1)S(1)} %bitcast.282, bf16[4096,256]{1,0:T(8,128)(2,1)S(1)} %bitcast.273), custom_call_target="tpu_custom_call" | custom-call | flops 4294967296 | bytes 3670016 | tf_op jit(solution)/shard_map/attend_forward/pallas_call | solution.py:109
  373.9 6.4 all-to-all-start.5
  384.6 31.2 %all-gather.14.cloned.1.call-done = bf16[26880,512]{1,0:T(8,128)(2,1)} async-done(((bf16[1680,512]{1,0:T(8,128)(2,1)}), bf16[26880,512]{1,0:T(8,128)(2,1)}) %all-gather.14.cloned.1.call-update) | async-done | bytes 27525136 | tf_op jit(solution)/shard_map/all_gather | solution.py:1135
  415.8 2.7 slice.553
  420.8 12.4 %project_out.1 = (f32[512,2048]{1,0:T(8,128)}, bf16[512,2048]{1,0:T(8,128)(2,1)}, bf16[512,32]{1,0:T(8,128)(2,1)S(1)}) custom-call(bf16[2,4,2,256,128]{4,3,2,1,0:T(8,128)(2,1)S(1)} %bitcast.265, bf16[2,4,2,256,128]{4,3,2,1,0:T(8,128)(2,1)S(1)} %bitcast.267, bf16[512,2048]{1,0:T(8,128)(2,1)} %bitcast.335, f32[1,2048]{1,0:T(1,128)S(1)} %get-tuple-element.373.refs_3_.gain_ref, ...), custom_call_target="tpu_custom_call" | custom-call | flops 4294967296 | bytes 18874368 | tf_op jit(solution)/shard_map/project_out/pallas_call | solution.py:732
  435.3 38.3 %feed_forward.4 = (f32[4,4,144,512]{3,2,1,0:T(8,128)}, f32[512,2048]{1,0:T(8,128)}, bf16[512,2048]{1,0:T(8,128)(2,1)}, bf16[512,32]{1,0:T(8,128)(2,1)}) custom-call(s32[1]{0:T(128)} %bitcast.67.group_ref, bf16[512,2048]{1,0:T(8,128)(2,1)} %get-tuple-element.135.h_ref, bf16[512,2048]{1,0:T(8,128)(2,1)} %bitcast.331, f32[512,64]{1,0:T(8,128)} %copy.231.mask_ref, ...), custom_call_target="tpu_custom_call" | custom-call | flops 21474836480 | bytes 37748736 | tf_op jit(solution)/shard_map/feed_forward/pallas_call | solution.py:619
  476.2 9.0 project_down.4.refs_0_
  486.7 37.7 %feed_forward.5 = (f32[4,4,144,512]{3,2,1,0:T(8,128)}, f32[512,2048]{1,0:T(8,128)}, bf16[512,2048]{1,0:T(8,128)(2,1)}, bf16[512,32]{1,0:T(8,128)(2,1)}) custom-call(s32[1]{0:T(128)} %bitcast.71.group_ref, bf16[512,2048]{1,0:T(8,128)(2,1)} %copy-done.49, bf16[512,2048]{1,0:T(8,128)(2,1)} %collective-permute-done.1.e_ref, ...), custom_call_target="tpu_custom_call", output_to_operand_aliasing={{0}: (10, {})} | custom-call | flops 21474836480 | bytes 37748736 | tf_op jit(solution)/shard_map/feed_forward/pallas_call | solution.py:619
  526.8 9.0 project_down.5.refs_0_
  535.8 32.1 %all-gather.16.cloned.1.call-done = bf16[26112,512]{1,0:T(8,128)(2,1)} async-done(((bf16[1632,512]{1,0:T(8,128)(2,1)}), bf16[26112,512]{1,0:T(8,128)(2,1)}) %all-gather.16.cloned.1.call-update) | async-done | bytes 26738704 | tf_op jit(solution)/shard_map/all_gather | solution.py:1135
  567.9 2.7 slice.556
  570.6 38.5 %feed_forward.6 = (f32[4,4,144,512]{3,2,1,0:T(8,128)}, bf16[512,2048]{1,0:T(8,128)(2,1)}, bf16[512,2048]{1,0:T(8,128)(2,1)}, bf16[512,32]{1,0:T(8,128)(2,1)}) custom-call(s32[1]{0:T(128)} %bitcast.71.group_ref, bf16[512,2048]{1,0:T(8,128)(2,1)} %copy-done.49, bf16[512,2048]{1,0:T(8,128)(2,1)} %collective-permute-done.1.e_ref, ...), custom_call_target="tpu_custom_call", output_to_operand_aliasing={{0}: (10, {})} | custom-call | flops 21474836480 | bytes 37748736 | tf_op jit(solution)/shard_map/feed_forward/pallas_call | solution.py:619
  611.3 39.5 %feed_forward.7 = (f32[4,4,144,512]{3,2,1,0:T(8,128)}, f32[512,2048]{1,0:T(8,128)}, bf16[512,2048]{1,0:T(8,128)(2,1)}, bf16[512,32]{1,0:T(8,128)(2,1)}) custom-call(s32[1]{0:T(128)} %bitcast.67.group_ref, bf16[512,2048]{1,0:T(8,128)(2,1)} %get-tuple-element.135.h_ref, bf16[512,2048]{1,0:T(8,128)(2,1)} %bitcast.332, ...), custom_call_target="tpu_custom_call", output_to_operand_aliasing={{0}: (10, {})} | custom-call | flops 21474836480 | bytes 37748736 | tf_op jit(solution)/shard_map/feed_forward/pallas_call | solution.py:619
  650.8 6.4 collective-permute-done.2.other_ref
  658.5 15.2 %project_out_back.1 = (f32[512,2048]{1,0:T(8,128)}, bf16[4,32,512]{2,1,0:T(8,128)(2,1)}, bf16[4,32,512]{2,1,0:T(8,128)(2,1)}, bf16[2,4,2,256,128]{4,3,2,1,0:T(8,128)(2,1)}, bf16[2,4,2,256,128]{4,3,2,1,0:T(8,128)(2,1)}) custom-call(f32[512,2048]{1,0:T(8,128)} %get-tuple-element.150.own_ref, bf16[512,2048]{1,0:T(8,128)(2,1)} %copy-done.53, ...), custom_call_target="tpu_custom_call" | custom-call | flops 4294967296 | bytes 27262976 | tf_op jit(solution)/shard_map/project_out_back/pallas_call | solution.py:807
  673.7 4.7 all-to-all-start.6
  678.4 4.3 convert_element_type.178
  682.8 8.4 project_down.7
  691.2 10.3 %project_down.6 = f32[4,512,512]{2,1,0:T(8,128)} custom-call(bf16[32,2048]{1,0:T(8,128)(2,1)S(1)} %get-tuple-element.344.second_ref, bf16[512,2048]{1,0:T(8,128)(2,1)S(1)} %copy-done.8, bf16[512,32]{1,0:T(8,128)(2,1)S(1)} %copy-done.35, bf16[4,4,1632,512]{3,2,1,0:T(8,128)(2,1)} %bitcast.321, f32[4,512,512]{2,1,0:T(8,128)} %project_down.4.refs_0_, ...), custom_call_target="tpu_custom_call" | custom-call | flops 4294967296 | bytes 16777216 | tf_op jit(solution)/shard_map/project_down/pallas_call | solution.py:677
  703.1 2.8 multiply_sine_fusion
  705.9 6.7 all-to-all-start.7
  718.1 63.1 %attend_backward.2 = (bf16[4096,128]{1,0:T(8,128)(2,1)}, f32[4096,128]{1,0:T(8,128)}) custom-call(s32[1,4096]{1,0:T(1,128)S(1)} %bitcast.301, f32[32,4096]{1,0:T(8,128)S(1)} %bitcast.297, f32[32,4096]{1,0:T(8,128)S(1)} %bitcast.295, bf16[4096,256]{1,0:T(8,128)(2,1)} %bitcast.274, bf16[4096,128]{1,0:T(8,128)(2,1)S(1)} %bitcast.290, ...), custom_call_target="tpu_custom_call" | custom-call | flops 10737418240 | bytes 6291456 | tf_op jit(solution)/shard_map/attend_backward/pallas_call | solution.py:245
  782.9 6.0 all-to-all-start.8
  791.8 4.8 fusion.4
  800.0 63.2 %attend_backward.3 = bf16[4096,256]{1,0:T(8,128)(2,1)} custom-call(s32[1,4096]{1,0:T(1,128)S(1)} %bitcast.302, f32[32,4096]{1,0:T(8,128)S(1)} %bitcast.298, f32[32,4096]{1,0:T(8,128)S(1)} %bitcast.296, bf16[4096,128]{1,0:T(8,128)(2,1)S(1)} %bitcast.283, bf16[4096,128]{1,0:T(8,128)(2,1)S(1)} %bitcast.287, bf16[4096,128]{1,0:T(8,128)(2,1)S(1)} %copy-done.20, ...), custom_call_target="tpu_custom_call" | custom-call | flops 10737418240 | bytes 6291456 | tf_op jit(solution)/shard_map/attend_backward/pallas_call | solution.py:245
  866.5 5.0 all-to-all-start.9
  873.6 3.5 copy.233
  887.9 24.8 %all-to-all-done.9 = bf16[16,256,256]{2,1,0:T(8,128)(2,1)} async-done(((bf16[16,256,256]{2,1,0:T(8,128)(2,1)}), bf16[16,256,256]{2,1,0:T(8,128)(2,1)}, u32[]{:S(2)}, u32[]{:S(2)}) %all-to-all-start.9) | async-done | bytes 2097184 | tf_op jit(solution)/shard_map/all_to_all | solution.py:1125
  914.5 5.4 qkv_grad_sums.1
  923.2 11.2 %all-to-all-start.10 = ((bf16[16,52,512]{2,1,0:T(8,128)(2,1)}), bf16[16,52,512]{2,1,0:T(8,128)(2,1)S(1)}, u32[]{:S(2)}, u32[]{:S(2)}) async-start(bf16[16,52,512]{2,1,0:T(8,128)(2,1)} %pad_maximum_fusion.8), calls=%async_computation.11 | async-start | bytes 1835008 | tf_op jit(solution)/shard_map/all_to_all | solution.py:1331
  934.4 15.6 %project_qkv_back.1 = bf16[4,512,512]{2,1,0:T(8,128)(2,1)} custom-call(bf16[512,2048]{1,0:T(8,128)(2,1)} %bitcast.337, f32[512,2048]{1,0:T(8,128)} %get-tuple-element.196.attended_ref, f32[1,2048]{1,0:T(1,128)} %copy-done.39, bf16[96,2048]{1,0:T(8,128)(2,1)} %bitcast.277, bf16[512,96]{1,0:T(8,128)(2,1)} %copy-done.43, ...), custom_call_target="tpu_custom_call" | custom-call | flops 25769803776 | bytes 23068672 | tf_op jit(solution)/shard_map/project_qkv_back/pallas_call | solution.py:495
  959.6 3.5 all-to-all-start.11
  968.4 9.8 collective-permute-done.9
  980.6 3.5 copy.246
  984.8 3.5 all-to-all-start.12
  992.8 3.1 all-to-all-done.12
  (475 shorter events, 150.4 us)
Async XLA Ops:
  7.2 60.5 %copy-start = (bf16[2048,128]{1,0:T(8,128)(2,1)S(1)}, bf16[2048,128]{1,0:T(8,128)(2,1)}, u32[]{:S(2)}) copy-start(bf16[2048,128]{1,0:T(8,128)(2,1)} %param.54) | copy-start | bytes 1572868
  7.2 170.0 %all-gather.12.cloned.1.call-start = ((), (), s32[]{:S(2)}) async-start(), calls=%async_computation.14 | async-start | bytes 22282240 | tf_op jit(solution)/shard_map/all_gather | solution.py:1020
  9.8 13.8 %copy-start.88 = (bf16[512,128]{1,0:T(8,128)(2,1)S(1)}, bf16[512,128]{1,0:T(8,128)(2,1)}, u32[]{:S(2)}) copy-start(bf16[512,128]{1,0:T(8,128)(2,1)} %param.48) | copy-start | bytes 393220
  9.8 13.9 %copy-start.89 = (bf16[128,512]{1,0:T(8,128)(2,1)S(1)}, bf16[128,512]{1,0:T(8,128)(2,1)}, u32[]{:S(2)}) copy-start(bf16[128,512]{1,0:T(8,128)(2,1)} %param.43) | copy-start | bytes 393220
  18.9 49.4 %copy-start.69 = (s32[64]{0:T(128)}, s32[64]{0:T(128)S(1)}, u32[]{:S(2)}) copy-start(s32[64]{0:T(128)S(1)} %and_select_fusion.1) | copy-start | bytes 772
  22.2 46.2 %copy-start.67 = (s32[64]{0:T(128)}, s32[64]{0:T(128)S(1)}, u32[]{:S(2)}) copy-start(s32[64]{0:T(128)S(1)} %fusion.37) | copy-start | bytes 772
  22.2 46.1 %copy-start.71 = (s32[128]{0:T(128)}, s32[128]{0:T(128)S(1)}, u32[]{:S(2)}) copy-start(s32[128]{0:T(128)S(1)} %get-tuple-element.400) | copy-start | bytes 1540
  22.2 46.1 %copy-start.74 = (s32[128]{0:T(128)}, s32[128]{0:T(128)S(1)}, u32[]{:S(2)}) copy-start(s32[128]{0:T(128)S(1)} %get-tuple-element.401) | copy-start | bytes 1540
  23.7 30.9 %copy-start.54 = (bf16[1024,2,512]{2,1,0:T(2,128)(2,1)S(1)}, bf16[1024,2,512]{2,1,0:T(2,128)(2,1)}, u32[]{:S(2)}) copy-start(bf16[1024,2,512]{2,1,0:T(2,128)(2,1)} %param.28) | copy-start | bytes 6291460
  53.9 21.7 %copy-start.52 = (bf16[4,4,33,512]{3,1,2,0:T(4,128)(2,1)}, bf16[4,4,33,512]{3,1,2,0:T(4,128)(2,1)S(1)}, u32[]{:S(2)}) copy-start(bf16[4,4,33,512]{3,1,2,0:T(4,128)(2,1)S(1)} %copy.252) | copy-start | bytes 1622020
  56.5 53.0 %all-to-all-start = ((bf16[4,2,256,512]{3,2,1,0:T(8,128)(2,1)}), bf16[4,2,256,512]{3,2,1,0:T(8,128)(2,1)}, u32[]{:S(2)}, u32[]{:S(2)}) async-start(bf16[4,2,256,512]{3,2,1,0:T(8,128)(2,1)} %copy.209), calls=%async_computation | async-start | bytes 4194304 | tf_op jit(solution)/shard_map/all_to_all | solution.py:866
  61.0 354.8 %all-gather.14.cloned.1.call-start = ((), (), s32[]{:S(2)}) async-start(), calls=%async_computation.16 | async-start | bytes 29245440 | tf_op jit(solution)/shard_map/all_gather | solution.py:1135
  75.4 345.4 %copy-start.4 = (f32[512,32]{1,0:T(8,128)}, f32[512,32]{1,0:T(8,128)S(1)}, u32[]{:S(2)}) copy-start(f32[512,32]{1,0:T(8,128)S(1)} %compare_select_fusion.refs_4_.mask_ref) | copy-start | bytes 196612
  170.5 397.4 %all-gather.16.cloned.1.call-start = ((), (), s32[]{:S(2)}) async-start(), calls=%async_computation.17 | async-start | bytes 28409856 | tf_op jit(solution)/shard_map/all_gather | solution.py:1135
  172.9 23.0 %copy-start.39 = (f32[1,2048]{1,0:T(1,128)}, f32[1,2048]{1,0:T(1,128)S(1)}, u32[]{:S(2)}) copy-start(f32[1,2048]{1,0:T(1,128)S(1)} %get-tuple-element.374.gain_ref) | copy-start | bytes 24580
  172.9 247.9 %copy-start.38 = (f32[1,2048]{1,0:T(1,128)}, f32[1,2048]{1,0:T(1,128)S(1)}, u32[]{:S(2)}) copy-start(f32[1,2048]{1,0:T(1,128)S(1)} %get-tuple-element.373.refs_3_.gain_ref) | copy-start | bytes 24580
  195.9 79.5 %copy-start.41 = (bf16[512,96]{1,0:T(8,128)(2,1)}, bf16[512,96]{1,0:T(8,128)(2,1)S(1)}, u32[]{:S(2)}) copy-start(bf16[512,96]{1,0:T(8,128)(2,1)S(1)} %get-tuple-element.187.low_ref) | copy-start | bytes 294916
  275.3 54.4 %copy-start.11 = (bf16[16,256,256]{2,1,0:T(8,128)(2,1)}, bf16[16,256,256]{2,1,0:T(8,128)(2,1)S(1)}, u32[]{:S(2)}) copy-start(bf16[16,256,256]{2,1,0:T(8,128)(2,1)S(1)} %all_to_all.66) | copy-start | bytes 6291460
  275.4 47.3 %all-to-all-start.4 = ((bf16[16,256,128]{2,1,0:T(8,128)(2,1)}), bf16[16,256,128]{2,1,0:T(8,128)(2,1)S(1)}, u32[]{:S(2)}, u32[]{:S(2)}) async-start(bf16[16,256,128]{2,1,0:T(8,128)(2,1)} %bitcast.289), calls=%async_computation.4 | async-start | bytes 2097152 | tf_op jit(solution)/shard_map/all_to_all | solution.py:1125
  323.6 50.3 %all-to-all-start.3 = ((bf16[16,256,128]{2,1,0:T(8,128)(2,1)}), bf16[16,256,128]{2,1,0:T(8,128)(2,1)S(1)}, u32[]{:S(2)}, u32[]{:S(2)}) async-start(bf16[16,256,128]{2,1,0:T(8,128)(2,1)} %bitcast.288), calls=%async_computation.3 | async-start | bytes 2097152 | tf_op jit(solution)/shard_map/all_to_all | solution.py:1125
  373.9 46.9 %copy-start.2 = (bf16[16,256,128]{2,1,0:T(8,128)(2,1)}, bf16[16,256,128]{2,1,0:T(8,128)(2,1)S(1)}, u32[]{:S(2)}) copy-start(bf16[16,256,128]{2,1,0:T(8,128)(2,1)S(1)} %all-to-all-done.3) | copy-start | bytes 3145732
  373.9 46.9 %all-to-all-start.5 = ((bf16[16,256,128]{2,1,0:T(8,128)(2,1)}), bf16[16,256,128]{2,1,0:T(8,128)(2,1)S(1)}, u32[]{:S(2)}, u32[]{:S(2)}) async-start(bf16[16,256,128]{2,1,0:T(8,128)(2,1)} %bitcast.284), calls=%async_computation.5 | async-start | bytes 2097152 | tf_op jit(solution)/shard_map/all_to_all | solution.py:1125
  382.3 38.5 %copy-start.13 = (bf16[4,8,4,512]{3,1,2,0:T(8,128)(2,1)}, bf16[4,8,4,512]{3,1,2,0:T(8,128)(2,1)S(1)}, u32[]{:S(2)}) copy-start(bf16[4,8,4,512]{3,1,2,0:T(8,128)(2,1)S(1)} %copy.272) | copy-start | bytes 393220
  383.1 102.1 %collective-permute-start.1 = (bf16[512,2048]{1,0:T(8,128)(2,1)}, bf16[512,2048]{1,0:T(8,128)(2,1)}, u32[]{:S(2)}, u32[]{:S(2)}) collective-permute-start(bf16[512,2048]{1,0:T(8,128)(2,1)} %bitcast.330), channel_id=1, source_target_pairs={{0,16},{16,0},{1,17},{17,1},{2,18},{18,2},{3,19},{19,3},{4,20},{20... | collective-permute-start | bytes 6291464 | tf_op jit(solution)/shard_map/ppermute | solution.py:1167
  420.8 14.6 %copy-start.48 = (bf16[4,8,8,512]{3,2,0,1:T(8,128)(2,1)}, bf16[4,8,8,512]{3,2,0,1:T(8,128)(2,1)S(1)}, u32[]{:S(2)}) copy-start(bf16[4,8,8,512]{3,2,0,1:T(8,128)(2,1)S(1)} %copy.263) | copy-start | bytes 786436
  433.8 51.4 %collective-permute-start = (bf16[512,2048]{1,0:T(8,128)(2,1)}, bf16[512,2048]{1,0:T(8,128)(2,1)S(1)}, u32[]{:S(2)}, u32[]{:S(2)}) collective-permute-start(bf16[512,2048]{1,0:T(8,128)(2,1)} %get-tuple-element.135.h_ref), channel_id=1, source_target_pairs={{0,16},{16,0},{1,17},{17,1},{2,18},{18,2},{3,19},{19,3},{4,20},{20... | collective-permute-start | bytes 6291464 | tf_op jit(solution)/shard_map/ppermute | solution.py:1167
  609.1 48.0 %collective-permute-start.2 = (bf16[512,2048]{1,0:T(8,128)(2,1)}, bf16[512,2048]{1,0:T(8,128)(2,1)S(1)}, u32[]{:S(2)}, u32[]{:S(2)}) collective-permute-start(bf16[512,2048]{1,0:T(8,128)(2,1)} %get-tuple-element.151), channel_id=1, source_target_pairs={{0,16},{16,0},{1,17},{17,1},{2,18},{18,2},{3,19},{19,3},{4,20},{20... | collective-permute-start | bytes 6291464 | tf_op jit(solution)/shard_map/ppermute | solution.py:1167
  673.7 27.9 %all-to-all-start.6 = ((bf16[16,256,128]{2,1,0:T(8,128)(2,1)}), bf16[16,256,128]{2,1,0:T(8,128)(2,1)S(1)}, u32[]{:S(2)}, u32[]{:S(2)}) async-start(bf16[16,256,128]{2,1,0:T(8,128)(2,1)} %bitcast.390), calls=%async_computation.6 | async-start | bytes 2097152 | tf_op jit(solution)/shard_map/all_to_all | solution.py:1125
  678.4 102.9 %reduce-scatter.2.cloned.1.call-start = ((), (), s32[]{:S(2)}) async-start(), calls=%async_computation.15 | async-start | bytes 2506752 | tf_op jit(solution)/shard_map/reduce_scatter | solution.py:1240
  701.5 79.7 %collective-permute-start.3 = (bf16[4,512,512]{2,1,0:T(8,128)(2,1)S(1)}, bf16[4,512,512]{2,1,0:T(8,128)(2,1)}, u32[]{:S(2)}, u32[]{:S(2)}) collective-permute-start(bf16[4,512,512]{2,1,0:T(8,128)(2,1)S(1)} %project_down.7), channel_id=1, source_target_pairs={{0,16},{16,0},{1,17},{17,1},{2,18},{18,2},{3,19},{19,3},{4,20},{20... | collective-permute-start | bytes 6291464 | tf_op jit(solution)/shard_map/ppermute | solution.py:1167
  705.9 77.0 %all-to-all-start.7 = ((bf16[16,256,128]{2,1,0:T(8,128)(2,1)}), bf16[16,256,128]{2,1,0:T(8,128)(2,1)S(1)}, u32[]{:S(2)}, u32[]{:S(2)}) async-start(bf16[16,256,128]{2,1,0:T(8,128)(2,1)} %bitcast.389), calls=%async_computation.7 | async-start | bytes 2097152 | tf_op jit(solution)/shard_map/all_to_all | solution.py:1125
  712.5 150.7 %all-gather.20.cloned.1.call-start = ((), (), s32[]{:S(2)}) async-start(), calls=%async_computation.19 | async-start | bytes 1179648 | tf_op jit(solution)/shard_map/all_gather | solution.py:1260
  782.9 82.6 %all-to-all-start.8 = ((bf16[16,256,128]{2,1,0:T(8,128)(2,1)}), bf16[16,256,128]{2,1,0:T(8,128)(2,1)S(1)}, u32[]{:S(2)}, u32[]{:S(2)}) async-start(bf16[16,256,128]{2,1,0:T(8,128)(2,1)} %bitcast.91), calls=%async_computation.9 | async-start | bytes 2097152 | tf_op jit(solution)/shard_map/all_to_all | solution.py:1125
  788.9 75.5 %all-gather.18.cloned.1.call-start = ((), (), s32[]{:S(2)}) async-start(), calls=%async_computation.18 | async-start | bytes 1179648 | tf_op jit(solution)/shard_map/all_gather | solution.py:1259
  796.6 68.9 %collective-permute-start.4 = (bf16[512,512]{1,0:T(8,128)(2,1)}, bf16[512,512]{1,0:T(8,128)(2,1)}, u32[]{:S(2)}, u32[]{:S(2)}) collective-permute-start(bf16[512,512]{1,0:T(8,128)(2,1)} %get-tuple-element.294), channel_id=1, source_target_pairs={{0,4},{4,8},{8,12},{12,0},{1,5},{5,9},{9,13},{13,1},{2,6},{6,10},{... | collective-permute-start | bytes 1572872 | tf_op jit(solution)/shard_map/ppermute | solution.py:878
  797.0 68.5 %collective-permute-start.5 = (bf16[512,512]{1,0:T(8,128)(2,1)}, bf16[512,512]{1,0:T(8,128)(2,1)}, u32[]{:S(2)}, u32[]{:S(2)}) collective-permute-start(bf16[512,512]{1,0:T(8,128)(2,1)} %get-tuple-element.293), channel_id=1, source_target_pairs={{0,8},{4,12},{8,0},{12,4},{1,9},{5,13},{9,1},{13,5},{2,10},{6,14},... | collective-permute-start | bytes 1572872 | tf_op jit(solution)/shard_map/ppermute | solution.py:878
  798.7 66.9 %collective-permute-start.6 = (bf16[512,512]{1,0:T(8,128)(2,1)}, bf16[512,512]{1,0:T(8,128)(2,1)}, u32[]{:S(2)}, u32[]{:S(2)}) collective-permute-start(bf16[512,512]{1,0:T(8,128)(2,1)} %get-tuple-element.292), channel_id=1, source_target_pairs={{0,12},{4,0},{8,4},{12,8},{1,13},{5,1},{9,5},{13,9},{2,14},{6,2},{... | collective-permute-start | bytes 1572872 | tf_op jit(solution)/shard_map/ppermute | solution.py:878
  865.5 48.9 %copy-start.21 = (bf16[16,256,128]{2,1,0:T(8,128)(2,1)}, bf16[16,256,128]{2,1,0:T(8,128)(2,1)S(1)}, u32[]{:S(2)}) copy-start(bf16[16,256,128]{2,1,0:T(8,128)(2,1)S(1)} %all-to-all-done.8) | copy-start | bytes 3145732
  866.5 46.2 %all-to-all-start.9 = ((bf16[16,256,256]{2,1,0:T(8,128)(2,1)}), bf16[16,256,256]{2,1,0:T(8,128)(2,1)}, u32[]{:S(2)}, u32[]{:S(2)}) async-start(bf16[16,256,256]{2,1,0:T(8,128)(2,1)} %bitcast.378), calls=%async_computation.10 | async-start | bytes 4194304 | tf_op jit(solution)/shard_map/all_to_all | solution.py:1125
  887.9 26.5 %copy-start.6 = (bf16[4,96,768]{2,1,0:T(8,128)(2,1)S(1)}, bf16[4,96,768]{2,1,0:T(8,128)(2,1)}, u32[]{:S(2)}) copy-start(bf16[4,96,768]{2,1,0:T(8,128)(2,1)} %pad_maximum_fusion.9.second_ref) | copy-start | bytes 1769476
  887.9 26.5 %copy-start.15 = (f32[512,96]{1,0:T(8,128)S(1)}, f32[512,96]{1,0:T(8,128)}, u32[]{:S(2)}) copy-start(f32[512,96]{1,0:T(8,128)} %copy.222.mask_ref) | copy-start | bytes 589828
  887.9 26.5 %copy-start.40 = (f32[1,2048]{1,0:T(1,128)S(1)}, f32[1,2048]{1,0:T(1,128)}, u32[]{:S(2)}) copy-start(f32[1,2048]{1,0:T(1,128)} %copy-done.39) | copy-start | bytes 24580
  923.2 35.4 %all-to-all-start.10 = ((bf16[16,52,512]{2,1,0:T(8,128)(2,1)}), bf16[16,52,512]{2,1,0:T(8,128)(2,1)S(1)}, u32[]{:S(2)}, u32[]{:S(2)}) async-start(bf16[16,52,512]{2,1,0:T(8,128)(2,1)} %pad_maximum_fusion.8), calls=%async_computation.11 | async-start | bytes 1835008 | tf_op jit(solution)/shard_map/all_to_all | solution.py:1331
  952.5 14.5 %collective-permute-start.7 = (bf16[512,512]{1,0:T(8,128)(2,1)}, bf16[512,512]{1,0:T(8,128)(2,1)}, u32[]{:S(2)}, u32[]{:S(2)}) collective-permute-start(bf16[512,512]{1,0:T(8,128)(2,1)} %get-tuple-element.303), channel_id=1, source_target_pairs={{0,4},{4,8},{8,12},{12,0},{1,5},{5,9},{9,13},{13,1},{2,6},{6,10},{... | collective-permute-start | bytes 1572872 | tf_op jit(solution)/shard_map/ppermute | solution.py:878
  953.0 15.5 %collective-permute-start.8 = (bf16[512,512]{1,0:T(8,128)(2,1)S(1)}, bf16[512,512]{1,0:T(8,128)(2,1)}, u32[]{:S(2)}, u32[]{:S(2)}) collective-permute-start(bf16[512,512]{1,0:T(8,128)(2,1)S(1)} %get-tuple-element.302), channel_id=1, source_target_pairs={{0,8},{4,12},{8,0},{12,4},{1,9},{5,13},{9,1},{13,5},{2,10},{6,14},... | collective-permute-start | bytes 1572872 | tf_op jit(solution)/shard_map/ppermute | solution.py:878
  954.6 23.7 %collective-permute-start.9 = (bf16[512,512]{1,0:T(8,128)(2,1)S(1)}, bf16[512,512]{1,0:T(8,128)(2,1)}, u32[]{:S(2)}, u32[]{:S(2)}) collective-permute-start(bf16[512,512]{1,0:T(8,128)(2,1)S(1)} %get-tuple-element.301), channel_id=1, source_target_pairs={{0,12},{4,0},{8,4},{12,8},{1,13},{5,1},{9,5},{13,9},{2,14},{6,2},{... | collective-permute-start | bytes 1572872 | tf_op jit(solution)/shard_map/ppermute | solution.py:878
  959.6 24.5 %all-to-all-start.11 = ((f32[8,32,512]{2,1,0:T(8,128)}), f32[8,32,512]{2,1,0:T(8,128)S(1)}, u32[]{:S(2)}, u32[]{:S(2)}) async-start(f32[8,32,512]{2,1,0:T(8,128)} %broadcast_in_dim.21), calls=%async_computation.12 | async-start | bytes 1048576 | tf_op jit(solution)/shard_map/all_to_all | solution.py:1296
  984.8 11.0 %all-to-all-start.12 = ((f32[8,20,512]{2,1,0:T(8,128)}), f32[8,20,512]{2,1,0:T(8,128)S(1)}, u32[]{:S(2)}, u32[]{:S(2)}) async-start(f32[8,20,512]{2,1,0:T(8,128)} %broadcast_in_dim.22), calls=%async_computation.13 | async-start | bytes 786432 | tf_op jit(solution)/shard_map/all_to_all | solution.py:1296
  (82 other events, 420.7 us)
Sparse Core Ops, SparseCore 0:
  12.3 164.8 all-gather.11
  178.8 236.9 all-gather.13
  417.4 150.4 all-gather.15
  701.7 65.9 reduce-scatter.1
  783.0 33.3 all-gather.19
  819.2 40.2 all-gather.17

commit v4 on v3

--- a/solution.py
+++ b/solution.py
@@ -334,12 +334,11 @@
     width = second.shape[2]
     chunk = width // 3
     part = count // seqs
-    ahead = lanes // chunk
     whole = lambda shape: pl.BlockSpec(shape, lambda c: (0,) * len(shape))
     message = lambda wide: (seqs, cols, units // (seqs * cols), part, wide)
     widths = [pair_width + 2 * HEAD_DIM] + [pair_width] * (pairs - 1)
     block = lambda wide: pl.BlockSpec((seqs, 1) + message(wide)[2:], lambda c: (0, c, 0, 0, 0))
-    weights = lambda at: pl.BlockSpec((1, rows, lanes, chunk), lambda c: (c, 0, 0, ahead + at))
+    weights = lambda at: pl.BlockSpec((1, rows, lanes, chunk), lambda c: (c, 0, 0, at))
     return pl.pallas_call(
         functools.partial(qkv_kernel, pairs, kv_heads),
         grid=(cols,),
@@ -369,6 +368,10 @@
     )(tokens, gain, mask, first, second, cosine, sine, weight, weight, weight)
 
 
+def lanes_of_unit(values, at, wide):
+    return pl.BlockSpec((values.shape[0], 1) + values.shape[2:4] + (wide,), lambda c: (0, c, 0, 0, at))
+
+
 def joined_messages(query_refs, kv_ref):
     seqs, _, kv_heads = kv_ref.shape[:3]
     units = query_refs[0].shape[2]
@@ -420,7 +423,6 @@
     rank = mask.shape[1] // 3
     lanes = features // rows
     whole = lambda shape: buffered_once(shape, lambda c: (0,) * len(shape))
-    by_unit = lambda v: pl.BlockSpec((v.shape[0], 1) + v.shape[2:], lambda c: (0, c, 0, 0, 0))
     return pl.pallas_call(
         qkv_sums_kernel,
         grid=(cols,),
@@ -430,9 +432,9 @@
             whole(mask.shape),
             pl.BlockSpec((1,) + second.shape[1:], lambda c: (c, 0, 0)),
             whole(low_qkv.shape),
-            by_unit(kv),
+            lanes_of_unit(*kv),
         ]
-        + [by_unit(q) for q in queries],
+        + [lanes_of_unit(*q) for q in queries],
         out_specs=[
             pl.BlockSpec(mask.shape, lambda c: (0, 0)),
             pl.BlockSpec((rows, 3 * rank, lanes), lambda c: (0, 0, 0)),
@@ -454,7 +456,7 @@
             transcendentals=count,
         ),
         name="qkv_grad_sums",
-    )(tokens, gain, mask, second, low_qkv, kv, *queries)
+    )(tokens, gain, mask, second, low_qkv, kv[0], *[q[0] for q in queries])
 
 
 def qkv_back_kernel(token_ref, attended_ref, gain_ref, first_ref, lowered_ref, kv_ref, *refs):
@@ -483,15 +485,12 @@
             out_ref[r] = out[:, r * lanes : (r + 1) * lanes]
 
 
-def project_qkv_back(tokens, attended_grad, gain, first, lowered, kv, queries, weight):
+def project_qkv_back(tokens, attended_grad, gain, first, lowered, kv, queries, weight, width):
     count, features = tokens.shape
-    cols, rows, lanes, wide = weight.shape
-    width = wide - lanes
+    cols, rows, lanes, _ = weight.shape
     chunk = width // 3
-    ahead = lanes // chunk
     whole = lambda shape: buffered_once(shape, lambda c: (0,) * len(shape))
-    by_unit = lambda v: pl.BlockSpec((v.shape[0], 1) + v.shape[2:], lambda c: (0, c, 0, 0, 0))
-    weights = lambda at: pl.BlockSpec((1, rows, lanes, chunk), lambda c: (c, 0, 0, ahead + at))
+    weights = lambda at: pl.BlockSpec((1, rows, lanes, chunk), lambda c: (c, 0, 0, at))
     return pl.pallas_call(
         qkv_back_kernel,
         grid=(cols,),
@@ -501,9 +500,9 @@
             whole((1, features)),
             whole(first.shape),
             whole(lowered.shape),
-            by_unit(kv),
+            lanes_of_unit(*kv),
         ]
-        + [by_unit(q) for q in queries]
+        + [lanes_of_unit(*q) for q in queries]
         + [weights(0), weights(1), weights(2)],
         out_specs=pl.BlockSpec((rows, count, lanes), lambda c: (0, 0, 0)),
         out_shape=jax.ShapeDtypeStruct((rows, count, lanes), jnp.bfloat16),
@@ -515,7 +514,7 @@
             transcendentals=count,
         ),
         name="project_qkv_back",
-    )(tokens, attended_grad, gain, first, lowered, kv, *queries, weight, weight, weight)
+    )(tokens, attended_grad, gain, first, lowered, kv[0], *[q[0] for q in queries], weight, weight, weight)
 
 
 def mlp_kernel(fresh, goes_on, block, group_ref, h_ref, e_ref, mask_ref, first_ref, second_ref, gate_ref, up_ref, down_ref, mids_ref, *refs):
@@ -525,22 +524,21 @@
     elif not fresh:
         refs = refs[1:]
     sums_ref, grad_out_ref, hidden_ref, low_down_ref = refs[:4]
-    low_ref, low_turned_ref, lowered_ref, lowered_turned_ref, sum_front_ref, sum_down_ref = refs[4:10]
-    grad_ref = refs[10] if len(refs) > 10 else grad_out_ref
+    low_refs, turned_refs, sum_refs = refs[4:7], refs[7:10], refs[10:13]
+    grad_ref = refs[13] if len(refs) > 13 else grad_out_ref
     c = pl.program_id(0)
     rows, lanes = gate_ref.shape[1], gate_ref.shape[3]
     rank = second_ref.shape[0]
 
     @pl.when(c == 0)
     def _():
-        low_now = nt(h_ref[...], first_ref[...]) * mask_ref[...]
-        low_ref[...] = low_now.astype(jnp.bfloat16)
-        low_turned_ref[...] = low_now.T.astype(jnp.bfloat16)
-        lowered_now = nt(e_ref[...], second_ref[...]) * mask_ref[:, :rank]
-        lowered_ref[...] = lowered_now.astype(jnp.bfloat16)
-        lowered_turned_ref[...] = lowered_now.T.astype(jnp.bfloat16)
-        sum_front_ref[...] = jnp.zeros_like(sum_front_ref)
-        sum_down_ref[...] = jnp.zeros_like(sum_down_ref)
+        low_front = nt(h_ref[...], first_ref[...])
+        lows = low_front[:, :rank], low_front[:, rank:], nt(e_ref[...], second_ref[...])
+        for low, low_ref, turned_ref, sum_ref in zip(lows, low_refs, turned_refs, sum_refs):
+            low = low * mask_ref[...]
+            low_ref[...] = low.astype(jnp.bfloat16)
+            turned_ref[...] = low.T.astype(jnp.bfloat16)
+            sum_ref[...] = jnp.zeros_like(sum_ref)
         if goes_on:
             grad_ref[...] = grad_in_ref[...]
             sums_ref[...] = sums_in_ref[...]
@@ -549,10 +547,10 @@
             sums_ref[...] = jnp.zeros_like(sums_ref)
 
     h = h_ref[...]
-    gate_second, up_second, down_first = mids_ref[0, 0, 0], mids_ref[0, 0, 1], mids_ref[0, 0, 2, :rank]
-    gate = nn(h, gate_ref[0].reshape(rows * lanes, lanes)) + nn(low_ref[...], gate_second)
-    up = nn(h, up_ref[0].reshape(rows * lanes, lanes)) + nn(low_ref[...], up_second)
-    upstream = nn(lowered_ref[...], down_first)
+    gate_second, up_second, down_first = mids_ref[0, 0, 0], mids_ref[0, 0, 1], mids_ref[0, 0, 2]
+    gate = nn(h, gate_ref[0].reshape(rows * lanes, lanes)) + nn(low_refs[0][...], gate_second)
+    up = nn(h, up_ref[0].reshape(rows * lanes, lanes)) + nn(low_refs[1][...], up_second)
+    upstream = nn(low_refs[2][...], down_first)
     for r in range(rows):
         upstream += nt(e_ref[:, r * lanes : (r + 1) * lanes], down_ref[0, r])
     sigmoid = 1.0 / (1.0 + jnp.exp(-gate))
@@ -564,12 +562,10 @@
         at = slice(r * lanes, (r + 1) * lanes)
         grad_ref[:, at] += nt(gate_grad, gate_ref[0, r]) + nt(up_grad, up_ref[0, r])
     hidden_ref[...] = hidden
-    sum_front_ref[...] += nt(gate_grad, gate_second) + nt(up_grad, up_second)
-    sum_down_ref[...] += nt(hidden, down_first)
-    col_sum = jnp.concatenate(
-        [nn(low_turned_ref[:rank], gate_grad), nn(low_turned_ref[rank:], up_grad), nn(lowered_turned_ref[...], hidden)],
-        axis=0,
-    )
+    outs = gate_grad, up_grad, hidden
+    for out, sum_ref, middle in zip(outs, sum_refs, (gate_second, up_second, down_first)):
+        sum_ref[...] += nt(out, middle)
+    col_sum = jnp.concatenate([nn(turned_ref[...], out) for turned_ref, out in zip(turned_refs, outs)], axis=0)
     row_share, col_share = 3 * rank // sums_ref.shape[1], 3 * rank // rows
     begin = share_height(row_share) + block * share_height(col_share)
     for r in range(rows):
@@ -577,15 +573,16 @@
 
     @pl.when(c == pl.num_programs(0) - 1)
     def _():
-        front_now = sum_front_ref[...] * mask_ref[...]
-        grad_out_ref[...] = (grad_ref[...] + nn(front_now.astype(jnp.bfloat16), first_ref[...])).astype(grad_out_ref.dtype)
-        down_now = sum_down_ref[...] * mask_ref[:, :rank]
+        gate_now, up_now, down_now = (sum_ref[...] * mask_ref[...] for sum_ref in sum_refs)
+        front_now = jnp.concatenate([gate_now, up_now], axis=1)
+        total = grad_ref[...] + nn(front_now.astype(jnp.bfloat16), first_ref[...])
+        grad_out_ref[...] = total.astype(grad_out_ref.dtype)
         low_down_ref[...] = down_now.astype(jnp.bfloat16)
-        front_sum = nn(front_now.T.astype(jnp.bfloat16), h_ref[...])
-        down_sum = nn(down_now.T.astype(jnp.bfloat16), e_ref[...])
+        row_sum = jnp.concatenate(
+            [nn(v.T.astype(jnp.bfloat16), w[...]) for v, w in ((front_now, h_ref), (down_now, e_ref))], axis=0
+        )
         for r in range(rows):
-            at = slice(r * lanes, (r + 1) * lanes)
-            now = jnp.concatenate([front_sum[:, at], down_sum[:, at]], axis=0)
+            now = row_sum[:, r * lanes : (r + 1) * lanes]
             for to in range(sums_ref.shape[1]):
                 sums_ref[r, to, :row_share] += now[to * row_share : (to + 1) * row_share]
 
@@ -597,7 +594,7 @@
 def feed_forward(group, block, blocks, h, e, mask, first, second, weight, mids, sums, earlier, dtype):
     count, features = h.shape
     cols, rows, _, lanes = weight.shape
-    rank = mids.shape[3] // 2
+    rank = mids.shape[3]
     groups = mids.shape[1]
     goes_on = earlier is not None
     fresh = sums is None
@@ -606,14 +603,9 @@
     height = share_height(3 * rank // cols) + blocks * share_height(3 * rank // rows)
     sums_shape = (rows, cols, height, lanes)
     anywhere = pl.BlockSpec(memory_space=pl.ANY)
-    scratch = [
-        pltpu.VMEM((count, 2 * rank), jnp.bfloat16),
-        pltpu.VMEM((2 * rank, count), jnp.bfloat16),
-        pltpu.VMEM((count, rank), jnp.bfloat16),
-        pltpu.VMEM((rank, count), jnp.bfloat16),
-        pltpu.VMEM((count, 2 * rank), jnp.float32),
-        pltpu.VMEM((count, rank), jnp.float32),
-    ]
+    scratch = [pltpu.VMEM((count, rank), jnp.bfloat16)] * 3
+    scratch += [pltpu.VMEM((rank, count), jnp.bfloat16)] * 3
+    scratch += [pltpu.VMEM((count, rank), jnp.float32)] * 3
     if dtype != jnp.float32:
         scratch += [pltpu.VMEM((count, features), jnp.float32)]
     return pl.pallas_call(
@@ -624,13 +616,13 @@
             in_specs=[
                 whole((count, features)),
                 whole((count, features)),
-                whole((count, 2 * rank)),
+                whole((count, rank)),
                 pl.BlockSpec((2 * rank, features), lambda c, g: (g[0], 0)),
                 pl.BlockSpec((rank, features), lambda c, g: (g[0], 0)),
                 weights(0),
                 weights(1),
                 weights(2),
-                pl.BlockSpec((1, 1, 3, 2 * rank, lanes), lambda c, g: (c, g[0], 0, 0, 0)),
+                pl.BlockSpec((1, 1, 3, rank, lanes), lambda c, g: (c, g[0], 0, 0, 0)),
             ]
             + ([] if fresh else [buffered_once(sums_shape, lambda c, g: (0, 0, g[0], 0)) if goes_on else anywhere])
             + ([whole((count, features))] if goes_on else []),
@@ -696,11 +688,17 @@
     )(second, hidden, low_down, weight, *kept)
 
 
-def out_kernel(pairs, *refs):
+def lanes_of_part(me_ref, step, copies, r, lanes):
+    wide = lanes // copies
+    return pl.ds(pl.multiple_of(r * lanes + (me_ref[0] + copies - step) % copies * wide, wide), wide)
+
+
+def out_kernel(pairs, copies, me_ref, *refs):
     message_refs, refs = refs[:pairs], refs[pairs:]
-    residual_ref, gain_ref, mask_ref, first_ref, second_ref, weight_ref, attended_ref, normed_ref, low_ref, heads_ref = refs
+    residual_ref, gain_ref, mask_ref, first_ref, second_ref = refs[:5]
+    weight_refs, (attended_ref, normed_ref, low_ref, heads_ref) = refs[5 : 5 + copies], refs[5 + copies :]
     r = pl.program_id(0)
-    cols, lanes = weight_ref.shape[0], weight_ref.shape[3]
+    cols, lanes = weight_refs[0].shape[0], weight_refs[0].shape[2]
 
     @pl.when(r == 0)
     def _():
@@ -712,42 +710,39 @@
                     heads_ref[s * part : (s + 1) * part, begin : begin + width] = message_refs[p][s, u // units, u % units]
         low_ref[...] = (nt(heads_ref[...], first_ref[...]) * mask_ref[...]).astype(jnp.bfloat16)
 
-    at = pl.ds(pl.multiple_of(r * lanes, lanes), lanes)
-    attended_ref[:, at] = (
-        residual_ref[...].astype(jnp.float32)
-        + nn(heads_ref[...], weight_ref[:, 0].reshape(cols * lanes, lanes))
-        + nn(low_ref[...], second_ref[0])
-    )
+    for step, weight_ref in enumerate(weight_refs):
+        at = lanes_of_part(me_ref, step, copies, r, lanes)
+        attended_ref[:, at] = (
+            residual_ref[:, at].astype(jnp.float32)
+            + nn(heads_ref[...], weight_ref[:, 0].reshape(cols * lanes, lanes // copies))
+            + nn(low_ref[...], second_ref[:, at])
+        )
 
     @pl.when(r == pl.num_programs(0) - 1)
     def _():
         normed_ref[...] = normalized(attended_ref[...], gain_ref[...])[1]
 
 
-def project_out(messages, residual, gain, mask, first, second, weight):
+def project_out(me, messages, residual, gain, mask, first, second, weights):
     count, features = residual.shape
-    cols, rows, lanes, _ = weight.shape
+    cols, rows, lanes, _ = weights[0][0].shape
+    copies = len(weights)
     rank = mask.shape[1]
-    whole = lambda shape: pl.BlockSpec(shape, lambda r: (0,) * len(shape))
+    whole = lambda shape: buffered_once(shape, lambda r, m: (0,) * len(shape))
+    part = lambda at: pl.BlockSpec((cols, 1, lanes, lanes // copies), lambda r, m: (0, r, 0, at))
+    outs = [(count, features), (count, features), (count, rank)]
     return pl.pallas_call(
-        functools.partial(out_kernel, len(messages)),
-        grid=(rows,),
-        in_specs=[buffered_once(m.shape, lambda r: (0,) * 5) for m in messages]
-        + [
-            pl.BlockSpec((count, lanes), lambda r: (0, r)),
-            whole((1, features)),
-            whole((count, rank)),
-            whole(first.shape),
-            pl.BlockSpec((1, rank, lanes), lambda r: (r, 0, 0)),
-            pl.BlockSpec((cols, 1, lanes, lanes), lambda r: (0, r, 0, 0)),
-        ],
-        out_specs=[whole((count, features)), whole((count, features)), whole((count, rank))],
-        out_shape=[
-            jax.ShapeDtypeStruct((count, features), jnp.float32),
-            jax.ShapeDtypeStruct((count, features), jnp.bfloat16),
-            jax.ShapeDtypeStruct((count, rank), jnp.bfloat16),
-        ],
-        scratch_shapes=[pltpu.VMEM((count, cols * lanes), jnp.bfloat16)],
+        functools.partial(out_kernel, len(messages), copies),
+        grid_spec=pltpu.PrefetchScalarGridSpec(
+            num_scalar_prefetch=1,
+            grid=(rows,),
+            in_specs=[whole(m.shape) for m in messages]
+            + [whole((count, features)), whole((1, features)), whole((count, rank)), whole(first.shape), whole(second.shape)]
+            + [part(at) for _, at in weights],
+            out_specs=[pl.BlockSpec(shape, lambda r, m: (0, 0)) for shape in outs],
+            scratch_shapes=[pltpu.VMEM((count, cols * lanes), jnp.bfloat16)],
+        ),
+        out_shape=[jax.ShapeDtypeStruct(s, t) for s, t in zip(outs, (jnp.float32, jnp.bfloat16, jnp.bfloat16))],
         compiler_params=pltpu.CompilerParams(vmem_limit_bytes=48 * 2**20),
         cost_estimate=pl.CostEstimate(
             flops=2 * count * features * cols * lanes,
@@ -755,18 +750,19 @@
             transcendentals=count,
         ),
         name="project_out",
-    )(*messages, residual, gain, mask, first, second, weight)
+    )(me, *messages, residual, gain, mask, first, second, *[w for w, _ in weights])
 
 
 def out_back_kernel(
-    pairs, pair_width, own_ref, other_ref, upstream_ref, attended_ref, gain_ref, mask_ref, first_ref, second_ref, low_ref, weight_ref, *refs
+    pairs, copies, pair_width, me_ref, own_ref, other_ref, upstream_ref, attended_ref, gain_ref, mask_ref, first_ref, second_ref, low_ref, *refs
 ):
+    weight_refs, refs = refs[:copies], refs[copies:]
     heads_refs, refs = refs[:pairs], refs[pairs:]
     attended_grad_ref, rows_ref, cols_ref, *refs = refs
     message_refs = refs[:pairs]
     e_ref, lowered_ref, lowered_turned_ref = refs[pairs:]
     c = pl.program_id(0)
-    rows, lanes = weight_ref.shape[1], weight_ref.shape[3]
+    rows, lanes = weight_refs[0].shape[1:3]
     seqs, _, units, part, _ = message_refs[0].shape
 
     @pl.when(c == 0)
@@ -787,7 +783,8 @@
 
     grad = nn(lowered_ref[...], first_ref[...])
     for r in range(rows):
-        grad += nt(e_ref[:, r * lanes : (r + 1) * lanes], weight_ref[0, r])
+        for step, weight_ref in enumerate(weight_refs):
+            grad += nt(e_ref[:, lanes_of_part(me_ref, step, copies, r, lanes)], weight_ref[0, r])
     grad = grad.astype(jnp.bfloat16)
     for s in range(seqs):
         for u in range(units):
@@ -798,42 +795,50 @@
     cols_ref[0] = nn(lowered_turned_ref[...], jnp.concatenate(heads, axis=1)).astype(cols_ref.dtype)
 
 
-def project_out_back(own, other, upstream, attended, gain, mask, first, second, heads, low_out, weight, seqs, units, pairs, pair_width):
+def project_out_back(me, own, other, upstream, attended, gain, mask, first, second, heads, low_out, weights, seqs, units, pair_width):
     count, features = attended.shape
-    cols, rows, lanes, _ = weight.shape
+    cols, rows, lanes, _ = weights[0][0].shape
+    copies, pairs = len(weights), len(heads)
     rank = mask.shape[1]
-    whole = lambda shape: buffered_once(shape, lambda c: (0,) * len(shape))
+    whole = lambda shape: buffered_once(shape, lambda c, m: (0,) * len(shape))
     message = (seqs, cols, units // (seqs * cols), count // seqs, pair_width)
+    by_unit = pl.BlockSpec((seqs, 1) + message[2:], lambda c, m: (0, c, 0, 0, 0))
     return pl.pallas_call(
-        functools.partial(out_back_kernel, pairs, pair_width),
-        grid=(cols,),
-        in_specs=[whole((count, features))] * 4
-        + [
-            whole((1, features)),
-            whole((count, rank)),
-            pl.BlockSpec((rank, lanes), lambda c: (0, c)),
-            whole((rank, features)),
-            whole((count, rank)),
-            pl.BlockSpec((1, rows, lanes, lanes), lambda c: (c, 0, 0, 0)),
-        ]
-        + [pl.BlockSpec((seqs, 1) + message[2:], lambda c: (0, c, 0, 0, 0))] * pairs,
-        out_specs=[
-            pl.BlockSpec((count, features), lambda c: (0, 0)),
-            pl.BlockSpec((rows, rank, lanes), lambda c: (0, 0, 0)),
-            pl.BlockSpec((1, rank, lanes), lambda c: (c, 0, 0)),
-        ]
-        + [pl.BlockSpec((seqs, 1) + message[2:], lambda c: (0, c, 0, 0, 0))] * pairs,
+        functools.partial(out_back_kernel, pairs, copies, pair_width),
+        grid_spec=pltpu.PrefetchScalarGridSpec(
+            num_scalar_prefetch=1,
+            grid=(cols,),
+            in_specs=[whole((count, features))] * 4
+            + [
+                whole((1, features)),
+                whole((count, rank)),
+                pl.BlockSpec((rank, lanes), lambda c, m: (0, c)),
+                whole((rank, features)),
+                whole((count, rank)),
+            ]
+            + [
+                pl.BlockSpec((1, rows, lanes, lanes // copies), functools.partial(lambda at, c, m: (c, 0, 0, at), at))
+                for _, at in weights
+            ]
+            + [by_unit] * pairs,
+            out_specs=[
+                pl.BlockSpec((count, features), lambda c, m: (0, 0)),
+                pl.BlockSpec((rows, rank, lanes), lambda c, m: (0, 0, 0)),
+                pl.BlockSpec((1, rank, lanes), lambda c, m: (c, 0, 0)),
+            ]
+            + [by_unit] * pairs,
+            scratch_shapes=[
+                pltpu.VMEM((count, features), jnp.bfloat16),
+                pltpu.VMEM((count, rank), jnp.bfloat16),
+                pltpu.VMEM((rank, count), jnp.bfloat16),
+            ],
+        ),
         out_shape=[
             jax.ShapeDtypeStruct((count, features), jnp.float32),
             jax.ShapeDtypeStruct((rows, rank, lanes), jnp.bfloat16),
             jax.ShapeDtypeStruct((cols, rank, lanes), jnp.bfloat16),
         ]
         + [jax.ShapeDtypeStruct(message, jnp.bfloat16)] * pairs,
-        scratch_shapes=[
-            pltpu.VMEM((count, features), jnp.bfloat16),
-            pltpu.VMEM((count, rank), jnp.bfloat16),
-            pltpu.VMEM((rank, count), jnp.bfloat16),
-        ],
         compiler_params=pltpu.CompilerParams(vmem_limit_bytes=60 * 2**20),
         cost_estimate=pl.CostEstimate(
             flops=2 * count * features * cols * lanes,
@@ -841,7 +846,7 @@
             transcendentals=count,
         ),
         name="project_out_back",
-    )(own, other, upstream, attended, gain, mask, first, second, low_out, weight, *heads)
+    )(me, own, other, upstream, attended, gain, mask, first, second, low_out, *[w for w, _ in weights], *heads)
 
 
 def dot(left, right):
@@ -988,7 +993,8 @@
 
     def unpack(moved, share, by_row, by_col):
         of_rows = moved[:, :, :share].transpose(1, 0, 2, 3).reshape(rows, -1, lanes)
-        of_cols = moved[:, :, share:].reshape(cols, -1, lanes)
+        count = -(-sum(v.size for v in by_col) // (lanes * rows))
+        of_cols = moved[:, :, share : share + count].reshape(cols, -1, lanes)
         outs = []
         for group, source in zip((by_row, by_col), (of_rows, of_cols)):
             at, out = 0, []
@@ -1010,6 +1016,7 @@
         return jnp.concatenate(parts, axis=1)
 
     half = me * width_ff
+    width_qkv = width_q + 2 * width_kv
     gate_half = lax.dynamic_slice_in_dim(gate_weight, half, width_ff, 1)
     up_half = lax.dynamic_slice_in_dim(up_weight, half, width_ff, 1)
     down_half = lax.dynamic_slice_in_dim(down_weight, half, width_ff, 0)
@@ -1017,12 +1024,6 @@
     up_second_half = lax.dynamic_slice_in_dim(up_second_factor, half, width_ff, 1)
     down_first_half = lax.dynamic_slice_in_dim(down_first_factor, half, width_ff, 0)
 
-    attn_weight = lax.all_gather(
-        jnp.concatenate([output_weight, by_head(query_weight, key_weight, value_weight)], axis=1),
-        turned_both,
-        axis=0,
-        tiled=True,
-    ).reshape(cols, rows, lanes, -1)
     attn_small = (
         [
             jnp.concatenate([first_of(m, choose_own) for m in (query_first_factor, key_first_factor, value_first_factor)]),
@@ -1074,25 +1075,36 @@
         at = slice(n * lanes, (n + 1) * lanes)
         return jnp.stack(
             [
-                jnp.stack(
-                    [
-                        jnp.pad(of_group(m, g)[:, at], ((rank, 0), (0, 0)) if i == 1 else ((0, rank), (0, 0)))
-                        for i, m in enumerate(hidden_parts)
-                    ]
-                )
+                jnp.stack([of_group(m, g)[:, at] for m in hidden_parts])
                 for g in range(copies)
             ]
         )
 
-    packs = [pack(mlp_small if n == 0 else [], [middle(n)]) for n in range(blocks_ff)]
+    middles = [middle(n) for n in range(blocks_ff)]
+    packed, mlp_share = pack(mlp_small, middles)
+    packed = jnp.pad(packed, ((0, -packed.shape[0] % 16), (0, 0)))
+    part_lanes = lanes // copies
+    attn_weight = lax.all_gather(
+        jnp.concatenate(
+            [
+                by_head(query_weight, key_weight, value_weight),
+                lax.dynamic_slice_in_dim(output_weight, me * part_lanes, part_lanes, 1),
+                jnp.zeros((lanes, 128), jnp.bfloat16),
+            ],
+            axis=1,
+        ),
+        turned_both,
+        axis=0,
+        tiled=True,
+    ).reshape(cols, rows, lanes, -1)
     mlp_shards = [
         jnp.concatenate(
             [
                 gate_half[:, n * lanes : (n + 1) * lanes],
                 up_half[:, n * lanes : (n + 1) * lanes],
                 down_half[n * lanes : (n + 1) * lanes],
-                packs[n][0],
-            ],
+            ]
+            + ([packed] if n == 0 else []),
             axis=0,
         )
         for n in range(blocks_ff)
@@ -1100,7 +1112,7 @@
 
     row_seq = jnp.arange(seqs * part) // part
     mask = (row_seq[:, None] == jnp.arange(rank)[None, :] // RANK).astype(jnp.float32) * scale
-    mask_twice, mask_thrice = jnp.tile(mask, (1, 2)), jnp.tile(mask, (1, 3))
+    mask_thrice = jnp.tile(mask, (1, 3))
 
     positions = (lax.axis_index("col") * rows + lax.axis_index("row")) * part + jnp.arange(part)
     cosine, sine = rope_tables(jnp.tile(positions, seqs))
@@ -1151,20 +1163,22 @@
         unit_outs.append(out)
         log_sums.append(log_sum)
     heads_out = to_messages([exchange(v[:, :pair_width]) for v in unit_outs])
-    unpacked = [
-        unpack(mlp_weights[n][:, :, 3 * lanes :], packs[n][1], mlp_small if n == 0 else [], [middle(n)])
-        for n in range(blocks_ff)
-    ]
-    front_first, down_second = (joined_rows(v) for v in unpacked[0][0])
-    heads_out, front_first, down_second, unpacked[0][1][0] = ordered(
-        (heads_out, front_first, down_second, unpacked[0][1][0])
-    )
-    attended, normed_mlp, low_out = project_out(
-        heads_out, residual, gains[1:2], mask, out_first, out_second, attn_weight
-    )
+    (front_first, down_second), middles = unpack(
+        mlp_weights[0][:, :, 3 * lanes :], mlp_share, mlp_small, middles
+    )
+    front_first, down_second = joined_rows(front_first), joined_rows(down_second)
+    out_second = joined_rows(out_second)
 
     def swap(values, step):
         return lax.ppermute(values, "dp", [(i, (i + step) % copies) for i in range(copies)])
+
+    out_weight = attn_weight[..., width_qkv : width_qkv + part_lanes]
+    out_weights = [(attn_weight, width_qkv // part_lanes)] + [(swap(out_weight, step), 0) for step in range(1, copies)]
+    this_copy = me.reshape(1)
+    heads_out, front_first, down_second, middles = ordered((heads_out, front_first, down_second, middles))
+    attended, normed_mlp, low_out = project_out(
+        this_copy, heads_out, residual, gains[1:2], mask, out_first, out_second, out_weights
+    )
 
     tokens_of = [(normed_mlp, upstream)]
     for step in range(1, copies):
@@ -1183,11 +1197,11 @@
                 n,
                 blocks_ff,
                 *tokens_of[step],
-                mask_twice,
+                mask,
                 front_first,
                 down_second,
                 mlp_weights[n],
-                unpacked[n][1][0],
+                middles[n],
                 adapter_sums,
                 grads[step],
                 jnp.float32 if not last or step == 0 else jnp.bfloat16,
@@ -1204,6 +1218,7 @@
         grad_other = grad_back if step == 1 else grad_other + grad_back
 
     attended_grad, out_rows, out_cols, *grad_messages = project_out_back(
+        this_copy,
         grad_part,
         grad_other,
         upstream,
@@ -1211,16 +1226,23 @@
         gains[1:2],
         mask,
         out_first,
-        joined_rows(out_second),
+        out_second,
         heads_out,
         low_out,
-        attn_weight,
+        out_weights,
         seqs,
         units,
-        pairs,
         pair_width,
     )
-    shares = low(adapter_sums)
+    out_share, out_row, out_col = adapter_sums.shape[2], rank // cols, rank // rows
+    shares = jnp.concatenate(
+        [
+            low(adapter_sums),
+            out_rows.reshape(rows, cols, out_row, lanes),
+            out_cols.reshape(cols, rows, out_col, lanes).transpose(1, 0, 2, 3),
+        ],
+        axis=2,
+    )
     row_share, col_share = 3 * rank // cols, 3 * rank // rows
     row_height, col_height = share_height(row_share), share_height(col_share)
     grad_messages, hidden = ordered((grad_messages, hidden))
@@ -1249,15 +1271,22 @@
             if p > 0:
                 shares, mixed_backs, kv_grad = ordered((shares, mixed_backs, kv_grad))
             mixed_parts = send_features(mixed_own, *mixed_backs)
-            shares = shares.reshape(copies, -1, lanes)
+            out_shares = shares[out_share:]
+            shares = shares[:out_share].reshape(copies, -1, lanes)
             parts = (
-                shares[:, :row_share].reshape(-1, lanes),
-                shares[:, row_height:].reshape(copies, blocks_ff, col_height, lanes)[:, :, :col_share].reshape(-1, lanes),
+                jnp.concatenate([shares[:, :row_share].reshape(-1, lanes), out_shares[:out_row]], axis=0),
+                jnp.concatenate(
+                    [
+                        shares[:, row_height:].reshape(copies, blocks_ff, col_height, lanes)[:, :, :col_share].reshape(-1, lanes),
+                        out_shares[out_row:],
+                    ],
+                    axis=0,
+                ),
             )
             counts = [v.shape[0] for v in parts]
             parts = [jnp.pad(low(v), ((0, -v.shape[0] % GATHER_ROWS), (0, 0))) for v in parts]
-            row_total = lax.all_gather(parts[0], ("dp", "col"))[..., : counts[0], :]
-            col_total = lax.all_gather(parts[1], ("dp", "row"))[..., : counts[1], :]
+            row_total = lax.all_gather(parts[0], ("dp", "col")).reshape(copies, cols, -1, lanes)
+            col_total = lax.all_gather(parts[1], ("dp", "row")).reshape(copies, rows, -1, lanes)
         query_now, *kv_now = attend_back(
             unit_queries[p],
             unit_grads[p],
@@ -1283,17 +1312,21 @@
             query_now = query_now[:, :pair_width]
         query_moved.append(exchange(query_now))
     mixed_out = join_features(mixed_parts, seqs)
-    kv_moved = query_moved[-1][..., pair_width:].reshape(seqs, cols, kv_heads, kv_copies, part, -1)
-    kv_moved = low(kv_moved.astype(jnp.float32).sum(axis=3)) if kv_copies > 1 else kv_moved[:, :, :, 0]
-    query_moved[-1] = query_moved[-1][..., :pair_width]
-    query_moved = to_messages(query_moved)
+    last_moved = query_moved[-1].reshape(seqs, cols, -1, part, pair_width + 2 * HEAD_DIM)
+    if kv_copies > 1 or pair_pad:
+        kv_moved = last_moved[..., pair_width:].reshape(seqs, cols, kv_heads, kv_copies, part, -1)
+        kv_moved = (low(kv_moved.astype(jnp.float32).sum(axis=3)), 0, 2 * HEAD_DIM)
+        last_moved = last_moved[..., :pair_width]
+    else:
+        kv_moved = (last_moved, pair_width // (2 * HEAD_DIM), 2 * HEAD_DIM)
+    query_moved = [(v, 0, pair_width) for v in (*to_messages(query_moved[:-1]), last_moved)]
     lowered_qkv, qkv_rows, qkv_cols = qkv_grad_sums(
         residual, gains[0:1], mask_thrice, qkv_second, low_qkv, kv_moved, query_moved, rows
     )
 
     def everywhere(values, axes, count):
-        copied = jnp.broadcast_to(values[None], (count,) + values.shape)
-        return lax.all_to_all(copied, axes, 0, 0, tiled=True).reshape(copies, -1, lanes)
+        copied = jnp.broadcast_to(low(values)[None], (count,) + values.shape)
+        return lax.all_to_all(copied, axes, 0, 0, tiled=True).astype(jnp.float32).reshape(copies, -1, lanes)
 
     def wide_second(values):
         return lax.dot_general(
@@ -1305,11 +1338,15 @@
             values, choose_wide, (((0,), (1,)), ((), ())), precision=lax.Precision.HIGHEST, preferred_element_type=jnp.float32
         )
 
-    row_total = row_total.astype(jnp.float32).reshape(copies, cols, copies, row_share, lanes).sum(axis=0)
+    out_rows = row_total[:, :, counts[0] - out_row : counts[0]].astype(jnp.float32).reshape(-1, lanes)
+    out_cols = col_total[:, :, counts[1] - out_col : counts[1]].astype(jnp.float32).reshape(-1, lanes)
+    row_total = row_total[:, :, : counts[0] - out_row].astype(jnp.float32)
+    row_total = row_total.reshape(copies, cols, copies, row_share, lanes).sum(axis=0)
     row_total = row_total.transpose(1, 0, 2, 3).reshape(copies, 3, rank, lanes)
     gate_first_gradient, up_first_gradient = (wide_first(row_total[:, i].reshape(-1, lanes)) for i in range(2))
     down_second_gradient = wide_second(row_total[:, 2].reshape(-1, lanes))
-    col_total = col_total.astype(jnp.float32).reshape(copies, rows, copies, blocks_ff, col_share, lanes)
+    col_total = col_total[:, :, : counts[1] - out_col].astype(jnp.float32)
+    col_total = col_total.reshape(copies, rows, copies, blocks_ff, col_share, lanes)
     col_total = col_total.transpose(0, 2, 3, 1, 4, 5).reshape(copies, copies, blocks_ff, 3, rank, lanes)
     pieces = [
         [col_total[x, :, n, i].reshape(-1, lanes) for x in range(copies) for n in range(blocks_ff)] for i in range(3)
@@ -1319,28 +1356,27 @@
     )
     down_first_gradient = jnp.concatenate([wide_first(v) for v in pieces[2]], axis=0)
 
-    row_cut = jnp.concatenate([qkv_rows, out_rows], axis=1).reshape(rows, cols, -1, lanes)
-    col_cut = jnp.concatenate([qkv_cols.reshape(cols, -1, lanes), out_cols], axis=1)
-    col_cut = col_cut.reshape(cols, rows, -1, lanes).transpose(1, 0, 2, 3)
+    row_cut = qkv_rows.reshape(rows, cols, -1, lanes)
+    col_cut = qkv_cols.reshape(cols, rows, -1, lanes).transpose(1, 0, 2, 3)
     cut = row_cut.shape[2]
     attn_shares = jnp.concatenate([row_cut, col_cut], axis=2).reshape(units, -1, lanes)
     attn_shares, lowered_qkv = ordered((attn_shares, lowered_qkv))
     token_grad = project_qkv_back(
-        residual, attended_grad, gains[0:1], qkv_first, lowered_qkv, kv_moved, query_moved, attn_weight
+        residual, attended_grad, gains[0:1], qkv_first, lowered_qkv, kv_moved, query_moved, attn_weight, width_qkv
     )
     attn_sums = jnp.sum(lax.all_to_all(attn_shares, both, 0, 0, tiled=True).astype(jnp.float32), axis=0)
     token_parts = send_features(token_grad)
     attn_rows, token_parts[0] = ordered((attn_sums[:cut], token_parts[0]))
     attn_rows = everywhere(attn_rows, ("dp", "col"), copies * cols)
     attn_cols, attn_rows = ordered((attn_sums[cut:], attn_rows))
-    attn_rows = attn_rows.reshape(copies, 4, rank, lanes)
+    attn_rows = attn_rows.reshape(copies, 3, rank, lanes)
     attn_cols = everywhere(attn_cols, ("dp", "row"), copies * rows)
     query_first_gradient, key_first_gradient, value_first_gradient = (
         wide_first(attn_rows[:, i].reshape(-1, lanes)) for i in range(3)
     )
-    output_second_gradient = wide_second(attn_rows[:, 3].reshape(-1, lanes))
-    output_first_gradient = wide_first(attn_cols[:, -rank:].reshape(-1, lanes))
-    qkv_second_gradient = wide_second(attn_cols[:, :-rank].reshape(copies * rank, -1)).reshape(
+    output_second_gradient = wide_second(out_rows)
+    output_first_gradient = wide_first(out_cols)
+    qkv_second_gradient = wide_second(attn_cols.reshape(copies * rank, -1)).reshape(
         adapter_cols, kv_heads, -1
     )
     query_second_gradient = qkv_second_gradient[..., :head_q].reshape(adapter_cols, -1)

time: 1010 us -> 990 us (0.980)
  waiting for transfers between devices: 128 us -> 104 us
    all_gather x2, waiting for transfers between devices: 63.3 us -> 34.4 us  [local(): lax.all_gather(v, turned_both).reshape(cols, rows, -1, lanes)]
    all_to_all x7, waiting for transfers between devices: 24.8 us -> 35.2 us  [exchange(): lax.all_to_all(values.reshape(units, part, -1), turned_both, 0, 0, tiled=...]
    unnamed x236 -> x235, local copies, waits for them, and re-layouts: 40.4 us -> 44.3 us
  transfers between devices with their start and end apart: 27 -> 28, of which waited for: 11 -> 11; matrix products, arithmetic and copies ran while one was open for 11% -> 12% of each run, Pallas kernels for 40% -> 41%
where the time goes in v4:
time: 990 us; the launch traced here: 984 us
  Pallas kernels  465 us (47%)
  blocking collectives  162 us (16%)
  local copies, waits for them, and re-layouts  111 us (11%)
  waiting for transfers between devices  104 us (11%)
  starting transfers between devices  75.8 us (8%)
  other arithmetic  31.2 us (3%)
  between operations  17.9 us (2%)
  matrix products  17.6 us (2%)
    pallas_call x4, Pallas kernels, feed_forward(): pl.pallas_call(functools.partial(mlp_kernel, fresh, goes_on, block), grid...  153 us
    pallas_call x2, Pallas kernels, attend_back(): pl.pallas_call(functools.partial(bwd_kernel, heads, factor, last), grid=(...  126 us
    pallas_call x2, Pallas kernels, attend(): pl.pallas_call(functools.partial(fwd_kernel, heads, factor), grid=(length...  82.8 us
    all_to_all x1, blocking collectives, exchange(): lax.all_to_all(values.reshape(units, part, -1), turned_both, 0, 0, tiled=...  77.2 us
    all_to_all x1, blocking collectives, to_tokens(): moved = lax.all_to_all(cut, 'row', 0, 0, tiled=True)  49.7 us
    unnamed x235, local copies, waits for them, and re-layouts  44.3 us
    all_to_all x7, starting transfers between devices, exchange(): lax.all_to_all(values.reshape(units, part, -1), turned_both, 0, 0, tiled=...  37.9 us
    pallas_call x4, Pallas kernels, project_down(): pl.pallas_call(down_kernel, grid=(rows,), in_specs=[pl.BlockSpec((rank, l...  36.6 us
  transfers between devices with their start and end apart: 28, of which 11 were waited for; matrix products, arithmetic and copies ran while one was open for 12% of the time, Pallas kernels for 41%

profile of v4, /device:TPU:0, one launch (start us, length us, event | category | flops | bytes accessed | tf_op | source)
XLA Modules:
  0.0 984.1 jit_solution(15635124265752331567)
XLA Ops:
  9.9 2.5 concatenate.131
  13.9 5.2 all-reduce.5
  19.7 2.6 fusion.45
  24.2 29.6 %all-gather.5 = bf16[16,53,512]{2,1,0:T(8,128)(2,1)S(1)} all-gather(bf16[1,53,512]{2,1,0:T(8,128)(2,1)S(1)} %maximum_bitcast_fusion.4), channel_id=2, replica_groups=mesh['dp'=2,'row'=4,'col'=4] {'col','row'}, dimensions={0}, use_global_device_ids=true | all-gather | bytes 922624 | tf_op jit(solution)/shard_map/all_gather | solution.py:1042
  56.7 4.5 all-to-all-start
  100.3 9.5 all-to-all-done
  109.7 3.2 copy.179
  116.1 49.7 %all_to_all.65 = bf16[4,2,256,512]{3,2,1,0:T(8,128)(2,1)S(1)} all-to-all(bf16[4,2,256,512]{3,2,1,0:T(8,128)(2,1)S(1)} %copy.189), channel_id=1, replica_groups=mesh['dp'=2,'row'=4,'col'=4] {'row'}, dimensions={0} | all-to-all | bytes 4194304 | tf_op jit(solution)/shard_map/all_to_all | solution.py:871
  174.8 16.7 %project_qkv.1 = (bf16[2,4,2,256,256]{4,3,2,1,0:T(8,128)(2,1)}, bf16[2,4,2,256,128]{4,3,2,1,0:T(8,128)(2,1)S(1)}, bf16[512,96]{1,0:T(8,128)(2,1)S(1)}) custom-call(bf16[512,2048]{1,0:T(8,128)(2,1)} %bitcast.270, f32[1,2048]{1,0:T(1,128)S(1)} %get-tuple-element.375.gain_ref, f32[512,96]{1,0:T(8,128)S(1)} %copy-done.16, bf16[96,2048]{1,0:T(8,128)(2,1)S(1)} %bitcast.287, ...), custom_call_target="tpu_custom_call" | custom-call | flops 6442450944 | bytes 16777216 | tf_op jit(solution)/shard_map/project_qkv/pallas_call | solution.py:342
  192.5 77.2 %all_to_all.66 = bf16[16,256,256]{2,1,0:T(8,128)(2,1)S(1)} all-to-all(bf16[16,256,256]{2,1,0:T(8,128)(2,1)} %bitcast.382), channel_id=1, replica_groups=mesh['dp'=2,'row'=4,'col'=4] {'col','row'}, dimensions={0} | all-to-all | bytes 4194304 | tf_op jit(solution)/shard_map/all_to_all | solution.py:1137
  269.8 3.7 all-to-all-start.4
  273.9 4.6 slice.569
  279.9 41.5 %attend_forward.2 = (bf16[4096,128]{1,0:T(8,128)(2,1)S(1)}, f32[8,4096]{1,0:T(8,128)S(1)}) custom-call(s32[1,4096]{1,0:T(1,128)S(1)} %bitcast.307, bf16[4096,256]{1,0:T(8,128)(2,1)S(1)} %bitcast.280, bf16[4096,256]{1,0:T(8,128)(2,1)S(1)} %bitcast.281), custom_call_target="tpu_custom_call" | custom-call | flops 4294967296 | bytes 3670016 | tf_op jit(solution)/shard_map/attend_forward/pallas_call | solution.py:109
  324.1 6.1 all-to-all-start.3
  331.4 41.3 %attend_forward.3 = (bf16[4096,128]{1,0:T(8,128)(2,1)S(1)}, f32[8,4096]{1,0:T(8,128)S(1)}) custom-call(s32[1,4096]{1,0:T(1,128)S(1)} %bitcast.308, bf16[4096,128]{1,0:T(8,128)(2,1)S(1)} %bitcast.292, bf16[4096,256]{1,0:T(8,128)(2,1)S(1)} %bitcast.282), custom_call_target="tpu_custom_call" | custom-call | flops 4294967296 | bytes 3670016 | tf_op jit(solution)/shard_map/attend_forward/pallas_call | solution.py:109
  374.3 6.3 all-to-all-start.5
  383.4 10.4 %all-gather.14.cloned.1.call-done = bf16[26880,512]{1,0:T(8,128)(2,1)} async-done(((bf16[1680,512]{1,0:T(8,128)(2,1)}), bf16[26880,512]{1,0:T(8,128)(2,1)}) %all-gather.14.cloned.1.call-update) | async-done | bytes 27525136 | tf_op jit(solution)/shard_map/all_gather | solution.py:1147
  398.8 11.8 %all-to-all-done.5 = bf16[16,256,128]{2,1,0:T(8,128)(2,1)S(1)} async-done(((bf16[16,256,128]{2,1,0:T(8,128)(2,1)}), bf16[16,256,128]{2,1,0:T(8,128)(2,1)S(1)}, u32[]{:S(2)}, u32[]{:S(2)}) %all-to-all-start.5) | async-done | bytes 1048608 | tf_op jit(solution)/shard_map/all_to_all | solution.py:1137
  410.7 12.6 %project_out.1 = (f32[512,2048]{1,0:T(8,128)}, bf16[512,2048]{1,0:T(8,128)(2,1)}, bf16[512,32]{1,0:T(8,128)(2,1)S(1)}) custom-call(s32[1]{0:T(128)} %bitcast.68.me_ref, bf16[2,4,2,256,128]{4,3,2,1,0:T(8,128)(2,1)S(1)} %bitcast.274, bf16[2,4,2,256,128]{4,3,2,1,0:T(8,128)(2,1)S(1)} %bitcast.276, bf16[512,2048]{1,0:T(8,128)(2,1)} %bitcast.271, ...), custom_call_target="tpu_custom_call" | custom-call | flops 4294967296 | bytes 18874368 | tf_op jit(solution)/shard_map/project_out/pallas_call | solution.py:734
  424.6 37.4 %feed_forward.4 = (f32[4,4,144,512]{3,2,1,0:T(8,128)}, f32[512,2048]{1,0:T(8,128)}, bf16[512,2048]{1,0:T(8,128)(2,1)}, bf16[512,32]{1,0:T(8,128)(2,1)}) custom-call(s32[1]{0:T(128)} %bitcast.69.group_ref, bf16[512,2048]{1,0:T(8,128)(2,1)} %get-tuple-element.136.h_ref, bf16[512,2048]{1,0:T(8,128)(2,1)} %bitcast.339, f32[512,32]{1,0:T(8,128)} %copy-done.3, ...), custom_call_target="tpu_custom_call" | custom-call | flops 21474836480 | bytes 37748736 | tf_op jit(solution)/shard_map/feed_forward/pallas_call | solution.py:611
  464.6 9.0 project_down.4.refs_0_
  477.3 38.0 %feed_forward.5 = (f32[4,4,144,512]{3,2,1,0:T(8,128)}, f32[512,2048]{1,0:T(8,128)}, bf16[512,2048]{1,0:T(8,128)(2,1)}, bf16[512,32]{1,0:T(8,128)(2,1)}) custom-call(s32[1]{0:T(128)} %bitcast.73.group_ref, bf16[512,2048]{1,0:T(8,128)(2,1)} %copy-done.51, bf16[512,2048]{1,0:T(8,128)(2,1)} %collective-permute-done.2.e_ref, ...), custom_call_target="tpu_custom_call", output_to_operand_aliasing={{0}: (10, {})} | custom-call | flops 21474836480 | bytes 37748736 | tf_op jit(solution)/shard_map/feed_forward/pallas_call | solution.py:611
  517.9 8.9 project_down.5.refs_0_
  526.8 24.0 %all-gather.16.cloned.1.call-done = bf16[24576,512]{1,0:T(8,128)(2,1)} async-done(((bf16[1536,512]{1,0:T(8,128)(2,1)}), bf16[24576,512]{1,0:T(8,128)(2,1)}) %all-gather.16.cloned.1.call-update) | async-done | bytes 25165840 | tf_op jit(solution)/shard_map/all_gather | solution.py:1147
  550.8 38.6 %feed_forward.6 = (f32[4,4,144,512]{3,2,1,0:T(8,128)}, bf16[512,2048]{1,0:T(8,128)(2,1)}, bf16[512,2048]{1,0:T(8,128)(2,1)}, bf16[512,32]{1,0:T(8,128)(2,1)}) custom-call(s32[1]{0:T(128)} %bitcast.73.group_ref, bf16[512,2048]{1,0:T(8,128)(2,1)} %copy-done.51, bf16[512,2048]{1,0:T(8,128)(2,1)} %collective-permute-done.2.e_ref, ...), custom_call_target="tpu_custom_call", output_to_operand_aliasing={{0}: (10, {})} | custom-call | flops 21474836480 | bytes 37748736 | tf_op jit(solution)/shard_map/feed_forward/pallas_call | solution.py:611
  590.9 39.5 %feed_forward.7 = (f32[4,4,144,512]{3,2,1,0:T(8,128)}, f32[512,2048]{1,0:T(8,128)}, bf16[512,2048]{1,0:T(8,128)(2,1)}, bf16[512,32]{1,0:T(8,128)(2,1)}) custom-call(s32[1]{0:T(128)} %bitcast.69.group_ref, bf16[512,2048]{1,0:T(8,128)(2,1)} %get-tuple-element.136.h_ref, bf16[512,2048]{1,0:T(8,128)(2,1)} %bitcast.340, ...), custom_call_target="tpu_custom_call", output_to_operand_aliasing={{0}: (10, {})} | custom-call | flops 21474836480 | bytes 37748736 | tf_op jit(solution)/shard_map/feed_forward/pallas_call | solution.py:611
  630.3 7.1 collective-permute-done.3.other_ref
  638.7 16.4 %project_out_back.1 = (f32[512,2048]{1,0:T(8,128)}, bf16[4,32,512]{2,1,0:T(8,128)(2,1)}, bf16[4,32,512]{2,1,0:T(8,128)(2,1)}, bf16[2,4,2,256,128]{4,3,2,1,0:T(8,128)(2,1)}, bf16[2,4,2,256,128]{4,3,2,1,0:T(8,128)(2,1)}) custom-call(s32[1]{0:T(128)} %bitcast.68.me_ref, f32[512,2048]{1,0:T(8,128)} %get-tuple-element.152.own_ref, bf16[512,2048]{1,0:T(8,128)(2,1)} %copy-done.54, ...), custom_call_target="tpu_custom_call" | custom-call | flops 4294967296 | bytes 27262976 | tf_op jit(solution)/shard_map/project_out_back/pallas_call | solution.py:806
  655.1 4.7 all-to-all-start.6
  659.9 2.7 convert_element_type.176
  665.2 8.4 project_down.7
  673.6 10.3 %project_down.6 = f32[4,512,512]{2,1,0:T(8,128)} custom-call(bf16[32,2048]{1,0:T(8,128)(2,1)S(1)} %get-tuple-element.345.second_ref, bf16[512,2048]{1,0:T(8,128)(2,1)S(1)} %copy-done.9, bf16[512,32]{1,0:T(8,128)(2,1)S(1)} %copy-done.37, bf16[4,4,1536,512]{3,2,1,0:T(8,128)(2,1)} %bitcast.328, f32[4,512,512]{2,1,0:T(8,128)} %project_down.4.refs_0_, ...), custom_call_target="tpu_custom_call" | custom-call | flops 4294967296 | bytes 16777216 | tf_op jit(solution)/shard_map/project_down/pallas_call | solution.py:669
  685.5 2.8 multiply_sine_fusion
  688.3 6.0 all-to-all-start.7
  699.9 62.8 %attend_backward.2 = (bf16[4096,128]{1,0:T(8,128)(2,1)S(1)}, f32[4096,128]{1,0:T(8,128)}) custom-call(s32[1,4096]{1,0:T(1,128)S(1)} %bitcast.309, f32[32,4096]{1,0:T(8,128)S(1)} %bitcast.304, f32[32,4096]{1,0:T(8,128)S(1)} %bitcast.302, bf16[4096,256]{1,0:T(8,128)(2,1)} %bitcast.283, bf16[4096,128]{1,0:T(8,128)(2,1)S(1)} %bitcast.301, ...), custom_call_target="tpu_custom_call" | custom-call | flops 10737418240 | bytes 6291456 | tf_op jit(solution)/shard_map/attend_backward/pallas_call | solution.py:245
  766.0 6.0 all-to-all-start.8
  773.4 5.0 fusion.4
  781.8 63.2 %attend_backward.3 = bf16[4096,256]{1,0:T(8,128)(2,1)} custom-call(s32[1,4096]{1,0:T(1,128)S(1)} %bitcast.310, f32[32,4096]{1,0:T(8,128)S(1)} %bitcast.305, f32[32,4096]{1,0:T(8,128)S(1)} %bitcast.303, bf16[4096,128]{1,0:T(8,128)(2,1)S(1)} %bitcast.293, bf16[4096,128]{1,0:T(8,128)(2,1)S(1)} %bitcast.297, bf16[4096,128]{1,0:T(8,128)(2,1)S(1)} %copy-done.22, ...), custom_call_target="tpu_custom_call" | custom-call | flops 10737418240 | bytes 6291456 | tf_op jit(solution)/shard_map/attend_backward/pallas_call | solution.py:245
  850.6 5.0 all-to-all-start.9
  857.7 3.5 copy.196
  873.4 23.4 %all-to-all-done.9 = bf16[16,256,256]{2,1,0:T(8,128)(2,1)} async-done(((bf16[16,256,256]{2,1,0:T(8,128)(2,1)}), bf16[16,256,256]{2,1,0:T(8,128)(2,1)}, u32[]{:S(2)}, u32[]{:S(2)}) %all-to-all-start.9) | async-done | bytes 2097184 | tf_op jit(solution)/shard_map/all_to_all | solution.py:1137
  899.0 4.8 qkv_grad_sums.1
  905.4 11.2 %all-to-all-start.10 = ((bf16[16,36,512]{2,1,0:T(8,128)(2,1)}), bf16[16,36,512]{2,1,0:T(8,128)(2,1)S(1)}, u32[]{:S(2)}, u32[]{:S(2)}) async-start(bf16[16,36,512]{2,1,0:T(8,128)(2,1)} %pad_maximum_fusion.9), calls=%async_computation.11 | async-start | bytes 1310720 | tf_op jit(solution)/shard_map/all_to_all | solution.py:1367
  916.6 15.6 %project_qkv_back.1 = bf16[4,512,512]{2,1,0:T(8,128)(2,1)} custom-call(bf16[512,2048]{1,0:T(8,128)(2,1)} %bitcast.272, f32[512,2048]{1,0:T(8,128)} %get-tuple-element.198.attended_ref, f32[1,2048]{1,0:T(1,128)} %copy-done.41, bf16[96,2048]{1,0:T(8,128)(2,1)} %bitcast.286, bf16[512,96]{1,0:T(8,128)(2,1)} %copy-done.45, ...), custom_call_target="tpu_custom_call" | custom-call | flops 25769803776 | bytes 23068672 | tf_op jit(solution)/shard_map/project_qkv_back/pallas_call | solution.py:494
  940.3 4.9 all-to-all-start.11
  949.4 9.6 collective-permute-done.10
  961.1 3.5 copy.207
  965.3 3.4 all-to-all-start.12
  (461 shorter events, 151.6 us)
Async XLA Ops:
  7.2 61.9 %copy-start = (bf16[128,2048]{1,0:T(8,128)(2,1)S(1)}, bf16[128,2048]{1,0:T(8,128)(2,1)}, u32[]{:S(2)}) copy-start(bf16[128,2048]{1,0:T(8,128)(2,1)} %param.51) | copy-start | bytes 1572868
  7.2 164.6 %all-gather.12.cloned.1.call-start = ((), (), s32[]{:S(2)}) async-start(), calls=%async_computation.14 | async-start | bytes 20054016 | tf_op jit(solution)/shard_map/all_gather | solution.py:1087
  19.1 50.4 %copy-start.69 = (s32[64]{0:T(128)}, s32[64]{0:T(128)S(1)}, u32[]{:S(2)}) copy-start(s32[64]{0:T(128)S(1)} %and_select_fusion.1) | copy-start | bytes 772
  22.3 47.2 %copy-start.67 = (s32[64]{0:T(128)}, s32[64]{0:T(128)S(1)}, u32[]{:S(2)}) copy-start(s32[64]{0:T(128)S(1)} %fusion.45) | copy-start | bytes 772
  22.4 47.2 %copy-start.71 = (s32[128]{0:T(128)}, s32[128]{0:T(128)S(1)}, u32[]{:S(2)}) copy-start(s32[128]{0:T(128)S(1)} %get-tuple-element.401) | copy-start | bytes 1540
  22.4 47.2 %copy-start.74 = (s32[128]{0:T(128)}, s32[128]{0:T(128)S(1)}, u32[]{:S(2)}) copy-start(s32[128]{0:T(128)S(1)} %get-tuple-element.402) | copy-start | bytes 1540
  23.9 30.9 %copy-start.55 = (bf16[1024,2,512]{2,1,0:T(2,128)(2,1)S(1)}, bf16[1024,2,512]{2,1,0:T(2,128)(2,1)}, u32[]{:S(2)}) copy-start(bf16[1024,2,512]{2,1,0:T(2,128)(2,1)} %param.28) | copy-start | bytes 6291460
  54.1 22.7 %copy-start.53 = (bf16[4,4,33,512]{3,0,2,1:T(4,128)(2,1)}, bf16[4,4,33,512]{3,0,2,1:T(4,128)(2,1)S(1)}, u32[]{:S(2)}) copy-start(bf16[4,4,33,512]{3,0,2,1:T(4,128)(2,1)S(1)} %copy.176) | copy-start | bytes 1622020
  56.7 53.0 %all-to-all-start = ((bf16[4,2,256,512]{3,2,1,0:T(8,128)(2,1)}), bf16[4,2,256,512]{3,2,1,0:T(8,128)(2,1)}, u32[]{:S(2)}, u32[]{:S(2)}) async-start(bf16[4,2,256,512]{3,2,1,0:T(8,128)(2,1)} %copy.178), calls=%async_computation | async-start | bytes 4194304 | tf_op jit(solution)/shard_map/all_to_all | solution.py:871
  61.2 332.6 %all-gather.14.cloned.1.call-start = ((), (), s32[]{:S(2)}) async-start(), calls=%async_computation.16 | async-start | bytes 29245440 | tf_op jit(solution)/shard_map/all_gather | solution.py:1147
  75.9 334.8 %copy-start.3 = (f32[512,32]{1,0:T(8,128)}, f32[512,32]{1,0:T(8,128)S(1)}, u32[]{:S(2)}) copy-start(f32[512,32]{1,0:T(8,128)S(1)} %compare_select_fusion.refs_4_.mask_ref) | copy-start | bytes 196612
  169.4 381.3 %all-gather.16.cloned.1.call-start = ((), (), s32[]{:S(2)}) async-start(), calls=%async_computation.17 | async-start | bytes 26738688 | tf_op jit(solution)/shard_map/all_gather | solution.py:1147
  171.8 238.9 %copy-start.40 = (f32[1,2048]{1,0:T(1,128)}, f32[1,2048]{1,0:T(1,128)S(1)}, u32[]{:S(2)}) copy-start(f32[1,2048]{1,0:T(1,128)S(1)} %get-tuple-element.374.refs_3_.gain_ref) | copy-start | bytes 24580
  191.6 78.2 %copy-start.43 = (bf16[512,96]{1,0:T(8,128)(2,1)}, bf16[512,96]{1,0:T(8,128)(2,1)S(1)}, u32[]{:S(2)}) copy-start(bf16[512,96]{1,0:T(8,128)(2,1)S(1)} %get-tuple-element.191.low_ref) | copy-start | bytes 294916
  269.8 60.4 %copy-start.12 = (bf16[16,256,256]{2,1,0:T(8,128)(2,1)}, bf16[16,256,256]{2,1,0:T(8,128)(2,1)S(1)}, u32[]{:S(2)}) copy-start(bf16[16,256,256]{2,1,0:T(8,128)(2,1)S(1)} %all_to_all.66) | copy-start | bytes 6291460
  269.8 53.3 %all-to-all-start.4 = ((bf16[16,256,128]{2,1,0:T(8,128)(2,1)}), bf16[16,256,128]{2,1,0:T(8,128)(2,1)S(1)}, u32[]{:S(2)}, u32[]{:S(2)}) async-start(bf16[16,256,128]{2,1,0:T(8,128)(2,1)} %bitcast.300), calls=%async_computation.4 | async-start | bytes 2097152 | tf_op jit(solution)/shard_map/all_to_all | solution.py:1137
  278.4 132.2 %collective-permute-start = (bf16[4,4,512,256]{3,2,1,0:T(8,128)(2,1)}, bf16[4,4,512,256]{3,2,1,0:T(8,128)(2,1)}, u32[]{:S(2)}, u32[]{:S(2)}) collective-permute-start(bf16[4,4,512,256]{3,2,1,0:T(8,128)(2,1)} %slice.569), channel_id=1, source_target_pairs={{0,16},{16,0},{1,17},{17,1},{2,18},{18,2},{3,19},{19,3},{4,20},{20... | collective-permute-start | bytes 12582920 | tf_op jit(solution)/shard_map/ppermute | solution.py:1173
  324.1 50.3 %all-to-all-start.3 = ((bf16[16,256,128]{2,1,0:T(8,128)(2,1)}), bf16[16,256,128]{2,1,0:T(8,128)(2,1)S(1)}, u32[]{:S(2)}, u32[]{:S(2)}) async-start(bf16[16,256,128]{2,1,0:T(8,128)(2,1)} %bitcast.299), calls=%async_computation.3 | async-start | bytes 2097152 | tf_op jit(solution)/shard_map/all_to_all | solution.py:1137
  374.3 36.4 %copy-start.4 = (bf16[16,256,128]{2,1,0:T(8,128)(2,1)}, bf16[16,256,128]{2,1,0:T(8,128)(2,1)S(1)}, u32[]{:S(2)}) copy-start(bf16[16,256,128]{2,1,0:T(8,128)(2,1)S(1)} %all-to-all-done.3) | copy-start | bytes 3145732
  374.3 36.3 %all-to-all-start.5 = ((bf16[16,256,128]{2,1,0:T(8,128)(2,1)}), bf16[16,256,128]{2,1,0:T(8,128)(2,1)S(1)}, u32[]{:S(2)}, u32[]{:S(2)}) async-start(bf16[16,256,128]{2,1,0:T(8,128)(2,1)} %bitcast.294), calls=%async_computation.5 | async-start | bytes 2097152 | tf_op jit(solution)/shard_map/all_to_all | solution.py:1137
  382.7 28.0 %copy-start.14 = (bf16[4,8,4,512]{3,1,2,0:T(8,128)(2,1)}, bf16[4,8,4,512]{3,1,2,0:T(8,128)(2,1)S(1)}, u32[]{:S(2)}) copy-start(bf16[4,8,4,512]{3,1,2,0:T(8,128)(2,1)S(1)} %copy.231) | copy-start | bytes 393220
  382.8 28.0 %copy-start.15 = (bf16[4,8,4,512]{3,1,2,0:T(8,128)(2,1)}, bf16[4,8,4,512]{3,1,2,0:T(8,128)(2,1)S(1)}, u32[]{:S(2)}) copy-start(bf16[4,8,4,512]{3,1,2,0:T(8,128)(2,1)S(1)} %copy.230) | copy-start | bytes 393220
  382.8 90.9 %collective-permute-start.2 = (bf16[512,2048]{1,0:T(8,128)(2,1)}, bf16[512,2048]{1,0:T(8,128)(2,1)}, u32[]{:S(2)}, u32[]{:S(2)}) collective-permute-start(bf16[512,2048]{1,0:T(8,128)(2,1)} %bitcast.338), channel_id=1, source_target_pairs={{0,16},{16,0},{1,17},{17,1},{2,18},{18,2},{3,19},{19,3},{4,20},{20... | collective-permute-start | bytes 6291464 | tf_op jit(solution)/shard_map/ppermute | solution.py:1173
  397.5 27.1 %copy-start.50 = (bf16[4,8,8,512]{3,2,0,1:T(8,128)(2,1)}, bf16[4,8,8,512]{3,2,0,1:T(8,128)(2,1)S(1)}, u32[]{:S(2)}) copy-start(bf16[4,8,8,512]{3,2,0,1:T(8,128)(2,1)S(1)} %copy.222) | copy-start | bytes 786436
  424.0 52.0 %collective-permute-start.1 = (bf16[512,2048]{1,0:T(8,128)(2,1)}, bf16[512,2048]{1,0:T(8,128)(2,1)S(1)}, u32[]{:S(2)}, u32[]{:S(2)}) collective-permute-start(bf16[512,2048]{1,0:T(8,128)(2,1)} %get-tuple-element.136.h_ref), channel_id=1, source_target_pairs={{0,16},{16,0},{1,17},{17,1},{2,18},{18,2},{3,19},{19,3},{4,20},{20... | collective-permute-start | bytes 6291464 | tf_op jit(solution)/shard_map/ppermute | solution.py:1173
  589.3 48.1 %collective-permute-start.3 = (bf16[512,2048]{1,0:T(8,128)(2,1)}, bf16[512,2048]{1,0:T(8,128)(2,1)S(1)}, u32[]{:S(2)}, u32[]{:S(2)}) collective-permute-start(bf16[512,2048]{1,0:T(8,128)(2,1)} %get-tuple-element.153), channel_id=1, source_target_pairs={{0,16},{16,0},{1,17},{17,1},{2,18},{18,2},{3,19},{19,3},{4,20},{20... | collective-permute-start | bytes 6291464 | tf_op jit(solution)/shard_map/ppermute | solution.py:1173
  655.1 28.8 %all-to-all-start.6 = ((bf16[16,256,128]{2,1,0:T(8,128)(2,1)}), bf16[16,256,128]{2,1,0:T(8,128)(2,1)S(1)}, u32[]{:S(2)}, u32[]{:S(2)}) async-start(bf16[16,256,128]{2,1,0:T(8,128)(2,1)} %bitcast.392), calls=%async_computation.6 | async-start | bytes 2097152 | tf_op jit(solution)/shard_map/all_to_all | solution.py:1137
  659.8 103.8 %reduce-scatter.2.cloned.1.call-start = ((), (), s32[]{:S(2)}) async-start(), calls=%async_computation.15 | async-start | bytes 2785280 | tf_op jit(solution)/shard_map/reduce_scatter | solution.py:1262
  683.9 79.8 %collective-permute-start.4 = (bf16[4,512,512]{2,1,0:T(8,128)(2,1)S(1)}, bf16[4,512,512]{2,1,0:T(8,128)(2,1)}, u32[]{:S(2)}, u32[]{:S(2)}) collective-permute-start(bf16[4,512,512]{2,1,0:T(8,128)(2,1)S(1)} %project_down.7), channel_id=1, source_target_pairs={{0,16},{16,0},{1,17},{17,1},{2,18},{18,2},{3,19},{19,3},{4,20},{20... | collective-permute-start | bytes 6291464 | tf_op jit(solution)/shard_map/ppermute | solution.py:1173
  688.3 77.7 %all-to-all-start.7 = ((bf16[16,256,128]{2,1,0:T(8,128)(2,1)}), bf16[16,256,128]{2,1,0:T(8,128)(2,1)S(1)}, u32[]{:S(2)}, u32[]{:S(2)}) async-start(bf16[16,256,128]{2,1,0:T(8,128)(2,1)} %bitcast.391), calls=%async_computation.7 | async-start | bytes 2097152 | tf_op jit(solution)/shard_map/all_to_all | solution.py:1137
  694.3 150.7 %all-gather.20.cloned.1.call-start = ((), (), s32[]{:S(2)}) async-start(), calls=%async_computation.19 | async-start | bytes 1179648 | tf_op jit(solution)/shard_map/all_gather | solution.py:1289
  766.0 78.9 %all-to-all-start.8 = ((bf16[16,256,128]{2,1,0:T(8,128)(2,1)}), bf16[16,256,128]{2,1,0:T(8,128)(2,1)S(1)}, u32[]{:S(2)}, u32[]{:S(2)}) async-start(bf16[16,256,128]{2,1,0:T(8,128)(2,1)} %bitcast.298), calls=%async_computation.9 | async-start | bytes 2097152 | tf_op jit(solution)/shard_map/all_to_all | solution.py:1137
  772.1 72.9 %all-gather.18.cloned.1.call-start = ((), (), s32[]{:S(2)}) async-start(), calls=%async_computation.18 | async-start | bytes 1179648 | tf_op jit(solution)/shard_map/all_gather | solution.py:1288
  778.3 66.6 %collective-permute-start.5 = (bf16[512,512]{1,0:T(8,128)(2,1)}, bf16[512,512]{1,0:T(8,128)(2,1)}, u32[]{:S(2)}, u32[]{:S(2)}) collective-permute-start(bf16[512,512]{1,0:T(8,128)(2,1)} %get-tuple-element.296), channel_id=1, source_target_pairs={{0,4},{4,8},{8,12},{12,0},{1,5},{5,9},{9,13},{13,1},{2,6},{6,10},{... | collective-permute-start | bytes 1572872 | tf_op jit(solution)/shard_map/ppermute | solution.py:883
  778.7 66.2 %collective-permute-start.6 = (bf16[512,512]{1,0:T(8,128)(2,1)}, bf16[512,512]{1,0:T(8,128)(2,1)}, u32[]{:S(2)}, u32[]{:S(2)}) collective-permute-start(bf16[512,512]{1,0:T(8,128)(2,1)} %get-tuple-element.295), channel_id=1, source_target_pairs={{0,8},{4,12},{8,0},{12,4},{1,9},{5,13},{9,1},{13,5},{2,10},{6,14},... | collective-permute-start | bytes 1572872 | tf_op jit(solution)/shard_map/ppermute | solution.py:883
  780.4 64.5 %collective-permute-start.7 = (bf16[512,512]{1,0:T(8,128)(2,1)}, bf16[512,512]{1,0:T(8,128)(2,1)}, u32[]{:S(2)}, u32[]{:S(2)}) collective-permute-start(bf16[512,512]{1,0:T(8,128)(2,1)} %get-tuple-element.294), channel_id=1, source_target_pairs={{0,12},{4,0},{8,4},{12,8},{1,13},{5,1},{9,5},{13,9},{2,14},{6,2},{... | collective-permute-start | bytes 1572872 | tf_op jit(solution)/shard_map/ppermute | solution.py:883
  850.6 46.2 %all-to-all-start.9 = ((bf16[16,256,256]{2,1,0:T(8,128)(2,1)}), bf16[16,256,256]{2,1,0:T(8,128)(2,1)}, u32[]{:S(2)}, u32[]{:S(2)}) async-start(bf16[16,256,256]{2,1,0:T(8,128)(2,1)} %bitcast.102), calls=%async_computation.10 | async-start | bytes 4194304 | tf_op jit(solution)/shard_map/all_to_all | solution.py:1137
  871.3 25.5 %copy-start.2 = (bf16[64,8,4,512]{3,1,2,0:T(8,128)(2,1)S(1)}, bf16[64,8,4,512]{3,1,2,0:T(8,128)(2,1)}, u32[]{:S(2)}) copy-start(bf16[64,8,4,512]{3,1,2,0:T(8,128)(2,1)} %copy.224) | copy-start | bytes 6291460
  871.3 25.5 %copy-start.7 = (bf16[4,96,768]{2,1,0:T(8,128)(2,1)S(1)}, bf16[4,96,768]{2,1,0:T(8,128)(2,1)}, u32[]{:S(2)}) copy-start(bf16[4,96,768]{2,1,0:T(8,128)(2,1)} %pad_maximum_fusion.10.second_ref) | copy-start | bytes 1769476
  871.3 25.5 %copy-start.17 = (f32[512,96]{1,0:T(8,128)S(1)}, f32[512,96]{1,0:T(8,128)}, u32[]{:S(2)}) copy-start(f32[512,96]{1,0:T(8,128)} %copy.191.mask_ref) | copy-start | bytes 589828
  871.3 25.5 %copy-start.42 = (f32[1,2048]{1,0:T(1,128)S(1)}, f32[1,2048]{1,0:T(1,128)}, u32[]{:S(2)}) copy-start(f32[1,2048]{1,0:T(1,128)} %copy-done.41) | copy-start | bytes 24580
  905.4 34.0 %all-to-all-start.10 = ((bf16[16,36,512]{2,1,0:T(8,128)(2,1)}), bf16[16,36,512]{2,1,0:T(8,128)(2,1)S(1)}, u32[]{:S(2)}, u32[]{:S(2)}) async-start(bf16[16,36,512]{2,1,0:T(8,128)(2,1)} %pad_maximum_fusion.9), calls=%async_computation.11 | async-start | bytes 1310720 | tf_op jit(solution)/shard_map/all_to_all | solution.py:1367
  934.0 13.3 %collective-permute-start.8 = (bf16[512,512]{1,0:T(8,128)(2,1)S(1)}, bf16[512,512]{1,0:T(8,128)(2,1)S(1)}, u32[]{:S(2)}, u32[]{:S(2)}) collective-permute-start(bf16[512,512]{1,0:T(8,128)(2,1)S(1)} %get-tuple-element.305), channel_id=1, source_target_pairs={{0,4},{4,8},{8,12},{12,0},{1,5},{5,9},{9,13},{13,1},{2,6},{6,10},{... | collective-permute-start | bytes 1572872 | tf_op jit(solution)/shard_map/ppermute | solution.py:883
  934.5 14.9 %collective-permute-start.9 = (bf16[512,512]{1,0:T(8,128)(2,1)S(1)}, bf16[512,512]{1,0:T(8,128)(2,1)}, u32[]{:S(2)}, u32[]{:S(2)}) collective-permute-start(bf16[512,512]{1,0:T(8,128)(2,1)S(1)} %get-tuple-element.304), channel_id=1, source_target_pairs={{0,8},{4,12},{8,0},{12,4},{1,9},{5,13},{9,1},{13,5},{2,10},{6,14},... | collective-permute-start | bytes 1572872 | tf_op jit(solution)/shard_map/ppermute | solution.py:883
  936.1 22.8 %collective-permute-start.10 = (bf16[512,512]{1,0:T(8,128)(2,1)S(1)}, bf16[512,512]{1,0:T(8,128)(2,1)}, u32[]{:S(2)}, u32[]{:S(2)}) collective-permute-start(bf16[512,512]{1,0:T(8,128)(2,1)S(1)} %get-tuple-element.303), channel_id=1, source_target_pairs={{0,12},{4,0},{8,4},{12,8},{1,13},{5,1},{9,5},{13,9},{2,14},{6,2},{... | collective-permute-start | bytes 1572872 | tf_op jit(solution)/shard_map/ppermute | solution.py:883
  939.6 20.9 %copy-start.78 = (bf16[36,512]{1,0:T(8,128)(2,1)}, bf16[36,512]{1,0:T(8,128)(2,1)S(1)}, u32[]{:S(2)}) copy-start(bf16[36,512]{1,0:T(8,128)(2,1)S(1)} %convert_reduce_fusion) | copy-start | bytes 110596
  940.3 24.3 %all-to-all-start.11 = ((bf16[8,24,512]{2,1,0:T(8,128)(2,1)}), bf16[8,24,512]{2,1,0:T(8,128)(2,1)S(1)}, u32[]{:S(2)}, u32[]{:S(2)}) async-start(bf16[8,24,512]{2,1,0:T(8,128)(2,1)} %broadcast_in_dim.24), calls=%async_computation.12 | async-start | bytes 393216 | tf_op jit(solution)/shard_map/all_to_all | solution.py:1329
  965.3 8.6 all-to-all-start.12
  (83 other events, 418.0 us)
Sparse Core Ops, SparseCore 0:
  12.5 154.1 all-gather.11
  169.5 224.1 all-gather.13
  395.4 155.3 all-gather.15
  684.0 66.3 reduce-scatter.1
  766.1 34.1 all-gather.19
  802.9 40.0 all-gather.17

commit v5 on v4

--- a/solution.py
+++ b/solution.py
@@ -524,14 +524,31 @@
     elif not fresh:
         refs = refs[1:]
     sums_ref, grad_out_ref, hidden_ref, low_down_ref = refs[:4]
-    low_refs, turned_refs, sum_refs = refs[4:7], refs[7:10], refs[10:13]
-    grad_ref = refs[13] if len(refs) > 13 else grad_out_ref
+    low_refs, turned_refs, sum_refs, arrived = refs[4:7], refs[7:10], refs[10:13], refs[13]
+    grad_ref = refs[14] if len(refs) > 14 else grad_out_ref
     c = pl.program_id(0)
     rows, lanes = gate_ref.shape[1], gate_ref.shape[3]
     rank = second_ref.shape[0]
 
+    def earlier(which):
+        if which == 0:
+            return pltpu.make_async_copy(grad_in_ref, grad_ref, arrived.at[0])
+        height = sums_ref.shape[2]
+        at = pl.ds(pl.multiple_of(group_ref[0] * height, 8), height)
+        return pltpu.make_async_copy(sums_in_ref.at[:, :, at, :], sums_ref, arrived.at[1])
+
+    def arrive(which):
+        if goes_on:
+
+            @pl.when(c == 0)
+            def _():
+                earlier(which).wait()
+
     @pl.when(c == 0)
     def _():
+        if goes_on:
+            earlier(0).start()
+            earlier(1).start()
         low_front = nt(h_ref[...], first_ref[...])
         lows = low_front[:, :rank], low_front[:, rank:], nt(e_ref[...], second_ref[...])
         for low, low_ref, turned_ref, sum_ref in zip(lows, low_refs, turned_refs, sum_refs):
@@ -539,10 +556,7 @@
             low_ref[...] = low.astype(jnp.bfloat16)
             turned_ref[...] = low.T.astype(jnp.bfloat16)
             sum_ref[...] = jnp.zeros_like(sum_ref)
-        if goes_on:
-            grad_ref[...] = grad_in_ref[...]
-            sums_ref[...] = sums_in_ref[...]
-        else:
+        if not goes_on:
             grad_ref[...] = jnp.zeros_like(grad_ref)
             sums_ref[...] = jnp.zeros_like(sums_ref)
 
@@ -558,6 +572,7 @@
     hidden = (swish * up).astype(jnp.bfloat16)
     gate_grad = (upstream * up * (sigmoid + swish * (1.0 - sigmoid))).astype(jnp.bfloat16)
     up_grad = (upstream * swish).astype(jnp.bfloat16)
+    arrive(0)
     for r in range(rows):
         at = slice(r * lanes, (r + 1) * lanes)
         grad_ref[:, at] += nt(gate_grad, gate_ref[0, r]) + nt(up_grad, up_ref[0, r])
@@ -568,6 +583,7 @@
     col_sum = jnp.concatenate([nn(turned_ref[...], out) for turned_ref, out in zip(turned_refs, outs)], axis=0)
     row_share, col_share = 3 * rank // sums_ref.shape[1], 3 * rank // rows
     begin = share_height(row_share) + block * share_height(col_share)
+    arrive(1)
     for r in range(rows):
         sums_ref[r, c, begin : begin + col_share] = col_sum[r * col_share : (r + 1) * col_share]
 
@@ -606,6 +622,7 @@
     scratch = [pltpu.VMEM((count, rank), jnp.bfloat16)] * 3
     scratch += [pltpu.VMEM((rank, count), jnp.bfloat16)] * 3
     scratch += [pltpu.VMEM((count, rank), jnp.float32)] * 3
+    scratch += [pltpu.SemaphoreType.DMA((2,))]
     if dtype != jnp.float32:
         scratch += [pltpu.VMEM((count, features), jnp.float32)]
     return pl.pallas_call(
@@ -624,8 +641,8 @@
                 weights(2),
                 pl.BlockSpec((1, 1, 3, rank, lanes), lambda c, g: (c, g[0], 0, 0, 0)),
             ]
-            + ([] if fresh else [buffered_once(sums_shape, lambda c, g: (0, 0, g[0], 0)) if goes_on else anywhere])
-            + ([whole((count, features))] if goes_on else []),
+            + ([] if fresh else [anywhere])
+            + ([anywhere] if goes_on else []),
             out_specs=[
                 pl.BlockSpec(sums_shape, lambda c, g: (0, 0, g[0], 0)),
                 pl.BlockSpec((count, features), lambda c, g: (0, 0)),
@@ -1302,9 +1319,7 @@
             last,
         )
         if last:
-            query_now, mixed_parts, row_total, col_total, query_moved = ordered(
-                (query_now, mixed_parts, row_total, col_total, query_moved)
-            )
+            query_now, mixed_parts, query_moved = ordered((query_now, mixed_parts, query_moved))
             if pair_pad:
                 query_now = jnp.concatenate([query_now[:, :pair_width], query_now[:, -2 * HEAD_DIM :]], axis=1)
         else:
@@ -1366,6 +1381,7 @@
     )
     attn_sums = jnp.sum(lax.all_to_all(attn_shares, both, 0, 0, tiled=True).astype(jnp.float32), axis=0)
     token_parts = send_features(token_grad)
+    attn_sums, row_total, col_total = ordered((attn_sums, row_total, col_total))
     attn_rows, token_parts[0] = ordered((attn_sums[:cut], token_parts[0]))
     attn_rows = everywhere(attn_rows, ("dp", "col"), copies * cols)
     attn_cols, attn_rows = ordered((attn_sums[cut:], attn_rows))

time: 990 us -> 985 us (level)
  no operation moved by 1% of the time
where the time goes in v5:
time: 985 us; the launch traced here: 978 us
  Pallas kernels  463 us (47%)
  blocking collectives  162 us (16%)
  local copies, waits for them, and re-layouts  112 us (11%)
  waiting for transfers between devices  99.7 us (10%)
  starting transfers between devices  75.5 us (8%)
  other arithmetic  30.9 us (3%)
  between operations  17.9 us (2%)
  matrix products  17.6 us (2%)
    pallas_call x4, Pallas kernels, feed_forward(): pl.pallas_call(functools.partial(mlp_kernel, fresh, goes_on, block), grid...  152 us
    pallas_call x2, Pallas kernels, attend_back(): pl.pallas_call(functools.partial(bwd_kernel, heads, factor, last), grid=(...  126 us
    pallas_call x2, Pallas kernels, attend(): pl.pallas_call(functools.partial(fwd_kernel, heads, factor), grid=(length...  82.8 us
    all_to_all x1, blocking collectives, exchange(): lax.all_to_all(values.reshape(units, part, -1), turned_both, 0, 0, tiled=...  77.2 us
    all_to_all x1, blocking collectives, to_tokens(): moved = lax.all_to_all(cut, 'row', 0, 0, tiled=True)  49.7 us
    unnamed x235, local copies, waits for them, and re-layouts  45.2 us
    all_to_all x7, starting transfers between devices, exchange(): lax.all_to_all(values.reshape(units, part, -1), turned_both, 0, 0, tiled=...  37.7 us
    pallas_call x4, Pallas kernels, project_down(): pl.pallas_call(down_kernel, grid=(rows,), in_specs=[pl.BlockSpec((rank, l...  36.6 us
  transfers between devices with their start and end apart: 28, of which 11 were waited for; matrix products, arithmetic and copies ran while one was open for 12% of the time, Pallas kernels for 41%

profile of v5, /device:TPU:0, one launch (start us, length us, event | category | flops | bytes accessed | tf_op | source)
XLA Modules:
  0.0 978.3 jit_solution(5241873227909759179)
XLA Ops:
  9.9 2.5 concatenate.131
  13.9 5.2 all-reduce.5
  19.7 2.6 fusion.45
  24.2 29.6 %all-gather.5 = bf16[16,53,512]{2,1,0:T(8,128)(2,1)S(1)} all-gather(bf16[1,53,512]{2,1,0:T(8,128)(2,1)S(1)} %maximum_bitcast_fusion.4), channel_id=2, replica_groups=mesh['dp'=2,'row'=4,'col'=4] {'col','row'}, dimensions={0}, use_global_device_ids=true | all-gather | bytes 922624 | tf_op jit(solution)/shard_map/all_gather | solution.py:1059
  56.7 4.5 all-to-all-start
  100.3 9.5 all-to-all-done
  109.7 3.2 copy.179
  116.1 49.7 %all_to_all.65 = bf16[4,2,256,512]{3,2,1,0:T(8,128)(2,1)S(1)} all-to-all(bf16[4,2,256,512]{3,2,1,0:T(8,128)(2,1)S(1)} %copy.189), channel_id=1, replica_groups=mesh['dp'=2,'row'=4,'col'=4] {'row'}, dimensions={0} | all-to-all | bytes 4194304 | tf_op jit(solution)/shard_map/all_to_all | solution.py:888
  174.8 16.7 %project_qkv.1 = (bf16[2,4,2,256,256]{4,3,2,1,0:T(8,128)(2,1)}, bf16[2,4,2,256,128]{4,3,2,1,0:T(8,128)(2,1)S(1)}, bf16[512,96]{1,0:T(8,128)(2,1)S(1)}) custom-call(bf16[512,2048]{1,0:T(8,128)(2,1)} %bitcast.270, f32[1,2048]{1,0:T(1,128)S(1)} %get-tuple-element.373.gain_ref, f32[512,96]{1,0:T(8,128)S(1)} %copy-done.16, bf16[96,2048]{1,0:T(8,128)(2,1)S(1)} %bitcast.287, ...), custom_call_target="tpu_custom_call" | custom-call | flops 6442450944 | bytes 16777216 | tf_op jit(solution)/shard_map/project_qkv/pallas_call | solution.py:342
  192.5 77.2 %all_to_all.66 = bf16[16,256,256]{2,1,0:T(8,128)(2,1)S(1)} all-to-all(bf16[16,256,256]{2,1,0:T(8,128)(2,1)} %bitcast.383), channel_id=1, replica_groups=mesh['dp'=2,'row'=4,'col'=4] {'col','row'}, dimensions={0} | all-to-all | bytes 4194304 | tf_op jit(solution)/shard_map/all_to_all | solution.py:1154
  269.8 3.7 all-to-all-start.4
  273.9 4.6 slice.569
  279.9 41.5 %attend_forward.2 = (bf16[4096,128]{1,0:T(8,128)(2,1)S(1)}, f32[8,4096]{1,0:T(8,128)S(1)}) custom-call(s32[1,4096]{1,0:T(1,128)S(1)} %bitcast.307, bf16[4096,256]{1,0:T(8,128)(2,1)S(1)} %bitcast.280, bf16[4096,256]{1,0:T(8,128)(2,1)S(1)} %bitcast.281), custom_call_target="tpu_custom_call" | custom-call | flops 4294967296 | bytes 3670016 | tf_op jit(solution)/shard_map/attend_forward/pallas_call | solution.py:109
  324.1 6.1 all-to-all-start.3
  331.4 41.3 %attend_forward.3 = (bf16[4096,128]{1,0:T(8,128)(2,1)S(1)}, f32[8,4096]{1,0:T(8,128)S(1)}) custom-call(s32[1,4096]{1,0:T(1,128)S(1)} %bitcast.308, bf16[4096,128]{1,0:T(8,128)(2,1)S(1)} %bitcast.292, bf16[4096,256]{1,0:T(8,128)(2,1)S(1)} %bitcast.282), custom_call_target="tpu_custom_call" | custom-call | flops 4294967296 | bytes 3670016 | tf_op jit(solution)/shard_map/attend_forward/pallas_call | solution.py:109
  374.3 6.3 all-to-all-start.5
  383.4 10.4 %all-gather.14.cloned.1.call-done = bf16[26880,512]{1,0:T(8,128)(2,1)} async-done(((bf16[1680,512]{1,0:T(8,128)(2,1)}), bf16[26880,512]{1,0:T(8,128)(2,1)}) %all-gather.14.cloned.1.call-update) | async-done | bytes 27525136 | tf_op jit(solution)/shard_map/all_gather | solution.py:1164
  398.8 11.8 %all-to-all-done.5 = bf16[16,256,128]{2,1,0:T(8,128)(2,1)S(1)} async-done(((bf16[16,256,128]{2,1,0:T(8,128)(2,1)}), bf16[16,256,128]{2,1,0:T(8,128)(2,1)S(1)}, u32[]{:S(2)}, u32[]{:S(2)}) %all-to-all-start.5) | async-done | bytes 1048608 | tf_op jit(solution)/shard_map/all_to_all | solution.py:1154
  410.7 12.6 %project_out.1 = (f32[512,2048]{1,0:T(8,128)}, bf16[512,2048]{1,0:T(8,128)(2,1)}, bf16[512,32]{1,0:T(8,128)(2,1)S(1)}) custom-call(s32[1]{0:T(128)} %bitcast.68.me_ref, bf16[2,4,2,256,128]{4,3,2,1,0:T(8,128)(2,1)S(1)} %bitcast.274, bf16[2,4,2,256,128]{4,3,2,1,0:T(8,128)(2,1)S(1)} %bitcast.276, bf16[512,2048]{1,0:T(8,128)(2,1)} %bitcast.271, ...), custom_call_target="tpu_custom_call" | custom-call | flops 4294967296 | bytes 18874368 | tf_op jit(solution)/shard_map/project_out/pallas_call | solution.py:751
  424.6 37.5 %feed_forward.4 = (f32[4,4,144,512]{3,2,1,0:T(8,128)}, f32[512,2048]{1,0:T(8,128)}, bf16[512,2048]{1,0:T(8,128)(2,1)}, bf16[512,32]{1,0:T(8,128)(2,1)}) custom-call(s32[1]{0:T(128)} %bitcast.69.group_ref, bf16[512,2048]{1,0:T(8,128)(2,1)} %get-tuple-element.135.h_ref, bf16[512,2048]{1,0:T(8,128)(2,1)} %bitcast.339, f32[512,32]{1,0:T(8,128)} %copy-done.3, ...), custom_call_target="tpu_custom_call" | custom-call | flops 21474836480 | bytes 37748736 | tf_op jit(solution)/shard_map/feed_forward/pallas_call | solution.py:628
  464.6 9.1 project_down.4.refs_0_
  477.3 38.0 %feed_forward.5 = (f32[4,4,144,512]{3,2,1,0:T(8,128)}, f32[512,2048]{1,0:T(8,128)}, bf16[512,2048]{1,0:T(8,128)(2,1)}, bf16[512,32]{1,0:T(8,128)(2,1)}) custom-call(s32[1]{0:T(128)} %bitcast.73.group_ref, bf16[512,2048]{1,0:T(8,128)(2,1)} %copy-done.51, bf16[512,2048]{1,0:T(8,128)(2,1)} %collective-permute-done.2.e_ref, ...), custom_call_target="tpu_custom_call", output_to_operand_aliasing={{0}: (10, {})} | custom-call | flops 21474836480 | bytes 37748736 | tf_op jit(solution)/shard_map/feed_forward/pallas_call | solution.py:628
  517.9 8.9 project_down.5.refs_0_
  526.8 23.9 %all-gather.16.cloned.1.call-done = bf16[24576,512]{1,0:T(8,128)(2,1)} async-done(((bf16[1536,512]{1,0:T(8,128)(2,1)}), bf16[24576,512]{1,0:T(8,128)(2,1)}) %all-gather.16.cloned.1.call-update) | async-done | bytes 25165840 | tf_op jit(solution)/shard_map/all_gather | solution.py:1164
  550.8 37.7 %feed_forward.6 = (f32[4,4,144,512]{3,2,1,0:T(8,128)}, bf16[512,2048]{1,0:T(8,128)(2,1)}, bf16[512,2048]{1,0:T(8,128)(2,1)}, bf16[512,32]{1,0:T(8,128)(2,1)}) custom-call(s32[1]{0:T(128)} %bitcast.73.group_ref, bf16[512,2048]{1,0:T(8,128)(2,1)} %copy-done.51, bf16[512,2048]{1,0:T(8,128)(2,1)} %collective-permute-done.2.e_ref, ...), custom_call_target="tpu_custom_call", output_to_operand_aliasing={{0}: (10, {})} | custom-call | flops 21474836480 | bytes 37748736 | tf_op jit(solution)/shard_map/feed_forward/pallas_call | solution.py:628
  590.0 38.6 %feed_forward.7 = (f32[4,4,144,512]{3,2,1,0:T(8,128)}, f32[512,2048]{1,0:T(8,128)}, bf16[512,2048]{1,0:T(8,128)(2,1)}, bf16[512,32]{1,0:T(8,128)(2,1)}) custom-call(s32[1]{0:T(128)} %bitcast.69.group_ref, bf16[512,2048]{1,0:T(8,128)(2,1)} %get-tuple-element.135.h_ref, bf16[512,2048]{1,0:T(8,128)(2,1)} %bitcast.340, ...), custom_call_target="tpu_custom_call", output_to_operand_aliasing={{0}: (10, {})} | custom-call | flops 21474836480 | bytes 37748736 | tf_op jit(solution)/shard_map/feed_forward/pallas_call | solution.py:628
  628.6 8.0 collective-permute-done.3.other_ref
  637.9 16.4 %project_out_back.1 = (f32[512,2048]{1,0:T(8,128)}, bf16[4,32,512]{2,1,0:T(8,128)(2,1)}, bf16[4,32,512]{2,1,0:T(8,128)(2,1)}, bf16[2,4,2,256,128]{4,3,2,1,0:T(8,128)(2,1)}, bf16[2,4,2,256,128]{4,3,2,1,0:T(8,128)(2,1)}) custom-call(s32[1]{0:T(128)} %bitcast.68.me_ref, f32[512,2048]{1,0:T(8,128)} %get-tuple-element.151.own_ref, bf16[512,2048]{1,0:T(8,128)(2,1)} %copy-done.54, ...), custom_call_target="tpu_custom_call" | custom-call | flops 4294967296 | bytes 27262976 | tf_op jit(solution)/shard_map/project_out_back/pallas_call | solution.py:823
  654.3 4.7 all-to-all-start.6
  659.1 2.7 convert_element_type.176
  664.4 8.4 project_down.7
  672.7 10.3 %project_down.6 = f32[4,512,512]{2,1,0:T(8,128)} custom-call(bf16[32,2048]{1,0:T(8,128)(2,1)S(1)} %get-tuple-element.343.second_ref, bf16[512,2048]{1,0:T(8,128)(2,1)S(1)} %copy-done.9, bf16[512,32]{1,0:T(8,128)(2,1)S(1)} %copy-done.37, bf16[4,4,1536,512]{3,2,1,0:T(8,128)(2,1)} %bitcast.328, f32[4,512,512]{2,1,0:T(8,128)} %project_down.4.refs_0_, ...), custom_call_target="tpu_custom_call" | custom-call | flops 4294967296 | bytes 16777216 | tf_op jit(solution)/shard_map/project_down/pallas_call | solution.py:686
  684.6 2.8 multiply_sine_fusion
  687.4 6.0 all-to-all-start.7
  699.1 62.8 %attend_backward.2 = (bf16[4096,128]{1,0:T(8,128)(2,1)S(1)}, f32[4096,128]{1,0:T(8,128)}) custom-call(s32[1,4096]{1,0:T(1,128)S(1)} %bitcast.309, f32[32,4096]{1,0:T(8,128)S(1)} %bitcast.304, f32[32,4096]{1,0:T(8,128)S(1)} %bitcast.302, bf16[4096,256]{1,0:T(8,128)(2,1)} %bitcast.283, bf16[4096,128]{1,0:T(8,128)(2,1)S(1)} %bitcast.301, ...), custom_call_target="tpu_custom_call" | custom-call | flops 10737418240 | bytes 6291456 | tf_op jit(solution)/shard_map/attend_backward/pallas_call | solution.py:245
  765.2 6.0 all-to-all-start.8
  772.6 5.0 fusion.4
  780.9 63.2 %attend_backward.3 = bf16[4096,256]{1,0:T(8,128)(2,1)} custom-call(s32[1,4096]{1,0:T(1,128)S(1)} %bitcast.310, f32[32,4096]{1,0:T(8,128)S(1)} %bitcast.305, f32[32,4096]{1,0:T(8,128)S(1)} %bitcast.303, bf16[4096,128]{1,0:T(8,128)(2,1)S(1)} %bitcast.293, bf16[4096,128]{1,0:T(8,128)(2,1)S(1)} %bitcast.297, bf16[4096,128]{1,0:T(8,128)(2,1)S(1)} %copy-done.22, ...), custom_call_target="tpu_custom_call" | custom-call | flops 10737418240 | bytes 6291456 | tf_op jit(solution)/shard_map/attend_backward/pallas_call | solution.py:245
  845.1 4.9 all-to-all-start.9
  852.0 3.5 copy.196
  873.0 18.1 %all-to-all-done.9 = bf16[16,256,256]{2,1,0:T(8,128)(2,1)} async-done(((bf16[16,256,256]{2,1,0:T(8,128)(2,1)}), bf16[16,256,256]{2,1,0:T(8,128)(2,1)}, u32[]{:S(2)}, u32[]{:S(2)}) %all-to-all-start.9) | async-done | bytes 2097184 | tf_op jit(solution)/shard_map/all_to_all | solution.py:1154
  893.2 4.8 qkv_grad_sums.1
  899.7 11.2 %all-to-all-start.10 = ((bf16[16,36,512]{2,1,0:T(8,128)(2,1)}), bf16[16,36,512]{2,1,0:T(8,128)(2,1)S(1)}, u32[]{:S(2)}, u32[]{:S(2)}) async-start(bf16[16,36,512]{2,1,0:T(8,128)(2,1)} %pad_maximum_fusion.9), calls=%async_computation.11 | async-start | bytes 1310720 | tf_op jit(solution)/shard_map/all_to_all | solution.py:1382
  910.9 15.6 %project_qkv_back.1 = bf16[4,512,512]{2,1,0:T(8,128)(2,1)} custom-call(bf16[512,2048]{1,0:T(8,128)(2,1)} %bitcast.272, f32[512,2048]{1,0:T(8,128)} %get-tuple-element.198.attended_ref, f32[1,2048]{1,0:T(1,128)} %copy-done.41, bf16[96,2048]{1,0:T(8,128)(2,1)} %bitcast.286, bf16[512,96]{1,0:T(8,128)(2,1)} %copy-done.45, ...), custom_call_target="tpu_custom_call" | custom-call | flops 25769803776 | bytes 23068672 | tf_op jit(solution)/shard_map/project_qkv_back/pallas_call | solution.py:494
  934.8 4.6 all-to-all-start.11
  943.6 9.6 collective-permute-done.10
  955.4 3.5 copy.207
  959.6 3.4 all-to-all-start.12
  (461 shorter events, 152.4 us)
Async XLA Ops:
  7.2 61.9 %copy-start = (bf16[128,2048]{1,0:T(8,128)(2,1)S(1)}, bf16[128,2048]{1,0:T(8,128)(2,1)}, u32[]{:S(2)}) copy-start(bf16[128,2048]{1,0:T(8,128)(2,1)} %param.51) | copy-start | bytes 1572868
  7.2 164.6 %all-gather.12.cloned.1.call-start = ((), (), s32[]{:S(2)}) async-start(), calls=%async_computation.14 | async-start | bytes 20054016 | tf_op jit(solution)/shard_map/all_gather | solution.py:1104
  19.1 50.4 %copy-start.69 = (s32[64]{0:T(128)}, s32[64]{0:T(128)S(1)}, u32[]{:S(2)}) copy-start(s32[64]{0:T(128)S(1)} %and_select_fusion.1) | copy-start | bytes 772
  22.3 47.2 %copy-start.67 = (s32[64]{0:T(128)}, s32[64]{0:T(128)S(1)}, u32[]{:S(2)}) copy-start(s32[64]{0:T(128)S(1)} %fusion.45) | copy-start | bytes 772
  22.4 47.2 %copy-start.71 = (s32[128]{0:T(128)}, s32[128]{0:T(128)S(1)}, u32[]{:S(2)}) copy-start(s32[128]{0:T(128)S(1)} %get-tuple-element.399) | copy-start | bytes 1540
  22.4 47.2 %copy-start.74 = (s32[128]{0:T(128)}, s32[128]{0:T(128)S(1)}, u32[]{:S(2)}) copy-start(s32[128]{0:T(128)S(1)} %get-tuple-element.400) | copy-start | bytes 1540
  23.9 30.9 %copy-start.55 = (bf16[1024,2,512]{2,1,0:T(2,128)(2,1)S(1)}, bf16[1024,2,512]{2,1,0:T(2,128)(2,1)}, u32[]{:S(2)}) copy-start(bf16[1024,2,512]{2,1,0:T(2,128)(2,1)} %param.28) | copy-start | bytes 6291460
  54.1 22.7 %copy-start.53 = (bf16[4,4,33,512]{3,0,2,1:T(4,128)(2,1)}, bf16[4,4,33,512]{3,0,2,1:T(4,128)(2,1)S(1)}, u32[]{:S(2)}) copy-start(bf16[4,4,33,512]{3,0,2,1:T(4,128)(2,1)S(1)} %copy.176) | copy-start | bytes 1622020
  56.7 53.0 %all-to-all-start = ((bf16[4,2,256,512]{3,2,1,0:T(8,128)(2,1)}), bf16[4,2,256,512]{3,2,1,0:T(8,128)(2,1)}, u32[]{:S(2)}, u32[]{:S(2)}) async-start(bf16[4,2,256,512]{3,2,1,0:T(8,128)(2,1)} %copy.178), calls=%async_computation | async-start | bytes 4194304 | tf_op jit(solution)/shard_map/all_to_all | solution.py:888
  61.2 332.6 %all-gather.14.cloned.1.call-start = ((), (), s32[]{:S(2)}) async-start(), calls=%async_computation.16 | async-start | bytes 29245440 | tf_op jit(solution)/shard_map/all_gather | solution.py:1164
  75.9 334.8 %copy-start.3 = (f32[512,32]{1,0:T(8,128)}, f32[512,32]{1,0:T(8,128)S(1)}, u32[]{:S(2)}) copy-start(f32[512,32]{1,0:T(8,128)S(1)} %compare_select_fusion.refs_4_.mask_ref) | copy-start | bytes 196612
  169.4 381.3 %all-gather.16.cloned.1.call-start = ((), (), s32[]{:S(2)}) async-start(), calls=%async_computation.17 | async-start | bytes 26738688 | tf_op jit(solution)/shard_map/all_gather | solution.py:1164
  171.8 238.9 %copy-start.40 = (f32[1,2048]{1,0:T(1,128)}, f32[1,2048]{1,0:T(1,128)S(1)}, u32[]{:S(2)}) copy-start(f32[1,2048]{1,0:T(1,128)S(1)} %get-tuple-element.372.refs_3_.gain_ref) | copy-start | bytes 24580
  191.6 78.2 %copy-start.43 = (bf16[512,96]{1,0:T(8,128)(2,1)}, bf16[512,96]{1,0:T(8,128)(2,1)S(1)}, u32[]{:S(2)}) copy-start(bf16[512,96]{1,0:T(8,128)(2,1)S(1)} %get-tuple-element.189.low_ref) | copy-start | bytes 294916
  269.8 60.4 %copy-start.12 = (bf16[16,256,256]{2,1,0:T(8,128)(2,1)}, bf16[16,256,256]{2,1,0:T(8,128)(2,1)S(1)}, u32[]{:S(2)}) copy-start(bf16[16,256,256]{2,1,0:T(8,128)(2,1)S(1)} %all_to_all.66) | copy-start | bytes 6291460
  269.8 53.3 %all-to-all-start.4 = ((bf16[16,256,128]{2,1,0:T(8,128)(2,1)}), bf16[16,256,128]{2,1,0:T(8,128)(2,1)S(1)}, u32[]{:S(2)}, u32[]{:S(2)}) async-start(bf16[16,256,128]{2,1,0:T(8,128)(2,1)} %bitcast.300), calls=%async_computation.4 | async-start | bytes 2097152 | tf_op jit(solution)/shard_map/all_to_all | solution.py:1154
  278.4 132.2 %collective-permute-start = (bf16[4,4,512,256]{3,2,1,0:T(8,128)(2,1)}, bf16[4,4,512,256]{3,2,1,0:T(8,128)(2,1)}, u32[]{:S(2)}, u32[]{:S(2)}) collective-permute-start(bf16[4,4,512,256]{3,2,1,0:T(8,128)(2,1)} %slice.569), channel_id=1, source_target_pairs={{0,16},{16,0},{1,17},{17,1},{2,18},{18,2},{3,19},{19,3},{4,20},{20... | collective-permute-start | bytes 12582920 | tf_op jit(solution)/shard_map/ppermute | solution.py:1190
  324.1 50.3 %all-to-all-start.3 = ((bf16[16,256,128]{2,1,0:T(8,128)(2,1)}), bf16[16,256,128]{2,1,0:T(8,128)(2,1)S(1)}, u32[]{:S(2)}, u32[]{:S(2)}) async-start(bf16[16,256,128]{2,1,0:T(8,128)(2,1)} %bitcast.299), calls=%async_computation.3 | async-start | bytes 2097152 | tf_op jit(solution)/shard_map/all_to_all | solution.py:1154
  374.3 36.4 %copy-start.4 = (bf16[16,256,128]{2,1,0:T(8,128)(2,1)}, bf16[16,256,128]{2,1,0:T(8,128)(2,1)S(1)}, u32[]{:S(2)}) copy-start(bf16[16,256,128]{2,1,0:T(8,128)(2,1)S(1)} %all-to-all-done.3) | copy-start | bytes 3145732
  374.3 36.3 %all-to-all-start.5 = ((bf16[16,256,128]{2,1,0:T(8,128)(2,1)}), bf16[16,256,128]{2,1,0:T(8,128)(2,1)S(1)}, u32[]{:S(2)}, u32[]{:S(2)}) async-start(bf16[16,256,128]{2,1,0:T(8,128)(2,1)} %bitcast.294), calls=%async_computation.5 | async-start | bytes 2097152 | tf_op jit(solution)/shard_map/all_to_all | solution.py:1154
  382.7 28.0 %copy-start.14 = (bf16[4,8,4,512]{3,1,2,0:T(8,128)(2,1)}, bf16[4,8,4,512]{3,1,2,0:T(8,128)(2,1)S(1)}, u32[]{:S(2)}) copy-start(bf16[4,8,4,512]{3,1,2,0:T(8,128)(2,1)S(1)} %copy.231) | copy-start | bytes 393220
  382.8 28.0 %copy-start.15 = (bf16[4,8,4,512]{3,1,2,0:T(8,128)(2,1)}, bf16[4,8,4,512]{3,1,2,0:T(8,128)(2,1)S(1)}, u32[]{:S(2)}) copy-start(bf16[4,8,4,512]{3,1,2,0:T(8,128)(2,1)S(1)} %copy.230) | copy-start | bytes 393220
  382.8 90.9 %collective-permute-start.2 = (bf16[512,2048]{1,0:T(8,128)(2,1)}, bf16[512,2048]{1,0:T(8,128)(2,1)}, u32[]{:S(2)}, u32[]{:S(2)}) collective-permute-start(bf16[512,2048]{1,0:T(8,128)(2,1)} %bitcast.338), channel_id=1, source_target_pairs={{0,16},{16,0},{1,17},{17,1},{2,18},{18,2},{3,19},{19,3},{4,20},{20... | collective-permute-start | bytes 6291464 | tf_op jit(solution)/shard_map/ppermute | solution.py:1190
  397.5 27.1 %copy-start.50 = (bf16[4,8,8,512]{3,2,0,1:T(8,128)(2,1)}, bf16[4,8,8,512]{3,2,0,1:T(8,128)(2,1)S(1)}, u32[]{:S(2)}) copy-start(bf16[4,8,8,512]{3,2,0,1:T(8,128)(2,1)S(1)} %copy.222) | copy-start | bytes 786436
  424.0 52.0 %collective-permute-start.1 = (bf16[512,2048]{1,0:T(8,128)(2,1)}, bf16[512,2048]{1,0:T(8,128)(2,1)S(1)}, u32[]{:S(2)}, u32[]{:S(2)}) collective-permute-start(bf16[512,2048]{1,0:T(8,128)(2,1)} %get-tuple-element.135.h_ref), channel_id=1, source_target_pairs={{0,16},{16,0},{1,17},{17,1},{2,18},{18,2},{3,19},{19,3},{4,20},{20... | collective-permute-start | bytes 6291464 | tf_op jit(solution)/shard_map/ppermute | solution.py:1190
  588.5 48.1 %collective-permute-start.3 = (bf16[512,2048]{1,0:T(8,128)(2,1)}, bf16[512,2048]{1,0:T(8,128)(2,1)S(1)}, u32[]{:S(2)}, u32[]{:S(2)}) collective-permute-start(bf16[512,2048]{1,0:T(8,128)(2,1)} %get-tuple-element.152), channel_id=1, source_target_pairs={{0,16},{16,0},{1,17},{17,1},{2,18},{18,2},{3,19},{19,3},{4,20},{20... | collective-permute-start | bytes 6291464 | tf_op jit(solution)/shard_map/ppermute | solution.py:1190
  654.3 28.8 %all-to-all-start.6 = ((bf16[16,256,128]{2,1,0:T(8,128)(2,1)}), bf16[16,256,128]{2,1,0:T(8,128)(2,1)S(1)}, u32[]{:S(2)}, u32[]{:S(2)}) async-start(bf16[16,256,128]{2,1,0:T(8,128)(2,1)} %bitcast.393), calls=%async_computation.6 | async-start | bytes 2097152 | tf_op jit(solution)/shard_map/all_to_all | solution.py:1154
  659.0 103.8 %reduce-scatter.2.cloned.1.call-start = ((), (), s32[]{:S(2)}) async-start(), calls=%async_computation.15 | async-start | bytes 2785280 | tf_op jit(solution)/shard_map/reduce_scatter | solution.py:1279
  683.1 79.7 %collective-permute-start.4 = (bf16[4,512,512]{2,1,0:T(8,128)(2,1)S(1)}, bf16[4,512,512]{2,1,0:T(8,128)(2,1)}, u32[]{:S(2)}, u32[]{:S(2)}) collective-permute-start(bf16[4,512,512]{2,1,0:T(8,128)(2,1)S(1)} %project_down.7), channel_id=1, source_target_pairs={{0,16},{16,0},{1,17},{17,1},{2,18},{18,2},{3,19},{19,3},{4,20},{20... | collective-permute-start | bytes 6291464 | tf_op jit(solution)/shard_map/ppermute | solution.py:1190
  687.4 77.7 %all-to-all-start.7 = ((bf16[16,256,128]{2,1,0:T(8,128)(2,1)}), bf16[16,256,128]{2,1,0:T(8,128)(2,1)S(1)}, u32[]{:S(2)}, u32[]{:S(2)}) async-start(bf16[16,256,128]{2,1,0:T(8,128)(2,1)} %bitcast.392), calls=%async_computation.7 | async-start | bytes 2097152 | tf_op jit(solution)/shard_map/all_to_all | solution.py:1154
  693.5 162.0 %all-gather.20.cloned.1.call-start = ((), (), s32[]{:S(2)}) async-start(), calls=%async_computation.19 | async-start | bytes 1179648 | tf_op jit(solution)/shard_map/all_gather | solution.py:1306
  765.2 78.9 %all-to-all-start.8 = ((bf16[16,256,128]{2,1,0:T(8,128)(2,1)}), bf16[16,256,128]{2,1,0:T(8,128)(2,1)S(1)}, u32[]{:S(2)}, u32[]{:S(2)}) async-start(bf16[16,256,128]{2,1,0:T(8,128)(2,1)} %bitcast.298), calls=%async_computation.9 | async-start | bytes 2097152 | tf_op jit(solution)/shard_map/all_to_all | solution.py:1154
  771.2 86.4 %all-gather.18.cloned.1.call-start = ((), (), s32[]{:S(2)}) async-start(), calls=%async_computation.18 | async-start | bytes 1179648 | tf_op jit(solution)/shard_map/all_gather | solution.py:1305
  777.5 66.6 %collective-permute-start.5 = (bf16[512,512]{1,0:T(8,128)(2,1)}, bf16[512,512]{1,0:T(8,128)(2,1)}, u32[]{:S(2)}, u32[]{:S(2)}) collective-permute-start(bf16[512,512]{1,0:T(8,128)(2,1)} %get-tuple-element.294), channel_id=1, source_target_pairs={{0,4},{4,8},{8,12},{12,0},{1,5},{5,9},{9,13},{13,1},{2,6},{6,10},{... | collective-permute-start | bytes 1572872 | tf_op jit(solution)/shard_map/ppermute | solution.py:900
  777.9 66.2 %collective-permute-start.6 = (bf16[512,512]{1,0:T(8,128)(2,1)}, bf16[512,512]{1,0:T(8,128)(2,1)}, u32[]{:S(2)}, u32[]{:S(2)}) collective-permute-start(bf16[512,512]{1,0:T(8,128)(2,1)} %get-tuple-element.293), channel_id=1, source_target_pairs={{0,8},{4,12},{8,0},{12,4},{1,9},{5,13},{9,1},{13,5},{2,10},{6,14},... | collective-permute-start | bytes 1572872 | tf_op jit(solution)/shard_map/ppermute | solution.py:900
  779.6 64.5 %collective-permute-start.7 = (bf16[512,512]{1,0:T(8,128)(2,1)}, bf16[512,512]{1,0:T(8,128)(2,1)}, u32[]{:S(2)}, u32[]{:S(2)}) collective-permute-start(bf16[512,512]{1,0:T(8,128)(2,1)} %get-tuple-element.292), channel_id=1, source_target_pairs={{0,12},{4,0},{8,4},{12,8},{1,13},{5,1},{9,5},{13,9},{2,14},{6,2},{... | collective-permute-start | bytes 1572872 | tf_op jit(solution)/shard_map/ppermute | solution.py:900
  845.1 46.0 %all-to-all-start.9 = ((bf16[16,256,256]{2,1,0:T(8,128)(2,1)}), bf16[16,256,256]{2,1,0:T(8,128)(2,1)}, u32[]{:S(2)}, u32[]{:S(2)}) async-start(bf16[16,256,256]{2,1,0:T(8,128)(2,1)} %bitcast.382), calls=%async_computation.10 | async-start | bytes 4194304 | tf_op jit(solution)/shard_map/all_to_all | solution.py:1154
  870.9 20.2 %copy-start.2 = (bf16[64,8,4,512]{3,1,2,0:T(8,128)(2,1)S(1)}, bf16[64,8,4,512]{3,1,2,0:T(8,128)(2,1)}, u32[]{:S(2)}) copy-start(bf16[64,8,4,512]{3,1,2,0:T(8,128)(2,1)} %copy.224) | copy-start | bytes 6291460
  870.9 20.2 %copy-start.7 = (bf16[4,96,768]{2,1,0:T(8,128)(2,1)S(1)}, bf16[4,96,768]{2,1,0:T(8,128)(2,1)}, u32[]{:S(2)}) copy-start(bf16[4,96,768]{2,1,0:T(8,128)(2,1)} %pad_maximum_fusion.10.second_ref) | copy-start | bytes 1769476
  870.9 20.2 %copy-start.17 = (f32[512,96]{1,0:T(8,128)S(1)}, f32[512,96]{1,0:T(8,128)}, u32[]{:S(2)}) copy-start(f32[512,96]{1,0:T(8,128)} %copy.191.mask_ref) | copy-start | bytes 589828
  870.9 20.2 %copy-start.42 = (f32[1,2048]{1,0:T(1,128)S(1)}, f32[1,2048]{1,0:T(1,128)}, u32[]{:S(2)}) copy-start(f32[1,2048]{1,0:T(1,128)} %copy-done.41) | copy-start | bytes 24580
  899.7 34.3 %all-to-all-start.10 = ((bf16[16,36,512]{2,1,0:T(8,128)(2,1)}), bf16[16,36,512]{2,1,0:T(8,128)(2,1)S(1)}, u32[]{:S(2)}, u32[]{:S(2)}) async-start(bf16[16,36,512]{2,1,0:T(8,128)(2,1)} %pad_maximum_fusion.9), calls=%async_computation.11 | async-start | bytes 1310720 | tf_op jit(solution)/shard_map/all_to_all | solution.py:1382
  928.3 13.3 %collective-permute-start.8 = (bf16[512,512]{1,0:T(8,128)(2,1)S(1)}, bf16[512,512]{1,0:T(8,128)(2,1)S(1)}, u32[]{:S(2)}, u32[]{:S(2)}) collective-permute-start(bf16[512,512]{1,0:T(8,128)(2,1)S(1)} %get-tuple-element.303), channel_id=1, source_target_pairs={{0,4},{4,8},{8,12},{12,0},{1,5},{5,9},{9,13},{13,1},{2,6},{6,10},{... | collective-permute-start | bytes 1572872 | tf_op jit(solution)/shard_map/ppermute | solution.py:900
  928.7 14.9 %collective-permute-start.9 = (bf16[512,512]{1,0:T(8,128)(2,1)S(1)}, bf16[512,512]{1,0:T(8,128)(2,1)}, u32[]{:S(2)}, u32[]{:S(2)}) collective-permute-start(bf16[512,512]{1,0:T(8,128)(2,1)S(1)} %get-tuple-element.302), channel_id=1, source_target_pairs={{0,8},{4,12},{8,0},{12,4},{1,9},{5,13},{9,1},{13,5},{2,10},{6,14},... | collective-permute-start | bytes 1572872 | tf_op jit(solution)/shard_map/ppermute | solution.py:900
  930.4 22.8 %collective-permute-start.10 = (bf16[512,512]{1,0:T(8,128)(2,1)S(1)}, bf16[512,512]{1,0:T(8,128)(2,1)}, u32[]{:S(2)}, u32[]{:S(2)}) collective-permute-start(bf16[512,512]{1,0:T(8,128)(2,1)S(1)} %get-tuple-element.301), channel_id=1, source_target_pairs={{0,12},{4,0},{8,4},{12,8},{1,13},{5,1},{9,5},{13,9},{2,14},{6,2},{... | collective-permute-start | bytes 1572872 | tf_op jit(solution)/shard_map/ppermute | solution.py:900
  934.1 20.6 %copy-start.78 = (bf16[36,512]{1,0:T(8,128)(2,1)}, bf16[36,512]{1,0:T(8,128)(2,1)S(1)}, u32[]{:S(2)}) copy-start(bf16[36,512]{1,0:T(8,128)(2,1)S(1)} %convert_reduce_fusion) | copy-start | bytes 110596
  934.8 24.1 %all-to-all-start.11 = ((bf16[8,24,512]{2,1,0:T(8,128)(2,1)}), bf16[8,24,512]{2,1,0:T(8,128)(2,1)S(1)}, u32[]{:S(2)}, u32[]{:S(2)}) async-start(bf16[8,24,512]{2,1,0:T(8,128)(2,1)} %broadcast_in_dim.24), calls=%async_computation.12 | async-start | bytes 393216 | tf_op jit(solution)/shard_map/all_to_all | solution.py:1344
  959.6 8.5 all-to-all-start.12
  (83 other events, 419.2 us)
Sparse Core Ops, SparseCore 0:
  12.5 154.1 all-gather.11
  169.5 224.1 all-gather.13
  395.4 155.3 all-gather.15
  683.2 66.2 reduce-scatter.1
  765.3 34.1 all-gather.19
  802.1 40.0 all-gather.17
